TPU v7x, 32 devices: a whole 2x2x4 slice. The times are simulated.
32 devices in a mesh: ty: 8 (over z, core), tx: 4 (over y, x).
Axes of the slice: x: 2, y: 2, z: 4, core: 2. Of those that a mesh axis runs over, the one named last changes fastest.
Arguments:
- image: float32 [4096, 4096], P('ty', 'tx'), may hold values from -6 to 6
- noise: float32 [2, 4096, 4096], P(None, 'ty', 'tx'), may hold values from -6 to 6
- offsets: int32 [2, 2], replicated, may hold values from 1 to 7, as said below
- key_mask: int32 [256, 256], P('ty', 'tx'), may hold values 0 or 1
- gains: float32 [2, 4096, 4096], P(None, ('ty', 'tx')), may hold values from -1 to 1
- observed: float32 [2, 4096, 4096], P(None, ('ty', 'tx')), may hold values from -6 to 6
- vis_weight: float32 [4096, 4096], P(('ty', 'tx')), may hold values from 0.05 to 1
- w_embed: bfloat16 [256, 512], replicated, may hold values from -0.375 to 0.375
- w_qkv: bfloat16 [2, 512, 1536], replicated, as said below
- w_proj: bfloat16 [2, 512, 512], replicated, may hold values from -0.25 to 0.25
- w_up: bfloat16 [2, 512, 2048], replicated, may hold values from -0.25 to 0.25
- w_down: bfloat16 [2, 2048, 512], replicated, may hold values from -0.125 to 0.125
- w_unembed: bfloat16 [512, 256], replicated, may hold values from -0.25 to 0.25
- norm_gains: float32 [2, 2, 512], replicated, may hold values from 0.1 to 1.9
Outputs:
- sampled: float32 [4096, 4096], P('ty', 'tx')
Inputs may be any that keep to these rules, and one draw needn't show every extreme that they name: `offsets`: each entry lies in 1 to 7, and some entry equals 7. `w_qkv`: columns ordered by query, key or value, then head, then feature of the head.
All inputs are finite; a program needn't handle non-finite values. No bound on the sum of `key_mask` on one device may be relied on, other than what follows from the above.
Results may differ from a plain program's by a relative error of at most 0.04.
Values may be sent and summed in bfloat16 or wider, within the bound.
No kernel may reach another device: no remote copies, remote signals or barrier semaphores. Data moves between devices by JAX's collectives and lax.ppermute only.
A program may use at most 192 MiB of HBM per device.

v0:
```python
import functools
import math

import jax
import jax.numpy as jnp
import ml_dtypes
import numpy as np
from jax import lax
from jax.experimental import pallas as pl
from jax.experimental.pallas import tpu as pltpu
from jax.sharding import PartitionSpec as P

N = 4096
PATCH = 16
PIXELS = PATCH * PATCH
WIN = 8
D = 512
HEADS = 8
STEPS = 2
SPAN = WIN * WIN
LANES = 128
TOK = N // PATCH

SIGMAS = (0.8, 0.5, 0.3)
STEP_SIZES = (0.9, 0.7)
EPSILON = 1e-05
HIGHEST = lax.Precision.HIGHEST
BF16 = jnp.bfloat16
F32 = jnp.float32
GELU_IN = math.sqrt(2.0 / math.pi)
GELU_CUBE = 0.044715 * GELU_IN
VMEM_LIMIT = 56 * 1024 * 1024
PARAMS = pltpu.CompilerParams(vmem_limit_bytes=VMEM_LIMIT)
TN = (((0,), (0,)), ((), ()))
NT = (((1,), (1,)), ((), ()))
NN = (((1,), (0,)), ((), ()))


def mm(left, right, dims=NN):
    return lax.dot_general(left, right, dims, preferred_element_type=F32)


def counting(length):
    return jnp.arange(length, dtype=jnp.int32)


def roots(length, outer, inner, sign):
    product = outer[:, None] * inner[None, :] % length
    angle = 2.0 * math.pi / length * product.astype(F32)
    return (jnp.cos(angle), sign * jnp.sin(angle))


def complex_einsum(form, left, right):
    real = jnp.einsum(form, left[0], right[0], precision=HIGHEST) - jnp.einsum(
        form, left[1], right[1], precision=HIGHEST
    )
    imag = jnp.einsum(form, left[0], right[1], precision=HIGHEST) + jnp.einsum(
        form, left[1], right[0], precision=HIGHEST
    )
    return (real, imag)


def complex_times(left, right):
    return (left[0] * right[0] - left[1] * right[1], left[0] * right[1] + left[1] * right[0])


def along_last(real_part, imag_part, groups, sign):
    rows, length = real_part.shape
    inner = length // groups
    first = roots(groups, counting(groups), counting(groups), sign)
    twist = roots(length, counting(inner), counting(groups), sign)
    second = roots(inner, counting(inner), counting(inner), sign)
    shaped = real_part.reshape(rows, groups, inner)
    if imag_part is None:
        partial_value = (
            jnp.einsum("mab,ka->mbk", shaped, first[0], precision=HIGHEST),
            jnp.einsum("mab,ka->mbk", shaped, first[1], precision=HIGHEST),
        )
    else:
        partial_value = complex_einsum(
            "mab,ka->mbk", (shaped, imag_part.reshape(rows, groups, inner)), first
        )
    partial_value = complex_times(partial_value, twist)
    result = complex_einsum("jb,mbk->mjk", second, partial_value)
    return (result[0].reshape(rows, length), result[1].reshape(rows, length))


def across_groups(pair, groups, sign):
    inner, cols = pair[0].shape
    width = cols // groups
    length = groups * inner
    first = roots(groups, counting(groups), counting(groups), sign)
    twist = roots(length, counting(inner), counting(groups), sign)
    second = roots(inner, counting(inner), counting(inner), sign)
    shaped = (pair[0].reshape(inner, groups, width), pair[1].reshape(inner, groups, width))
    partial_value = complex_einsum("bhc,kh->cbk", shaped, first)
    partial_value = complex_times(partial_value, twist)
    result = complex_einsum("jb,cbk->cjk", second, partial_value)
    return (result[0].reshape(width, length), result[1].reshape(width, length))


def exchange_pair(pair):
    return tuple(
        lax.all_to_all(
            part.astype(BF16), ("ty", "tx"), split_axis=1, concat_axis=1, tiled=True
        ).astype(F32)
        for part in pair
    )


def plain_gradient(tile, gains, observed, vis_weight):
    devices = lax.axis_size("ty") * lax.axis_size("tx")
    slab = lax.all_to_all(tile.astype(BF16), "tx", split_axis=0, concat_axis=1, tiled=True)
    moved = exchange_pair(along_last(slab.astype(F32), None, devices, -1.0))
    spectrum = across_groups(moved, devices, -1.0)
    spectrum = (spectrum[0] * (1.0 / N), spectrum[1] * (1.0 / N))
    model = complex_times((gains[0], gains[1]), spectrum)
    misfit = (vis_weight * (model[0] - observed[0]), vis_weight * (model[1] - observed[1]))
    back = complex_times((gains[0], -gains[1]), misfit)
    returned = exchange_pair(along_last(back[0], back[1], devices, 1.0))
    slab_grad = across_groups(returned, devices, 1.0)[0] * (1.0 / N)
    return lax.all_to_all(slab_grad.astype(BF16), "tx", split_axis=1, concat_axis=0, tiled=True)


def embed_complex(angle, row_axis, col_axis):
    cos, sin = np.cos(angle), np.sin(angle)
    top = np.stack([cos, sin], axis=col_axis)
    bottom = np.stack([-sin, cos], axis=col_axis)
    return np.stack([top, bottom], axis=row_axis)


def wheel(length, product):
    return 2.0 * math.pi / length * (product % length)


@functools.lru_cache(maxsize=None)
def row_constants():
    k = np.arange(TOK)
    angle = wheel(TOK, k[:, None] * k[None, :])
    first = np.concatenate([np.cos(angle), -np.sin(angle)], axis=1)
    b = np.repeat(np.arange(PATCH), PATCH)
    angle = wheel(N, b[:, None] * k[None, :])
    twist = np.stack([np.cos(angle), -np.sin(angle)])
    p = np.arange(PATCH)
    small = embed_complex(wheel(PATCH, p[:, None] * p[None, :]), 1, 1)
    second = np.einsum("kpqb,xy->kpxqby", small, np.eye(PATCH)).reshape(2 * PIXELS, 2 * PIXELS)
    return (
        first.astype(ml_dtypes.bfloat16),
        twist.astype(np.float32),
        second.astype(ml_dtypes.bfloat16),
        np.ascontiguousarray(second.T).astype(ml_dtypes.bfloat16),
    )


@functools.lru_cache(maxsize=None)
def half_constants():
    _, twist, second, _ = row_constants()
    half, quarter = TOK // 2, TOK // 4
    low = np.concatenate([1 + np.arange(quarter), 1 + half + np.arange(quarter)])
    digits = np.concatenate([low, low - 1])
    k = np.arange(TOK)
    angle = wheel(TOK, k[:, None] * digits[None, :])
    first = np.concatenate([np.cos(angle), -np.sin(angle)], axis=1)
    zero_line = np.concatenate([np.tile(np.eye(PATCH), PATCH), np.zeros((PATCH, PIXELS))], axis=1)
    upper = np.concatenate([second[PIXELS:].astype(np.float32), zero_line])
    lower = second[:PIXELS].astype(np.float32)
    return (first.astype(ml_dtypes.bfloat16), np.ascontiguousarray(twist[:, :, digits])) + tuple(
        np.ascontiguousarray(value).astype(ml_dtypes.bfloat16)
        for value in (lower, upper, lower.T, upper.T)
    )


@functools.lru_cache(maxsize=None)
def column_constants(devices, rows):
    s = np.arange(devices)
    small = embed_complex(wheel(devices, s[:, None] * s[None, :]), 1, 2)
    wide = devices * 2 * PATCH
    outer = np.einsum("qpsr,xy->qpxsry", small, np.eye(PATCH)).reshape(wide, wide)
    kr = s[:, None] + devices * np.arange(rows)[None, :]
    angle = wheel(N, kr[:, :, None] * np.arange(rows)[None, None, :])
    inner = embed_complex(angle, 1, 2).reshape(devices, 2 * rows, 2 * rows) / N
    return tuple(
        np.ascontiguousarray(value).astype(ml_dtypes.bfloat16)
        for value in (outer, outer.T, inner, inner.transpose(0, 2, 1))
    )


def row_forward(x_ref, first_ref, twist_ref, second_ref, out_ref):
    count = x_ref.shape[1]

    def step(i, carry):
        band = x_ref[:, i].reshape(TOK, PIXELS)
        mixed = mm(band, first_ref[...], TN)
        real, imag = mixed[:, :TOK], mixed[:, TOK:]
        tr, ti = twist_ref[0], twist_ref[1]
        turned = jnp.concatenate(
            [(real * tr - imag * ti).astype(BF16), (real * ti + imag * tr).astype(BF16)], axis=0
        )
        result = mm(second_ref[...], turned).astype(BF16).reshape(PATCH, 2, PATCH, TOK)
        half = TOK // 2
        rows = pl.ds(pl.multiple_of(i * PATCH, PATCH), PATCH)
        out_ref[:, 0, :, rows, :] = result[..., :half]
        out_ref[:, 1, :, rows, :] = result[..., half:]
        return carry

    lax.fori_loop(0, count, step, 0, unroll=4)


def row_inverse(v_ref, first_ref, twist_ref, second_ref, out_ref):
    parts, count, cols, _ = out_ref.shape

    def step(i, carry):
        rows = pl.ds(pl.multiple_of(i * PATCH, PATCH), PATCH)
        wide = jnp.concatenate(
            [
                v_ref[:, 0, :, rows, :].reshape(2 * PIXELS, TOK // 2),
                v_ref[:, 1, :, rows, :].reshape(2 * PIXELS, TOK // 2),
            ],
            axis=1,
        )
        mixed = mm(second_ref[...], wide)
        real, imag = mixed[:PIXELS], mixed[PIXELS:]
        tr, ti = twist_ref[0], twist_ref[1]
        turned = jnp.concatenate(
            [(real * tr + imag * ti).astype(BF16), (imag * tr - real * ti).astype(BF16)], axis=1
        )
        result = mm(first_ref[...], turned, NT).astype(BF16)
        out_ref[:, i] = result.reshape(parts, cols, PIXELS)
        return carry

    lax.fori_loop(0, count, step, 0, unroll=4)


def lane_index(shape):
    return lax.broadcasted_iota(jnp.int32, shape, len(shape) - 1)


def swap_halves(values):
    return pltpu.roll(values, values.shape[-1] // 2, len(values.shape) - 1)


def row_forward_half(x_ref, first_ref, twist_ref, lower_ref, upper_ref, out_ref):
    count = x_ref.shape[1]
    half = TOK // 2

    def packed(real, imag, rows, high):
        left = lane_index(real.shape) < half // 2
        out_ref[high, 0, rows, :] = jnp.where(left, real, swap_halves(imag)).astype(BF16)
        out_ref[high, 1, rows, :] = jnp.where(left, swap_halves(real), imag).astype(BF16)

    def step(i, carry):
        band = x_ref[:, i].reshape(TOK, PIXELS)
        mixed = mm(band, first_ref[...], TN)
        real, imag = mixed[:, :TOK], mixed[:, TOK:]
        tr, ti = twist_ref[0], twist_ref[1]
        turned = jnp.concatenate(
            [(real * tr - imag * ti).astype(BF16), (real * ti + imag * tr).astype(BF16)], axis=0
        )
        rows = pl.ds(pl.multiple_of(i * PATCH, PATCH), PATCH)
        lower = mm(lower_ref[...], turned[:, :half]).reshape(PATCH // 2, 2, PATCH, half)
        packed(lower[:, 0], lower[:, 1], rows, slice(0, PATCH // 2))
        upper = mm(upper_ref[...], turned[:, half:])
        line = upper[PIXELS:]
        upper = upper[:PIXELS].reshape(PATCH // 2, 2, PATCH, half)
        imag = upper[:, 1]
        head = jnp.where(lane_index(line.shape) == 0, line, imag[0])
        imag = jnp.concatenate([head[None], imag[1:]], axis=0)
        packed(upper[:, 0], imag, rows, slice(PATCH // 2, PATCH))
        return carry

    lax.fori_loop(0, count, step, 0, unroll=4)


def row_inverse_half(v_ref, first_ref, twist_ref, lower_ref, upper_ref, out_ref):
    parts, count, cols, _ = out_ref.shape
    half = TOK // 2

    def unpacked(rows, high):
        even = v_ref[high, 0, rows, :].astype(F32)
        odd = v_ref[high, 1, rows, :].astype(F32)
        left = lane_index(even.shape) < half // 2
        return jnp.where(left, even, swap_halves(odd)), jnp.where(left, swap_halves(even), odd)

    def step(i, carry):
        rows = pl.ds(pl.multiple_of(i * PATCH, PATCH), PATCH)
        real, imag = unpacked(rows, slice(0, PATCH // 2))
        lower = jnp.stack([real, imag], axis=1).reshape(PIXELS, half)
        real, imag = unpacked(rows, slice(PATCH // 2, PATCH))
        head = imag[0]
        at_zero = lane_index(head.shape) == 0
        nothing = jnp.zeros_like(head)
        imag = jnp.concatenate([jnp.where(at_zero, nothing, head)[None], imag[1:]], axis=0)
        upper = jnp.stack([real, imag], axis=1).reshape(PIXELS, half)
        upper = jnp.concatenate([upper, jnp.where(at_zero, head, nothing)], axis=0)
        mixed = jnp.concatenate(
            [mm(lower_ref[...], lower.astype(BF16)), mm(upper_ref[...], upper.astype(BF16))], axis=1
        )
        real, imag = mixed[:PIXELS], mixed[PIXELS:]
        tr, ti = twist_ref[0], twist_ref[1]
        turned = jnp.concatenate(
            [(real * tr + imag * ti).astype(BF16), (imag * tr - real * ti).astype(BF16)], axis=1
        )
        result = mm(first_ref[...], turned, NT).astype(BF16)
        out_ref[:, i] = result.reshape(parts, cols, PIXELS)
        return carry

    lax.fori_loop(0, count, step, 0, unroll=4)


def column_kernel(halved, *refs):
    if halved:
        flag_ref, phase_ref, refs = refs[0], refs[1], refs[2:]
    x_ref, outer_ref, *refs = refs
    count = 4 if halved else 5
    sources, out_ref = refs[:count], refs[count]
    mid_ref, *targets, sems = refs[count + 1 :]
    copies = [
        pltpu.make_async_copy(source, target, sems.at[n])
        for n, (source, target) in enumerate(zip(sources, targets))
    ]
    for copy in copies:
        copy.start()
    inner_ref, scale_ref, inner_t_ref, outer_t_ref = targets[:4]
    devices, _, rows, width = mid_ref.shape
    wide = devices * 2 * PATCH
    if halved:
        lane = lane_index((devices, PATCH, width))
        centre = flag_ref[0] == 1
        half = width // 2
        hidden = (lane == half) | (centre & (lane == 0))
        real_lane = (lane < half) | (centre & (lane == half))

    def load(group):
        place = slice(group * PATCH, (group + 1) * PATCH)
        if not halved:
            return x_ref[:, :, place, :].reshape(wide, width)
        piece = x_ref[:, place, :]
        other = swap_halves(piece.astype(F32))
        other = jnp.where(hidden, jnp.zeros_like(other), other).astype(BF16)
        return jnp.stack([piece, other], axis=1).reshape(wide, width)

    def store(group, value):
        place = slice(group * PATCH, (group + 1) * PATCH)
        value = value.reshape(devices, 2, PATCH, width)
        if halved:
            value = jnp.where(real_lane, value[:, 0], swap_halves(value[:, 1])).astype(BF16)
            out_ref[:, place, :] = value
        else:
            out_ref[:, :, place, :] = value.astype(BF16)

    for pair in range(0, rows // PATCH, 2):
        result = mm(outer_ref[...], jnp.concatenate([load(pair), load(pair + 1)], axis=1))
        result = result.astype(BF16)
        for n in range(2):
            place = slice((pair + n) * PATCH, (pair + n + 1) * PATCH)
            mid_ref[:, :, place, :] = result[:, n * width : (n + 1) * width].reshape(
                devices, 2, PATCH, width
            )

    for n, copy in enumerate(copies):
        if n != 3:
            copy.wait()

    def step(q, carry):
        spectrum = mm(inner_ref[q], mid_ref[q].reshape(2 * rows, width))
        real, imag = spectrum[:rows], spectrum[rows:]
        scale = scale_ref[q].astype(F32)
        if halved:
            pr, pi = phase_ref[q, 0], phase_ref[q, 1]
            real = real.reshape(rows // 8, 8, width)
            imag = imag.reshape(rows // 8, 8, width)
            real, imag = real * pr - imag * pi, real * pi + imag * pr
            real, imag = real.reshape(rows, width) * scale, imag.reshape(rows, width) * scale
        else:
            data_ref = targets[4]
            real = real * scale - data_ref[0, q].astype(F32)
            imag = imag * scale - data_ref[1, q].astype(F32)
        back = jnp.concatenate([real.astype(BF16), imag.astype(BF16)], axis=0)
        mid_ref[q] = mm(inner_t_ref[q], back).astype(BF16).reshape(2, rows, width)
        return carry

    lax.fori_loop(0, devices, step, 0, unroll=8)
    copies[3].wait()

    for pair in range(0, rows // PATCH, 2):
        both = jnp.concatenate(
            [
                mid_ref[:, :, n * PATCH : (n + 1) * PATCH, :].reshape(wide, width)
                for n in (pair, pair + 1)
            ],
            axis=1,
        )
        result = mm(outer_t_ref[...], both)
        store(pair, result[:, :width])
        store(pair + 1, result[:, width:])


def turned(value, devices):
    lines = value.shape[0]
    return value.astype(BF16).reshape(lines, N // devices, devices).transpose(2, 1, 0)


def spectrum_inputs(gains, observed, vis_weight, devices):
    gr, gi = gains[0], gains[1]
    weight = (vis_weight * (gr * gr + gi * gi)).astype(BF16)
    data = jnp.stack(
        [
            turned(vis_weight * (gr * observed[0] + gi * observed[1]), devices),
            turned(vis_weight * (gr * observed[1] - gi * observed[0]), devices),
        ]
    )
    return weight, turned(weight, devices), data


def mirror_kernel(scale_ref, got_ref, pick_ref, flip_ref, out_ref):
    devices = out_ref.shape[0]
    for q in range(devices):
        facing = mm(flip_ref[min(q, 1)], got_ref[(devices - q) % devices]).astype(BF16)
        total = mm(scale_ref[q], pick_ref[0]) + mm(facing, pick_ref[1])
        out_ref[q] = total.astype(BF16)


def mirrored_exchange(weight):
    devices = N // weight.shape[0]
    half, middle = weight.shape[0] // 2, devices // 2
    facing = [(e, devices - 1 - e) for e in range(devices)]
    partner = [(e, devices - e) for e in range(1, devices) if e != middle]
    partner = partner + [(0, middle), (middle, 0)]
    upper = lax.ppermute(weight[half:], ("ty", "tx"), facing)
    line = lax.ppermute(weight[:1], ("ty", "tx"), partner)
    return upper, line


def mirrored_weight(scale, upper, line):
    devices, slab, _ = scale.shape
    half, middle = slab // 2, devices // 2
    me = lax.axis_index(("ty", "tx"))
    got = jnp.concatenate([upper, jnp.broadcast_to(line, (half, N))], axis=0)
    source = lax.broadcasted_iota(jnp.int32, (slab, slab), 0)
    slot = lax.broadcasted_iota(jnp.int32, (slab, slab), 1)
    low = (me < middle).astype(jnp.int32)
    own = (slot < half) & (source == slot + low)
    other = (slot < half) & (source == half - low - slot)
    other = other & ((me != middle) | (slot > 0))
    other = other | ((me == middle) & (slot == half) & (source == half))
    picks = jnp.stack([own, other]).astype(BF16)
    q2 = np.arange(slab)
    flips = np.stack([q2[:, None] == (slab - q2) % slab, q2[:, None] == slab - 1 - q2])
    return pl.pallas_call(
        mirror_kernel,
        out_shape=jax.ShapeDtypeStruct(scale.shape, BF16),
        compiler_params=PARAMS,
    )(scale, turned(got, devices), picks, jnp.asarray(flips.astype(ml_dtypes.bfloat16)))


def row_matrix(shift):
    first = half_constants()[0]
    twice = jnp.asarray(np.concatenate([first, first[: 2 * WIN]], axis=0))
    return lax.dynamic_slice(twice, (shift, jnp.zeros((), jnp.int32)), first.shape)


def phase_table(shift, devices, width):
    kr = counting(devices)[:, None] + devices * counting(8)[None, :]
    angle = 2.0 * math.pi / TOK * (kr * shift % TOK).astype(F32)
    table = jnp.stack([jnp.cos(angle), -jnp.sin(angle)], axis=1)
    return jnp.broadcast_to(table[..., None], (devices, 2, 8, width))


def patch_gradient(state, scale, data, shift, mirror, beside):
    lanes = lax.axis_size("tx")
    devices = lax.axis_size("ty") * lanes
    rows, cols, _ = state.shape
    own = rows // lanes
    slab = N // devices
    halved = data is None
    outer, outer_t, inner, inner_t = (
        jnp.asarray(value) for value in column_constants(devices, slab)
    )
    if halved:
        first, twist, low, high, low_t, high_t = (jnp.asarray(value) for value in half_constants())
        part = (devices, slab, slab)
        onward = (row_forward_half, (row_matrix(shift[1]), twist, low, high))
        backward = (row_inverse_half, (first, twist, low_t, high_t))
        middle = lax.axis_index(("ty", "tx")) == devices // 2
    else:
        first, twist, second, second_t = (jnp.asarray(value) for value in row_constants())
        part = (devices, 2, slab, slab)
        onward = (row_forward, (first, twist, second))
        backward = (row_inverse, (first, twist, second_t))
        extra = ()
        away = (inner, scale, inner_t, outer_t, data)
    split = (PATCH, devices // PATCH) + part[1:]
    gathered = lax.all_to_all(
        state.reshape(lanes, own, cols, PIXELS), "tx", split_axis=0, concat_axis=0, tiled=True
    )
    sent = pl.pallas_call(
        onward[0], out_shape=jax.ShapeDtypeStruct(split, BF16), compiler_params=PARAMS
    )(gathered, *onward[1])
    if halved:
        sent, mirror, shift = lax.optimization_barrier((sent, mirror, shift))
        extra = (middle.astype(jnp.int32).reshape(1), phase_table(shift[0], devices, slab))
        away = (inner, mirrored_weight(scale, *mirror), inner_t, outer_t)
    moved = lax.all_to_all(
        sent.reshape(part), ("ty", "tx"), split_axis=0, concat_axis=0, tiled=True
    )
    spaces = [pltpu.SMEM, pltpu.VMEM][: len(extra)] + [pltpu.VMEM] * 2 + [pl.ANY] * len(away)
    wave = pl.pallas_call(
        functools.partial(column_kernel, halved),
        in_specs=[pl.BlockSpec(memory_space=space) for space in spaces],
        out_shape=jax.ShapeDtypeStruct(part, BF16),
        scratch_shapes=[pltpu.VMEM((devices, 2, slab, slab), BF16)]
        + [pltpu.VMEM(value.shape, BF16) for value in away]
        + [pltpu.SemaphoreType.DMA((len(away),))],
        compiler_params=PARAMS,
    )(*extra, moved, outer, *away)
    returned = lax.all_to_all(wave, ("ty", "tx"), split_axis=0, concat_axis=0, tiled=True)
    returned, beside = lax.optimization_barrier((returned, beside))
    slabs = pl.pallas_call(
        backward[0],
        out_shape=jax.ShapeDtypeStruct((lanes, own, cols, PIXELS), BF16),
        compiler_params=PARAMS,
    )(returned.reshape(split), *backward[1])
    grad = lax.all_to_all(slabs, "tx", split_axis=0, concat_axis=0, tiled=True)
    return grad.reshape(rows, cols, PIXELS), beside


def layer_norm(values, gain):
    centre = jnp.mean(values, axis=-1, keepdims=True)
    shifted = values - centre
    spread = jnp.mean(shifted * shifted, axis=-1, keepdims=True)
    return (shifted * lax.rsqrt(spread + EPSILON) * gain).astype(BF16)


def to_windows(band):
    rows, cols, feats = band.shape
    pieces = [
        band[:, w * WIN : (w + 1) * WIN, :].reshape(SPAN, feats) for w in range(cols // WIN)
    ]
    return jnp.concatenate(pieces, axis=0)


def from_windows(tokens, cols):
    feats = tokens.shape[-1]
    pieces = [
        tokens[w * SPAN : (w + 1) * SPAN].reshape(WIN, WIN, feats) for w in range(cols // WIN)
    ]
    return jnp.concatenate(pieces, axis=1)


def swin_band(
    flow, bias_ref, qkv_ref, proj_ref, up_ref, down_ref, gain_ref, mixed_ref, score_ref, prob_ref
):
    count = flow.shape[0] // SPAN
    pairs = HEADS // 2
    depth = D // HEADS
    wide = 2 * depth
    normed = layer_norm(flow, gain_ref[0:1, :])
    scale = 1.0 / math.sqrt(depth)
    mixed_ref[:, :D] = (mm(normed, qkv_ref[:, :D]) * scale).astype(BF16)
    mixed_ref[:, D : 2 * D] = mm(normed, qkv_ref[:, D : 2 * D]).astype(BF16)
    mixed_ref[:, 2 * D :] = mm(normed, qkv_ref[:, 2 * D :]).astype(BF16)
    lower = lax.broadcasted_iota(jnp.int32, (SPAN, wide), 1) < depth
    for w in range(count):
        rows = slice(w * SPAN, (w + 1) * SPAN)
        for p in range(pairs):
            query = mixed_ref[rows, p * wide : (p + 1) * wide]
            key = mixed_ref[rows, D + p * wide : D + (p + 1) * wide]
            zero = jnp.zeros_like(query)
            split = jnp.concatenate(
                [jnp.where(lower, query, zero), jnp.where(lower, zero, query)], axis=0
            )
            score_ref[w, :, p * wide : (p + 1) * wide] = mm(key, split, NT)
    for w in range(count):
        bias = bias_ref[w]
        for p in range(pairs):
            lanes = slice(p * wide, (p + 1) * wide)
            scores = score_ref[w, :, lanes] + bias
            weights = jnp.exp(scores - jnp.max(scores, axis=0, keepdims=True))
            share = 1.0 / jnp.sum(weights, axis=0, keepdims=True)
            prob_ref[w, :, lanes] = (weights * share).astype(BF16)
    for w in range(count):
        rows = slice(w * SPAN, (w + 1) * SPAN)
        for p in range(pairs):
            lanes = slice(p * wide, (p + 1) * wide)
            value = mixed_ref[rows, 2 * D + p * wide : 2 * D + (p + 1) * wide]
            mixture = mm(prob_ref[w, :, lanes], value, TN)
            mixed_ref[rows, lanes] = jnp.where(lower, mixture[:SPAN], mixture[SPAN:]).astype(BF16)
    flow = flow + mm(mixed_ref[:, :D], proj_ref[...])
    normed = layer_norm(flow, gain_ref[1:2, :])
    chunks = up_ref.shape[1] // D
    total = jnp.zeros_like(flow)
    ahead = mm(normed, up_ref[:, :D])
    for c in range(chunks):
        value = ahead
        if c + 1 < chunks:
            ahead = mm(normed, up_ref[:, (c + 1) * D : (c + 2) * D])
        inside = value * (GELU_IN + GELU_CUBE * (value * value))
        active = (value + value * jnp.tanh(inside)).astype(BF16)
        total = total + mm(active, down_ref[c * D : (c + 1) * D, :])
    return flow + 0.5 * total


def first_kernel(zeta, sigma, count, *refs):
    state_ref, grad_refs, refs = refs[0], refs[1 : 1 + count], refs[1 + count :]
    if sigma is not None:
        noise_ref, refs = refs[0], refs[1:]
    bias_ref, embed_ref, qkv_ref, proj_ref, up_ref, down_ref, gain_ref = refs[:7]
    base_ref, out_ref, *scratch = refs[7:]
    step = zeta * sum(grad_ref[...].astype(F32) for grad_ref in grad_refs)
    half = state_ref[...] - step
    tokens = mm(to_windows(half).astype(BF16), embed_ref[...]).astype(BF16).astype(F32)
    if sigma is None:
        base_ref[...] = half
    else:
        noise = sigma * noise_ref[...]
        base_ref[...] = half + noise
        out_ref[:, :, D:] = (noise - step).astype(BF16)
    flow = swin_band(tokens, bias_ref, qkv_ref, proj_ref, up_ref, down_ref, gain_ref, *scratch)
    out_ref[:, :, :D] = from_windows(flow, half.shape[1]).astype(BF16)


def second_kernel(sigma, *refs):
    shift_ref, grid_ref, bias_ref, qkv_ref, proj_ref, up_ref, down_ref, gain_ref = refs[:8]
    unembed_ref, out_ref, *scratch = refs[8:]
    if sigma is not None:
        state_ref, scratch = scratch[0], scratch[1:]
    cols = out_ref.shape[1]
    top = pl.program_id(0) * WIN + shift_ref[0]
    wide = grid_ref[pl.ds(top, WIN)]
    place = lax.broadcasted_iota(jnp.int32, (cols, wide.shape[1]), 1)
    target = lax.broadcasted_iota(jnp.int32, (cols, wide.shape[1]), 0) + shift_ref[1]
    pick = jnp.where(place == target, 1.0, 0.0).astype(BF16)
    band = jnp.stack([mm(pick, wide[n]) for n in range(WIN)])
    tokens = to_windows(band[:, :, :D])
    flow = swin_band(tokens, bias_ref, qkv_ref, proj_ref, up_ref, down_ref, gain_ref, *scratch)
    estimate = from_windows(mm(flow.astype(BF16), unembed_ref[...]), cols)
    out_ref[...] = estimate.astype(BF16)
    if sigma is not None:
        state_ref[...] = (band[:, :, D:] - sigma * estimate).astype(BF16)


def whole(array):
    zeros = (0,) * array.ndim
    return pl.BlockSpec(array.shape, lambda *_: zeros)


def band_of(step, cols):
    return pl.BlockSpec((step, cols, PIXELS), lambda n: (n, 0, 0))


def member(array, j):
    place = (j,) + (0,) * (array.ndim - 1)
    return pl.BlockSpec((None,) + array.shape[1:], lambda *_: place)


def band_spec(cols, feats):
    return pl.BlockSpec((WIN, cols, feats), lambda n, *_: (n, 0, 0))


def bias_spec(cols):
    return pl.BlockSpec((cols // WIN, SPAN, 2 * SPAN), lambda n, *_: (n, 0, 0))


def band_scratch(cols):
    count = cols // WIN
    return [
        pltpu.VMEM((WIN * cols, 3 * D), BF16),
        pltpu.VMEM((count, SPAN, HEADS * SPAN), F32),
        pltpu.VMEM((count, SPAN, HEADS * SPAN), BF16),
    ]


def first_block(zeta, sigma, state, grads, noise, bias, w_embed, weights):
    rows, cols, _ = state.shape
    fields = [state, *grads] + ([] if sigma is None else [noise])
    feats = D if sigma is None else D + PIXELS
    return pl.pallas_call(
        functools.partial(first_kernel, zeta, sigma, len(grads)),
        grid=(rows // WIN,),
        in_specs=[band_spec(cols, PIXELS)] * len(fields)
        + [bias_spec(cols), whole(w_embed)]
        + [member(value, 0) for value in weights],
        out_specs=[band_spec(cols, PIXELS), band_spec(cols, feats)],
        out_shape=[
            jax.ShapeDtypeStruct((rows, cols, PIXELS), F32),
            jax.ShapeDtypeStruct((rows, cols, feats), BF16),
        ],
        scratch_shapes=band_scratch(cols),
        compiler_params=PARAMS,
    )(*fields, bias, w_embed, *weights)


def second_block(sigma, shift, grid, bias, w_unembed, weights):
    rows, cols = grid.shape[0] - WIN, grid.shape[1] - WIN
    outs = 1 if sigma is None else 2
    return pl.pallas_call(
        functools.partial(second_kernel, sigma),
        grid_spec=pltpu.PrefetchScalarGridSpec(
            num_scalar_prefetch=1,
            grid=(rows // WIN,),
            in_specs=[whole(grid), bias_spec(cols)]
            + [member(value, 1) for value in weights]
            + [whole(w_unembed)],
            out_specs=[band_spec(cols, PIXELS)] * outs,
            scratch_shapes=band_scratch(cols),
        ),
        out_shape=[jax.ShapeDtypeStruct((rows, cols, PIXELS), BF16)] * outs,
        compiler_params=PARAMS,
    )(shift, grid, bias, *weights, w_unembed)


def from_behind(shard, axis, by):
    size = lax.axis_size(axis)
    return lax.ppermute(shard, axis, [(i, (i + by) % size) for i in range(size)])


def with_next(grid):
    wide = jnp.concatenate([grid, from_behind(grid[:, :WIN], "tx", -1)], axis=1)
    return jnp.concatenate([wide, from_behind(wide[:WIN], "ty", -1)], axis=0)


def with_previous(grid):
    wide = jnp.concatenate([from_behind(grid[:, -WIN:], "tx", 1), grid], axis=1)
    return jnp.concatenate([from_behind(wide[-WIN:], "ty", 1), wide], axis=0)


def windows_of(grid):
    rows, cols = grid.shape
    shaped = grid.reshape(rows // WIN, WIN, cols // WIN, WIN).transpose(0, 2, 1, 3)
    return shaped.reshape(rows // WIN * (cols // WIN), SPAN)


def bias_of(labels, keep):
    allowed = jnp.ones((1, SPAN, SPAN), bool)
    if labels is not None:
        label = windows_of(labels)
        allowed = label[:, :, None] == label[:, None, :]
    if keep is not None:
        kept = windows_of(keep)[:, :, None] == 1
        allowed = allowed & (kept | jnp.eye(SPAN, dtype=bool)[None])
    bias = jnp.where(allowed, 0.0, -1e30).astype(F32)
    return jnp.concatenate([bias, bias], axis=2)


def region(index, shift):
    return jnp.where(index < TOK - WIN, 0, jnp.where(index < TOK - shift, 1, 2)).astype(jnp.int32)


@functools.lru_cache(maxsize=None)
def lane_order(cols):
    parts = LANES // cols
    groups = PATCH // parts
    lane = np.arange(PATCH * cols)
    g, h, k = lane // LANES, lane % LANES // cols, lane % cols
    source = PATCH * k + h * groups + g
    matrix = np.zeros((PATCH * cols, PATCH * cols), np.float32)
    matrix[source, lane] = 1.0
    return matrix.astype(ml_dtypes.bfloat16), np.ascontiguousarray(matrix.T).astype(
        ml_dtypes.bfloat16
    )


def move_lanes(values, matrix):
    high = values.astype(BF16)
    low = (values - high.astype(F32)).astype(BF16)
    return mm(high, matrix) + mm(low, matrix)


def to_patches_kernel(tile_ref, order_ref, out_ref):
    count, cols, _ = out_ref.shape
    parts = LANES // cols
    groups = PATCH // parts
    if out_ref.dtype == BF16:
        ordered = mm(tile_ref[...].astype(BF16), order_ref[...])
    else:
        ordered = move_lanes(tile_ref[...], order_ref[...])
    for i in range(count):
        band = ordered[i * PATCH : (i + 1) * PATCH]
        stacked = jnp.concatenate(
            [band[:, g * LANES : (g + 1) * LANES] for g in range(groups)], axis=0
        )
        turned = stacked.T
        patch = jnp.concatenate([turned[h * cols : (h + 1) * cols] for h in range(parts)], axis=1)
        out_ref[i] = patch.astype(out_ref.dtype)


def to_tile_kernel(scale, patch_ref, noise_ref, order_ref, out_ref):
    count, cols, _ = patch_ref.shape
    parts = LANES // cols
    groups = PATCH // parts
    width = groups * PATCH
    bands = []
    for i in range(count):
        patch = patch_ref[i]
        stacked = jnp.concatenate(
            [patch[:, h * width : (h + 1) * width] for h in range(parts)], axis=0
        )
        turned = stacked.T
        bands.append(
            jnp.concatenate([turned[g * PATCH : (g + 1) * PATCH] for g in range(groups)], axis=1)
        )
    moved = move_lanes(jnp.concatenate(bands, axis=0), order_ref[...])
    out_ref[...] = moved + scale * noise_ref[...]


def patches_of(tiles, j, kind=F32):
    rows, cols = tiles.shape[1] // PATCH, tiles.shape[2] // PATCH
    order = jnp.asarray(lane_order(cols)[0])
    step = rows // 4
    return pl.pallas_call(
        to_patches_kernel,
        grid=(rows // step,),
        in_specs=[
            pl.BlockSpec((None, step * PATCH, cols * PATCH), lambda n: (j, n, 0)),
            whole(order),
        ],
        out_specs=band_of(step, cols),
        out_shape=jax.ShapeDtypeStruct((rows, cols, PIXELS), kind),
        compiler_params=PARAMS,
    )(tiles, order)


def tile_of(patches, scale, noise, j):
    rows, cols, _ = patches.shape
    order = jnp.asarray(lane_order(cols)[1])
    step = rows // 4
    return pl.pallas_call(
        functools.partial(to_tile_kernel, scale),
        grid=(rows // step,),
        in_specs=[
            band_of(step, cols),
            pl.BlockSpec((None, step * PATCH, cols * PATCH), lambda n: (j, n, 0)),
            whole(order),
        ],
        out_specs=pl.BlockSpec((step * PATCH, cols * PATCH), lambda n: (n, 0)),
        out_shape=jax.ShapeDtypeStruct((rows * PATCH, cols * PATCH), F32),
        compiler_params=PARAMS,
    )(patches, noise, order)


def per_device(
    image, noise, offsets, key_mask, gains, observed, vis_weight,
    w_embed, w_qkv, w_proj, w_up, w_down, w_unembed, norm_gains,
):
    rows = image.shape[0] // PATCH
    cols = image.shape[1] // PATCH
    devices = lax.axis_size("ty") * lax.axis_size("tx")
    fast = N // devices == TOK // 2
    row_index = lax.axis_index("ty") * rows + counting(rows)
    col_index = lax.axis_index("tx") * cols + counting(cols)
    weights = (w_qkv, w_proj, w_up, w_down, norm_gains)
    w_embed = w_embed.reshape(PATCH, PATCH, D).transpose(1, 0, 2).reshape(PIXELS, D)
    w_unembed = w_unembed.reshape(D, PATCH, PATCH).transpose(0, 2, 1).reshape(D, PIXELS)
    state = patches_of(image[None], 0)
    extras = [patches_of(noise, step) for step in range(STEPS - 1)] + [None]
    first_bias = bias_of(None, key_mask)
    biases = []
    for step in range(STEPS):
        labels = (
            3 * region(row_index, offsets[step, 0])[:, None]
            + region(col_index, offsets[step, 1])[None, :]
        )
        biases.append(bias_of(labels, None))
    beside = (state, extras, first_bias, biases, w_embed, w_unembed)
    shift = moving = mirror = None
    grads = []
    if fast:
        weight, scale, data = spectrum_inputs(gains, observed, vis_weight, devices)
        grad, beside = patch_gradient(
            patches_of(image[None], 0, BF16), scale, data, None, None, beside
        )
        grads = [grad]
        state, extras, first_bias, biases, w_embed, w_unembed = beside
    for step in range(STEPS):
        if not fast:
            grad = plain_gradient(tile_of(state, 0.0, noise, 0), gains, observed, vis_weight)
            grads = [patches_of(grad.astype(F32)[None], 0, BF16)]
        elif step > 0:
            grads = grads + [patch_gradient(moving, scale, None, shift, mirror, ())[0]]
        last = step + 1 == STEPS
        sigma = None if last else SIGMAS[step + 1]
        base, first = first_block(
            STEP_SIZES[step], sigma, state, grads, extras[step], first_bias, w_embed, weights
        )
        shift = offsets[step]
        grid = with_next(first)
        if fast and step == 0:
            grid, weight = lax.optimization_barrier((grid, weight))
            mirror = mirrored_exchange(weight)
        rolled, *moving = second_block(
            None if last else SIGMAS[step], shift, grid, biases[step], w_unembed, weights
        )
        moving = None if last else moving[0]
        corner = (WIN - shift[0], WIN - shift[1], jnp.zeros((), jnp.int32))
        estimate = lax.dynamic_slice(with_previous(rolled), corner, base.shape)
        state = base - SIGMAS[step] * estimate.astype(F32)
    return tile_of(state, SIGMAS[STEPS], noise, STEPS - 1)


def solution(mesh):
    in_specs = (
        P("ty", "tx"),
        P(None, "ty", "tx"),
        P(),
        P("ty", "tx"),
        P(None, ("ty", "tx"), None),
        P(None, ("ty", "tx"), None),
        P(("ty", "tx"), None),
        P(),
        P(),
        P(),
        P(),
        P(),
        P(),
        P(),
    )
    out_specs = P("ty", "tx")
    return jax.shard_map(
        per_device, mesh=mesh, in_specs=in_specs, out_specs=out_specs, check_vma=False
    )
```

profile of v0, /device:TPU:0, one launch (start us, length us, event | category | flops | bytes accessed | tf_op | source)
XLA Modules:
  0.0 502.4 jit_solution(5099573379549887652)
XLA Ops:
  0.0 5.4 %shard_map.298 = bf16[32,64,256]{2,1,0:T(8,128)(2,1)} custom-call(f32[1,512,1024]{2,1,0:T(8,128)} %bitcast.78, bf16[1024,1024]{1,0:T(8,128)(2,1)} %constant.120.clone.order_ref), custom_call_target="tpu_custom_call" | custom-call | tf_op jit(solution)/shard_map/pallas_call | solution.py:810
  5.4 20.0 %all_to_all.40.x_ref = bf16[4,8,64,256]{3,2,1,0:T(8,128)(2,1)} all-to-all(bf16[4,8,64,256]{3,2,1,0:T(8,128)(2,1)} %bitcast.86), channel_id=1, replica_groups=mesh['ty'=8,'tx'=4] {'tx'}, dimensions={0} | all-to-all | bytes 2097152 | tf_op jit(solution)/shard_map/all_to_all | solution.py:493
  25.3 5.8 %shard_map.299 = bf16[16,2,2,128,128]{4,3,2,1,0:T(8,128)(2,1)} custom-call(bf16[4,8,64,256]{3,2,1,0:T(8,128)(2,1)} %all_to_all.40.x_ref, bf16[256,512]{1,0:T(8,128)(2,1)} %constant.125.clone.first_ref, f32[2,256,256]{2,1,0:T(8,128)} %constant.126.clone.twist_ref, bf16[512,512]{1,0:T(8,128)(2,1)} %constant.127.clone.second_ref), custom_call_target="tpu_custom_call" | custom-call | tf_op jit(solution)/shard_map/pallas_call | solution.py:496
  35.6 4.7 fusion.21
  59.6 5.1 %fusion.1 = (bf16[128,4096]{0,1:T(8,128)(2,1)S(1)}, bf16[128,4096]{0,1:T(8,128)(2,1)S(1)}, bf16[128,4096]{0,1:T(8,128)(2,1)S(1)}) fusion(f32[128,4096]{0,1:T(8,128)} %copy.72, f32[1,128,4096]{1,2,0:T(8,128)} %copy.92, f32[1,128,4096]{1,2,0:T(8,128)} %copy.94, f32[1,128,4096]{1,2,0:T(8,128)} %copy.91, f32[1,128,4096]{1,2,0:T(8,128)} %copy.93), kind=kLoop, calls=%fused_computation.6 | loop fusion | flops 7864320 | bytes 13631488 | tf_op jit(solution)/shard_map/convert_element_type | solution.py:400
  68.5 15.9 %all-to-all-done.1.refs_0_ = bf16[32,2,128,128]{3,2,1,0:T(8,128)(2,1)S(1)} async-done(((bf16[32,2,128,128]{3,2,1,0:T(8,128)(2,1)}), bf16[32,2,128,128]{3,2,1,0:T(8,128)(2,1)S(1)}, u32[]{:S(2)}, u32[]{:S(2)}) %all-to-all-start.1) | async-done | bytes 2097184 | tf_op jit(solution)/shard_map/all_to_all | solution.py:503
  85.7 14.4 %shard_map.300 = bf16[32,2,128,128]{3,2,1,0:T(8,128)(2,1)} custom-call(bf16[32,2,128,128]{3,2,1,0:T(8,128)(2,1)} %copy-done.2, bf16[1024,1024]{1,0:T(8,128)(2,1)} %constant.121.clone.refs_1_.refs_3_, bf16[32,256,256]{2,1,0:T(8,128)(2,1)} %constant.123.clone.refs_2_.refs_4_, bf16[32,128,128]{2,1,0:T(8,128)(2,1)} %bitcast.74, ...), custom_call_target="tpu_custom_call" | custom-call | tf_op jit(solution)/shard_map/pallas_call | solution.py:507
  100.1 4.8 all-to-all-start.2
  104.9 6.5 %shard_map.301.refs_0_ = f32[32,64,256]{2,1,0:T(8,128)} custom-call(f32[1,512,1024]{2,1,0:T(8,128)} %bitcast.79, bf16[1024,1024]{1,0:T(8,128)(2,1)} %constant.120.clone.order_ref), custom_call_target="tpu_custom_call" | custom-call | tf_op jit(solution)/shard_map/pallas_call | solution.py:810
  115.4 6.6 %shard_map.302.refs_2_ = f32[32,64,256]{2,1,0:T(8,128)} custom-call(f32[2,512,1024]{2,1,0:T(8,128)} %noise_ref.1, bf16[1024,1024]{1,0:T(8,128)(2,1)} %constant.120.clone.order_ref), custom_call_target="tpu_custom_call" | custom-call | tf_op jit(solution)/shard_map/pallas_call | solution.py:810
  130.8 22.8 %all-to-all-done.2 = bf16[32,2,128,128]{3,2,1,0:T(8,128)(2,1)S(1)} async-done(((bf16[32,2,128,128]{3,2,1,0:T(8,128)(2,1)}), bf16[32,2,128,128]{3,2,1,0:T(8,128)(2,1)S(1)}, u32[]{:S(2)}, u32[]{:S(2)}) %all-to-all-start.2) | async-done | bytes 2097184 | tf_op jit(solution)/shard_map/all_to_all | solution.py:516
  155.0 7.4 %shard_map.303 = bf16[4,8,64,256]{3,2,1,0:T(8,128)(2,1)} custom-call(bf16[16,2,2,128,128]{4,3,2,1,0:T(8,128)(2,1)} %bitcast.80, bf16[256,512]{1,0:T(8,128)(2,1)} %constant.125.clone.first_ref, f32[2,256,256]{2,1,0:T(8,128)} %constant.126.clone.twist_ref, bf16[512,512]{1,0:T(8,128)(2,1)} %constant.128.clone.second_ref), custom_call_target="tpu_custom_call" | custom-call | tf_op jit(solution)/shard_map/pallas_call | solution.py:518
  162.4 18.6 %all_to_all.41 = bf16[4,8,64,256]{3,2,1,0:T(8,128)(2,1)} all-to-all(bf16[4,8,64,256]{3,2,1,0:T(8,128)(2,1)} %shard_map.303), channel_id=1, replica_groups=mesh['ty'=8,'tx'=4] {'tx'}, dimensions={0} | all-to-all | bytes 2097152 | tf_op jit(solution)/shard_map/all_to_all | solution.py:523
  180.9 26.3 %shard_map.304 = (f32[32,64,256]{2,1,0:T(8,128)}, bf16[32,64,768]{2,1,0:T(8,128)(2,1)}) custom-call(f32[32,64,256]{2,1,0:T(8,128)} %shard_map.301.refs_0_, bf16[32,64,256]{2,1,0:T(8,128)(2,1)} %bitcast.76, f32[32,64,256]{2,1,0:T(8,128)} %shard_map.302.refs_2_, f32[32,64,128]{2,1,0:T(8,128)} %pad_maximum_fusion.3.refs_3_, bf16[256,512]{1,0:T(8,128)(2,1)} %bitcast.90, ...), custom_call_target="tpu_custom_call" | custom-call | tf_op jit(solution)/shard_map/pallas_call | solution.py:677
  211.3 6.3 %collective-permute-done = bf16[32,8,768]{2,1,0:T(8,128)(2,1)S(1)} collective-permute-done((bf16[32,8,768]{2,1,0:T(8,128)(2,1)S(1)}, bf16[32,8,768]{2,1,0:T(8,128)(2,1)S(1)}, u32[]{:S(2)}, u32[]{:S(2)}) %collective-permute-start) | collective-permute-done | bytes 393248 | tf_op jit(solution)/shard_map/ppermute | solution.py:714
  221.7 9.1 %collective-permute-done.1 = bf16[8,72,768]{2,1,0:T(8,128)(2,1)S(1)} collective-permute-done((bf16[8,72,768]{2,1,0:T(8,128)(2,1)S(1)}, bf16[8,72,768]{2,1,0:T(8,128)(2,1)S(1)}, u32[]{:S(2)}, u32[]{:S(2)}) %collective-permute-start.1) | collective-permute-done | bytes 884768 | tf_op jit(solution)/shard_map/ppermute | solution.py:714
  235.2 29.2 %shard_map.305 = (bf16[32,64,256]{2,1,0:T(8,128)(2,1)}, bf16[32,64,256]{2,1,0:T(8,128)(2,1)}) custom-call(s32[2]{0:T(128)} %get-tuple-element.38.refs_0_, bf16[40,72,768]{2,1,0:T(8,128)(2,1)} %pad_maximum_fusion.refs_1_, f32[32,64,128]{2,1,0:T(8,128)} %pad_maximum_fusion.4.refs_2_, bf16[2,512,1536]{2,1,0:T(8,128)(2,1)} %refs_3_.4, ...), custom_call_target="tpu_custom_call" | custom-call | tf_op jit(solution)/shard_map/pallas_call | solution.py:696
  270.5 5.5 %collective-permute-start.4 = (bf16[64,4096]{1,0:T(8,128)(2,1)}, bf16[64,4096]{1,0:T(8,128)(2,1)S(1)}, u32[]{:S(2)}, u32[]{:S(2)}) collective-permute-start(bf16[64,4096]{1,0:T(8,128)(2,1)} %copy.85), channel_id=1, source_target_pairs={{0,31},{1,30},{2,29},{3,28},{4,27},{5,26},{6,25},{7,24},{8,23},{9,... | collective-permute-start | bytes 1572872 | tf_op jit(solution)/shard_map/ppermute | solution.py:429
  279.1 14.6 %all-to-all-done.4.x_ref = bf16[4,8,64,256]{3,2,1,0:T(8,128)(2,1)S(1)} async-done(((bf16[4,8,64,256]{3,2,1,0:T(8,128)(2,1)}), bf16[4,8,64,256]{3,2,1,0:T(8,128)(2,1)S(1)}, u32[]{:S(2)}, u32[]{:S(2)}) %all-to-all-start.4) | async-done | bytes 1048608 | tf_op jit(solution)/shard_map/all_to_all | solution.py:493
  294.7 6.2 %shard_map.306 = bf16[16,2,128,128]{3,2,1,0:T(8,128)(2,1)} custom-call(bf16[4,8,64,256]{3,2,1,0:T(8,128)(2,1)} %copy-done.7, bf16[256,512]{1,0:T(8,128)(2,1)} %constant_dynamic-slice_fusion.first_ref, f32[2,256,256]{2,1,0:T(8,128)} %constant.130.clone.twist_ref, bf16[256,512]{1,0:T(8,128)(2,1)} %constant.131.clone.lower_ref, ...), custom_call_target="tpu_custom_call" | custom-call | tf_op jit(solution)/shard_map/pallas_call | solution.py:496
  309.6 5.4 %shard_map.307.refs_5_ = bf16[32,128,128]{2,1,0:T(8,128)(2,1)} custom-call(bf16[32,128,128]{2,1,0:T(8,128)(2,1)} %bitcast.75, bf16[32,128,128]{2,1,0:T(8,128)(2,1)} %bitcast.84, bf16[2,128,128]{2,1,0:T(8,128)(2,1)} %add_convert_fusion.pick_ref, bf16[2,128,128]{2,1,0:T(8,128)(2,1)} %constant.136.clone.flip_ref), custom_call_target="tpu_custom_call" | custom-call | tf_op jit(solution)/shard_map/pallas_call | solution.py:449
  315.0 16.9 %all-to-all-done.5.refs_2_ = bf16[32,128,128]{2,1,0:T(8,128)(2,1)S(1)} async-done(((bf16[32,128,128]{2,1,0:T(8,128)(2,1)}), bf16[32,128,128]{2,1,0:T(8,128)(2,1)S(1)}, u32[]{:S(2)}, u32[]{:S(2)}) %all-to-all-start.5) | async-done | bytes 1048608 | tf_op jit(solution)/shard_map/all_to_all | solution.py:503
  332.9 12.7 %shard_map.308 = bf16[32,128,128]{2,1,0:T(8,128)(2,1)} custom-call(s32[1]{0:T(128)} %bitcast.30.refs_0_, f32[32,2,8,128]{3,2,1,0:T(8,128)} %broadcast_in_dim.75.refs_1_, bf16[32,128,128]{2,1,0:T(8,128)(2,1)} %copy-done.4, bf16[1024,1024]{1,0:T(8,128)(2,1)} %constant.121.clone.refs_1_.refs_3_, bf16[32,256,256]{2,1,0:T(8,128)(2,1)} %constant.123.clone.refs_2_.refs_4_, ...), custom_call_target="tpu_custom_call" | custom-call | tf_op jit(solution)/shard_map/pallas_call | solution.py:507
  350.9 24.6 %all-to-all-done.6 = bf16[32,128,128]{2,1,0:T(8,128)(2,1)S(1)} async-done(((bf16[32,128,128]{2,1,0:T(8,128)(2,1)}), bf16[32,128,128]{2,1,0:T(8,128)(2,1)S(1)}, u32[]{:S(2)}, u32[]{:S(2)}) %all-to-all-start.6) | async-done | bytes 1048608 | tf_op jit(solution)/shard_map/all_to_all | solution.py:516
  376.5 6.5 %shard_map.309 = bf16[4,8,64,256]{3,2,1,0:T(8,128)(2,1)} custom-call(bf16[16,2,128,128]{3,2,1,0:T(8,128)(2,1)} %bitcast.83, bf16[256,512]{1,0:T(8,128)(2,1)} %constant.129.clone.first_ref, f32[2,256,256]{2,1,0:T(8,128)} %constant.130.clone.twist_ref, bf16[512,256]{1,0:T(8,128)(2,1)} %constant.133.clone.lower_ref, bf16[512,272]{1,0:T(8,128)(2,1)} %constant.134.clone.upper_ref), custom_call_target="tpu_custom_call" | custom-call | tf_op jit(solution)/shard_map/pallas_call | solution.py:518
  389.4 5.4 %collective-permute-done.3 = bf16[8,72,256]{2,1,0:T(8,128)(2,1)S(1)} collective-permute-done((bf16[8,72,256]{2,1,0:T(8,128)(2,1)S(1)}, bf16[8,72,256]{2,1,0:T(8,128)(2,1)S(1)}, u32[]{:S(2)}, u32[]{:S(2)}) %collective-permute-start.3) | collective-permute-done | bytes 294944 | tf_op jit(solution)/shard_map/ppermute | solution.py:714
  401.5 26.1 %shard_map.310 = (f32[32,64,256]{2,1,0:T(8,128)}, bf16[32,64,512]{2,1,0:T(8,128)(2,1)}) custom-call(f32[32,64,256]{2,1,0:T(8,128)} %multiply_subtract_fusion.1.refs_0_, bf16[32,64,256]{2,1,0:T(8,128)(2,1)} %bitcast.77, bf16[32,64,256]{2,1,0:T(8,128)(2,1)} %bitcast.82, f32[32,64,128]{2,1,0:T(8,128)} %pad_maximum_fusion.3.refs_3_, bf16[256,512]{1,0:T(8,128)(2,1)} %bitcast.91, ...), custom_call_target="tpu_custom_call" | custom-call | tf_op jit(solution)/shard_map/pallas_call | solution.py:677
  436.2 7.4 %collective-permute-done.7 = bf16[8,72,512]{2,1,0:T(8,128)(2,1)S(1)} collective-permute-done((bf16[8,72,512]{2,1,0:T(8,128)(2,1)S(1)}, bf16[8,72,512]{2,1,0:T(8,128)(2,1)S(1)}, u32[]{:S(2)}, u32[]{:S(2)}) %collective-permute-start.7) | collective-permute-done | bytes 589856 | tf_op jit(solution)/shard_map/ppermute | solution.py:714
  445.4 28.5 %shard_map.311 = bf16[32,64,256]{2,1,0:T(8,128)(2,1)} custom-call(s32[2]{0:T(128)} %get-tuple-element.52.refs_0_, bf16[40,72,512]{2,1,0:T(8,128)(2,1)} %pad_maximum_fusion.1.refs_1_, f32[32,64,128]{2,1,0:T(8,128)} %pad_maximum_fusion.5.refs_2_, bf16[2,512,1536]{2,1,0:T(8,128)(2,1)} %refs_3_.4, bf16[2,512,512]{2,1,0:T(8,128)(2,1)} %refs_4_.5, ...), custom_call_target="tpu_custom_call" | custom-call | tf_op jit(solution)/shard_map/pallas_call | solution.py:696
  477.2 5.0 collective-permute-done.8
  486.6 5.5 %collective-permute-done.9 = bf16[8,72,256]{2,1,0:T(8,128)(2,1)} collective-permute-done((bf16[8,72,256]{2,1,0:T(8,128)(2,1)}, bf16[8,72,256]{2,1,0:T(8,128)(2,1)}, u32[]{:S(2)}, u32[]{:S(2)}) %collective-permute-start.9) | collective-permute-done | bytes 294944 | tf_op jit(solution)/shard_map/ppermute | solution.py:714
  495.1 6.9 %shard_map.312 = f32[512,1024]{1,0:T(8,128)} custom-call(f32[32,64,256]{2,1,0:T(8,128)} %multiply_subtract_fusion.patch_ref, f32[2,512,1024]{2,1,0:T(8,128)} %noise_ref.1, bf16[1024,1024]{1,0:T(8,128)(2,1)} %constant.137.clone.order_ref), custom_call_target="tpu_custom_call" | custom-call | tf_op jit(solution)/shard_map/pallas_call | solution.py:827
  (118 shorter events, 106.0 us)
Async XLA Ops:
  31.1 53.2 %all-to-all-start.1 = ((bf16[32,2,128,128]{3,2,1,0:T(8,128)(2,1)}), bf16[32,2,128,128]{3,2,1,0:T(8,128)(2,1)S(1)}, u32[]{:S(2)}, u32[]{:S(2)}) async-start(bf16[32,2,128,128]{3,2,1,0:T(8,128)(2,1)} %bitcast.81), calls=%async_computation.1 | async-start | bytes 4194304 | tf_op jit(solution)/shard_map/all_to_all | solution.py:503
  84.4 1.3 copy-start.2
  100.1 53.6 %all-to-all-start.2 = ((bf16[32,2,128,128]{3,2,1,0:T(8,128)(2,1)}), bf16[32,2,128,128]{3,2,1,0:T(8,128)(2,1)S(1)}, u32[]{:S(2)}, u32[]{:S(2)}) async-start(bf16[32,2,128,128]{3,2,1,0:T(8,128)(2,1)} %shard_map.300), calls=%async_computation.2 | async-start | bytes 4194304 | tf_op jit(solution)/shard_map/all_to_all | solution.py:516
  104.9 6.5 %copy-start.13 = (s32[2,2]{1,0:T(2,128)S(1)}, s32[2,2]{1,0:T(2,128)}, u32[]{:S(2)}) copy-start(s32[2,2]{1,0:T(2,128)} %param.34) | copy-start | bytes 52
  104.9 10.2 %copy-start.12 = (s32[32,64]{1,0:T(8,128)S(1)}, s32[32,64]{1,0:T(8,128)}, u32[]{:S(2)}) copy-start(s32[32,64]{1,0:T(8,128)} %param.35) | copy-start | bytes 24580
  115.4 6.6 %copy-start.10 = (bf16[512,256]{1,0:T(8,128)(2,1)S(1)}, bf16[512,256]{1,0:T(8,128)(2,1)}, u32[]{:S(2)}) copy-start(bf16[512,256]{1,0:T(8,128)(2,1)} %param.44) | copy-start | bytes 786436
  153.6 1.3 copy-start.3
  208.2 9.4 %collective-permute-start = (bf16[32,8,768]{2,1,0:T(8,128)(2,1)S(1)}, bf16[32,8,768]{2,1,0:T(8,128)(2,1)S(1)}, u32[]{:S(2)}, u32[]{:S(2)}) collective-permute-start(bf16[32,8,768]{2,1,0:T(8,128)(2,1)S(1)} %slice.87), channel_id=1, source_target_pairs={{0,3},{1,0},{2,1},{3,2},{4,7},{5,4},{6,5},{7,6},{8,11},{9,8},{10,9... | collective-permute-start | bytes 1179656 | tf_op jit(solution)/shard_map/ppermute | solution.py:714
  217.6 1.8 copy-start
  219.5 11.3 %collective-permute-start.1 = (bf16[8,72,768]{2,1,0:T(8,128)(2,1)S(1)}, bf16[8,72,768]{2,1,0:T(8,128)(2,1)S(1)}, u32[]{:S(2)}, u32[]{:S(2)}) collective-permute-start(bf16[8,72,768]{2,1,0:T(8,128)(2,1)S(1)} %slice.99), channel_id=1, source_target_pairs={{0,28},{4,0},{8,4},{12,8},{16,12},{20,16},{24,20},{28,24},{1,29},{... | collective-permute-start | bytes 2654216 | tf_op jit(solution)/shard_map/ppermute | solution.py:714
  264.5 29.2 %all-to-all-start.4 = ((bf16[4,8,64,256]{3,2,1,0:T(8,128)(2,1)}), bf16[4,8,64,256]{3,2,1,0:T(8,128)(2,1)S(1)}, u32[]{:S(2)}, u32[]{:S(2)}) async-start(bf16[4,8,64,256]{3,2,1,0:T(8,128)(2,1)} %bitcast.92), calls=%async_computation.4 | async-start | bytes 2097152 | tf_op jit(solution)/shard_map/all_to_all | solution.py:493
  269.0 9.3 %copy-start.11 = (bf16[272,512]{1,0:T(8,128)(2,1)S(1)}, bf16[272,512]{1,0:T(8,128)(2,1)}, u32[]{:S(2)}) copy-start(bf16[272,512]{1,0:T(8,128)(2,1)} %constant.135.clone) | copy-start | bytes 835588
  270.5 30.4 %collective-permute-start.4 = (bf16[64,4096]{1,0:T(8,128)(2,1)}, bf16[64,4096]{1,0:T(8,128)(2,1)S(1)}, u32[]{:S(2)}, u32[]{:S(2)}) collective-permute-start(bf16[64,4096]{1,0:T(8,128)(2,1)} %copy.85), channel_id=1, source_target_pairs={{0,31},{1,30},{2,29},{3,28},{4,27},{5,26},{6,25},{7,24},{8,23},{9,... | collective-permute-start | bytes 1572872 | tf_op jit(solution)/shard_map/ppermute | solution.py:429
  278.3 22.6 %collective-permute-start.5 = (bf16[1,4096]{1,0:T(2,128)(2,1)S(1)}, bf16[1,4096]{1,0:T(2,128)(2,1)S(1)}, u32[]{:S(2)}, u32[]{:S(2)}) collective-permute-start(bf16[1,4096]{1,0:T(2,128)(2,1)S(1)} %copy.86), channel_id=1, source_target_pairs={{1,31},{2,30},{3,29},{4,28},{5,27},{6,26},{7,25},{8,24},{9,23},{10... | collective-permute-start | bytes 24584 | tf_op jit(solution)/shard_map/ppermute | solution.py:430
  293.7 1.0 copy-start.7
  300.9 30.9 %all-to-all-start.5 = ((bf16[32,128,128]{2,1,0:T(8,128)(2,1)}), bf16[32,128,128]{2,1,0:T(8,128)(2,1)S(1)}, u32[]{:S(2)}, u32[]{:S(2)}) async-start(bf16[32,128,128]{2,1,0:T(8,128)(2,1)} %bitcast.87), calls=%async_computation.5 | async-start | bytes 2097152 | tf_op jit(solution)/shard_map/all_to_all | solution.py:503
  307.3 2.0 copy-start.14
  331.8 1.1 copy-start.4
  345.6 3.4 copy-start.9
  345.7 29.9 %all-to-all-start.6 = ((bf16[32,128,128]{2,1,0:T(8,128)(2,1)}), bf16[32,128,128]{2,1,0:T(8,128)(2,1)S(1)}, u32[]{:S(2)}, u32[]{:S(2)}) async-start(bf16[32,128,128]{2,1,0:T(8,128)(2,1)} %shard_map.308), calls=%async_computation.6 | async-start | bytes 2097152 | tf_op jit(solution)/shard_map/all_to_all | solution.py:516
  349.1 37.4 %collective-permute-start.2 = (bf16[32,8,256]{2,1,0:T(8,128)(2,1)S(1)}, bf16[32,8,256]{2,1,0:T(8,128)(2,1)S(1)}, u32[]{:S(2)}, u32[]{:S(2)}) collective-permute-start(bf16[32,8,256]{2,1,0:T(8,128)(2,1)S(1)} %slice.89), channel_id=1, source_target_pairs={{0,1},{1,2},{2,3},{3,0},{4,5},{5,6},{6,7},{7,4},{8,9},{9,10},{10,1... | collective-permute-start | bytes 393224 | tf_op jit(solution)/shard_map/ppermute | solution.py:714
  375.5 1.0 copy-start.6
  382.9 17.5 %all-to-all-start.7 = ((bf16[4,8,64,256]{3,2,1,0:T(8,128)(2,1)}), bf16[4,8,64,256]{3,2,1,0:T(8,128)(2,1)S(1)}, u32[]{:S(2)}, u32[]{:S(2)}) async-start(bf16[4,8,64,256]{3,2,1,0:T(8,128)(2,1)} %shard_map.309), calls=%async_computation.7 | async-start | bytes 2097152 | tf_op jit(solution)/shard_map/all_to_all | solution.py:523
  386.6 8.3 %collective-permute-start.3 = (bf16[8,72,256]{2,1,0:T(8,128)(2,1)S(1)}, bf16[8,72,256]{2,1,0:T(8,128)(2,1)S(1)}, u32[]{:S(2)}, u32[]{:S(2)}) collective-permute-start(bf16[8,72,256]{2,1,0:T(8,128)(2,1)S(1)} %slice.100), channel_id=1, source_target_pairs={{0,4},{4,8},{8,12},{12,16},{16,20},{20,24},{24,28},{28,0},{1,5},{5... | collective-permute-start | bytes 884744 | tf_op jit(solution)/shard_map/ppermute | solution.py:714
  400.4 1.0 copy-start.5
  428.6 7.5 %collective-permute-start.6 = (bf16[32,8,512]{2,1,0:T(8,128)(2,1)S(1)}, bf16[32,8,512]{2,1,0:T(8,128)(2,1)S(1)}, u32[]{:S(2)}, u32[]{:S(2)}) collective-permute-start(bf16[32,8,512]{2,1,0:T(8,128)(2,1)S(1)} %slice.95), channel_id=1, source_target_pairs={{0,3},{1,0},{2,1},{3,2},{4,7},{5,4},{6,5},{7,6},{8,11},{9,8},{10,9... | collective-permute-start | bytes 786440 | tf_op jit(solution)/shard_map/ppermute | solution.py:714
  436.1 7.5 %collective-permute-start.7 = (bf16[8,72,512]{2,1,0:T(8,128)(2,1)S(1)}, bf16[8,72,512]{2,1,0:T(8,128)(2,1)S(1)}, u32[]{:S(2)}, u32[]{:S(2)}) collective-permute-start(bf16[8,72,512]{2,1,0:T(8,128)(2,1)S(1)} %slice.101), channel_id=1, source_target_pairs={{0,28},{4,0},{8,4},{12,8},{16,12},{20,16},{24,20},{28,24},{1,29},{... | collective-permute-start | bytes 1769480 | tf_op jit(solution)/shard_map/ppermute | solution.py:714
  445.4 46.7 %copy-start.8 = (f32[32,64,256]{2,1,0:T(8,128)S(1)}, f32[32,64,256]{2,1,0:T(8,128)}, u32[]{:S(2)}) copy-start(f32[32,64,256]{2,1,0:T(8,128)} %get-tuple-element.42) | copy-start | bytes 6291460
  473.9 18.2 %copy-start.1 = (bf16[32,64,256]{2,1,0:T(8,128)(2,1)S(1)}, bf16[32,64,256]{2,1,0:T(8,128)(2,1)}, u32[]{:S(2)}) copy-start(bf16[32,64,256]{2,1,0:T(8,128)(2,1)} %shard_map.311) | copy-start | bytes 3145732
  474.9 7.3 %collective-permute-start.8 = (bf16[32,8,256]{2,1,0:T(8,128)(2,1)S(1)}, bf16[32,8,256]{2,1,0:T(8,128)(2,1)S(1)}, u32[]{:S(2)}, u32[]{:S(2)}) collective-permute-start(bf16[32,8,256]{2,1,0:T(8,128)(2,1)S(1)} %slice.102), channel_id=1, source_target_pairs={{0,1},{1,2},{2,3},{3,0},{4,5},{5,6},{6,7},{7,4},{8,9},{9,10},{10,1... | collective-permute-start | bytes 393224 | tf_op jit(solution)/shard_map/ppermute | solution.py:714
  483.8 8.3 %collective-permute-start.9 = (bf16[8,72,256]{2,1,0:T(8,128)(2,1)}, bf16[8,72,256]{2,1,0:T(8,128)(2,1)}, u32[]{:S(2)}, u32[]{:S(2)}) collective-permute-start(bf16[8,72,256]{2,1,0:T(8,128)(2,1)} %pad_maximum_fusion.7), channel_id=1, source_target_pairs={{0,4},{4,8},{8,12},{12,16},{16,20},{20,24},{24,28},{28,0},{1,5},{5... | collective-permute-start | bytes 884744 | tf_op jit(solution)/shard_map/ppermute | solution.py:714
where the time goes:
time: 511 us; the launch traced here: 502 us
  Pallas kernels  194 us (38%)
  waiting for transfers between devices  140 us (27%)
  local copies, waits for them, and re-layouts  53.4 us (10%)
  blocking collectives  38.5 us (8%)
  starting transfers between devices  38.5 us (8%)
  other arithmetic  27.9 us (5%)
  between operations  10.6 us (2%)
    pallas_call x2, Pallas kernels, second_block(): pl.pallas_call(functools.partial(second_kernel, sigma), grid_spec=pltpu.P...  57.7 us
    pallas_call x2, Pallas kernels, first_block(): pl.pallas_call(functools.partial(first_kernel, zeta, sigma, len(grads)),...  52.4 us
    all_to_all x2, waiting for transfers between devices, patch_gradient(): lax.all_to_all(wave, ('ty', 'tx'), split_axis=0, concat_axis=0, tiled=True)  47.4 us
    ppermute x8, waiting for transfers between devices, from_behind(): lax.ppermute(shard, axis, [(i, (i + by) % size) for i in range(size)])  43 us
    all_to_all x2, waiting for transfers between devices, patch_gradient(): lax.all_to_all(sent.reshape(part), ('ty', 'tx'), split_axis=0, concat_axi...  32.7 us
    pallas_call x2, Pallas kernels, patch_gradient(): pl.pallas_call(functools.partial(column_kernel, halved), in_specs=[pl.Blo...  27.1 us
    unnamed x39, local copies, waits for them, and re-layouts  26.9 us
    all_to_all x1, blocking collectives, patch_gradient(): lax.all_to_all(state.reshape(lanes, own, cols, PIXELS), 'tx', split_axis=...  20 us
  transfers between devices with their start and end apart: 16, of which 13 were waited for; matrix products, arithmetic and copies ran while one was open for 12% of the time, Pallas kernels for 6%

commit v1 on v0

--- a/solution.py
+++ b/solution.py
@@ -600,41 +600,80 @@
     return flow + 0.5 * total
 
 
-def first_kernel(zeta, sigma, count, *refs):
-    state_ref, grad_refs, refs = refs[0], refs[1 : 1 + count], refs[1 + count :]
+def rolled_band(sign, shift_ref, refs, rows):
+    main_ref, side_ref, edge_ref, corner_ref = refs
+    cols = main_ref.shape[1]
+    top = pl.program_id(0) * WIN + sign * shift_ref[0]
+    behind = -rows if sign > 0 else WIN
+    beside = -cols if sign > 0 else WIN
+
+    def pick(width, offset):
+        source = lax.broadcasted_iota(jnp.int32, (cols, width), 1)
+        wanted = lax.broadcasted_iota(jnp.int32, (cols, width), 0) + sign * shift_ref[1] + offset
+        return jnp.where(source == wanted, 1.0, 0.0).astype(BF16)
+
+    pick_main, pick_side = pick(cols, 0), pick(WIN, beside)
+    band = []
+    for j in range(WIN):
+        row = top + j
+        inside = (row >= 0) & (row < rows)
+        here, there = jnp.clip(row, 0, rows - 1), jnp.clip(row + behind, 0, WIN - 1)
+        main = jnp.where(inside, main_ref[here], edge_ref[there])
+        side = jnp.where(inside, side_ref[here], corner_ref[there])
+        band.append(mm(pick_main, main) + mm(pick_side, side))
+    return jnp.stack(band)
+
+
+def first_kernel(zeta, sigma, count, rows, before, *refs):
+    shift_ref, state_ref, *refs = refs
+    state = state_ref[...]
+    if before is not None:
+        state = state - before * rolled_band(-1, shift_ref, refs[:4], rows)
+        refs = refs[4:]
+    grad_refs, refs = refs[:count], refs[count:]
     if sigma is not None:
-        noise_ref, refs = refs[0], refs[1:]
+        noise_ref, *refs = refs
     bias_ref, embed_ref, qkv_ref, proj_ref, up_ref, down_ref, gain_ref = refs[:7]
-    base_ref, out_ref, *scratch = refs[7:]
+    base_ref, out_ref, side_ref, edge_ref, corner_ref, *scratch = refs[7:]
     step = zeta * sum(grad_ref[...].astype(F32) for grad_ref in grad_refs)
-    half = state_ref[...] - step
+    half = state - step
     tokens = mm(to_windows(half).astype(BF16), embed_ref[...]).astype(BF16).astype(F32)
+    flow = swin_band(tokens, bias_ref, qkv_ref, proj_ref, up_ref, down_ref, gain_ref, *scratch)
+    result = from_windows(flow, half.shape[1]).astype(BF16)
+    out_ref[:, :, :D] = result
+    side_ref[:, :, :D] = result[:, :WIN]
     if sigma is None:
         base_ref[...] = half
     else:
         noise = sigma * noise_ref[...]
         base_ref[...] = half + noise
-        out_ref[:, :, D:] = (noise - step).astype(BF16)
-    flow = swin_band(tokens, bias_ref, qkv_ref, proj_ref, up_ref, down_ref, gain_ref, *scratch)
-    out_ref[:, :, :D] = from_windows(flow, half.shape[1]).astype(BF16)
-
-
-def second_kernel(sigma, *refs):
-    shift_ref, grid_ref, bias_ref, qkv_ref, proj_ref, up_ref, down_ref, gain_ref = refs[:8]
-    unembed_ref, out_ref, *scratch = refs[8:]
+        change = (noise - step).astype(BF16)
+        out_ref[:, :, D:] = change
+        side_ref[:, :, D:] = change[:, :WIN]
+
+    @pl.when(pl.program_id(0) == 0)
+    def _():
+        edge_ref[...] = out_ref[...]
+        corner_ref[...] = side_ref[...]
+
+
+def second_kernel(sigma, rows, *refs):
+    shift_ref, *refs = refs
+    tile_refs, refs = refs[:4], refs[4:]
+    bias_ref, qkv_ref, proj_ref, up_ref, down_ref, gain_ref, unembed_ref = refs[:7]
+    out_ref, side_ref, edge_ref, corner_ref, *scratch = refs[7:]
     if sigma is not None:
-        state_ref, scratch = scratch[0], scratch[1:]
+        state_ref, *scratch = scratch
     cols = out_ref.shape[1]
-    top = pl.program_id(0) * WIN + shift_ref[0]
-    wide = grid_ref[pl.ds(top, WIN)]
-    place = lax.broadcasted_iota(jnp.int32, (cols, wide.shape[1]), 1)
-    target = lax.broadcasted_iota(jnp.int32, (cols, wide.shape[1]), 0) + shift_ref[1]
-    pick = jnp.where(place == target, 1.0, 0.0).astype(BF16)
-    band = jnp.stack([mm(pick, wide[n]) for n in range(WIN)])
+    band = rolled_band(1, shift_ref, tile_refs, rows)
     tokens = to_windows(band[:, :, :D])
     flow = swin_band(tokens, bias_ref, qkv_ref, proj_ref, up_ref, down_ref, gain_ref, *scratch)
     estimate = from_windows(mm(flow.astype(BF16), unembed_ref[...]), cols)
-    out_ref[...] = estimate.astype(BF16)
+    narrow = estimate.astype(BF16)
+    out_ref[...] = narrow
+    edge_ref[...] = narrow
+    side_ref[...] = narrow[:, cols - WIN :]
+    corner_ref[...] = narrow[:, cols - WIN :]
     if sigma is not None:
         state_ref[...] = (band[:, :, D:] - sigma * estimate).astype(BF16)
 
@@ -645,7 +684,7 @@
 
 
 def band_of(step, cols):
-    return pl.BlockSpec((step, cols, PIXELS), lambda n: (n, 0, 0))
+    return pl.BlockSpec((step, cols, PIXELS), lambda n, *_: (n, 0, 0))
 
 
 def member(array, j):
@@ -670,58 +709,72 @@
     ]
 
 
-def first_block(zeta, sigma, state, grads, noise, bias, w_embed, weights):
+def strip_outs(rows, cols, feats):
+    specs = [band_spec(cols, feats), band_spec(WIN, feats)]
+    specs += [
+        pl.BlockSpec((WIN, width, feats), lambda *_: (0, 0, 0)) for width in (cols, WIN)
+    ]
+    shapes = [(rows, cols), (rows, WIN), (WIN, cols), (WIN, WIN)]
+    return specs, [jax.ShapeDtypeStruct(shape + (feats,), BF16) for shape in shapes]
+
+
+def first_block(zeta, sigma, state, before, shift, back, grads, noise, bias, w_embed, weights):
     rows, cols, _ = state.shape
-    fields = [state, *grads] + ([] if sigma is None else [noise])
+    fields = [*grads] + ([] if sigma is None else [noise])
     feats = D if sigma is None else D + PIXELS
+    specs, shapes = strip_outs(rows, cols, feats)
     return pl.pallas_call(
-        functools.partial(first_kernel, zeta, sigma, len(grads)),
-        grid=(rows // WIN,),
-        in_specs=[band_spec(cols, PIXELS)] * len(fields)
-        + [bias_spec(cols), whole(w_embed)]
-        + [member(value, 0) for value in weights],
-        out_specs=[band_spec(cols, PIXELS), band_spec(cols, feats)],
-        out_shape=[
-            jax.ShapeDtypeStruct((rows, cols, PIXELS), F32),
-            jax.ShapeDtypeStruct((rows, cols, feats), BF16),
-        ],
-        scratch_shapes=band_scratch(cols),
-        compiler_params=PARAMS,
-    )(*fields, bias, w_embed, *weights)
-
-
-def second_block(sigma, shift, grid, bias, w_unembed, weights):
-    rows, cols = grid.shape[0] - WIN, grid.shape[1] - WIN
-    outs = 1 if sigma is None else 2
-    return pl.pallas_call(
-        functools.partial(second_kernel, sigma),
+        functools.partial(first_kernel, zeta, sigma, len(grads), rows, before),
         grid_spec=pltpu.PrefetchScalarGridSpec(
             num_scalar_prefetch=1,
             grid=(rows // WIN,),
-            in_specs=[whole(grid), bias_spec(cols)]
+            in_specs=[band_spec(cols, PIXELS)]
+            + [whole(value) for value in back]
+            + [band_spec(cols, PIXELS)] * len(fields)
+            + [bias_spec(cols), whole(w_embed)]
+            + [member(value, 0) for value in weights],
+            out_specs=[band_spec(cols, PIXELS)] + specs,
+            scratch_shapes=band_scratch(cols),
+        ),
+        out_shape=[jax.ShapeDtypeStruct((rows, cols, PIXELS), F32)] + shapes,
+        compiler_params=PARAMS,
+    )(shift, state, *back, *fields, bias, w_embed, *weights)
+
+
+def second_block(sigma, shift, tile, bias, w_unembed, weights):
+    rows, cols, _ = tile[0].shape
+    specs, shapes = strip_outs(rows, cols, PIXELS)
+    if sigma is not None:
+        specs, shapes = specs + specs[:1], shapes + shapes[:1]
+    return pl.pallas_call(
+        functools.partial(second_kernel, sigma, rows),
+        grid_spec=pltpu.PrefetchScalarGridSpec(
+            num_scalar_prefetch=1,
+            grid=(rows // WIN,),
+            in_specs=[whole(value) for value in tile]
+            + [bias_spec(cols)]
             + [member(value, 1) for value in weights]
             + [whole(w_unembed)],
-            out_specs=[band_spec(cols, PIXELS)] * outs,
+            out_specs=specs,
             scratch_shapes=band_scratch(cols),
         ),
-        out_shape=[jax.ShapeDtypeStruct((rows, cols, PIXELS), BF16)] * outs,
+        out_shape=shapes,
         compiler_params=PARAMS,
-    )(shift, grid, bias, *weights, w_unembed)
-
-
-def from_behind(shard, axis, by):
-    size = lax.axis_size(axis)
-    return lax.ppermute(shard, axis, [(i, (i + by) % size) for i in range(size)])
-
-
-def with_next(grid):
-    wide = jnp.concatenate([grid, from_behind(grid[:, :WIN], "tx", -1)], axis=1)
-    return jnp.concatenate([wide, from_behind(wide[:WIN], "ty", -1)], axis=0)
-
-
-def with_previous(grid):
-    wide = jnp.concatenate([from_behind(grid[:, -WIN:], "tx", 1), grid], axis=1)
-    return jnp.concatenate([from_behind(wide[-WIN:], "ty", 1), wide], axis=0)
+    )(shift, *tile, bias, *weights, w_unembed)
+
+
+def from_neighbours(tile, by):
+    main, side, edge, corner = tile
+    ty, tx = lax.axis_size("ty"), lax.axis_size("tx")
+    across = [
+        (i * tx + k, (i + by) % ty * tx + (k + by) % tx) for i in range(ty) for k in range(tx)
+    ]
+    return (
+        main,
+        lax.ppermute(side, "tx", [(k, (k + by) % tx) for k in range(tx)]),
+        lax.ppermute(edge, "ty", [(i, (i + by) % ty) for i in range(ty)]),
+        lax.ppermute(corner, ("ty", "tx"), across),
+    )
 
 
 def windows_of(grid):
@@ -784,16 +837,18 @@
         out_ref[i] = patch.astype(out_ref.dtype)
 
 
-def to_tile_kernel(scale, patch_ref, noise_ref, order_ref, out_ref):
-    count, cols, _ = patch_ref.shape
+def to_tile_kernel(sigma, scale, rows, *refs):
+    shift_ref, base_ref, *refs = refs
+    noise_ref, order_ref, out_ref = refs[4:]
+    count, cols, _ = base_ref.shape
     parts = LANES // cols
     groups = PATCH // parts
     width = groups * PATCH
+    state = base_ref[...] - sigma * rolled_band(-1, shift_ref, refs[:4], rows)
     bands = []
     for i in range(count):
-        patch = patch_ref[i]
         stacked = jnp.concatenate(
-            [patch[:, h * width : (h + 1) * width] for h in range(parts)], axis=0
+            [state[i, :, h * width : (h + 1) * width] for h in range(parts)], axis=0
         )
         turned = stacked.T
         bands.append(
@@ -820,22 +875,25 @@
     )(tiles, order)
 
 
-def tile_of(patches, scale, noise, j):
-    rows, cols, _ = patches.shape
+def tile_of(base, sigma, shift, back, scale, noise, j):
+    rows, cols, _ = base.shape
     order = jnp.asarray(lane_order(cols)[1])
-    step = rows // 4
     return pl.pallas_call(
-        functools.partial(to_tile_kernel, scale),
-        grid=(rows // step,),
-        in_specs=[
-            band_of(step, cols),
-            pl.BlockSpec((None, step * PATCH, cols * PATCH), lambda n: (j, n, 0)),
-            whole(order),
-        ],
-        out_specs=pl.BlockSpec((step * PATCH, cols * PATCH), lambda n: (n, 0)),
+        functools.partial(to_tile_kernel, sigma, scale, rows),
+        grid_spec=pltpu.PrefetchScalarGridSpec(
+            num_scalar_prefetch=1,
+            grid=(rows // WIN,),
+            in_specs=[band_spec(cols, PIXELS)]
+            + [whole(value) for value in back]
+            + [
+                pl.BlockSpec((None, WIN * PATCH, cols * PATCH), lambda n, *_: (j, n, 0)),
+                whole(order),
+            ],
+            out_specs=pl.BlockSpec((WIN * PATCH, cols * PATCH), lambda n, *_: (n, 0)),
+        ),
         out_shape=jax.ShapeDtypeStruct((rows * PATCH, cols * PATCH), F32),
         compiler_params=PARAMS,
-    )(patches, noise, order)
+    )(shift, base, *back, noise, order)
 
 
 def per_device(
@@ -862,7 +920,7 @@
         )
         biases.append(bias_of(labels, None))
     beside = (state, extras, first_bias, biases, w_embed, w_unembed)
-    shift = moving = mirror = None
+    shift, before, back, moving, mirror = offsets[0], None, (), None, None
     grads = []
     if fast:
         weight, scale, data = spectrum_inputs(gains, observed, vis_weight, devices)
@@ -873,28 +931,31 @@
         state, extras, first_bias, biases, w_embed, w_unembed = beside
     for step in range(STEPS):
         if not fast:
-            grad = plain_gradient(tile_of(state, 0.0, noise, 0), gains, observed, vis_weight)
+            tile = image if step == 0 else tile_of(state, before, shift, back, 0.0, noise, 0)
+            grad = plain_gradient(tile, gains, observed, vis_weight)
             grads = [patches_of(grad.astype(F32)[None], 0, BF16)]
         elif step > 0:
             grads = grads + [patch_gradient(moving, scale, None, shift, mirror, ())[0]]
         last = step + 1 == STEPS
         sigma = None if last else SIGMAS[step + 1]
-        base, first = first_block(
-            STEP_SIZES[step], sigma, state, grads, extras[step], first_bias, w_embed, weights
-        )
-        shift = offsets[step]
-        grid = with_next(first)
+        state, *first = first_block(
+            STEP_SIZES[step], sigma, state, before, shift, back, grads, extras[step], first_bias,
+            w_embed, weights,
+        )
+        shift, before = offsets[step], SIGMAS[step]
+        first = from_neighbours(first, -1)
         if fast and step == 0:
-            grid, weight = lax.optimization_barrier((grid, weight))
+            first, weight = lax.optimization_barrier((first, weight))
             mirror = mirrored_exchange(weight)
-        rolled, *moving = second_block(
-            None if last else SIGMAS[step], shift, grid, biases[step], w_unembed, weights
-        )
-        moving = None if last else moving[0]
-        corner = (WIN - shift[0], WIN - shift[1], jnp.zeros((), jnp.int32))
-        estimate = lax.dynamic_slice(with_previous(rolled), corner, base.shape)
-        state = base - SIGMAS[step] * estimate.astype(F32)
-    return tile_of(state, SIGMAS[STEPS], noise, STEPS - 1)
+        rolled = second_block(
+            None if last else before, shift, first, biases[step], w_unembed, weights
+        )
+        if not last:
+            *rolled, moving = rolled
+        if fast and step == 0:
+            moving, mirror = lax.optimization_barrier((moving, mirror))
+        back = from_neighbours(rolled, 1)
+    return tile_of(state, before, shift, back, SIGMAS[STEPS], noise, STEPS - 1)
 
 
 def solution(mesh):

time: 511 us -> 484 us (0.947)
  waiting for transfers between devices: 140 us -> 113 us
  other arithmetic: 27.9 us -> 15.9 us
  blocking collectives: 38.5 us -> 50 us
  Pallas kernels: 194 us -> 201 us
  between operations: 10.6 us -> 5.01 us
  local copies, waits for them, and re-layouts: 53.4 us -> 48 us
    all_to_all x2 -> x1, waiting for transfers between devices: 47.4 us -> 19.4 us  [patch_gradient(): lax.all_to_all(wave, ('ty', 'tx'), split_axis=0, concat_axis=0, tiled=True)]
    all_to_all x1, blocking collectives: 18.6 us -> 30 us  [patch_gradient(): lax.all_to_all(wave, ('ty', 'tx'), split_axis=0, concat_axis=0, tiled=True)]
    all_to_all x1 -> x2, waiting for transfers between devices: 2.04 us -> 12.9 us  [patch_gradient(): grad = lax.all_to_all(slabs, 'tx', split_axis=0, concat_axis=0, tiled=True)]
    concatenate x3 -> x0, other arithmetic: 7.95 us -> none  [the longest x2 6.27 us: with_next(): return jnp.concatenate([wide, from_behind(wide[:WIN], 'ty', -1)], axis=0)]
    ppermute x8 -> x12, starting transfers between devices: 7.7 us -> 14.9 us  [the longest x4 7.84 us: from_neighbours(): lax.ppermute(corner, ('ty', 'tx'), across)]
    pallas_call x5, Pallas kernels: 117 us -> 124 us  [the longest x2 59.4 us: second_block(): pl.pallas_call(functools.partial(second_kernel, sigma, rows), grid_spec=p...]
    ppermute x8 -> x12, waiting for transfers between devices: 43 us -> 35.9 us  [the longest x4 31.6 us: from_neighbours(): lax.ppermute(corner, ('ty', 'tx'), across)]
    sub x2 -> x0, other arithmetic: 6.54 us -> none  [per_device(): state = base - SIGMAS[step] * estimate.astype(F32)]
  transfers between devices with their start and end apart: 16 -> 20, of which waited for: 13 -> 12; matrix products, arithmetic and copies ran while one was open for 12% -> 11% of each run, Pallas kernels for 6% -> 10%
where the time goes in v1:
time: 484 us; the launch traced here: 476 us
  Pallas kernels  201 us (42%)
  waiting for transfers between devices  113 us (23%)
  blocking collectives  50 us (10%)
  local copies, waits for them, and re-layouts  48 us (10%)
  starting transfers between devices  43.1 us (9%)
  other arithmetic  15.9 us (3%)
  between operations  5.01 us (1%)
    pallas_call x2, Pallas kernels, second_block(): pl.pallas_call(functools.partial(second_kernel, sigma, rows), grid_spec=p...  59.4 us
    pallas_call x2, Pallas kernels, first_block(): pl.pallas_call(functools.partial(first_kernel, zeta, sigma, len(grads), r...  56.1 us
    all_to_all x2, waiting for transfers between devices, patch_gradient(): lax.all_to_all(sent.reshape(part), ('ty', 'tx'), split_axis=0, concat_axi...  32.8 us
    ppermute x4, waiting for transfers between devices, from_neighbours(): lax.ppermute(corner, ('ty', 'tx'), across)  31.6 us
    all_to_all x1, blocking collectives, patch_gradient(): lax.all_to_all(wave, ('ty', 'tx'), split_axis=0, concat_axis=0, tiled=True)  30 us
    pallas_call x2, Pallas kernels, patch_gradient(): pl.pallas_call(functools.partial(column_kernel, halved), in_specs=[pl.Blo...  27 us
    unnamed x66, local copies, waits for them, and re-layouts  24.6 us
    all_to_all x1, blocking collectives, patch_gradient(): lax.all_to_all(state.reshape(lanes, own, cols, PIXELS), 'tx', split_axis=...  20 us
  transfers between devices with their start and end apart: 20, of which 12 were waited for; matrix products, arithmetic and copies ran while one was open for 11% of the time, Pallas kernels for 10%

profile of v1, /device:TPU:0, one launch (start us, length us, event | category | flops | bytes accessed | tf_op | source)
XLA Modules:
  0.0 476.0 jit_solution(11807269702489252028)
XLA Ops:
  0.0 5.4 %shard_map.298 = bf16[32,64,256]{2,1,0:T(8,128)(2,1)} custom-call(f32[1,512,1024]{2,1,0:T(8,128)} %bitcast.72, bf16[1024,1024]{1,0:T(8,128)(2,1)} %constant.99.clone.order_ref), custom_call_target="tpu_custom_call" | custom-call | tf_op jit(solution)/shard_map/pallas_call | solution.py:865
  5.4 20.0 %all_to_all.40.x_ref = bf16[4,8,64,256]{3,2,1,0:T(8,128)(2,1)} all-to-all(bf16[4,8,64,256]{3,2,1,0:T(8,128)(2,1)} %bitcast.79), channel_id=1, replica_groups=mesh['ty'=8,'tx'=4] {'tx'}, dimensions={0} | all-to-all | bytes 2097152 | tf_op jit(solution)/shard_map/all_to_all | solution.py:493
  25.4 5.8 %shard_map.299 = bf16[16,2,2,128,128]{4,3,2,1,0:T(8,128)(2,1)} custom-call(bf16[4,8,64,256]{3,2,1,0:T(8,128)(2,1)} %all_to_all.40.x_ref, bf16[256,512]{1,0:T(8,128)(2,1)} %constant.104.clone.first_ref, f32[2,256,256]{2,1,0:T(8,128)} %constant.105.clone.twist_ref, bf16[512,512]{1,0:T(8,128)(2,1)} %constant.106.clone.second_ref), custom_call_target="tpu_custom_call" | custom-call | tf_op jit(solution)/shard_map/pallas_call | solution.py:496
  31.1 4.5 all-to-all-start.1
  38.6 4.7 fusion.18
  46.2 4.7 fusion.17
  59.6 5.1 %fusion.1 = (bf16[128,4096]{0,1:T(8,128)(2,1)S(1)}, bf16[128,4096]{0,1:T(8,128)(2,1)S(1)}, bf16[128,4096]{0,1:T(8,128)(2,1)S(1)}) fusion(f32[128,4096]{0,1:T(8,128)} %copy.72, f32[1,128,4096]{1,2,0:T(8,128)} %copy.92, f32[1,128,4096]{1,2,0:T(8,128)} %copy.94, f32[1,128,4096]{1,2,0:T(8,128)} %copy.91, f32[1,128,4096]{1,2,0:T(8,128)} %copy.93), kind=kLoop, calls=%fused_computation.4 | loop fusion | flops 7864320 | bytes 13631488 | tf_op jit(solution)/shard_map/convert_element_type | solution.py:400
  68.5 15.9 %all-to-all-done.1.refs_0_ = bf16[32,2,128,128]{3,2,1,0:T(8,128)(2,1)S(1)} async-done(((bf16[32,2,128,128]{3,2,1,0:T(8,128)(2,1)}), bf16[32,2,128,128]{3,2,1,0:T(8,128)(2,1)S(1)}, u32[]{:S(2)}, u32[]{:S(2)}) %all-to-all-start.1) | async-done | bytes 2097184 | tf_op jit(solution)/shard_map/all_to_all | solution.py:503
  85.7 14.4 %shard_map.300 = bf16[32,2,128,128]{3,2,1,0:T(8,128)(2,1)} custom-call(bf16[32,2,128,128]{3,2,1,0:T(8,128)(2,1)} %copy-done.1, bf16[1024,1024]{1,0:T(8,128)(2,1)} %constant.100.clone.refs_1_.refs_3_, bf16[32,256,256]{2,1,0:T(8,128)(2,1)} %constant.102.clone.refs_2_.refs_4_, bf16[32,128,128]{2,1,0:T(8,128)(2,1)} %bitcast.68, ...), custom_call_target="tpu_custom_call" | custom-call | tf_op jit(solution)/shard_map/pallas_call | solution.py:507
  100.0 4.8 %all-to-all-start.2 = ((bf16[32,2,128,128]{3,2,1,0:T(8,128)(2,1)}), bf16[32,2,128,128]{3,2,1,0:T(8,128)(2,1)S(1)}, u32[]{:S(2)}, u32[]{:S(2)}) async-start(bf16[32,2,128,128]{3,2,1,0:T(8,128)(2,1)} %shard_map.300), calls=%async_computation.2 | async-start | bytes 4194304 | tf_op jit(solution)/shard_map/all_to_all | solution.py:516
  104.9 6.5 %shard_map.301.refs_1_ = f32[32,64,256]{2,1,0:T(8,128)} custom-call(f32[1,512,1024]{2,1,0:T(8,128)} %bitcast.73, bf16[1024,1024]{1,0:T(8,128)(2,1)} %constant.99.clone.order_ref), custom_call_target="tpu_custom_call" | custom-call | tf_op jit(solution)/shard_map/pallas_call | solution.py:865
  111.4 6.6 %shard_map.302.refs_3_ = f32[32,64,256]{2,1,0:T(8,128)} custom-call(f32[2,512,1024]{2,1,0:T(8,128)} %refs_6_.8, bf16[1024,1024]{1,0:T(8,128)(2,1)} %constant.99.clone.order_ref), custom_call_target="tpu_custom_call" | custom-call | tf_op jit(solution)/shard_map/pallas_call | solution.py:865
  134.2 19.4 %all-to-all-done.2 = bf16[32,2,128,128]{3,2,1,0:T(8,128)(2,1)S(1)} async-done(((bf16[32,2,128,128]{3,2,1,0:T(8,128)(2,1)}), bf16[32,2,128,128]{3,2,1,0:T(8,128)(2,1)S(1)}, u32[]{:S(2)}, u32[]{:S(2)}) %all-to-all-start.2) | async-done | bytes 2097184 | tf_op jit(solution)/shard_map/all_to_all | solution.py:516
  154.9 7.5 %shard_map.303 = bf16[4,8,64,256]{3,2,1,0:T(8,128)(2,1)} custom-call(bf16[16,2,2,128,128]{4,3,2,1,0:T(8,128)(2,1)} %bitcast.74, bf16[256,512]{1,0:T(8,128)(2,1)} %constant.104.clone.first_ref, f32[2,256,256]{2,1,0:T(8,128)} %constant.105.clone.twist_ref, bf16[512,512]{1,0:T(8,128)(2,1)} %constant.107.clone.second_ref), custom_call_target="tpu_custom_call" | custom-call | tf_op jit(solution)/shard_map/pallas_call | solution.py:518
  166.8 12.9 %all-to-all-done.3 = bf16[4,8,64,256]{3,2,1,0:T(8,128)(2,1)S(1)} async-done(((bf16[4,8,64,256]{3,2,1,0:T(8,128)(2,1)}), bf16[4,8,64,256]{3,2,1,0:T(8,128)(2,1)S(1)}, u32[]{:S(2)}, u32[]{:S(2)}) %all-to-all-start.3) | async-done | bytes 1048608 | tf_op jit(solution)/shard_map/all_to_all | solution.py:523
  180.8 27.6 %shard_map.304 = (f32[32,64,256]{2,1,0:T(8,128)}, bf16[32,64,768]{2,1,0:T(8,128)(2,1)}, bf16[32,8,768]{2,1,0:T(8,128)(2,1)}, bf16[8,64,768]{2,1,0:T(8,128)(2,1)}, bf16[8,8,768]{2,1,0:T(8,128)(2,1)}) custom-call(s32[2]{0:T(128)} %get-tuple-element.69.refs_0_, f32[32,64,256]{2,1,0:T(8,128)} %shard_map.301.refs_1_, bf16[32,64,256]{2,1,0:T(8,128)(2,1)} %bitcast.70, ...), custom_call_target="tpu_custom_call" | custom-call | tf_op jit(solution)/shard_map/pallas_call | solution.py:726
  213.1 8.5 %collective-permute-done.2.refs_4_ = bf16[8,8,768]{2,1,0:T(8,128)(2,1)S(1)} collective-permute-done((bf16[8,8,768]{2,1,0:T(8,128)(2,1)}, bf16[8,8,768]{2,1,0:T(8,128)(2,1)S(1)}, u32[]{:S(2)}, u32[]{:S(2)}) %collective-permute-start.2) | collective-permute-done | bytes 98336 | tf_op jit(solution)/shard_map/ppermute | solution.py:776
  229.4 30.3 %shard_map.305 = (bf16[32,64,256]{2,1,0:T(8,128)(2,1)}, bf16[32,8,256]{2,1,0:T(8,128)(2,1)}, bf16[8,64,256]{2,1,0:T(8,128)(2,1)}, bf16[8,8,256]{2,1,0:T(8,128)(2,1)}, bf16[32,64,256]{2,1,0:T(8,128)(2,1)}) custom-call(s32[2]{0:T(128)} %get-tuple-element.69.refs_0_, bf16[32,64,768]{2,1,0:T(8,128)(2,1)} %get-tuple-element.54.refs_1_, ...), custom_call_target="tpu_custom_call" | custom-call | tf_op jit(solution)/shard_map/pallas_call | solution.py:749
  259.7 4.6 all-to-all-start.4
  266.8 12.4 %all-to-all-done.4.x_ref = bf16[4,8,64,256]{3,2,1,0:T(8,128)(2,1)S(1)} async-done(((bf16[4,8,64,256]{3,2,1,0:T(8,128)(2,1)}), bf16[4,8,64,256]{3,2,1,0:T(8,128)(2,1)S(1)}, u32[]{:S(2)}, u32[]{:S(2)}) %all-to-all-start.4) | async-done | bytes 1048608 | tf_op jit(solution)/shard_map/all_to_all | solution.py:493
  280.2 6.1 %shard_map.306 = bf16[16,2,128,128]{3,2,1,0:T(8,128)(2,1)} custom-call(bf16[4,8,64,256]{3,2,1,0:T(8,128)(2,1)} %copy-done.4, bf16[256,512]{1,0:T(8,128)(2,1)} %constant_dynamic-slice_fusion.first_ref, f32[2,256,256]{2,1,0:T(8,128)} %constant.109.clone.twist_ref, bf16[256,512]{1,0:T(8,128)(2,1)} %constant.110.clone.lower_ref, ...), custom_call_target="tpu_custom_call" | custom-call | tf_op jit(solution)/shard_map/pallas_call | solution.py:496
  293.7 5.4 %shard_map.307.refs_5_ = bf16[32,128,128]{2,1,0:T(8,128)(2,1)} custom-call(bf16[32,128,128]{2,1,0:T(8,128)(2,1)} %bitcast.69, bf16[32,128,128]{2,1,0:T(8,128)(2,1)} %bitcast.77, bf16[2,128,128]{2,1,0:T(8,128)(2,1)} %add_convert_fusion.pick_ref, bf16[2,128,128]{2,1,0:T(8,128)(2,1)} %constant.115.clone.flip_ref), custom_call_target="tpu_custom_call" | custom-call | tf_op jit(solution)/shard_map/pallas_call | solution.py:449
  299.1 16.9 %all-to-all-done.5.refs_2_ = bf16[32,128,128]{2,1,0:T(8,128)(2,1)S(1)} async-done(((bf16[32,128,128]{2,1,0:T(8,128)(2,1)}), bf16[32,128,128]{2,1,0:T(8,128)(2,1)S(1)}, u32[]{:S(2)}, u32[]{:S(2)}) %all-to-all-start.5) | async-done | bytes 1048608 | tf_op jit(solution)/shard_map/all_to_all | solution.py:503
  317.0 12.7 %shard_map.308 = bf16[32,128,128]{2,1,0:T(8,128)(2,1)} custom-call(s32[1]{0:T(128)} %bitcast.29.refs_0_, f32[32,2,8,128]{3,2,1,0:T(8,128)} %broadcast_in_dim.75.refs_1_, bf16[32,128,128]{2,1,0:T(8,128)(2,1)} %copy-done.3, bf16[1024,1024]{1,0:T(8,128)(2,1)} %constant.100.clone.refs_1_.refs_3_, bf16[32,256,256]{2,1,0:T(8,128)(2,1)} %constant.102.clone.refs_2_.refs_4_, ...), custom_call_target="tpu_custom_call" | custom-call | tf_op jit(solution)/shard_map/pallas_call | solution.py:507
  329.7 30.0 %all_to_all.41 = bf16[32,128,128]{2,1,0:T(8,128)(2,1)} all-to-all(bf16[32,128,128]{2,1,0:T(8,128)(2,1)} %shard_map.308), channel_id=1, replica_groups=mesh['ty'=8,'tx'=4] {'ty','tx'}, dimensions={0} | all-to-all | bytes 2097152 | tf_op jit(solution)/shard_map/all_to_all | solution.py:516
  359.6 6.4 %shard_map.309 = bf16[4,8,64,256]{3,2,1,0:T(8,128)(2,1)} custom-call(bf16[16,2,128,128]{3,2,1,0:T(8,128)(2,1)} %bitcast.76, bf16[256,512]{1,0:T(8,128)(2,1)} %constant.108.clone.first_ref, f32[2,256,256]{2,1,0:T(8,128)} %constant.109.clone.twist_ref, bf16[512,256]{1,0:T(8,128)(2,1)} %constant.112.clone.lower_ref, bf16[512,272]{1,0:T(8,128)(2,1)} %constant.113.clone.upper_ref), custom_call_target="tpu_custom_call" | custom-call | tf_op jit(solution)/shard_map/pallas_call | solution.py:518
  374.6 10.2 %collective-permute-done.5.refs_5_ = bf16[8,8,256]{2,1,0:T(8,128)(2,1)S(1)} collective-permute-done((bf16[8,8,256]{2,1,0:T(8,128)(2,1)S(1)}, bf16[8,8,256]{2,1,0:T(8,128)(2,1)S(1)}, u32[]{:S(2)}, u32[]{:S(2)}) %collective-permute-start.5) | collective-permute-done | bytes 32800 | tf_op jit(solution)/shard_map/ppermute | solution.py:776
  388.7 28.6 %shard_map.310 = (f32[32,64,256]{2,1,0:T(8,128)}, bf16[32,64,512]{2,1,0:T(8,128)(2,1)}, bf16[32,8,512]{2,1,0:T(8,128)(2,1)}, bf16[8,64,512]{2,1,0:T(8,128)(2,1)}, bf16[8,8,512]{2,1,0:T(8,128)(2,1)}) custom-call(s32[2]{0:T(128)} %get-tuple-element.69.refs_0_, f32[32,64,256]{2,1,0:T(8,128)} %get-tuple-element.49.refs_1_, ...), custom_call_target="tpu_custom_call" | custom-call | tf_op jit(solution)/shard_map/pallas_call | solution.py:726
  419.9 6.8 %collective-permute-done.10.refs_4_ = bf16[8,8,512]{2,1,0:T(8,128)(2,1)S(1)} collective-permute-done((bf16[8,8,512]{2,1,0:T(8,128)(2,1)}, bf16[8,8,512]{2,1,0:T(8,128)(2,1)S(1)}, u32[]{:S(2)}, u32[]{:S(2)}) %collective-permute-start.10) | collective-permute-done | bytes 65568 | tf_op jit(solution)/shard_map/ppermute | solution.py:776
  428.6 29.1 %shard_map.311 = (bf16[32,64,256]{2,1,0:T(8,128)(2,1)}, bf16[32,8,256]{2,1,0:T(8,128)(2,1)}, bf16[8,64,256]{2,1,0:T(8,128)(2,1)}, bf16[8,8,256]{2,1,0:T(8,128)(2,1)}) custom-call(s32[2]{0:T(128)} %get-tuple-element.95.refs_0_, bf16[32,64,512]{2,1,0:T(8,128)(2,1)} %get-tuple-element.74.refs_1_, bf16[32,8,512]{2,1,0:T(8,128)(2,1)} %copy-done.11, ...), custom_call_target="tpu_custom_call" | custom-call | tf_op jit(solution)/shard_map/pallas_call | solution.py:749
  460.2 6.1 %collective-permute-done.13.refs_5_ = bf16[8,8,256]{2,1,0:T(8,128)(2,1)S(1)} collective-permute-done((bf16[8,8,256]{2,1,0:T(8,128)(2,1)}, bf16[8,8,256]{2,1,0:T(8,128)(2,1)S(1)}, u32[]{:S(2)}, u32[]{:S(2)}) %collective-permute-start.13) | collective-permute-done | bytes 32800 | tf_op jit(solution)/shard_map/ppermute | solution.py:776
  467.1 8.5 %shard_map.312 = f32[512,1024]{1,0:T(8,128)} custom-call(s32[2]{0:T(128)} %get-tuple-element.95.refs_0_, f32[32,64,256]{2,1,0:T(8,128)} %get-tuple-element.73.refs_1_, bf16[32,64,256]{2,1,0:T(8,128)(2,1)} %get-tuple-element.79.refs_2_, bf16[32,8,256]{2,1,0:T(8,128)(2,1)} %copy-done.18, bf16[8,64,256]{2,1,0:T(8,128)(2,1)} %copy-done.12, ...), custom_call_target="tpu_custom_call" | custom-call | tf_op jit(solution)/shard_map/pallas_call | solution.py:881
  (138 shorter events, 82.8 us)
Async XLA Ops:
  31.1 53.2 %all-to-all-start.1 = ((bf16[32,2,128,128]{3,2,1,0:T(8,128)(2,1)}), bf16[32,2,128,128]{3,2,1,0:T(8,128)(2,1)S(1)}, u32[]{:S(2)}, u32[]{:S(2)}) async-start(bf16[32,2,128,128]{3,2,1,0:T(8,128)(2,1)} %bitcast.75), calls=%async_computation.1 | async-start | bytes 4194304 | tf_op jit(solution)/shard_map/all_to_all | solution.py:503
  100.0 53.5 %all-to-all-start.2 = ((bf16[32,2,128,128]{3,2,1,0:T(8,128)(2,1)}), bf16[32,2,128,128]{3,2,1,0:T(8,128)(2,1)S(1)}, u32[]{:S(2)}, u32[]{:S(2)}) async-start(bf16[32,2,128,128]{3,2,1,0:T(8,128)(2,1)} %shard_map.300), calls=%async_computation.2 | async-start | bytes 4194304 | tf_op jit(solution)/shard_map/all_to_all | solution.py:516
  111.4 6.6 %copy-start.23 = (s32[32,64]{1,0:T(8,128)S(1)}, s32[32,64]{1,0:T(8,128)}, u32[]{:S(2)}) copy-start(s32[32,64]{1,0:T(8,128)} %param.35) | copy-start | bytes 24580
  111.4 7.5 %copy-start.25 = (s32[2,2]{1,0:T(2,128)S(1)}, s32[2,2]{1,0:T(2,128)}, u32[]{:S(2)}) copy-start(s32[2,2]{1,0:T(2,128)} %param.34) | copy-start | bytes 52
  111.4 13.3 %copy-start.13 = (bf16[256,512]{1,0:T(8,128)(2,1)S(1)}, bf16[256,512]{1,0:T(8,128)(2,1)}, u32[]{:S(2)}) copy-start(bf16[256,512]{1,0:T(8,128)(2,1)} %param.39) | copy-start | bytes 786436
  162.4 17.4 %all-to-all-start.3 = ((bf16[4,8,64,256]{3,2,1,0:T(8,128)(2,1)}), bf16[4,8,64,256]{3,2,1,0:T(8,128)(2,1)S(1)}, u32[]{:S(2)}, u32[]{:S(2)}) async-start(bf16[4,8,64,256]{3,2,1,0:T(8,128)(2,1)} %shard_map.303), calls=%async_computation.3 | async-start | bytes 2097152 | tf_op jit(solution)/shard_map/all_to_all | solution.py:523
  208.3 13.9 %collective-permute-start.1 = (bf16[8,64,768]{2,1,0:T(8,128)(2,1)}, bf16[8,64,768]{2,1,0:T(8,128)(2,1)S(1)}, u32[]{:S(2)}, u32[]{:S(2)}) collective-permute-start(bf16[8,64,768]{2,1,0:T(8,128)(2,1)} %get-tuple-element.52), channel_id=1, source_target_pairs={{0,28},{4,0},{8,4},{12,8},{16,12},{20,16},{24,20},{28,24},{1,29},{... | collective-permute-start | bytes 2359304 | tf_op jit(solution)/shard_map/ppermute | solution.py:775
  209.4 12.8 %collective-permute-start = (bf16[32,8,768]{2,1,0:T(8,128)(2,1)}, bf16[32,8,768]{2,1,0:T(8,128)(2,1)S(1)}, u32[]{:S(2)}, u32[]{:S(2)}) collective-permute-start(bf16[32,8,768]{2,1,0:T(8,128)(2,1)} %get-tuple-element.51), channel_id=1, source_target_pairs={{0,3},{1,0},{2,1},{3,2},{4,7},{5,4},{6,5},{7,6},{8,11},{9,8},{10,9... | collective-permute-start | bytes 1179656 | tf_op jit(solution)/shard_map/ppermute | solution.py:774
  210.8 10.9 %collective-permute-start.2 = (bf16[8,8,768]{2,1,0:T(8,128)(2,1)}, bf16[8,8,768]{2,1,0:T(8,128)(2,1)S(1)}, u32[]{:S(2)}, u32[]{:S(2)}) collective-permute-start(bf16[8,8,768]{2,1,0:T(8,128)(2,1)} %get-tuple-element.53), channel_id=1, source_target_pairs={{0,31},{1,28},{2,29},{3,30},{4,3},{5,0},{6,1},{7,2},{8,7},{9,4},{1... | collective-permute-start | bytes 294920 | tf_op jit(solution)/shard_map/ppermute | solution.py:776
  221.7 7.7 %copy-start.19 = (bf16[8,8,768]{2,1,0:T(8,128)(2,1)}, bf16[8,8,768]{2,1,0:T(8,128)(2,1)S(1)}, u32[]{:S(2)}) copy-start(bf16[8,8,768]{2,1,0:T(8,128)(2,1)S(1)} %collective-permute-done.2.refs_4_) | copy-start | bytes 294916
  223.0 5.5 %copy-start.6 = (bf16[8,64,768]{2,1,0:T(8,128)(2,1)}, bf16[8,64,768]{2,1,0:T(8,128)(2,1)S(1)}, u32[]{:S(2)}) copy-start(bf16[8,64,768]{2,1,0:T(8,128)(2,1)S(1)} %collective-permute-done.1.refs_3_) | copy-start | bytes 2359300
  224.4 35.3 %collective-permute-start.6 = (bf16[64,4096]{1,0:T(8,128)(2,1)}, bf16[64,4096]{1,0:T(8,128)(2,1)S(1)}, u32[]{:S(2)}, u32[]{:S(2)}) collective-permute-start(bf16[64,4096]{1,0:T(8,128)(2,1)} %copy.85), channel_id=1, source_target_pairs={{0,31},{1,30},{2,29},{3,28},{4,27},{5,26},{6,25},{7,24},{8,23},{9,... | collective-permute-start | bytes 1572872 | tf_op jit(solution)/shard_map/ppermute | solution.py:429
  228.5 31.2 %collective-permute-start.7 = (bf16[1,4096]{1,0:T(2,128)(2,1)S(1)}, bf16[1,4096]{1,0:T(2,128)(2,1)S(1)}, u32[]{:S(2)}, u32[]{:S(2)}) collective-permute-start(bf16[1,4096]{1,0:T(2,128)(2,1)S(1)} %copy.86), channel_id=1, source_target_pairs={{1,31},{2,30},{3,29},{4,28},{5,27},{6,26},{7,25},{8,24},{9,23},{10... | collective-permute-start | bytes 24584 | tf_op jit(solution)/shard_map/ppermute | solution.py:430
  259.7 6.3 %copy-start.15 = (bf16[272,512]{1,0:T(8,128)(2,1)S(1)}, bf16[272,512]{1,0:T(8,128)(2,1)}, u32[]{:S(2)}) copy-start(bf16[272,512]{1,0:T(8,128)(2,1)} %constant.114.clone) | copy-start | bytes 835588
  259.7 26.6 %copy-start.7 = (bf16[64,4096]{1,0:T(8,128)(2,1)}, bf16[64,4096]{1,0:T(8,128)(2,1)S(1)}, u32[]{:S(2)}) copy-start(bf16[64,4096]{1,0:T(8,128)(2,1)S(1)} %collective-permute-done.6) | copy-start | bytes 1572868
  259.7 19.5 %all-to-all-start.4 = ((bf16[4,8,64,256]{3,2,1,0:T(8,128)(2,1)}), bf16[4,8,64,256]{3,2,1,0:T(8,128)(2,1)S(1)}, u32[]{:S(2)}, u32[]{:S(2)}) async-start(bf16[4,8,64,256]{3,2,1,0:T(8,128)(2,1)} %bitcast.86), calls=%async_computation.4 | async-start | bytes 2097152 | tf_op jit(solution)/shard_map/all_to_all | solution.py:493
  266.8 23.5 %copy-start.24 = (s32[2]{0:T(128)S(1)}, s32[2]{0:T(128)}, u32[]{:S(2)}) copy-start(s32[2]{0:T(128)} %get-tuple-element.69.refs_0_) | copy-start | bytes 28
  286.3 4.3 copy-start.8
  286.3 29.7 %all-to-all-start.5 = ((bf16[32,128,128]{2,1,0:T(8,128)(2,1)}), bf16[32,128,128]{2,1,0:T(8,128)(2,1)S(1)}, u32[]{:S(2)}, u32[]{:S(2)}) async-start(bf16[32,128,128]{2,1,0:T(8,128)(2,1)} %bitcast.80), calls=%async_computation.5 | async-start | bytes 2097152 | tf_op jit(solution)/shard_map/all_to_all | solution.py:503
  359.6 10.0 %copy-start.27 = (bf16[8,64,256]{2,1,0:T(8,128)(2,1)S(1)}, bf16[8,64,256]{2,1,0:T(8,128)(2,1)}, u32[]{:S(2)}) copy-start(bf16[8,64,256]{2,1,0:T(8,128)(2,1)} %get-tuple-element.62) | copy-start | bytes 786436
  359.6 10.1 %copy-start.28 = (bf16[32,8,256]{2,1,0:T(8,128)(2,1)S(1)}, bf16[32,8,256]{2,1,0:T(8,128)(2,1)}, u32[]{:S(2)}) copy-start(bf16[32,8,256]{2,1,0:T(8,128)(2,1)} %get-tuple-element.61) | copy-start | bytes 393220
  359.6 12.0 %copy-start.29 = (bf16[8,8,256]{2,1,0:T(8,128)(2,1)S(1)}, bf16[8,8,256]{2,1,0:T(8,128)(2,1)}, u32[]{:S(2)}) copy-start(bf16[8,8,256]{2,1,0:T(8,128)(2,1)} %get-tuple-element.63) | copy-start | bytes 98308
  366.1 21.5 %all-to-all-start.7 = ((bf16[4,8,64,256]{3,2,1,0:T(8,128)(2,1)}), bf16[4,8,64,256]{3,2,1,0:T(8,128)(2,1)S(1)}, u32[]{:S(2)}, u32[]{:S(2)}) async-start(bf16[4,8,64,256]{3,2,1,0:T(8,128)(2,1)} %shard_map.309), calls=%async_computation.7 | async-start | bytes 2097152 | tf_op jit(solution)/shard_map/all_to_all | solution.py:523
  369.6 18.0 %collective-permute-start.4 = (bf16[8,64,256]{2,1,0:T(8,128)(2,1)S(1)}, bf16[8,64,256]{2,1,0:T(8,128)(2,1)S(1)}, u32[]{:S(2)}, u32[]{:S(2)}) collective-permute-start(bf16[8,64,256]{2,1,0:T(8,128)(2,1)S(1)} %copy-done.27), channel_id=1, source_target_pairs={{0,4},{4,8},{8,12},{12,16},{16,20},{20,24},{24,28},{28,0},{1,5},{5... | collective-permute-start | bytes 786440 | tf_op jit(solution)/shard_map/ppermute | solution.py:775
  369.7 17.9 %collective-permute-start.3 = (bf16[32,8,256]{2,1,0:T(8,128)(2,1)S(1)}, bf16[32,8,256]{2,1,0:T(8,128)(2,1)S(1)}, u32[]{:S(2)}, u32[]{:S(2)}) collective-permute-start(bf16[32,8,256]{2,1,0:T(8,128)(2,1)S(1)} %copy-done.28), channel_id=1, source_target_pairs={{0,1},{1,2},{2,3},{3,0},{4,5},{5,6},{6,7},{7,4},{8,9},{9,10},{10,1... | collective-permute-start | bytes 393224 | tf_op jit(solution)/shard_map/ppermute | solution.py:774
  371.7 13.1 %collective-permute-start.5 = (bf16[8,8,256]{2,1,0:T(8,128)(2,1)S(1)}, bf16[8,8,256]{2,1,0:T(8,128)(2,1)S(1)}, u32[]{:S(2)}, u32[]{:S(2)}) collective-permute-start(bf16[8,8,256]{2,1,0:T(8,128)(2,1)S(1)} %copy-done.29), channel_id=1, source_target_pairs={{0,5},{1,6},{2,7},{3,4},{4,9},{5,10},{6,11},{7,8},{8,13},{9,14},{1... | collective-permute-start | bytes 98312 | tf_op jit(solution)/shard_map/ppermute | solution.py:776
  417.3 10.4 %collective-permute-start.9 = (bf16[8,64,512]{2,1,0:T(8,128)(2,1)}, bf16[8,64,512]{2,1,0:T(8,128)(2,1)S(1)}, u32[]{:S(2)}, u32[]{:S(2)}) collective-permute-start(bf16[8,64,512]{2,1,0:T(8,128)(2,1)} %get-tuple-element.76), channel_id=1, source_target_pairs={{0,28},{4,0},{8,4},{12,8},{16,12},{20,16},{24,20},{28,24},{1,29},{... | collective-permute-start | bytes 1572872 | tf_op jit(solution)/shard_map/ppermute | solution.py:775
  418.4 9.2 %collective-permute-start.8 = (bf16[32,8,512]{2,1,0:T(8,128)(2,1)}, bf16[32,8,512]{2,1,0:T(8,128)(2,1)S(1)}, u32[]{:S(2)}, u32[]{:S(2)}) collective-permute-start(bf16[32,8,512]{2,1,0:T(8,128)(2,1)} %get-tuple-element.75), channel_id=1, source_target_pairs={{0,3},{1,0},{2,1},{3,2},{4,7},{5,4},{6,5},{7,6},{8,11},{9,8},{10,9... | collective-permute-start | bytes 786440 | tf_op jit(solution)/shard_map/ppermute | solution.py:774
  419.0 7.8 %collective-permute-start.10 = (bf16[8,8,512]{2,1,0:T(8,128)(2,1)}, bf16[8,8,512]{2,1,0:T(8,128)(2,1)S(1)}, u32[]{:S(2)}, u32[]{:S(2)}) collective-permute-start(bf16[8,8,512]{2,1,0:T(8,128)(2,1)} %get-tuple-element.77), channel_id=1, source_target_pairs={{0,31},{1,28},{2,29},{3,30},{4,3},{5,0},{6,1},{7,2},{8,7},{9,4},{1... | collective-permute-start | bytes 196616 | tf_op jit(solution)/shard_map/ppermute | solution.py:776
  457.7 8.6 %collective-permute-start.12 = (bf16[8,64,256]{2,1,0:T(8,128)(2,1)}, bf16[8,64,256]{2,1,0:T(8,128)(2,1)S(1)}, u32[]{:S(2)}, u32[]{:S(2)}) collective-permute-start(bf16[8,64,256]{2,1,0:T(8,128)(2,1)} %get-tuple-element.81), channel_id=1, source_target_pairs={{0,4},{4,8},{8,12},{12,16},{16,20},{20,24},{24,28},{28,0},{1,5},{5... | collective-permute-start | bytes 786440 | tf_op jit(solution)/shard_map/ppermute | solution.py:775
  457.8 8.5 %collective-permute-start.11 = (bf16[32,8,256]{2,1,0:T(8,128)(2,1)}, bf16[32,8,256]{2,1,0:T(8,128)(2,1)S(1)}, u32[]{:S(2)}, u32[]{:S(2)}) collective-permute-start(bf16[32,8,256]{2,1,0:T(8,128)(2,1)} %get-tuple-element.80), channel_id=1, source_target_pairs={{0,1},{1,2},{2,3},{3,0},{4,5},{5,6},{6,7},{7,4},{8,9},{9,10},{10,1... | collective-permute-start | bytes 393224 | tf_op jit(solution)/shard_map/ppermute | solution.py:774
  458.6 7.7 %collective-permute-start.13 = (bf16[8,8,256]{2,1,0:T(8,128)(2,1)}, bf16[8,8,256]{2,1,0:T(8,128)(2,1)S(1)}, u32[]{:S(2)}, u32[]{:S(2)}) collective-permute-start(bf16[8,8,256]{2,1,0:T(8,128)(2,1)} %get-tuple-element.82), channel_id=1, source_target_pairs={{0,5},{1,6},{2,7},{3,4},{4,9},{5,10},{6,11},{7,8},{8,13},{9,14},{1... | collective-permute-start | bytes 98312 | tf_op jit(solution)/shard_map/ppermute | solution.py:776
  (18 other events, 21.8 us)

commit v2 on v1

--- a/solution.py
+++ b/solution.py
@@ -503,6 +503,8 @@
     moved = lax.all_to_all(
         sent.reshape(part), ("ty", "tx"), split_axis=0, concat_axis=0, tiled=True
     )
+    if halved:
+        moved, beside = lax.optimization_barrier((moved, beside))
     spaces = [pltpu.SMEM, pltpu.VMEM][: len(extra)] + [pltpu.VMEM] * 2 + [pl.ANY] * len(away)
     wave = pl.pallas_call(
         functools.partial(column_kernel, halved),
@@ -514,7 +516,8 @@
         compiler_params=PARAMS,
     )(*extra, moved, outer, *away)
     returned = lax.all_to_all(wave, ("ty", "tx"), split_axis=0, concat_axis=0, tiled=True)
-    returned, beside = lax.optimization_barrier((returned, beside))
+    if not halved:
+        returned, beside = lax.optimization_barrier((returned, beside))
     slabs = pl.pallas_call(
         backward[0],
         out_shape=jax.ShapeDtypeStruct((lanes, own, cols, PIXELS), BF16),
@@ -547,20 +550,48 @@
     return jnp.concatenate(pieces, axis=1)
 
 
-def swin_band(
-    flow, bias_ref, qkv_ref, proj_ref, up_ref, down_ref, gain_ref, mixed_ref, score_ref, prob_ref
-):
+def gelu_twice(value):
+    value = value.astype(BF16)
+    inside = value * (BF16(GELU_IN) + BF16(GELU_CUBE) * (value * value))
+    return value + value * jnp.tanh(inside)
+
+
+def load_weights(j, sources, targets, sems):
+    copies = [
+        pltpu.make_async_copy(source.at[j], target, sems.at[n])
+        for n, (source, target) in enumerate(zip(sources, targets))
+    ]
+
+    @pl.when(pl.program_id(0) == 0)
+    def _():
+        for copy in copies:
+            copy.start()
+
+    def wait(which):
+        @pl.when(pl.program_id(0) == 0)
+        def _():
+            for n in which:
+                copies[n].wait()
+
+    return wait
+
+
+def swin_band(flow, wait, bias_ref, gain_ref, weight_refs, scratch):
+    qkv_ref, proj_ref, up_ref, down_ref = weight_refs
+    mixed_ref, score_ref, prob_ref, *active_ref = scratch
     count = flow.shape[0] // SPAN
     pairs = HEADS // 2
     depth = D // HEADS
     wide = 2 * depth
     normed = layer_norm(flow, gain_ref[0:1, :])
     scale = 1.0 / math.sqrt(depth)
+    wait((0,))
     mixed_ref[:, :D] = (mm(normed, qkv_ref[:, :D]) * scale).astype(BF16)
     mixed_ref[:, D : 2 * D] = mm(normed, qkv_ref[:, D : 2 * D]).astype(BF16)
     mixed_ref[:, 2 * D :] = mm(normed, qkv_ref[:, 2 * D :]).astype(BF16)
     lower = lax.broadcasted_iota(jnp.int32, (SPAN, wide), 1) < depth
-    for w in range(count):
+
+    def scores_of(w):
         rows = slice(w * SPAN, (w + 1) * SPAN)
         for p in range(pairs):
             query = mixed_ref[rows, p * wide : (p + 1) * wide]
@@ -570,7 +601,8 @@
                 [jnp.where(lower, query, zero), jnp.where(lower, zero, query)], axis=0
             )
             score_ref[w, :, p * wide : (p + 1) * wide] = mm(key, split, NT)
-    for w in range(count):
+
+    def probs_of(w):
         bias = bias_ref[w]
         for p in range(pairs):
             lanes = slice(p * wide, (p + 1) * wide)
@@ -578,25 +610,38 @@
             weights = jnp.exp(scores - jnp.max(scores, axis=0, keepdims=True))
             share = 1.0 / jnp.sum(weights, axis=0, keepdims=True)
             prob_ref[w, :, lanes] = (weights * share).astype(BF16)
-    for w in range(count):
+
+    def mixture_of(w):
         rows = slice(w * SPAN, (w + 1) * SPAN)
         for p in range(pairs):
             lanes = slice(p * wide, (p + 1) * wide)
             value = mixed_ref[rows, 2 * D + p * wide : 2 * D + (p + 1) * wide]
             mixture = mm(prob_ref[w, :, lanes], value, TN)
             mixed_ref[rows, lanes] = jnp.where(lower, mixture[:SPAN], mixture[SPAN:]).astype(BF16)
+
+    for turn in range(count + 2):
+        if turn < count:
+            scores_of(turn)
+        if 0 <= turn - 1 < count:
+            probs_of(turn - 1)
+        if 0 <= turn - 2:
+            mixture_of(turn - 2)
+    wait((1, 2, 3))
     flow = flow + mm(mixed_ref[:, :D], proj_ref[...])
     normed = layer_norm(flow, gain_ref[1:2, :])
     chunks = up_ref.shape[1] // D
+    if active_ref:
+        for c in range(chunks):
+            part = slice(c * D, (c + 1) * D)
+            active_ref[0][:, part] = gelu_twice(mm(normed, up_ref[:, part]))
+        return flow + 0.5 * mm(active_ref[0][...], down_ref[...])
     total = jnp.zeros_like(flow)
     ahead = mm(normed, up_ref[:, :D])
     for c in range(chunks):
         value = ahead
         if c + 1 < chunks:
             ahead = mm(normed, up_ref[:, (c + 1) * D : (c + 2) * D])
-        inside = value * (GELU_IN + GELU_CUBE * (value * value))
-        active = (value + value * jnp.tanh(inside)).astype(BF16)
-        total = total + mm(active, down_ref[c * D : (c + 1) * D, :])
+        total = total + mm(gelu_twice(value), down_ref[c * D : (c + 1) * D, :])
     return flow + 0.5 * total
 
 
@@ -626,19 +671,22 @@
 
 def first_kernel(zeta, sigma, count, rows, before, *refs):
     shift_ref, state_ref, *refs = refs
-    state = state_ref[...]
     if before is not None:
-        state = state - before * rolled_band(-1, shift_ref, refs[:4], rows)
-        refs = refs[4:]
+        back_refs, refs = refs[:4], refs[4:]
     grad_refs, refs = refs[:count], refs[count:]
     if sigma is not None:
         noise_ref, *refs = refs
-    bias_ref, embed_ref, qkv_ref, proj_ref, up_ref, down_ref, gain_ref = refs[:7]
+    bias_ref, embed_ref, gain_ref, *sources = refs[:7]
     base_ref, out_ref, side_ref, edge_ref, corner_ref, *scratch = refs[7:]
+    targets, sems, scratch = scratch[:4], scratch[4], scratch[5:]
+    wait = load_weights(0, sources, targets, sems)
+    state = state_ref[...]
+    if before is not None:
+        state = state - before * rolled_band(-1, shift_ref, back_refs, rows)
     step = zeta * sum(grad_ref[...].astype(F32) for grad_ref in grad_refs)
     half = state - step
     tokens = mm(to_windows(half).astype(BF16), embed_ref[...]).astype(BF16).astype(F32)
-    flow = swin_band(tokens, bias_ref, qkv_ref, proj_ref, up_ref, down_ref, gain_ref, *scratch)
+    flow = swin_band(tokens, wait, bias_ref, gain_ref, targets, scratch)
     result = from_windows(flow, half.shape[1]).astype(BF16)
     out_ref[:, :, :D] = result
     side_ref[:, :, :D] = result[:, :WIN]
@@ -660,14 +708,16 @@
 def second_kernel(sigma, rows, *refs):
     shift_ref, *refs = refs
     tile_refs, refs = refs[:4], refs[4:]
-    bias_ref, qkv_ref, proj_ref, up_ref, down_ref, gain_ref, unembed_ref = refs[:7]
+    bias_ref, unembed_ref, gain_ref, *sources = refs[:7]
     out_ref, side_ref, edge_ref, corner_ref, *scratch = refs[7:]
     if sigma is not None:
         state_ref, *scratch = scratch
+    targets, sems, scratch = scratch[:4], scratch[4], scratch[5:]
+    wait = load_weights(1, sources, targets, sems)
     cols = out_ref.shape[1]
     band = rolled_band(1, shift_ref, tile_refs, rows)
     tokens = to_windows(band[:, :, :D])
-    flow = swin_band(tokens, bias_ref, qkv_ref, proj_ref, up_ref, down_ref, gain_ref, *scratch)
+    flow = swin_band(tokens, wait, bias_ref, gain_ref, targets, scratch)
     estimate = from_windows(mm(flow.astype(BF16), unembed_ref[...]), cols)
     narrow = estimate.astype(BF16)
     out_ref[...] = narrow
@@ -700,9 +750,10 @@
     return pl.BlockSpec((cols // WIN, SPAN, 2 * SPAN), lambda n, *_: (n, 0, 0))
 
 
-def band_scratch(cols):
+def band_scratch(cols, weights):
     count = cols // WIN
-    return [
+    return [pltpu.VMEM(value.shape[1:], BF16) for value in weights] + [
+        pltpu.SemaphoreType.DMA((len(weights),)),
         pltpu.VMEM((WIN * cols, 3 * D), BF16),
         pltpu.VMEM((count, SPAN, HEADS * SPAN), F32),
         pltpu.VMEM((count, SPAN, HEADS * SPAN), BF16),
@@ -719,6 +770,7 @@
 
 
 def first_block(zeta, sigma, state, before, shift, back, grads, noise, bias, w_embed, weights):
+    *weights, gains = weights
     rows, cols, _ = state.shape
     fields = [*grads] + ([] if sigma is None else [noise])
     feats = D if sigma is None else D + PIXELS
@@ -731,17 +783,18 @@
             in_specs=[band_spec(cols, PIXELS)]
             + [whole(value) for value in back]
             + [band_spec(cols, PIXELS)] * len(fields)
-            + [bias_spec(cols), whole(w_embed)]
-            + [member(value, 0) for value in weights],
+            + [bias_spec(cols), whole(w_embed), member(gains, 0)]
+            + [pl.BlockSpec(memory_space=pl.ANY)] * len(weights),
             out_specs=[band_spec(cols, PIXELS)] + specs,
-            scratch_shapes=band_scratch(cols),
+            scratch_shapes=band_scratch(cols, weights),
         ),
         out_shape=[jax.ShapeDtypeStruct((rows, cols, PIXELS), F32)] + shapes,
         compiler_params=PARAMS,
-    )(shift, state, *back, *fields, bias, w_embed, *weights)
+    )(shift, state, *back, *fields, bias, w_embed, gains, *weights)
 
 
 def second_block(sigma, shift, tile, bias, w_unembed, weights):
+    *weights, gains = weights
     rows, cols, _ = tile[0].shape
     specs, shapes = strip_outs(rows, cols, PIXELS)
     if sigma is not None:
@@ -752,15 +805,15 @@
             num_scalar_prefetch=1,
             grid=(rows // WIN,),
             in_specs=[whole(value) for value in tile]
-            + [bias_spec(cols)]
-            + [member(value, 1) for value in weights]
-            + [whole(w_unembed)],
+            + [bias_spec(cols), whole(w_unembed), member(gains, 1)]
+            + [pl.BlockSpec(memory_space=pl.ANY)] * len(weights),
             out_specs=specs,
-            scratch_shapes=band_scratch(cols),
+            scratch_shapes=band_scratch(cols, weights)
+            + [pltpu.VMEM((WIN * cols, weights[2].shape[2]), BF16)],
         ),
         out_shape=shapes,
         compiler_params=PARAMS,
-    )(shift, *tile, bias, *weights, w_unembed)
+    )(shift, *tile, bias, w_unembed, gains, *weights)
 
 
 def from_neighbours(tile, by):
@@ -935,7 +988,8 @@
             grad = plain_gradient(tile, gains, observed, vis_weight)
             grads = [patches_of(grad.astype(F32)[None], 0, BF16)]
         elif step > 0:
-            grads = grads + [patch_gradient(moving, scale, None, shift, mirror, ())[0]]
+            grad, back = patch_gradient(moving, scale, None, shift, mirror, back)
+            grads = grads + [grad]
         last = step + 1 == STEPS
         sigma = None if last else SIGMAS[step + 1]
         state, *first = first_block(

time: 484 us -> 484 us (level)
  blocking collectives: 50 us -> 68.8 us
  waiting for transfers between devices: 113 us -> 98.5 us
    all_to_all x0 -> x1, blocking collectives: none -> 19 us  [patch_gradient(): grad = lax.all_to_all(slabs, 'tx', split_axis=0, concat_axis=0, tiled=True)]
    all_to_all x2, waiting for transfers between devices: 32.8 us -> 18.6 us  [patch_gradient(): lax.all_to_all(sent.reshape(part), ('ty', 'tx'), split_axis=0, concat_axi...]
    unnamed x66 -> x52, local copies, waits for them, and re-layouts: 24.6 us -> 23.6 us
    all_to_all x2 -> x1, waiting for transfers between devices: 12.9 us -> 13 us  [patch_gradient(): grad = lax.all_to_all(slabs, 'tx', split_axis=0, concat_axis=0, tiled=True)]
  transfers between devices with their start and end apart: 20 -> 19, of which waited for: 12 -> 10; matrix products, arithmetic and copies ran while one was open for 11% -> 11% of each run, Pallas kernels for 10% -> 10%
where the time goes in v2:
time: 484 us; the launch traced here: 476 us
  Pallas kernels  201 us (42%)
  waiting for transfers between devices  98.5 us (20%)
  blocking collectives  68.8 us (14%)
  local copies, waits for them, and re-layouts  47 us (10%)
  starting transfers between devices  39.7 us (8%)
  other arithmetic  16 us (3%)
  between operations  5.48 us (1%)
    pallas_call x2, Pallas kernels, second_block(): pl.pallas_call(functools.partial(second_kernel, sigma, rows), grid_spec=p...  58.8 us
    pallas_call x2, Pallas kernels, first_block(): pl.pallas_call(functools.partial(first_kernel, zeta, sigma, len(grads), r...  56.6 us
    ppermute x4, waiting for transfers between devices, from_neighbours(): lax.ppermute(corner, ('ty', 'tx'), across)  35.1 us
    all_to_all x1, blocking collectives, patch_gradient(): lax.all_to_all(wave, ('ty', 'tx'), split_axis=0, concat_axis=0, tiled=True)  29.8 us
    pallas_call x2, Pallas kernels, patch_gradient(): pl.pallas_call(functools.partial(column_kernel, halved), in_specs=[pl.Blo...  27.1 us
    unnamed x52, local copies, waits for them, and re-layouts  23.6 us
    all_to_all x1, blocking collectives, patch_gradient(): lax.all_to_all(state.reshape(lanes, own, cols, PIXELS), 'tx', split_axis=...  20 us
    all_to_all x1, waiting for transfers between devices, patch_gradient(): lax.all_to_all(wave, ('ty', 'tx'), split_axis=0, concat_axis=0, tiled=True)  19.1 us
  transfers between devices with their start and end apart: 19, of which 10 were waited for; matrix products, arithmetic and copies ran while one was open for 11% of the time, Pallas kernels for 10%

profile of v2, /device:TPU:0, one launch (start us, length us, event | category | flops | bytes accessed | tf_op | source)
XLA Modules:
  0.0 476.0 jit_solution(11131971510086315395)
XLA Ops:
  0.0 5.4 %shard_map.298 = bf16[32,64,256]{2,1,0:T(8,128)(2,1)} custom-call(f32[1,512,1024]{2,1,0:T(8,128)} %bitcast.72, bf16[1024,1024]{1,0:T(8,128)(2,1)} %constant.99.clone.order_ref), custom_call_target="tpu_custom_call" | custom-call | tf_op jit(solution)/shard_map/pallas_call | solution.py:918
  5.4 20.0 %all_to_all.40.x_ref = bf16[4,8,64,256]{3,2,1,0:T(8,128)(2,1)} all-to-all(bf16[4,8,64,256]{3,2,1,0:T(8,128)(2,1)} %bitcast.79), channel_id=1, replica_groups=mesh['ty'=8,'tx'=4] {'tx'}, dimensions={0} | all-to-all | bytes 2097152 | tf_op jit(solution)/shard_map/all_to_all | solution.py:493
  25.4 5.8 %shard_map.299 = bf16[16,2,2,128,128]{4,3,2,1,0:T(8,128)(2,1)} custom-call(bf16[4,8,64,256]{3,2,1,0:T(8,128)(2,1)} %all_to_all.40.x_ref, bf16[256,512]{1,0:T(8,128)(2,1)} %constant.104.clone.first_ref, f32[2,256,256]{2,1,0:T(8,128)} %constant.105.clone.twist_ref, bf16[512,512]{1,0:T(8,128)(2,1)} %constant.106.clone.second_ref), custom_call_target="tpu_custom_call" | custom-call | tf_op jit(solution)/shard_map/pallas_call | solution.py:496
  31.1 4.5 all-to-all-start.1
  38.6 4.7 fusion.18
  46.2 4.7 fusion.17
  59.7 5.1 %fusion.1 = (bf16[128,4096]{0,1:T(8,128)(2,1)S(1)}, bf16[128,4096]{0,1:T(8,128)(2,1)S(1)}, bf16[128,4096]{0,1:T(8,128)(2,1)S(1)}) fusion(f32[128,4096]{0,1:T(8,128)} %copy.72, f32[1,128,4096]{1,2,0:T(8,128)} %copy.92, f32[1,128,4096]{1,2,0:T(8,128)} %copy.94, f32[1,128,4096]{1,2,0:T(8,128)} %copy.91, f32[1,128,4096]{1,2,0:T(8,128)} %copy.93), kind=kLoop, calls=%fused_computation.4 | loop fusion | flops 7864320 | bytes 13631488 | tf_op jit(solution)/shard_map/convert_element_type | solution.py:400
  68.6 15.8 %all-to-all-done.1.refs_0_ = bf16[32,2,128,128]{3,2,1,0:T(8,128)(2,1)S(1)} async-done(((bf16[32,2,128,128]{3,2,1,0:T(8,128)(2,1)}), bf16[32,2,128,128]{3,2,1,0:T(8,128)(2,1)S(1)}, u32[]{:S(2)}, u32[]{:S(2)}) %all-to-all-start.1) | async-done | bytes 2097184 | tf_op jit(solution)/shard_map/all_to_all | solution.py:503
  85.7 14.3 %shard_map.300 = bf16[32,2,128,128]{3,2,1,0:T(8,128)(2,1)} custom-call(bf16[32,2,128,128]{3,2,1,0:T(8,128)(2,1)} %copy-done.1, bf16[1024,1024]{1,0:T(8,128)(2,1)} %constant.100.clone.refs_1_.refs_3_, bf16[32,256,256]{2,1,0:T(8,128)(2,1)} %constant.102.clone.refs_2_.refs_4_, bf16[32,128,128]{2,1,0:T(8,128)(2,1)} %bitcast.68, ...), custom_call_target="tpu_custom_call" | custom-call | tf_op jit(solution)/shard_map/pallas_call | solution.py:509
  100.0 4.8 %all-to-all-start.2 = ((bf16[32,2,128,128]{3,2,1,0:T(8,128)(2,1)}), bf16[32,2,128,128]{3,2,1,0:T(8,128)(2,1)S(1)}, u32[]{:S(2)}, u32[]{:S(2)}) async-start(bf16[32,2,128,128]{3,2,1,0:T(8,128)(2,1)} %shard_map.300), calls=%async_computation.2 | async-start | bytes 4194304 | tf_op jit(solution)/shard_map/all_to_all | solution.py:518
  104.9 6.5 %shard_map.301.refs_1_ = f32[32,64,256]{2,1,0:T(8,128)} custom-call(f32[1,512,1024]{2,1,0:T(8,128)} %bitcast.73, bf16[1024,1024]{1,0:T(8,128)(2,1)} %constant.99.clone.order_ref), custom_call_target="tpu_custom_call" | custom-call | tf_op jit(solution)/shard_map/pallas_call | solution.py:918
  111.4 6.6 %shard_map.302.refs_3_ = f32[32,64,256]{2,1,0:T(8,128)} custom-call(f32[2,512,1024]{2,1,0:T(8,128)} %refs_6_.4, bf16[1024,1024]{1,0:T(8,128)(2,1)} %constant.99.clone.order_ref), custom_call_target="tpu_custom_call" | custom-call | tf_op jit(solution)/shard_map/pallas_call | solution.py:918
  134.5 19.1 %all-to-all-done.2 = bf16[32,2,128,128]{3,2,1,0:T(8,128)(2,1)S(1)} async-done(((bf16[32,2,128,128]{3,2,1,0:T(8,128)(2,1)}), bf16[32,2,128,128]{3,2,1,0:T(8,128)(2,1)S(1)}, u32[]{:S(2)}, u32[]{:S(2)}) %all-to-all-start.2) | async-done | bytes 2097184 | tf_op jit(solution)/shard_map/all_to_all | solution.py:518
  154.9 7.5 %shard_map.303 = bf16[4,8,64,256]{3,2,1,0:T(8,128)(2,1)} custom-call(bf16[16,2,2,128,128]{4,3,2,1,0:T(8,128)(2,1)} %bitcast.74, bf16[256,512]{1,0:T(8,128)(2,1)} %constant.104.clone.first_ref, f32[2,256,256]{2,1,0:T(8,128)} %constant.105.clone.twist_ref, bf16[512,512]{1,0:T(8,128)(2,1)} %constant.107.clone.second_ref), custom_call_target="tpu_custom_call" | custom-call | tf_op jit(solution)/shard_map/pallas_call | solution.py:521
  166.7 13.0 %all-to-all-done.3 = bf16[4,8,64,256]{3,2,1,0:T(8,128)(2,1)S(1)} async-done(((bf16[4,8,64,256]{3,2,1,0:T(8,128)(2,1)}), bf16[4,8,64,256]{3,2,1,0:T(8,128)(2,1)S(1)}, u32[]{:S(2)}, u32[]{:S(2)}) %all-to-all-start.3) | async-done | bytes 1048608 | tf_op jit(solution)/shard_map/all_to_all | solution.py:526
  180.8 27.9 %shard_map.304 = (f32[32,64,256]{2,1,0:T(8,128)}, bf16[32,64,768]{2,1,0:T(8,128)(2,1)}, bf16[32,8,768]{2,1,0:T(8,128)(2,1)}, bf16[8,64,768]{2,1,0:T(8,128)(2,1)}, bf16[8,8,768]{2,1,0:T(8,128)(2,1)}) custom-call(s32[2]{0:T(128)} %get-tuple-element.79.refs_0_, f32[32,64,256]{2,1,0:T(8,128)} %shard_map.301.refs_1_, bf16[32,64,256]{2,1,0:T(8,128)(2,1)} %bitcast.70, ...), custom_call_target="tpu_custom_call" | custom-call | tf_op jit(solution)/shard_map/pallas_call | solution.py:778
  213.5 8.5 %collective-permute-done.2.refs_4_ = bf16[8,8,768]{2,1,0:T(8,128)(2,1)S(1)} collective-permute-done((bf16[8,8,768]{2,1,0:T(8,128)(2,1)}, bf16[8,8,768]{2,1,0:T(8,128)(2,1)S(1)}, u32[]{:S(2)}, u32[]{:S(2)}) %collective-permute-start.2) | collective-permute-done | bytes 98336 | tf_op jit(solution)/shard_map/ppermute | solution.py:829
  229.8 29.9 %shard_map.305 = (bf16[32,64,256]{2,1,0:T(8,128)(2,1)}, bf16[32,8,256]{2,1,0:T(8,128)(2,1)}, bf16[8,64,256]{2,1,0:T(8,128)(2,1)}, bf16[8,8,256]{2,1,0:T(8,128)(2,1)}, bf16[32,64,256]{2,1,0:T(8,128)(2,1)}) custom-call(s32[2]{0:T(128)} %get-tuple-element.79.refs_0_, bf16[32,64,768]{2,1,0:T(8,128)(2,1)} %get-tuple-element.59.refs_1_, ...), custom_call_target="tpu_custom_call" | custom-call | tf_op jit(solution)/shard_map/pallas_call | solution.py:802
  259.7 4.6 all-to-all-start.4
  267.2 12.0 %all-to-all-done.4.x_ref = bf16[4,8,64,256]{3,2,1,0:T(8,128)(2,1)S(1)} async-done(((bf16[4,8,64,256]{3,2,1,0:T(8,128)(2,1)}), bf16[4,8,64,256]{3,2,1,0:T(8,128)(2,1)S(1)}, u32[]{:S(2)}, u32[]{:S(2)}) %all-to-all-start.4) | async-done | bytes 1048608 | tf_op jit(solution)/shard_map/all_to_all | solution.py:493
  280.2 6.1 %shard_map.306 = bf16[16,2,128,128]{3,2,1,0:T(8,128)(2,1)} custom-call(bf16[4,8,64,256]{3,2,1,0:T(8,128)(2,1)} %copy-done.4, bf16[256,512]{1,0:T(8,128)(2,1)} %constant_dynamic-slice_fusion.first_ref, f32[2,256,256]{2,1,0:T(8,128)} %constant.109.clone.twist_ref, bf16[256,512]{1,0:T(8,128)(2,1)} %constant.110.clone.lower_ref, ...), custom_call_target="tpu_custom_call" | custom-call | tf_op jit(solution)/shard_map/pallas_call | solution.py:496
  298.2 5.4 %shard_map.307.refs_5_ = bf16[32,128,128]{2,1,0:T(8,128)(2,1)} custom-call(bf16[32,128,128]{2,1,0:T(8,128)(2,1)} %bitcast.69, bf16[32,128,128]{2,1,0:T(8,128)(2,1)} %bitcast.78, bf16[2,128,128]{2,1,0:T(8,128)(2,1)} %add_convert_fusion.pick_ref, bf16[2,128,128]{2,1,0:T(8,128)(2,1)} %constant.115.clone.flip_ref), custom_call_target="tpu_custom_call" | custom-call | tf_op jit(solution)/shard_map/pallas_call | solution.py:449
  303.5 12.6 %collective-permute-done.7.refs_5_ = bf16[8,8,256]{2,1,0:T(8,128)(2,1)} collective-permute-done((bf16[8,8,256]{2,1,0:T(8,128)(2,1)}, bf16[8,8,256]{2,1,0:T(8,128)(2,1)}, u32[]{:S(2)}, u32[]{:S(2)}) %collective-permute-start.7) | collective-permute-done | bytes 32800 | tf_op jit(solution)/shard_map/ppermute | solution.py:829
  320.0 12.7 %shard_map.308 = bf16[32,128,128]{2,1,0:T(8,128)(2,1)} custom-call(s32[1]{0:T(128)} %bitcast.31.refs_0_, f32[32,2,8,128]{3,2,1,0:T(8,128)} %broadcast_in_dim.75.refs_1_, bf16[32,128,128]{2,1,0:T(8,128)(2,1)} %copy-done.3, bf16[1024,1024]{1,0:T(8,128)(2,1)} %constant.100.clone.refs_1_.refs_3_, bf16[32,256,256]{2,1,0:T(8,128)(2,1)} %constant.102.clone.refs_2_.refs_4_, ...), custom_call_target="tpu_custom_call" | custom-call | tf_op jit(solution)/shard_map/pallas_call | solution.py:509
  332.7 29.8 %all_to_all.41 = bf16[32,128,128]{2,1,0:T(8,128)(2,1)} all-to-all(bf16[32,128,128]{2,1,0:T(8,128)(2,1)} %shard_map.308), channel_id=1, replica_groups=mesh['ty'=8,'tx'=4] {'ty','tx'}, dimensions={0} | all-to-all | bytes 2097152 | tf_op jit(solution)/shard_map/all_to_all | solution.py:518
  362.5 6.4 %shard_map.309 = bf16[4,8,64,256]{3,2,1,0:T(8,128)(2,1)} custom-call(bf16[16,2,128,128]{3,2,1,0:T(8,128)(2,1)} %bitcast.77, bf16[256,512]{1,0:T(8,128)(2,1)} %constant.108.clone.first_ref, f32[2,256,256]{2,1,0:T(8,128)} %constant.109.clone.twist_ref, bf16[512,256]{1,0:T(8,128)(2,1)} %constant.112.clone.lower_ref, bf16[512,272]{1,0:T(8,128)(2,1)} %constant.113.clone.upper_ref), custom_call_target="tpu_custom_call" | custom-call | tf_op jit(solution)/shard_map/pallas_call | solution.py:521
  368.9 19.0 %all_to_all.42 = bf16[4,8,64,256]{3,2,1,0:T(8,128)(2,1)} all-to-all(bf16[4,8,64,256]{3,2,1,0:T(8,128)(2,1)} %shard_map.309), channel_id=1, replica_groups=mesh['ty'=8,'tx'=4] {'tx'}, dimensions={0} | all-to-all | bytes 2097152 | tf_op jit(solution)/shard_map/all_to_all | solution.py:526
  387.9 28.7 %shard_map.310 = (f32[32,64,256]{2,1,0:T(8,128)}, bf16[32,64,512]{2,1,0:T(8,128)(2,1)}, bf16[32,8,512]{2,1,0:T(8,128)(2,1)}, bf16[8,64,512]{2,1,0:T(8,128)(2,1)}, bf16[8,8,512]{2,1,0:T(8,128)(2,1)}) custom-call(s32[2]{0:T(128)} %get-tuple-element.79.refs_0_, f32[32,64,256]{2,1,0:T(8,128)} %get-tuple-element.54.refs_1_, ...), custom_call_target="tpu_custom_call" | custom-call | tf_op jit(solution)/shard_map/pallas_call | solution.py:778
  419.5 7.5 %collective-permute-done.10.refs_4_ = bf16[8,8,512]{2,1,0:T(8,128)(2,1)S(1)} collective-permute-done((bf16[8,8,512]{2,1,0:T(8,128)(2,1)}, bf16[8,8,512]{2,1,0:T(8,128)(2,1)S(1)}, u32[]{:S(2)}, u32[]{:S(2)}) %collective-permute-start.10) | collective-permute-done | bytes 65568 | tf_op jit(solution)/shard_map/ppermute | solution.py:829
  427.9 28.9 %shard_map.311 = (bf16[32,64,256]{2,1,0:T(8,128)(2,1)}, bf16[32,8,256]{2,1,0:T(8,128)(2,1)}, bf16[8,64,256]{2,1,0:T(8,128)(2,1)}, bf16[8,8,256]{2,1,0:T(8,128)(2,1)}) custom-call(s32[2]{0:T(128)} %get-tuple-element.105.refs_0_, bf16[32,64,512]{2,1,0:T(8,128)(2,1)} %get-tuple-element.84.refs_1_, bf16[32,8,512]{2,1,0:T(8,128)(2,1)} %copy-done.8, ...), custom_call_target="tpu_custom_call" | custom-call | tf_op jit(solution)/shard_map/pallas_call | solution.py:802
  459.6 6.6 %collective-permute-done.13.refs_5_ = bf16[8,8,256]{2,1,0:T(8,128)(2,1)S(1)} collective-permute-done((bf16[8,8,256]{2,1,0:T(8,128)(2,1)}, bf16[8,8,256]{2,1,0:T(8,128)(2,1)S(1)}, u32[]{:S(2)}, u32[]{:S(2)}) %collective-permute-start.13) | collective-permute-done | bytes 32800 | tf_op jit(solution)/shard_map/ppermute | solution.py:829
  467.0 8.5 %shard_map.312 = f32[512,1024]{1,0:T(8,128)} custom-call(s32[2]{0:T(128)} %get-tuple-element.105.refs_0_, f32[32,64,256]{2,1,0:T(8,128)} %get-tuple-element.83.refs_1_, bf16[32,64,256]{2,1,0:T(8,128)(2,1)} %get-tuple-element.89.refs_2_, bf16[32,8,256]{2,1,0:T(8,128)(2,1)} %copy-done.15, bf16[8,64,256]{2,1,0:T(8,128)(2,1)} %copy-done.9, ...), custom_call_target="tpu_custom_call" | custom-call | tf_op jit(solution)/shard_map/pallas_call | solution.py:934
  (123 shorter events, 77.7 us)
Async XLA Ops:
  31.1 53.2 %all-to-all-start.1 = ((bf16[32,2,128,128]{3,2,1,0:T(8,128)(2,1)}), bf16[32,2,128,128]{3,2,1,0:T(8,128)(2,1)S(1)}, u32[]{:S(2)}, u32[]{:S(2)}) async-start(bf16[32,2,128,128]{3,2,1,0:T(8,128)(2,1)} %bitcast.75), calls=%async_computation.1 | async-start | bytes 4194304 | tf_op jit(solution)/shard_map/all_to_all | solution.py:503
  84.4 1.3 copy-start.1
  100.0 53.6 %all-to-all-start.2 = ((bf16[32,2,128,128]{3,2,1,0:T(8,128)(2,1)}), bf16[32,2,128,128]{3,2,1,0:T(8,128)(2,1)S(1)}, u32[]{:S(2)}, u32[]{:S(2)}) async-start(bf16[32,2,128,128]{3,2,1,0:T(8,128)(2,1)} %shard_map.300), calls=%async_computation.2 | async-start | bytes 4194304 | tf_op jit(solution)/shard_map/all_to_all | solution.py:518
  111.4 6.6 %copy-start.19 = (s32[32,64]{1,0:T(8,128)S(1)}, s32[32,64]{1,0:T(8,128)}, u32[]{:S(2)}) copy-start(s32[32,64]{1,0:T(8,128)} %param.35) | copy-start | bytes 24580
  111.4 7.5 %copy-start.21 = (s32[2,2]{1,0:T(2,128)S(1)}, s32[2,2]{1,0:T(2,128)}, u32[]{:S(2)}) copy-start(s32[2,2]{1,0:T(2,128)} %param.34) | copy-start | bytes 52
  111.4 13.6 %copy-start.10 = (bf16[256,512]{1,0:T(8,128)(2,1)S(1)}, bf16[256,512]{1,0:T(8,128)(2,1)}, u32[]{:S(2)}) copy-start(bf16[256,512]{1,0:T(8,128)(2,1)} %param.39) | copy-start | bytes 786436
  131.1 1.7 copy-start.13
  153.6 1.3 copy-start.2
  162.4 3.8 copy-start.22
  162.4 17.4 %all-to-all-start.3 = ((bf16[4,8,64,256]{3,2,1,0:T(8,128)(2,1)}), bf16[4,8,64,256]{3,2,1,0:T(8,128)(2,1)S(1)}, u32[]{:S(2)}, u32[]{:S(2)}) async-start(bf16[4,8,64,256]{3,2,1,0:T(8,128)(2,1)} %shard_map.303), calls=%async_computation.3 | async-start | bytes 2097152 | tf_op jit(solution)/shard_map/all_to_all | solution.py:526
  208.7 13.9 %collective-permute-start.1 = (bf16[8,64,768]{2,1,0:T(8,128)(2,1)}, bf16[8,64,768]{2,1,0:T(8,128)(2,1)S(1)}, u32[]{:S(2)}, u32[]{:S(2)}) collective-permute-start(bf16[8,64,768]{2,1,0:T(8,128)(2,1)} %get-tuple-element.57), channel_id=1, source_target_pairs={{0,28},{4,0},{8,4},{12,8},{16,12},{20,16},{24,20},{28,24},{1,29},{... | collective-permute-start | bytes 2359304 | tf_op jit(solution)/shard_map/ppermute | solution.py:828
  209.8 12.8 %collective-permute-start = (bf16[32,8,768]{2,1,0:T(8,128)(2,1)}, bf16[32,8,768]{2,1,0:T(8,128)(2,1)S(1)}, u32[]{:S(2)}, u32[]{:S(2)}) collective-permute-start(bf16[32,8,768]{2,1,0:T(8,128)(2,1)} %get-tuple-element.56), channel_id=1, source_target_pairs={{0,3},{1,0},{2,1},{3,2},{4,7},{5,4},{6,5},{7,6},{8,11},{9,8},{10,9... | collective-permute-start | bytes 1179656 | tf_op jit(solution)/shard_map/ppermute | solution.py:827
  211.2 10.9 %collective-permute-start.2 = (bf16[8,8,768]{2,1,0:T(8,128)(2,1)}, bf16[8,8,768]{2,1,0:T(8,128)(2,1)S(1)}, u32[]{:S(2)}, u32[]{:S(2)}) collective-permute-start(bf16[8,8,768]{2,1,0:T(8,128)(2,1)} %get-tuple-element.58), channel_id=1, source_target_pairs={{0,31},{1,28},{2,29},{3,30},{4,3},{5,0},{6,1},{7,2},{8,7},{9,4},{1... | collective-permute-start | bytes 294920 | tf_op jit(solution)/shard_map/ppermute | solution.py:829
  222.0 7.7 %copy-start.16 = (bf16[8,8,768]{2,1,0:T(8,128)(2,1)}, bf16[8,8,768]{2,1,0:T(8,128)(2,1)S(1)}, u32[]{:S(2)}) copy-start(bf16[8,8,768]{2,1,0:T(8,128)(2,1)S(1)} %collective-permute-done.2.refs_4_) | copy-start | bytes 294916
  223.3 5.5 %copy-start.5 = (bf16[8,64,768]{2,1,0:T(8,128)(2,1)}, bf16[8,64,768]{2,1,0:T(8,128)(2,1)S(1)}, u32[]{:S(2)}) copy-start(bf16[8,64,768]{2,1,0:T(8,128)(2,1)S(1)} %collective-permute-done.1.refs_3_) | copy-start | bytes 2359300
  224.8 34.9 %collective-permute-start.3 = (bf16[64,4096]{1,0:T(8,128)(2,1)}, bf16[64,4096]{1,0:T(8,128)(2,1)S(1)}, u32[]{:S(2)}, u32[]{:S(2)}) collective-permute-start(bf16[64,4096]{1,0:T(8,128)(2,1)} %copy.85), channel_id=1, source_target_pairs={{0,31},{1,30},{2,29},{3,28},{4,27},{5,26},{6,25},{7,24},{8,23},{9,... | collective-permute-start | bytes 1572872 | tf_op jit(solution)/shard_map/ppermute | solution.py:429
  228.9 30.9 %collective-permute-start.4 = (bf16[1,4096]{1,0:T(2,128)(2,1)S(1)}, bf16[1,4096]{1,0:T(2,128)(2,1)S(1)}, u32[]{:S(2)}, u32[]{:S(2)}) collective-permute-start(bf16[1,4096]{1,0:T(2,128)(2,1)S(1)} %copy.86), channel_id=1, source_target_pairs={{1,31},{2,30},{3,29},{4,28},{5,27},{6,26},{7,25},{8,24},{9,23},{10... | collective-permute-start | bytes 24584 | tf_op jit(solution)/shard_map/ppermute | solution.py:430
  259.7 6.7 %copy-start.12 = (bf16[272,512]{1,0:T(8,128)(2,1)S(1)}, bf16[272,512]{1,0:T(8,128)(2,1)}, u32[]{:S(2)}) copy-start(bf16[272,512]{1,0:T(8,128)(2,1)} %constant.114.clone) | copy-start | bytes 835588
  259.7 19.5 %all-to-all-start.4 = ((bf16[4,8,64,256]{3,2,1,0:T(8,128)(2,1)}), bf16[4,8,64,256]{3,2,1,0:T(8,128)(2,1)S(1)}, u32[]{:S(2)}, u32[]{:S(2)}) async-start(bf16[4,8,64,256]{3,2,1,0:T(8,128)(2,1)} %bitcast.86), calls=%async_computation.4 | async-start | bytes 2097152 | tf_op jit(solution)/shard_map/all_to_all | solution.py:493
  286.3 32.6 %all-to-all-start.5 = ((bf16[32,128,128]{2,1,0:T(8,128)(2,1)}), bf16[32,128,128]{2,1,0:T(8,128)(2,1)S(1)}, u32[]{:S(2)}, u32[]{:S(2)}) async-start(bf16[32,128,128]{2,1,0:T(8,128)(2,1)} %bitcast.80), calls=%async_computation.5 | async-start | bytes 2097152 | tf_op jit(solution)/shard_map/all_to_all | solution.py:503
  290.1 25.9 %collective-permute-start.5 = (bf16[32,8,256]{2,1,0:T(8,128)(2,1)}, bf16[32,8,256]{2,1,0:T(8,128)(2,1)S(1)}, u32[]{:S(2)}, u32[]{:S(2)}) collective-permute-start(bf16[32,8,256]{2,1,0:T(8,128)(2,1)} %get-tuple-element.72), channel_id=1, source_target_pairs={{0,1},{1,2},{2,3},{3,0},{4,5},{5,6},{6,7},{7,4},{8,9},{9,10},{10,1... | collective-permute-start | bytes 393224 | tf_op jit(solution)/shard_map/ppermute | solution.py:827
  291.9 24.2 %collective-permute-start.6 = (bf16[8,64,256]{2,1,0:T(8,128)(2,1)}, bf16[8,64,256]{2,1,0:T(8,128)(2,1)S(1)}, u32[]{:S(2)}, u32[]{:S(2)}) collective-permute-start(bf16[8,64,256]{2,1,0:T(8,128)(2,1)} %get-tuple-element.73), channel_id=1, source_target_pairs={{0,4},{4,8},{8,12},{12,16},{16,20},{20,24},{24,28},{28,0},{1,5},{5... | collective-permute-start | bytes 786440 | tf_op jit(solution)/shard_map/ppermute | solution.py:828
  291.9 24.1 %collective-permute-start.7 = (bf16[8,8,256]{2,1,0:T(8,128)(2,1)}, bf16[8,8,256]{2,1,0:T(8,128)(2,1)}, u32[]{:S(2)}, u32[]{:S(2)}) collective-permute-start(bf16[8,8,256]{2,1,0:T(8,128)(2,1)} %get-tuple-element.74), channel_id=1, source_target_pairs={{0,5},{1,6},{2,7},{3,4},{4,9},{5,10},{6,11},{7,8},{8,13},{9,14},{1... | collective-permute-start | bytes 98312 | tf_op jit(solution)/shard_map/ppermute | solution.py:829
  295.3 1.2 copy-start.20
  316.1 16.6 %copy-start.14 = (bf16[32,8,256]{2,1,0:T(8,128)(2,1)}, bf16[32,8,256]{2,1,0:T(8,128)(2,1)S(1)}, u32[]{:S(2)}) copy-start(bf16[32,8,256]{2,1,0:T(8,128)(2,1)S(1)} %collective-permute-done.5.refs_3_) | copy-start | bytes 393220
  316.1 16.6 %copy-start.11 = (bf16[8,64,256]{2,1,0:T(8,128)(2,1)}, bf16[8,64,256]{2,1,0:T(8,128)(2,1)S(1)}, u32[]{:S(2)}) copy-start(bf16[8,64,256]{2,1,0:T(8,128)(2,1)S(1)} %collective-permute-done.6.refs_4_) | copy-start | bytes 786436
  416.6 10.4 %collective-permute-start.9 = (bf16[8,64,512]{2,1,0:T(8,128)(2,1)}, bf16[8,64,512]{2,1,0:T(8,128)(2,1)S(1)}, u32[]{:S(2)}, u32[]{:S(2)}) collective-permute-start(bf16[8,64,512]{2,1,0:T(8,128)(2,1)} %get-tuple-element.86), channel_id=1, source_target_pairs={{0,28},{4,0},{8,4},{12,8},{16,12},{20,16},{24,20},{28,24},{1,29},{... | collective-permute-start | bytes 1572872 | tf_op jit(solution)/shard_map/ppermute | solution.py:828
  416.7 10.3 %collective-permute-start.8 = (bf16[32,8,512]{2,1,0:T(8,128)(2,1)}, bf16[32,8,512]{2,1,0:T(8,128)(2,1)S(1)}, u32[]{:S(2)}, u32[]{:S(2)}) collective-permute-start(bf16[32,8,512]{2,1,0:T(8,128)(2,1)} %get-tuple-element.85), channel_id=1, source_target_pairs={{0,3},{1,0},{2,1},{3,2},{4,7},{5,4},{6,5},{7,6},{8,11},{9,8},{10,9... | collective-permute-start | bytes 786440 | tf_op jit(solution)/shard_map/ppermute | solution.py:827
  417.7 9.3 %collective-permute-start.10 = (bf16[8,8,512]{2,1,0:T(8,128)(2,1)}, bf16[8,8,512]{2,1,0:T(8,128)(2,1)S(1)}, u32[]{:S(2)}, u32[]{:S(2)}) collective-permute-start(bf16[8,8,512]{2,1,0:T(8,128)(2,1)} %get-tuple-element.87), channel_id=1, source_target_pairs={{0,31},{1,28},{2,29},{3,30},{4,3},{5,0},{6,1},{7,2},{8,7},{9,4},{1... | collective-permute-start | bytes 196616 | tf_op jit(solution)/shard_map/ppermute | solution.py:829
  456.8 9.5 %collective-permute-start.12 = (bf16[8,64,256]{2,1,0:T(8,128)(2,1)}, bf16[8,64,256]{2,1,0:T(8,128)(2,1)S(1)}, u32[]{:S(2)}, u32[]{:S(2)}) collective-permute-start(bf16[8,64,256]{2,1,0:T(8,128)(2,1)} %get-tuple-element.91), channel_id=1, source_target_pairs={{0,4},{4,8},{8,12},{12,16},{16,20},{20,24},{24,28},{28,0},{1,5},{5... | collective-permute-start | bytes 786440 | tf_op jit(solution)/shard_map/ppermute | solution.py:828
  456.8 9.4 %collective-permute-start.11 = (bf16[32,8,256]{2,1,0:T(8,128)(2,1)}, bf16[32,8,256]{2,1,0:T(8,128)(2,1)S(1)}, u32[]{:S(2)}, u32[]{:S(2)}) collective-permute-start(bf16[32,8,256]{2,1,0:T(8,128)(2,1)} %get-tuple-element.90), channel_id=1, source_target_pairs={{0,1},{1,2},{2,3},{3,0},{4,5},{5,6},{6,7},{7,4},{8,9},{9,10},{10,1... | collective-permute-start | bytes 393224 | tf_op jit(solution)/shard_map/ppermute | solution.py:827
  458.7 7.5 %collective-permute-start.13 = (bf16[8,8,256]{2,1,0:T(8,128)(2,1)}, bf16[8,8,256]{2,1,0:T(8,128)(2,1)S(1)}, u32[]{:S(2)}, u32[]{:S(2)}) collective-permute-start(bf16[8,8,256]{2,1,0:T(8,128)(2,1)} %get-tuple-element.92), channel_id=1, source_target_pairs={{0,5},{1,6},{2,7},{3,4},{4,9},{5,10},{6,11},{7,8},{8,13},{9,14},{1... | collective-permute-start | bytes 98312 | tf_op jit(solution)/shard_map/ppermute | solution.py:829
  (10 other events, 8.1 us)

commit v3 on v2

--- a/solution.py
+++ b/solution.py
@@ -185,11 +185,12 @@
     )
 
 
-def row_forward(x_ref, first_ref, twist_ref, second_ref, out_ref):
-    count = x_ref.shape[1]
+def row_forward(*refs):
+    *x_refs, first_ref, twist_ref, second_ref, out_ref = refs
+    count = x_refs[0].shape[0]
 
     def step(i, carry):
-        band = x_ref[:, i].reshape(TOK, PIXELS)
+        band = jnp.concatenate([x_ref[i] for x_ref in x_refs], axis=0)
         mixed = mm(band, first_ref[...], TN)
         real, imag = mixed[:, :TOK], mixed[:, TOK:]
         tr, ti = twist_ref[0], twist_ref[1]
@@ -206,8 +207,8 @@
     lax.fori_loop(0, count, step, 0, unroll=4)
 
 
-def row_inverse(v_ref, first_ref, twist_ref, second_ref, out_ref):
-    parts, count, cols, _ = out_ref.shape
+def row_inverse(v_ref, first_ref, twist_ref, second_ref, *out_refs):
+    count, cols, _ = out_refs[0].shape
 
     def step(i, carry):
         rows = pl.ds(pl.multiple_of(i * PATCH, PATCH), PATCH)
@@ -225,7 +226,8 @@
             [(real * tr + imag * ti).astype(BF16), (imag * tr - real * ti).astype(BF16)], axis=1
         )
         result = mm(first_ref[...], turned, NT).astype(BF16)
-        out_ref[:, i] = result.reshape(parts, cols, PIXELS)
+        for m, out_ref in enumerate(out_refs):
+            out_ref[i] = result[m * cols : (m + 1) * cols]
         return carry
 
     lax.fori_loop(0, count, step, 0, unroll=4)
@@ -239,8 +241,9 @@
     return pltpu.roll(values, values.shape[-1] // 2, len(values.shape) - 1)
 
 
-def row_forward_half(x_ref, first_ref, twist_ref, lower_ref, upper_ref, out_ref):
-    count = x_ref.shape[1]
+def row_forward_half(*refs):
+    *x_refs, first_ref, twist_ref, lower_ref, upper_ref, out_ref = refs
+    count = x_refs[0].shape[0]
     half = TOK // 2
 
     def packed(real, imag, rows, high):
@@ -249,7 +252,7 @@
         out_ref[high, 1, rows, :] = jnp.where(left, swap_halves(real), imag).astype(BF16)
 
     def step(i, carry):
-        band = x_ref[:, i].reshape(TOK, PIXELS)
+        band = jnp.concatenate([x_ref[i] for x_ref in x_refs], axis=0)
         mixed = mm(band, first_ref[...], TN)
         real, imag = mixed[:, :TOK], mixed[:, TOK:]
         tr, ti = twist_ref[0], twist_ref[1]
@@ -271,8 +274,8 @@
     lax.fori_loop(0, count, step, 0, unroll=4)
 
 
-def row_inverse_half(v_ref, first_ref, twist_ref, lower_ref, upper_ref, out_ref):
-    parts, count, cols, _ = out_ref.shape
+def row_inverse_half(v_ref, first_ref, twist_ref, lower_ref, upper_ref, *out_refs):
+    count, cols, _ = out_refs[0].shape
     half = TOK // 2
 
     def unpacked(rows, high):
@@ -301,7 +304,8 @@
             [(real * tr + imag * ti).astype(BF16), (imag * tr - real * ti).astype(BF16)], axis=1
         )
         result = mm(first_ref[...], turned, NT).astype(BF16)
-        out_ref[:, i] = result.reshape(parts, cols, PIXELS)
+        for m, out_ref in enumerate(out_refs):
+            out_ref[i] = result[m * cols : (m + 1) * cols]
         return carry
 
     lax.fori_loop(0, count, step, 0, unroll=4)
@@ -420,14 +424,13 @@
         out_ref[q] = total.astype(BF16)
 
 
-def mirrored_exchange(weight):
-    devices = N // weight.shape[0]
-    half, middle = weight.shape[0] // 2, devices // 2
+def mirrored_exchange(upper, line, devices):
+    middle = devices // 2
     facing = [(e, devices - 1 - e) for e in range(devices)]
     partner = [(e, devices - e) for e in range(1, devices) if e != middle]
     partner = partner + [(0, middle), (middle, 0)]
-    upper = lax.ppermute(weight[half:], ("ty", "tx"), facing)
-    line = lax.ppermute(weight[:1], ("ty", "tx"), partner)
+    upper = lax.ppermute(upper, ("ty", "tx"), facing)
+    line = lax.ppermute(line, ("ty", "tx"), partner)
     return upper, line
 
 
@@ -453,10 +456,20 @@
     )(scale, turned(got, devices), picks, jnp.asarray(flips.astype(ml_dtypes.bfloat16)))
 
 
-def row_matrix(shift):
-    first = half_constants()[0]
+def row_matrix(first, cols, lanes, shift):
     twice = jnp.asarray(np.concatenate([first, first[: 2 * WIN]], axis=0))
-    return lax.dynamic_slice(twice, (shift, jnp.zeros((), jnp.int32)), first.shape)
+    me = lax.axis_index("tx")
+    zero = jnp.zeros((), jnp.int32)
+    starts = [(me ^ m) * cols + (0 if shift is None else shift) for m in range(lanes)]
+    rows = [lax.dynamic_slice(twice, (start, zero), (cols, first.shape[1])) for start in starts]
+    return jnp.concatenate(rows, axis=0)
+
+
+def swap_pieces(pieces):
+    lanes = len(pieces)
+    return [pieces[0]] + [
+        lax.ppermute(pieces[m], "tx", [(k, k ^ m) for k in range(lanes)]) for m in range(1, lanes)
+    ]
 
 
 def phase_table(shift, devices, width):
@@ -466,36 +479,34 @@
     return jnp.broadcast_to(table[..., None], (devices, 2, 8, width))
 
 
-def patch_gradient(state, scale, data, shift, mirror, beside):
+def patch_gradient(pieces, scale, data, shift, mirror, beside):
     lanes = lax.axis_size("tx")
     devices = lax.axis_size("ty") * lanes
-    rows, cols, _ = state.shape
-    own = rows // lanes
+    own, cols, _ = pieces[0].shape
     slab = N // devices
     halved = data is None
     outer, outer_t, inner, inner_t = (
         jnp.asarray(value) for value in column_constants(devices, slab)
     )
     if halved:
-        first, twist, low, high, low_t, high_t = (jnp.asarray(value) for value in half_constants())
+        first = half_constants()[0]
+        twist, low, high, low_t, high_t = (jnp.asarray(value) for value in half_constants()[1:])
         part = (devices, slab, slab)
-        onward = (row_forward_half, (row_matrix(shift[1]), twist, low, high))
-        backward = (row_inverse_half, (first, twist, low_t, high_t))
+        onward = (row_forward_half, (row_matrix(first, cols, lanes, shift[1]), twist, low, high))
+        backward = (row_inverse_half, (row_matrix(first, cols, lanes, None), twist, low_t, high_t))
         middle = lax.axis_index(("ty", "tx")) == devices // 2
     else:
-        first, twist, second, second_t = (jnp.asarray(value) for value in row_constants())
+        first = row_matrix(row_constants()[0], cols, lanes, None)
+        twist, second, second_t = (jnp.asarray(value) for value in row_constants()[1:])
         part = (devices, 2, slab, slab)
         onward = (row_forward, (first, twist, second))
         backward = (row_inverse, (first, twist, second_t))
         extra = ()
         away = (inner, scale, inner_t, outer_t, data)
     split = (PATCH, devices // PATCH) + part[1:]
-    gathered = lax.all_to_all(
-        state.reshape(lanes, own, cols, PIXELS), "tx", split_axis=0, concat_axis=0, tiled=True
-    )
     sent = pl.pallas_call(
         onward[0], out_shape=jax.ShapeDtypeStruct(split, BF16), compiler_params=PARAMS
-    )(gathered, *onward[1])
+    )(*swap_pieces(pieces), *onward[1])
     if halved:
         sent, mirror, shift = lax.optimization_barrier((sent, mirror, shift))
         extra = (middle.astype(jnp.int32).reshape(1), phase_table(shift[0], devices, slab))
@@ -520,11 +531,10 @@
         returned, beside = lax.optimization_barrier((returned, beside))
     slabs = pl.pallas_call(
         backward[0],
-        out_shape=jax.ShapeDtypeStruct((lanes, own, cols, PIXELS), BF16),
+        out_shape=[jax.ShapeDtypeStruct((own, cols, PIXELS), BF16)] * lanes,
         compiler_params=PARAMS,
     )(returned.reshape(split), *backward[1])
-    grad = lax.all_to_all(slabs, "tx", split_axis=0, concat_axis=0, tiled=True)
-    return grad.reshape(rows, cols, PIXELS), beside
+    return swap_pieces(slabs), beside
 
 
 def layer_norm(values, gain):
@@ -537,17 +547,23 @@
 def to_windows(band):
     rows, cols, feats = band.shape
     pieces = [
-        band[:, w * WIN : (w + 1) * WIN, :].reshape(SPAN, feats) for w in range(cols // WIN)
+        band[n : n + WIN, k : k + WIN, :].reshape(SPAN, feats)
+        for n in range(0, rows, WIN)
+        for k in range(0, cols, WIN)
     ]
     return jnp.concatenate(pieces, axis=0)
 
 
 def from_windows(tokens, cols):
     feats = tokens.shape[-1]
-    pieces = [
-        tokens[w * SPAN : (w + 1) * SPAN].reshape(WIN, WIN, feats) for w in range(cols // WIN)
-    ]
-    return jnp.concatenate(pieces, axis=1)
+    size = SPAN * cols // WIN
+    bands = []
+    for top in range(0, tokens.shape[0], size):
+        pieces = [
+            tokens[n : n + SPAN].reshape(WIN, WIN, feats) for n in range(top, top + size, SPAN)
+        ]
+        bands.append(jnp.concatenate(pieces, axis=1))
+    return jnp.concatenate(bands, axis=0)
 
 
 def gelu_twice(value):
@@ -645,10 +661,10 @@
     return flow + 0.5 * total
 
 
-def rolled_band(sign, shift_ref, refs, rows):
+def rolled_band(sign, shift_ref, refs, rows, count=WIN):
     main_ref, side_ref, edge_ref, corner_ref = refs
     cols = main_ref.shape[1]
-    top = pl.program_id(0) * WIN + sign * shift_ref[0]
+    top = pl.program_id(0) * count + sign * shift_ref[0]
     behind = -rows if sign > 0 else WIN
     beside = -cols if sign > 0 else WIN
 
@@ -659,7 +675,7 @@
 
     pick_main, pick_side = pick(cols, 0), pick(WIN, beside)
     band = []
-    for j in range(WIN):
+    for j in range(count):
         row = top + j
         inside = (row >= 0) & (row < rows)
         here, there = jnp.clip(row, 0, rows - 1), jnp.clip(row + behind, 0, WIN - 1)
@@ -669,11 +685,11 @@
     return jnp.stack(band)
 
 
-def first_kernel(zeta, sigma, count, rows, before, *refs):
+def first_kernel(zeta, sigma, count, parts, rows, before, *refs):
     shift_ref, state_ref, *refs = refs
     if before is not None:
         back_refs, refs = refs[:4], refs[4:]
-    grad_refs, refs = refs[:count], refs[count:]
+    grad_refs, refs = refs[: count * parts], refs[count * parts :]
     if sigma is not None:
         noise_ref, *refs = refs
     bias_ref, embed_ref, gain_ref, *sources = refs[:7]
@@ -683,7 +699,17 @@
     state = state_ref[...]
     if before is not None:
         state = state - before * rolled_band(-1, shift_ref, back_refs, rows)
-    step = zeta * sum(grad_ref[...].astype(F32) for grad_ref in grad_refs)
+    turn = pl.program_id(0) ^ shift_ref[2]
+    grad = 0.0
+    if parts == 1:
+        grad = grad_refs[0][...].astype(F32)
+        count = 0
+    for n in range(0, count * parts, parts):
+        piece = grad_refs[n][...]
+        for m in range(1, parts):
+            piece = jnp.where(turn == m, grad_refs[n + m][...], piece)
+        grad = grad + piece.astype(F32)
+    step = zeta * grad
     half = state - step
     tokens = mm(to_windows(half).astype(BF16), embed_ref[...]).astype(BF16).astype(F32)
     flow = swin_band(tokens, wait, bias_ref, gain_ref, targets, scratch)
@@ -705,27 +731,38 @@
         corner_ref[...] = side_ref[...]
 
 
-def second_kernel(sigma, rows, *refs):
+def write_pieces(turn, refs, value):
+    for m, ref in enumerate(refs):
+
+        def write(ref=ref):
+            ref[...] = value
+
+        pl.when(turn == m)(write)
+
+
+def second_kernel(sigma, rows, parts, *refs):
     shift_ref, *refs = refs
     tile_refs, refs = refs[:4], refs[4:]
     bias_ref, unembed_ref, gain_ref, *sources = refs[:7]
     out_ref, side_ref, edge_ref, corner_ref, *scratch = refs[7:]
-    if sigma is not None:
-        state_ref, *scratch = scratch
+    state_refs, scratch = scratch[:parts], scratch[parts:]
     targets, sems, scratch = scratch[:4], scratch[4], scratch[5:]
     wait = load_weights(1, sources, targets, sems)
-    cols = out_ref.shape[1]
-    band = rolled_band(1, shift_ref, tile_refs, rows)
+    height, cols, _ = out_ref.shape
+    band = rolled_band(1, shift_ref, tile_refs, rows, height)
     tokens = to_windows(band[:, :, :D])
     flow = swin_band(tokens, wait, bias_ref, gain_ref, targets, scratch)
     estimate = from_windows(mm(flow.astype(BF16), unembed_ref[...]), cols)
     narrow = estimate.astype(BF16)
     out_ref[...] = narrow
-    edge_ref[...] = narrow
     side_ref[...] = narrow[:, cols - WIN :]
-    corner_ref[...] = narrow[:, cols - WIN :]
-    if sigma is not None:
-        state_ref[...] = (band[:, :, D:] - sigma * estimate).astype(BF16)
+    edge_ref[...] = narrow[height - WIN :]
+    corner_ref[...] = narrow[height - WIN :, cols - WIN :]
+    if parts > 0:
+        change = (band[:, :, D:] - sigma * estimate).astype(BF16)
+        for n in range(height // WIN):
+            turn = (pl.program_id(0) * (height // WIN) + n) ^ shift_ref[2]
+            write_pieces(turn, state_refs, change[n * WIN : (n + 1) * WIN])
 
 
 def whole(array):
@@ -733,35 +770,32 @@
     return pl.BlockSpec(array.shape, lambda *_: zeros)
 
 
-def band_of(step, cols):
-    return pl.BlockSpec((step, cols, PIXELS), lambda n, *_: (n, 0, 0))
-
-
 def member(array, j):
     place = (j,) + (0,) * (array.ndim - 1)
     return pl.BlockSpec((None,) + array.shape[1:], lambda *_: place)
 
 
-def band_spec(cols, feats):
-    return pl.BlockSpec((WIN, cols, feats), lambda n, *_: (n, 0, 0))
-
-
-def bias_spec(cols):
-    return pl.BlockSpec((cols // WIN, SPAN, 2 * SPAN), lambda n, *_: (n, 0, 0))
-
-
-def band_scratch(cols, weights):
-    count = cols // WIN
+def band_spec(cols, feats, height=WIN):
+    return pl.BlockSpec((height, cols, feats), lambda n, *_: (n, 0, 0))
+
+
+def bias_spec(cols, height=WIN):
+    count = height * cols // SPAN
+    return pl.BlockSpec((count, SPAN, 2 * SPAN), lambda n, *_: (n, 0, 0))
+
+
+def band_scratch(cols, weights, height=WIN):
+    count = height * cols // SPAN
     return [pltpu.VMEM(value.shape[1:], BF16) for value in weights] + [
         pltpu.SemaphoreType.DMA((len(weights),)),
-        pltpu.VMEM((WIN * cols, 3 * D), BF16),
+        pltpu.VMEM((height * cols, 3 * D), BF16),
         pltpu.VMEM((count, SPAN, HEADS * SPAN), F32),
         pltpu.VMEM((count, SPAN, HEADS * SPAN), BF16),
     ]
 
 
-def strip_outs(rows, cols, feats):
-    specs = [band_spec(cols, feats), band_spec(WIN, feats)]
+def strip_outs(rows, cols, feats, height=WIN):
+    specs = [band_spec(cols, feats, height), band_spec(WIN, feats, height)]
     specs += [
         pl.BlockSpec((WIN, width, feats), lambda *_: (0, 0, 0)) for width in (cols, WIN)
     ]
@@ -772,16 +806,19 @@
 def first_block(zeta, sigma, state, before, shift, back, grads, noise, bias, w_embed, weights):
     *weights, gains = weights
     rows, cols, _ = state.shape
-    fields = [*grads] + ([] if sigma is None else [noise])
+    parts = len(grads[0])
+    pieces = [piece for grad in grads for piece in grad]
+    fields = [] if sigma is None else [noise]
     feats = D if sigma is None else D + PIXELS
     specs, shapes = strip_outs(rows, cols, feats)
     return pl.pallas_call(
-        functools.partial(first_kernel, zeta, sigma, len(grads), rows, before),
+        functools.partial(first_kernel, zeta, sigma, len(grads), parts, rows, before),
         grid_spec=pltpu.PrefetchScalarGridSpec(
             num_scalar_prefetch=1,
             grid=(rows // WIN,),
             in_specs=[band_spec(cols, PIXELS)]
             + [whole(value) for value in back]
+            + [band_spec(cols, PIXELS) if parts == 1 else whole(value) for value in pieces]
             + [band_spec(cols, PIXELS)] * len(fields)
             + [bias_spec(cols), whole(w_embed), member(gains, 0)]
             + [pl.BlockSpec(memory_space=pl.ANY)] * len(weights),
@@ -790,26 +827,27 @@
         ),
         out_shape=[jax.ShapeDtypeStruct((rows, cols, PIXELS), F32)] + shapes,
         compiler_params=PARAMS,
-    )(shift, state, *back, *fields, bias, w_embed, gains, *weights)
-
-
-def second_block(sigma, shift, tile, bias, w_unembed, weights):
+    )(shift, state, *back, *pieces, *fields, bias, w_embed, gains, *weights)
+
+
+def second_block(sigma, shift, tile, bias, w_unembed, weights, parts):
     *weights, gains = weights
     rows, cols, _ = tile[0].shape
-    specs, shapes = strip_outs(rows, cols, PIXELS)
-    if sigma is not None:
-        specs, shapes = specs + specs[:1], shapes + shapes[:1]
+    height = 2 * WIN
+    specs, shapes = strip_outs(rows, cols, PIXELS, height)
+    specs += [pl.BlockSpec((WIN, cols, PIXELS), lambda *_: (0, 0, 0))] * parts
+    shapes += [jax.ShapeDtypeStruct((WIN, cols, PIXELS), BF16)] * parts
     return pl.pallas_call(
-        functools.partial(second_kernel, sigma, rows),
+        functools.partial(second_kernel, sigma, rows, parts),
         grid_spec=pltpu.PrefetchScalarGridSpec(
             num_scalar_prefetch=1,
-            grid=(rows // WIN,),
+            grid=(rows // height,),
             in_specs=[whole(value) for value in tile]
-            + [bias_spec(cols), whole(w_unembed), member(gains, 1)]
+            + [bias_spec(cols, height), whole(w_unembed), member(gains, 1)]
             + [pl.BlockSpec(memory_space=pl.ANY)] * len(weights),
             out_specs=specs,
-            scratch_shapes=band_scratch(cols, weights)
-            + [pltpu.VMEM((WIN * cols, weights[2].shape[2]), BF16)],
+            scratch_shapes=band_scratch(cols, weights, height)
+            + [pltpu.VMEM((height * cols, weights[2].shape[2]), BF16)],
         ),
         out_shape=shapes,
         compiler_params=PARAMS,
@@ -872,22 +910,29 @@
     return mm(high, matrix) + mm(low, matrix)
 
 
-def to_patches_kernel(tile_ref, order_ref, out_ref):
-    count, cols, _ = out_ref.shape
+def to_patches_kernel(narrow, place_ref, tile_ref, order_ref, *out_refs):
+    count, cols, _ = out_refs[0].shape
     parts = LANES // cols
     groups = PATCH // parts
-    if out_ref.dtype == BF16:
+    if narrow:
         ordered = mm(tile_ref[...].astype(BF16), order_ref[...])
     else:
         ordered = move_lanes(tile_ref[...], order_ref[...])
+    patches = []
     for i in range(count):
         band = ordered[i * PATCH : (i + 1) * PATCH]
         stacked = jnp.concatenate(
             [band[:, g * LANES : (g + 1) * LANES] for g in range(groups)], axis=0
         )
         turned = stacked.T
-        patch = jnp.concatenate([turned[h * cols : (h + 1) * cols] for h in range(parts)], axis=1)
-        out_ref[i] = patch.astype(out_ref.dtype)
+        patches.append(
+            jnp.concatenate([turned[h * cols : (h + 1) * cols] for h in range(parts)], axis=1)
+        )
+    result = jnp.stack(patches).astype(out_refs[0].dtype)
+    if len(out_refs) == 1:
+        out_refs[0][...] = result
+    else:
+        write_pieces(pl.program_id(0) ^ place_ref[2], out_refs, result)
 
 
 def to_tile_kernel(sigma, scale, rows, *refs):
@@ -911,21 +956,27 @@
     out_ref[...] = moved + scale * noise_ref[...]
 
 
-def patches_of(tiles, j, kind=F32):
+def patches_of(tiles, j, place, kind=F32, parts=1):
     rows, cols = tiles.shape[1] // PATCH, tiles.shape[2] // PATCH
     order = jnp.asarray(lane_order(cols)[0])
-    step = rows // 4
+    spec, shape = band_spec(cols, PIXELS), (rows, cols, PIXELS)
+    if parts > 1:
+        spec = pl.BlockSpec((WIN, cols, PIXELS), lambda *_: (0, 0, 0))
+        shape = (WIN, cols, PIXELS)
     return pl.pallas_call(
-        to_patches_kernel,
-        grid=(rows // step,),
-        in_specs=[
-            pl.BlockSpec((None, step * PATCH, cols * PATCH), lambda n: (j, n, 0)),
-            whole(order),
-        ],
-        out_specs=band_of(step, cols),
-        out_shape=jax.ShapeDtypeStruct((rows, cols, PIXELS), kind),
+        functools.partial(to_patches_kernel, kind == BF16),
+        grid_spec=pltpu.PrefetchScalarGridSpec(
+            num_scalar_prefetch=1,
+            grid=(rows // WIN,),
+            in_specs=[
+                pl.BlockSpec((None, WIN * PATCH, cols * PATCH), lambda n, *_: (j, n, 0)),
+                whole(order),
+            ],
+            out_specs=[spec] * parts,
+        ),
+        out_shape=[jax.ShapeDtypeStruct(shape, kind)] * parts,
         compiler_params=PARAMS,
-    )(tiles, order)
+    )(place, tiles, order)
 
 
 def tile_of(base, sigma, shift, back, scale, noise, j):
@@ -956,14 +1007,19 @@
     rows = image.shape[0] // PATCH
     cols = image.shape[1] // PATCH
     devices = lax.axis_size("ty") * lax.axis_size("tx")
-    fast = N // devices == TOK // 2
+    lanes = lax.axis_size("tx")
+    fast = N // devices == TOK // 2 and rows == lanes * WIN and lanes & (lanes - 1) == 0
+    places = [
+        jnp.concatenate([offsets[step], lax.axis_index("tx")[None]]).astype(jnp.int32)
+        for step in range(STEPS)
+    ]
     row_index = lax.axis_index("ty") * rows + counting(rows)
     col_index = lax.axis_index("tx") * cols + counting(cols)
     weights = (w_qkv, w_proj, w_up, w_down, norm_gains)
     w_embed = w_embed.reshape(PATCH, PATCH, D).transpose(1, 0, 2).reshape(PIXELS, D)
     w_unembed = w_unembed.reshape(D, PATCH, PATCH).transpose(0, 2, 1).reshape(D, PIXELS)
-    state = patches_of(image[None], 0)
-    extras = [patches_of(noise, step) for step in range(STEPS - 1)] + [None]
+    state = patches_of(image[None], 0, places[0])[0]
+    extras = [patches_of(noise, step, places[0])[0] for step in range(STEPS - 1)] + [None]
     first_bias = bias_of(None, key_mask)
     biases = []
     for step in range(STEPS):
@@ -973,20 +1029,26 @@
         )
         biases.append(bias_of(labels, None))
     beside = (state, extras, first_bias, biases, w_embed, w_unembed)
-    shift, before, back, moving, mirror = offsets[0], None, (), None, None
+    shift, before, back, moving, mirror = places[0], None, (), None, None
     grads = []
     if fast:
         weight, scale, data = spectrum_inputs(gains, observed, vis_weight, devices)
-        grad, beside = patch_gradient(
-            patches_of(image[None], 0, BF16), scale, data, None, None, beside
-        )
+        half = weight.shape[0] // 2
+        lines = (weight[half:], weight[:1])
+        grad, (beside, lines) = patch_gradient(
+            patches_of(image[None], 0, places[0], BF16, lanes), scale, data, None, None,
+            (beside, lines),
+        )
+        grad, lines = lax.optimization_barrier((grad, lines))
+        mirror = mirrored_exchange(*lines, devices)
         grads = [grad]
         state, extras, first_bias, biases, w_embed, w_unembed = beside
     for step in range(STEPS):
         if not fast:
             tile = image if step == 0 else tile_of(state, before, shift, back, 0.0, noise, 0)
             grad = plain_gradient(tile, gains, observed, vis_weight)
-            grads = [patches_of(grad.astype(F32)[None], 0, BF16)]
+            grad = patches_of(grad.astype(F32)[None], 0, places[0], BF16)[0]
+            grads = [[grad]]
         elif step > 0:
             grad, back = patch_gradient(moving, scale, None, shift, mirror, back)
             grads = grads + [grad]
@@ -996,18 +1058,14 @@
             STEP_SIZES[step], sigma, state, before, shift, back, grads, extras[step], first_bias,
             w_embed, weights,
         )
-        shift, before = offsets[step], SIGMAS[step]
-        first = from_neighbours(first, -1)
+        shift, before = places[step], SIGMAS[step]
         if fast and step == 0:
-            first, weight = lax.optimization_barrier((first, weight))
-            mirror = mirrored_exchange(weight)
+            first, mirror = lax.optimization_barrier((first, mirror))
         rolled = second_block(
-            None if last else before, shift, first, biases[step], w_unembed, weights
-        )
-        if not last:
-            *rolled, moving = rolled
-        if fast and step == 0:
-            moving, mirror = lax.optimization_barrier((moving, mirror))
+            before, shift, from_neighbours(first, -1), biases[step], w_unembed, weights,
+            lanes if fast and not last else 0,
+        )
+        rolled, moving = rolled[:4], rolled[4:]
         back = from_neighbours(rolled, 1)
     return tile_of(state, before, shift, back, SIGMAS[STEPS], noise, STEPS - 1)
 

time: 484 us -> 475 us (0.981)
  blocking collectives: 68.8 us -> 0 us
  waiting for transfers between devices: 98.5 us -> 137 us
  starting transfers between devices: 39.7 us -> 53.1 us
    all_to_all x3 -> x0, blocking collectives: 68.8 us -> none  [the longest x1 29.8 us: patch_gradient(): lax.all_to_all(wave, ('ty', 'tx'), split_axis=0, concat_axis=0, tiled=True)]
    ppermute x2 -> x14, waiting for transfers between devices: 0.01 us -> 40.4 us  [the longest x12 40.4 us: swap_pieces(): lax.ppermute(pieces[m], 'tx', [(k, k ^ m) for k in range(lanes)])]
    all_to_all x2 -> x0, waiting for transfers between devices: 25 us -> none  [the longest x1 13 us: patch_gradient(): grad = lax.all_to_all(slabs, 'tx', split_axis=0, concat_axis=0, tiled=True)]
    all_to_all x1 -> x2, waiting for transfers between devices: 19.1 us -> 43.7 us  [patch_gradient(): lax.all_to_all(wave, ('ty', 'tx'), split_axis=0, concat_axis=0, tiled=True)]
    ppermute x2 -> x14, starting transfers between devices: 3.71 us -> 16.7 us  [the longest x12 15.4 us: swap_pieces(): lax.ppermute(pieces[m], 'tx', [(k, k ^ m) for k in range(lanes)])]
    all_to_all x2 -> x0, starting transfers between devices: 8.39 us -> none  [the longest x1 4.56 us: patch_gradient(): lax.all_to_all(state.reshape(lanes, own, cols, PIXELS), 'tx', split_axis=...]
    unnamed x52 -> x96, local copies, waits for them, and re-layouts: 23.6 us -> 25 us
  transfers between devices with their start and end apart: 19 -> 30, of which waited for: 10 -> 18; matrix products, arithmetic and copies ran while one was open for 11% -> 12% of each run, Pallas kernels for 10% -> 10%
where the time goes in v3:
time: 475 us; the launch traced here: 466 us
  Pallas kernels  200 us (42%)
  waiting for transfers between devices  137 us (29%)
  starting transfers between devices  53.1 us (11%)
  local copies, waits for them, and re-layouts  50.7 us (11%)
  other arithmetic  19.9 us (4%)
  between operations  5.59 us (1%)
    pallas_call x2, Pallas kernels, first_block(): pl.pallas_call(functools.partial(first_kernel, zeta, sigma, len(grads), p...  57.4 us
    pallas_call x2, Pallas kernels, second_block(): pl.pallas_call(functools.partial(second_kernel, sigma, rows, parts), grid...  54.9 us
    all_to_all x2, waiting for transfers between devices, patch_gradient(): lax.all_to_all(wave, ('ty', 'tx'), split_axis=0, concat_axis=0, tiled=True)  43.7 us
    ppermute x12, waiting for transfers between devices, swap_pieces(): lax.ppermute(pieces[m], 'tx', [(k, k ^ m) for k in range(lanes)])  40.4 us
    ppermute x4, waiting for transfers between devices, from_neighbours(): lax.ppermute(corner, ('ty', 'tx'), across)  33.1 us
    pallas_call x2, Pallas kernels, patch_gradient(): pl.pallas_call(functools.partial(column_kernel, halved), in_specs=[pl.Blo...  27 us
    unnamed x96, local copies, waits for them, and re-layouts  25 us
    pallas_call x3, Pallas kernels, patches_of(): pl.pallas_call(functools.partial(to_patches_kernel, kind == BF16), grid_s...  21 us
  transfers between devices with their start and end apart: 30, of which 18 were waited for; matrix products, arithmetic and copies ran while one was open for 12% of the time, Pallas kernels for 10%

profile of v3, /device:TPU:0, one launch (start us, length us, event | category | flops | bytes accessed | tf_op | source)
XLA Modules:
  0.0 466.1 jit_solution(1303435620427147811)
XLA Ops:
  2.0 6.4 %shard_map.298 = (bf16[8,64,256]{2,1,0:T(8,128)(2,1)}, bf16[8,64,256]{2,1,0:T(8,128)(2,1)}, bf16[8,64,256]{2,1,0:T(8,128)(2,1)}, bf16[8,64,256]{2,1,0:T(8,128)(2,1)}) custom-call(s32[3]{0:T(128)} %pad_add_fusion.1.place_ref.refs_0_, f32[1,512,1024]{2,1,0:T(8,128)} %bitcast.67, bf16[1024,1024]{1,0:T(8,128)(2,1)} %constant.98.clone.order_ref), custom_call_target="tpu_custom_call" | custom-call | tf_op jit(solution)/shard_map/pallas_call | solution.py:966
  18.7 6.3 %collective-permute-done.1.refs_2_ = bf16[8,64,256]{2,1,0:T(8,128)(2,1)S(1)} collective-permute-done((bf16[8,64,256]{2,1,0:T(8,128)(2,1)}, bf16[8,64,256]{2,1,0:T(8,128)(2,1)S(1)}, u32[]{:S(2)}, u32[]{:S(2)}) %collective-permute-start.1) | collective-permute-done | bytes 262176 | tf_op jit(solution)/shard_map/ppermute | solution.py:471
  25.7 5.8 %shard_map.299 = bf16[16,2,2,128,128]{4,3,2,1,0:T(8,128)(2,1)} custom-call(bf16[8,64,256]{2,1,0:T(8,128)(2,1)} %get-tuple-element.70.refs_0_, bf16[8,64,256]{2,1,0:T(8,128)(2,1)} %copy-done.13, bf16[8,64,256]{2,1,0:T(8,128)(2,1)} %copy-done.14, bf16[8,64,256]{2,1,0:T(8,128)(2,1)} %copy-done.15, bf16[256,512]{1,0:T(8,128)(2,1)} %pad_maximum_fusion.5.refs_4_.first_ref, ...), custom_call_target="tpu_custom_call" | custom-call | tf_op jit(solution)/shard_map/pallas_call | solution.py:507
  31.5 4.9 %all-to-all-start = ((bf16[32,2,128,128]{3,2,1,0:T(8,128)(2,1)}), bf16[32,2,128,128]{3,2,1,0:T(8,128)(2,1)S(1)}, u32[]{:S(2)}, u32[]{:S(2)}) async-start(bf16[32,2,128,128]{3,2,1,0:T(8,128)(2,1)} %bitcast.70), calls=%async_computation | async-start | bytes 4194304 | tf_op jit(solution)/shard_map/all_to_all | solution.py:514
  47.0 4.8 %fusion.17 = (f32[1,128,4096]{2,1,0:T(8,128)}, f32[1,128,4096]{2,1,0:T(8,128)}) fusion(f32[2,128,4096]{2,1,0:T(8,128)} %param.37), kind=kLoop, calls=%fused_computation.76 | loop fusion | bytes 8388608 | tf_op jit(solution)/shard_map/slice | solution.py:412
  60.5 5.1 %fusion.1 = (bf16[128,4096]{0,1:T(8,128)(2,1)S(1)}, bf16[128,4096]{0,1:T(8,128)(2,1)S(1)}, bf16[128,4096]{0,1:T(8,128)(2,1)S(1)}) fusion(f32[128,4096]{0,1:T(8,128)} %copy.72, f32[1,128,4096]{1,2,0:T(8,128)} %copy.92, f32[1,128,4096]{1,2,0:T(8,128)} %copy.94, f32[1,128,4096]{1,2,0:T(8,128)} %copy.91, f32[1,128,4096]{1,2,0:T(8,128)} %copy.93), kind=kLoop, calls=%fused_computation.4 | loop fusion | flops 7864320 | bytes 13631488 | tf_op jit(solution)/shard_map/convert_element_type | solution.py:404
  69.3 15.9 %all-to-all-done.refs_0_ = bf16[32,2,128,128]{3,2,1,0:T(8,128)(2,1)S(1)} async-done(((bf16[32,2,128,128]{3,2,1,0:T(8,128)(2,1)}), bf16[32,2,128,128]{3,2,1,0:T(8,128)(2,1)S(1)}, u32[]{:S(2)}, u32[]{:S(2)}) %all-to-all-start) | async-done | bytes 2097184 | tf_op jit(solution)/shard_map/all_to_all | solution.py:514
  86.5 14.3 %shard_map.300 = bf16[32,2,128,128]{3,2,1,0:T(8,128)(2,1)} custom-call(bf16[32,2,128,128]{3,2,1,0:T(8,128)(2,1)} %copy-done, bf16[1024,1024]{1,0:T(8,128)(2,1)} %constant.99.clone.refs_1_.refs_3_, bf16[32,256,256]{2,1,0:T(8,128)(2,1)} %constant.101.clone.refs_2_.refs_4_, bf16[32,128,128]{2,1,0:T(8,128)(2,1)} %bitcast.65, ...), custom_call_target="tpu_custom_call" | custom-call | tf_op jit(solution)/shard_map/pallas_call | solution.py:520
  105.4 7.2 %shard_map.301.refs_1_ = f32[32,64,256]{2,1,0:T(8,128)} custom-call(s32[3]{0:T(128)} %pad_add_fusion.1.place_ref.refs_0_, f32[1,512,1024]{2,1,0:T(8,128)} %bitcast.68, bf16[1024,1024]{1,0:T(8,128)(2,1)} %constant.98.clone.order_ref), custom_call_target="tpu_custom_call" | custom-call | tf_op jit(solution)/shard_map/pallas_call | solution.py:966
  113.9 7.4 %shard_map.302.refs_6_ = f32[32,64,256]{2,1,0:T(8,128)} custom-call(s32[3]{0:T(128)} %pad_add_fusion.1.place_ref.refs_0_, f32[2,512,1024]{2,1,0:T(8,128)} %refs_6_.4, bf16[1024,1024]{1,0:T(8,128)(2,1)} %constant.98.clone.order_ref), custom_call_target="tpu_custom_call" | custom-call | tf_op jit(solution)/shard_map/pallas_call | solution.py:966
  136.0 18.0 %all-to-all-done.1 = bf16[32,2,128,128]{3,2,1,0:T(8,128)(2,1)S(1)} async-done(((bf16[32,2,128,128]{3,2,1,0:T(8,128)(2,1)}), bf16[32,2,128,128]{3,2,1,0:T(8,128)(2,1)S(1)}, u32[]{:S(2)}, u32[]{:S(2)}) %all-to-all-start.1) | async-done | bytes 2097184 | tf_op jit(solution)/shard_map/all_to_all | solution.py:529
  155.4 7.4 %shard_map.303 = (bf16[8,64,256]{2,1,0:T(8,128)(2,1)}, bf16[8,64,256]{2,1,0:T(8,128)(2,1)}, bf16[8,64,256]{2,1,0:T(8,128)(2,1)}, bf16[8,64,256]{2,1,0:T(8,128)(2,1)}) custom-call(bf16[16,2,2,128,128]{4,3,2,1,0:T(8,128)(2,1)} %bitcast.69, bf16[256,512]{1,0:T(8,128)(2,1)} %pad_maximum_fusion.5.refs_4_.first_ref, ...), custom_call_target="tpu_custom_call" | custom-call | tf_op jit(solution)/shard_map/pallas_call | solution.py:532
  166.2 5.9 %collective-permute-done.3.refs_3_.refs_7_ = bf16[8,64,256]{2,1,0:T(8,128)(2,1)S(1)} collective-permute-done((bf16[8,64,256]{2,1,0:T(8,128)(2,1)}, bf16[8,64,256]{2,1,0:T(8,128)(2,1)S(1)}, u32[]{:S(2)}, u32[]{:S(2)}) %collective-permute-start.3) | collective-permute-done | bytes 262176 | tf_op jit(solution)/shard_map/ppermute | solution.py:471
  172.2 5.5 %collective-permute-done.4.refs_4_.refs_8_ = bf16[8,64,256]{2,1,0:T(8,128)(2,1)S(1)} collective-permute-done((bf16[8,64,256]{2,1,0:T(8,128)(2,1)}, bf16[8,64,256]{2,1,0:T(8,128)(2,1)S(1)}, u32[]{:S(2)}, u32[]{:S(2)}) %collective-permute-start.4) | collective-permute-done | bytes 262176 | tf_op jit(solution)/shard_map/ppermute | solution.py:471
  181.2 28.3 %shard_map.304 = (f32[32,64,256]{2,1,0:T(8,128)}, bf16[32,64,768]{2,1,0:T(8,128)(2,1)}, bf16[32,8,768]{2,1,0:T(8,128)(2,1)}, bf16[8,64,768]{2,1,0:T(8,128)(2,1)}, bf16[8,8,768]{2,1,0:T(8,128)(2,1)}) custom-call(s32[3]{0:T(128)} %pad_add_fusion.1.place_ref.refs_0_, f32[32,64,256]{2,1,0:T(8,128)} %shard_map.301.refs_1_, ...), custom_call_target="tpu_custom_call" | custom-call | tf_op jit(solution)/shard_map/pallas_call | solution.py:814
  209.5 5.2 %collective-permute-start.9 = (bf16[8,64,768]{2,1,0:T(8,128)(2,1)}, bf16[8,64,768]{2,1,0:T(8,128)(2,1)S(1)}, u32[]{:S(2)}, u32[]{:S(2)}) collective-permute-start(bf16[8,64,768]{2,1,0:T(8,128)(2,1)} %get-tuple-element.98), channel_id=1, source_target_pairs={{0,28},{4,0},{8,4},{12,8},{16,12},{20,16},{24,20},{28,24},{1,29},{... | collective-permute-start | bytes 2359304 | tf_op jit(solution)/shard_map/ppermute | solution.py:866
  218.4 7.2 %collective-permute-done.10.refs_4_ = bf16[8,8,768]{2,1,0:T(8,128)(2,1)S(1)} collective-permute-done((bf16[8,8,768]{2,1,0:T(8,128)(2,1)}, bf16[8,8,768]{2,1,0:T(8,128)(2,1)S(1)}, u32[]{:S(2)}, u32[]{:S(2)}) %collective-permute-start.10) | collective-permute-done | bytes 98336 | tf_op jit(solution)/shard_map/ppermute | solution.py:867
  228.2 28.2 %shard_map.305 = (bf16[32,64,256]{2,1,0:T(8,128)(2,1)}, bf16[32,8,256]{2,1,0:T(8,128)(2,1)}, bf16[8,64,256]{2,1,0:T(8,128)(2,1)}, bf16[8,8,256]{2,1,0:T(8,128)(2...) custom-call(s32[3]{0:T(128)} %pad_add_fusion.1.place_ref.refs_0_, ...), custom_call_target="tpu_custom_call" | custom-call | tf_op jit(solution)/shard_map/pallas_call | solution.py:840
  261.1 5.2 %collective-permute-done.11.refs_1_ = bf16[8,64,256]{2,1,0:T(8,128)(2,1)S(1)} collective-permute-done((bf16[8,64,256]{2,1,0:T(8,128)(2,1)}, bf16[8,64,256]{2,1,0:T(8,128)(2,1)S(1)}, u32[]{:S(2)}, u32[]{:S(2)}) %collective-permute-start.11) | collective-permute-done | bytes 262176 | tf_op jit(solution)/shard_map/ppermute | solution.py:471
  271.8 6.1 %shard_map.306 = bf16[16,2,128,128]{3,2,1,0:T(8,128)(2,1)} custom-call(bf16[8,64,256]{2,1,0:T(8,128)(2,1)} %get-tuple-element.102.refs_0_, bf16[8,64,256]{2,1,0:T(8,128)(2,1)} %copy-done.26, bf16[8,64,256]{2,1,0:T(8,128)(2,1)} %copy-done.27, bf16[8,64,256]{2,1,0:T(8,128)(2,1)} %copy-done.28, bf16[256,512]{1,0:T(8,128)(2,1)} %pad_maximum_fusion.6.refs_4_, ...), custom_call_target="tpu_custom_call" | custom-call | tf_op jit(solution)/shard_map/pallas_call | solution.py:507
  277.9 5.2 %all-to-all-start.2 = ((bf16[32,128,128]{2,1,0:T(8,128)(2,1)}), bf16[32,128,128]{2,1,0:T(8,128)(2,1)S(1)}, u32[]{:S(2)}, u32[]{:S(2)}) async-start(bf16[32,128,128]{2,1,0:T(8,128)(2,1)} %bitcast.73), calls=%async_computation.2 | async-start | bytes 2097152 | tf_op jit(solution)/shard_map/all_to_all | solution.py:514
  292.5 5.5 %shard_map.307.refs_5_ = bf16[32,128,128]{2,1,0:T(8,128)(2,1)} custom-call(bf16[32,128,128]{2,1,0:T(8,128)(2,1)} %bitcast.66, bf16[32,128,128]{2,1,0:T(8,128)(2,1)} %bitcast.72, bf16[2,128,128]{2,1,0:T(8,128)(2,1)} %add_convert_fusion.pick_ref, bf16[2,128,128]{2,1,0:T(8,128)(2,1)} %constant.113.clone.flip_ref), custom_call_target="tpu_custom_call" | custom-call | tf_op jit(solution)/shard_map/pallas_call | solution.py:452
  297.9 11.9 %collective-permute-done.16.refs_5_ = bf16[8,8,256]{2,1,0:T(8,128)(2,1)} collective-permute-done((bf16[8,8,256]{2,1,0:T(8,128)(2,1)}, bf16[8,8,256]{2,1,0:T(8,128)(2,1)}, u32[]{:S(2)}, u32[]{:S(2)}) %collective-permute-start.16) | collective-permute-done | bytes 32800 | tf_op jit(solution)/shard_map/ppermute | solution.py:867
  313.8 12.7 %shard_map.308 = bf16[32,128,128]{2,1,0:T(8,128)(2,1)} custom-call(s32[1]{0:T(128)} %bitcast.29.refs_0_, f32[32,2,8,128]{3,2,1,0:T(8,128)} %broadcast_in_dim.80.refs_1_, bf16[32,128,128]{2,1,0:T(8,128)(2,1)} %copy-done.2, bf16[1024,1024]{1,0:T(8,128)(2,1)} %constant.99.clone.refs_1_.refs_3_, bf16[32,256,256]{2,1,0:T(8,128)(2,1)} %constant.101.clone.refs_2_.refs_4_, ...), custom_call_target="tpu_custom_call" | custom-call | tf_op jit(solution)/shard_map/pallas_call | solution.py:520
  330.1 25.7 %all-to-all-done.3 = bf16[32,128,128]{2,1,0:T(8,128)(2,1)S(1)} async-done(((bf16[32,128,128]{2,1,0:T(8,128)(2,1)}), bf16[32,128,128]{2,1,0:T(8,128)(2,1)S(1)}, u32[]{:S(2)}, u32[]{:S(2)}) %all-to-all-start.3) | async-done | bytes 1048608 | tf_op jit(solution)/shard_map/all_to_all | solution.py:529
  356.7 6.4 %shard_map.309 = (bf16[8,64,256]{2,1,0:T(8,128)(2,1)}, bf16[8,64,256]{2,1,0:T(8,128)(2,1)}, bf16[8,64,256]{2,1,0:T(8,128)(2,1)}, bf16[8,64,256]{2,1,0:T(8,128)(2,1)}) custom-call(bf16[16,2,128,128]{3,2,1,0:T(8,128)(2,1)} %bitcast.74, bf16[256,512]{1,0:T(8,128)(2,1)} %pad_maximum_fusion.7.first_ref, f32[2,256,256]{2,1,0:T(8,128)} %constant.107.clone.refs_5_.twist_ref, ...), custom_call_target="tpu_custom_call" | custom-call | tf_op jit(solution)/shard_map/pallas_call | solution.py:532
  366.7 5.9 %collective-permute-done.17.refs_11_ = bf16[8,64,256]{2,1,0:T(8,128)(2,1)S(1)} collective-permute-done((bf16[8,64,256]{2,1,0:T(8,128)(2,1)}, bf16[8,64,256]{2,1,0:T(8,128)(2,1)S(1)}, u32[]{:S(2)}, u32[]{:S(2)}) %collective-permute-start.17) | collective-permute-done | bytes 262176 | tf_op jit(solution)/shard_map/ppermute | solution.py:471
  379.0 29.1 %shard_map.310 = (f32[32,64,256]{2,1,0:T(8,128)}, bf16[32,64,512]{2,1,0:T(8,128)(2,1)}, bf16[32,8,512]{2,1,0:T(8,128)(2,1)}, bf16[8,64,512]{2,1,0:T(8,128)(2,1)}, bf16[8,8,512]{2,1,0:T(8,128)(2,1)}) custom-call(s32[3]{0:T(128)} %pad_add_fusion.1.place_ref.refs_0_, f32[32,64,256]{2,1,0:T(8,128)} %get-tuple-element.89.refs_1_, ...), custom_call_target="tpu_custom_call" | custom-call | tf_op jit(solution)/shard_map/pallas_call | solution.py:814
  412.7 5.9 %collective-permute-done.22.refs_4_ = bf16[8,8,512]{2,1,0:T(8,128)(2,1)S(1)} collective-permute-done((bf16[8,8,512]{2,1,0:T(8,128)(2,1)}, bf16[8,8,512]{2,1,0:T(8,128)(2,1)S(1)}, u32[]{:S(2)}, u32[]{:S(2)}) %collective-permute-start.22) | collective-permute-done | bytes 65568 | tf_op jit(solution)/shard_map/ppermute | solution.py:867
  419.5 26.7 %shard_map.311 = (bf16[32,64,256]{2,1,0:T(8,128)(2,1)}, bf16[32,8,256]{2,1,0:T(8,128)(2,1)}, bf16[8,64,256]{2,1,0:T(8,128)(2,1)}, bf16[8,8,256]{2,1,0:T(8,128)(2,1)}) custom-call(s32[3]{0:T(128)} %pad_add_fusion.refs_0_, bf16[32,64,512]{2,1,0:T(8,128)(2,1)} %get-tuple-element.126.refs_1_, bf16[32,8,512]{2,1,0:T(8,128)(2,1)} %copy-done.12, ...), custom_call_target="tpu_custom_call" | custom-call | tf_op jit(solution)/shard_map/pallas_call | solution.py:840
  448.5 8.1 %collective-permute-done.25.refs_5_ = bf16[8,8,256]{2,1,0:T(8,128)(2,1)S(1)} collective-permute-done((bf16[8,8,256]{2,1,0:T(8,128)(2,1)}, bf16[8,8,256]{2,1,0:T(8,128)(2,1)S(1)}, u32[]{:S(2)}, u32[]{:S(2)}) %collective-permute-start.25) | collective-permute-done | bytes 32800 | tf_op jit(solution)/shard_map/ppermute | solution.py:867
  457.4 8.5 %shard_map.312 = f32[512,1024]{1,0:T(8,128)} custom-call(s32[3]{0:T(128)} %pad_add_fusion.refs_0_, f32[32,64,256]{2,1,0:T(8,128)} %get-tuple-element.125.refs_1_, bf16[32,64,256]{2,1,0:T(8,128)(2,1)} %get-tuple-element.131.refs_2_, bf16[32,8,256]{2,1,0:T(8,128)(2,1)} %copy-done.36, bf16[8,64,256]{2,1,0:T(8,128)(2,1)} %copy-done.16, ...), custom_call_target="tpu_custom_call" | custom-call | tf_op jit(solution)/shard_map/pallas_call | solution.py:985
  (191 shorter events, 114.0 us)
Async XLA Ops:
  8.4 10.3 %collective-permute-start = (bf16[8,64,256]{2,1,0:T(8,128)(2,1)}, bf16[8,64,256]{2,1,0:T(8,128)(2,1)S(1)}, u32[]{:S(2)}, u32[]{:S(2)}) collective-permute-start(bf16[8,64,256]{2,1,0:T(8,128)(2,1)} %get-tuple-element.71), channel_id=1, source_target_pairs={{0,1},{1,0},{2,3},{3,2},{4,5},{5,4},{6,7},{7,6},{8,9},{9,8},{10,11... | collective-permute-start | bytes 786440 | tf_op jit(solution)/shard_map/ppermute | solution.py:471
  11.3 13.6 %collective-permute-start.1 = (bf16[8,64,256]{2,1,0:T(8,128)(2,1)}, bf16[8,64,256]{2,1,0:T(8,128)(2,1)S(1)}, u32[]{:S(2)}, u32[]{:S(2)}) collective-permute-start(bf16[8,64,256]{2,1,0:T(8,128)(2,1)} %get-tuple-element.72), channel_id=1, source_target_pairs={{0,2},{1,3},{2,0},{3,1},{4,6},{5,7},{6,4},{7,5},{8,10},{9,11},{10,... | collective-permute-start | bytes 786440 | tf_op jit(solution)/shard_map/ppermute | solution.py:471
  12.8 12.1 %collective-permute-start.2 = (bf16[8,64,256]{2,1,0:T(8,128)(2,1)}, bf16[8,64,256]{2,1,0:T(8,128)(2,1)S(1)}, u32[]{:S(2)}, u32[]{:S(2)}) collective-permute-start(bf16[8,64,256]{2,1,0:T(8,128)(2,1)} %get-tuple-element.73), channel_id=1, source_target_pairs={{0,3},{1,2},{2,1},{3,0},{4,7},{5,6},{6,5},{7,4},{8,11},{9,10},{10,... | collective-permute-start | bytes 786440 | tf_op jit(solution)/shard_map/ppermute | solution.py:471
  31.5 53.6 %all-to-all-start = ((bf16[32,2,128,128]{3,2,1,0:T(8,128)(2,1)}), bf16[32,2,128,128]{3,2,1,0:T(8,128)(2,1)S(1)}, u32[]{:S(2)}, u32[]{:S(2)}) async-start(bf16[32,2,128,128]{3,2,1,0:T(8,128)(2,1)} %bitcast.70), calls=%async_computation | async-start | bytes 4194304 | tf_op jit(solution)/shard_map/all_to_all | solution.py:514
  100.8 53.3 %all-to-all-start.1 = ((bf16[32,2,128,128]{3,2,1,0:T(8,128)(2,1)}), bf16[32,2,128,128]{3,2,1,0:T(8,128)(2,1)S(1)}, u32[]{:S(2)}, u32[]{:S(2)}) async-start(bf16[32,2,128,128]{3,2,1,0:T(8,128)(2,1)} %shard_map.300), calls=%async_computation.1 | async-start | bytes 4194304 | tf_op jit(solution)/shard_map/all_to_all | solution.py:529
  162.7 9.4 %collective-permute-start.3 = (bf16[8,64,256]{2,1,0:T(8,128)(2,1)}, bf16[8,64,256]{2,1,0:T(8,128)(2,1)S(1)}, u32[]{:S(2)}, u32[]{:S(2)}) collective-permute-start(bf16[8,64,256]{2,1,0:T(8,128)(2,1)} %get-tuple-element.77), channel_id=1, source_target_pairs={{0,1},{1,0},{2,3},{3,2},{4,5},{5,4},{6,7},{7,6},{8,9},{9,8},{10,11... | collective-permute-start | bytes 786440 | tf_op jit(solution)/shard_map/ppermute | solution.py:471
  164.2 13.4 %collective-permute-start.4 = (bf16[8,64,256]{2,1,0:T(8,128)(2,1)}, bf16[8,64,256]{2,1,0:T(8,128)(2,1)S(1)}, u32[]{:S(2)}, u32[]{:S(2)}) collective-permute-start(bf16[8,64,256]{2,1,0:T(8,128)(2,1)} %get-tuple-element.78), channel_id=1, source_target_pairs={{0,2},{1,3},{2,0},{3,1},{4,6},{5,7},{6,4},{7,5},{8,10},{9,11},{10,... | collective-permute-start | bytes 786440 | tf_op jit(solution)/shard_map/ppermute | solution.py:471
  165.7 11.9 %collective-permute-start.5 = (bf16[8,64,256]{2,1,0:T(8,128)(2,1)}, bf16[8,64,256]{2,1,0:T(8,128)(2,1)S(1)}, u32[]{:S(2)}, u32[]{:S(2)}) collective-permute-start(bf16[8,64,256]{2,1,0:T(8,128)(2,1)} %get-tuple-element.79), channel_id=1, source_target_pairs={{0,3},{1,2},{2,1},{3,0},{4,7},{5,6},{6,5},{7,4},{8,11},{9,10},{10,... | collective-permute-start | bytes 786440 | tf_op jit(solution)/shard_map/ppermute | solution.py:471
  179.4 30.1 %collective-permute-start.6 = (bf16[64,4096]{1,0:T(8,128)(2,1)S(1)}, bf16[64,4096]{1,0:T(8,128)(2,1)S(1)}, u32[]{:S(2)}, u32[]{:S(2)}) collective-permute-start(bf16[64,4096]{1,0:T(8,128)(2,1)S(1)} %copy.84), channel_id=1, source_target_pairs={{0,31},{1,30},{2,29},{3,28},{4,27},{5,26},{6,25},{7,24},{8,23},{9,... | collective-permute-start | bytes 1572872 | tf_op jit(solution)/shard_map/ppermute | solution.py:432
  181.1 28.4 %collective-permute-start.7 = (bf16[1,4096]{1,0:T(2,128)(2,1)S(1)}, bf16[1,4096]{1,0:T(2,128)(2,1)S(1)}, u32[]{:S(2)}, u32[]{:S(2)}) collective-permute-start(bf16[1,4096]{1,0:T(2,128)(2,1)S(1)} %copy.85), channel_id=1, source_target_pairs={{1,31},{2,30},{3,29},{4,28},{5,27},{6,26},{7,25},{8,24},{9,23},{10... | collective-permute-start | bytes 24584 | tf_op jit(solution)/shard_map/ppermute | solution.py:433
  209.5 17.1 %collective-permute-start.9 = (bf16[8,64,768]{2,1,0:T(8,128)(2,1)}, bf16[8,64,768]{2,1,0:T(8,128)(2,1)S(1)}, u32[]{:S(2)}, u32[]{:S(2)}) collective-permute-start(bf16[8,64,768]{2,1,0:T(8,128)(2,1)} %get-tuple-element.98), channel_id=1, source_target_pairs={{0,28},{4,0},{8,4},{12,8},{16,12},{20,16},{24,20},{28,24},{1,29},{... | collective-permute-start | bytes 2359304 | tf_op jit(solution)/shard_map/ppermute | solution.py:866
  214.7 11.9 %collective-permute-start.8 = (bf16[32,8,768]{2,1,0:T(8,128)(2,1)}, bf16[32,8,768]{2,1,0:T(8,128)(2,1)S(1)}, u32[]{:S(2)}, u32[]{:S(2)}) collective-permute-start(bf16[32,8,768]{2,1,0:T(8,128)(2,1)} %get-tuple-element.97), channel_id=1, source_target_pairs={{0,3},{1,0},{2,1},{3,2},{4,7},{5,4},{6,5},{7,6},{8,11},{9,8},{10,9... | collective-permute-start | bytes 1179656 | tf_op jit(solution)/shard_map/ppermute | solution.py:865
  216.1 9.5 %collective-permute-start.10 = (bf16[8,8,768]{2,1,0:T(8,128)(2,1)}, bf16[8,8,768]{2,1,0:T(8,128)(2,1)S(1)}, u32[]{:S(2)}, u32[]{:S(2)}) collective-permute-start(bf16[8,8,768]{2,1,0:T(8,128)(2,1)} %get-tuple-element.99), channel_id=1, source_target_pairs={{0,31},{1,28},{2,29},{3,30},{4,3},{5,0},{6,1},{7,2},{8,7},{9,4},{1... | collective-permute-start | bytes 294920 | tf_op jit(solution)/shard_map/ppermute | solution.py:867
  218.4 42.0 %copy-start.24 = (bf16[64,512]{1,0:T(8,128)(2,1)S(1)}, bf16[64,512]{1,0:T(8,128)(2,1)}, u32[]{:S(2)}) copy-start(bf16[64,512]{1,0:T(8,128)(2,1)} %get-tuple-element.146) | copy-start | bytes 196612
  218.4 42.0 %copy-start.25 = (bf16[64,512]{1,0:T(8,128)(2,1)S(1)}, bf16[64,512]{1,0:T(8,128)(2,1)}, u32[]{:S(2)}) copy-start(bf16[64,512]{1,0:T(8,128)(2,1)} %get-tuple-element.147) | copy-start | bytes 196612
  256.4 9.9 %collective-permute-start.11 = (bf16[8,64,256]{2,1,0:T(8,128)(2,1)}, bf16[8,64,256]{2,1,0:T(8,128)(2,1)S(1)}, u32[]{:S(2)}, u32[]{:S(2)}) collective-permute-start(bf16[8,64,256]{2,1,0:T(8,128)(2,1)} %get-tuple-element.103), channel_id=1, source_target_pairs={{0,1},{1,0},{2,3},{3,2},{4,5},{5,4},{6,7},{7,6},{8,9},{9,8},{10,11... | collective-permute-start | bytes 786440 | tf_op jit(solution)/shard_map/ppermute | solution.py:471
  258.9 12.1 %collective-permute-start.12 = (bf16[8,64,256]{2,1,0:T(8,128)(2,1)}, bf16[8,64,256]{2,1,0:T(8,128)(2,1)S(1)}, u32[]{:S(2)}, u32[]{:S(2)}) collective-permute-start(bf16[8,64,256]{2,1,0:T(8,128)(2,1)} %get-tuple-element.104), channel_id=1, source_target_pairs={{0,2},{1,3},{2,0},{3,1},{4,6},{5,7},{6,4},{7,5},{8,10},{9,11},{10,... | collective-permute-start | bytes 786440 | tf_op jit(solution)/shard_map/ppermute | solution.py:471
  260.3 10.6 %collective-permute-start.13 = (bf16[8,64,256]{2,1,0:T(8,128)(2,1)}, bf16[8,64,256]{2,1,0:T(8,128)(2,1)S(1)}, u32[]{:S(2)}, u32[]{:S(2)}) collective-permute-start(bf16[8,64,256]{2,1,0:T(8,128)(2,1)} %get-tuple-element.105), channel_id=1, source_target_pairs={{0,3},{1,2},{2,1},{3,0},{4,7},{5,6},{6,5},{7,4},{8,11},{9,10},{10,... | collective-permute-start | bytes 786440 | tf_op jit(solution)/shard_map/ppermute | solution.py:471
  277.9 34.8 %all-to-all-start.2 = ((bf16[32,128,128]{2,1,0:T(8,128)(2,1)}), bf16[32,128,128]{2,1,0:T(8,128)(2,1)S(1)}, u32[]{:S(2)}, u32[]{:S(2)}) async-start(bf16[32,128,128]{2,1,0:T(8,128)(2,1)} %bitcast.73), calls=%async_computation.2 | async-start | bytes 2097152 | tf_op jit(solution)/shard_map/all_to_all | solution.py:514
  284.5 25.4 %collective-permute-start.14 = (bf16[32,8,256]{2,1,0:T(8,128)(2,1)}, bf16[32,8,256]{2,1,0:T(8,128)(2,1)S(1)}, u32[]{:S(2)}, u32[]{:S(2)}) collective-permute-start(bf16[32,8,256]{2,1,0:T(8,128)(2,1)} %get-tuple-element.110), channel_id=1, source_target_pairs={{0,1},{1,2},{2,3},{3,0},{4,5},{5,6},{6,7},{7,4},{8,9},{9,10},{10,1... | collective-permute-start | bytes 393224 | tf_op jit(solution)/shard_map/ppermute | solution.py:865
  286.4 23.5 %collective-permute-start.15 = (bf16[8,64,256]{2,1,0:T(8,128)(2,1)}, bf16[8,64,256]{2,1,0:T(8,128)(2,1)S(1)}, u32[]{:S(2)}, u32[]{:S(2)}) collective-permute-start(bf16[8,64,256]{2,1,0:T(8,128)(2,1)} %get-tuple-element.111), channel_id=1, source_target_pairs={{0,4},{4,8},{8,12},{12,16},{16,20},{20,24},{24,28},{28,0},{1,5},{5... | collective-permute-start | bytes 786440 | tf_op jit(solution)/shard_map/ppermute | solution.py:866
  286.4 23.5 %collective-permute-start.16 = (bf16[8,8,256]{2,1,0:T(8,128)(2,1)}, bf16[8,8,256]{2,1,0:T(8,128)(2,1)}, u32[]{:S(2)}, u32[]{:S(2)}) collective-permute-start(bf16[8,8,256]{2,1,0:T(8,128)(2,1)} %get-tuple-element.112), channel_id=1, source_target_pairs={{0,5},{1,6},{2,7},{3,4},{4,9},{5,10},{6,11},{7,8},{8,13},{9,14},{1... | collective-permute-start | bytes 98312 | tf_op jit(solution)/shard_map/ppermute | solution.py:867
  326.5 29.2 %all-to-all-start.3 = ((bf16[32,128,128]{2,1,0:T(8,128)(2,1)}), bf16[32,128,128]{2,1,0:T(8,128)(2,1)S(1)}, u32[]{:S(2)}, u32[]{:S(2)}) async-start(bf16[32,128,128]{2,1,0:T(8,128)(2,1)} %shard_map.308), calls=%async_computation.3 | async-start | bytes 2097152 | tf_op jit(solution)/shard_map/all_to_all | solution.py:529
  363.2 9.4 %collective-permute-start.17 = (bf16[8,64,256]{2,1,0:T(8,128)(2,1)}, bf16[8,64,256]{2,1,0:T(8,128)(2,1)S(1)}, u32[]{:S(2)}, u32[]{:S(2)}) collective-permute-start(bf16[8,64,256]{2,1,0:T(8,128)(2,1)} %get-tuple-element.122), channel_id=1, source_target_pairs={{0,1},{1,0},{2,3},{3,2},{4,5},{5,4},{6,7},{7,6},{8,9},{9,8},{10,11... | collective-permute-start | bytes 786440 | tf_op jit(solution)/shard_map/ppermute | solution.py:471
  364.5 12.3 %collective-permute-start.18 = (bf16[8,64,256]{2,1,0:T(8,128)(2,1)}, bf16[8,64,256]{2,1,0:T(8,128)(2,1)S(1)}, u32[]{:S(2)}, u32[]{:S(2)}) collective-permute-start(bf16[8,64,256]{2,1,0:T(8,128)(2,1)} %get-tuple-element.123), channel_id=1, source_target_pairs={{0,2},{1,3},{2,0},{3,1},{4,6},{5,7},{6,4},{7,5},{8,10},{9,11},{10,... | collective-permute-start | bytes 786440 | tf_op jit(solution)/shard_map/ppermute | solution.py:471
  365.9 12.4 %collective-permute-start.19 = (bf16[8,64,256]{2,1,0:T(8,128)(2,1)}, bf16[8,64,256]{2,1,0:T(8,128)(2,1)S(1)}, u32[]{:S(2)}, u32[]{:S(2)}) collective-permute-start(bf16[8,64,256]{2,1,0:T(8,128)(2,1)} %get-tuple-element.124), channel_id=1, source_target_pairs={{0,3},{1,2},{2,1},{3,0},{4,7},{5,6},{6,5},{7,4},{8,11},{9,10},{10,... | collective-permute-start | bytes 786440 | tf_op jit(solution)/shard_map/ppermute | solution.py:471
  408.2 10.4 %collective-permute-start.21 = (bf16[8,64,512]{2,1,0:T(8,128)(2,1)}, bf16[8,64,512]{2,1,0:T(8,128)(2,1)S(1)}, u32[]{:S(2)}, u32[]{:S(2)}) collective-permute-start(bf16[8,64,512]{2,1,0:T(8,128)(2,1)} %get-tuple-element.128), channel_id=1, source_target_pairs={{0,28},{4,0},{8,4},{12,8},{16,12},{20,16},{24,20},{28,24},{1,29},{... | collective-permute-start | bytes 1572872 | tf_op jit(solution)/shard_map/ppermute | solution.py:866
  408.2 10.3 %collective-permute-start.20 = (bf16[32,8,512]{2,1,0:T(8,128)(2,1)}, bf16[32,8,512]{2,1,0:T(8,128)(2,1)S(1)}, u32[]{:S(2)}, u32[]{:S(2)}) collective-permute-start(bf16[32,8,512]{2,1,0:T(8,128)(2,1)} %get-tuple-element.127), channel_id=1, source_target_pairs={{0,3},{1,0},{2,1},{3,2},{4,7},{5,4},{6,5},{7,6},{8,11},{9,8},{10,9... | collective-permute-start | bytes 786440 | tf_op jit(solution)/shard_map/ppermute | solution.py:865
  410.2 8.4 %collective-permute-start.22 = (bf16[8,8,512]{2,1,0:T(8,128)(2,1)}, bf16[8,8,512]{2,1,0:T(8,128)(2,1)S(1)}, u32[]{:S(2)}, u32[]{:S(2)}) collective-permute-start(bf16[8,8,512]{2,1,0:T(8,128)(2,1)} %get-tuple-element.129), channel_id=1, source_target_pairs={{0,31},{1,28},{2,29},{3,30},{4,3},{5,0},{6,1},{7,2},{8,7},{9,4},{1... | collective-permute-start | bytes 196616 | tf_op jit(solution)/shard_map/ppermute | solution.py:867
  446.2 10.4 %collective-permute-start.24 = (bf16[8,64,256]{2,1,0:T(8,128)(2,1)}, bf16[8,64,256]{2,1,0:T(8,128)(2,1)S(1)}, u32[]{:S(2)}, u32[]{:S(2)}) collective-permute-start(bf16[8,64,256]{2,1,0:T(8,128)(2,1)} %get-tuple-element.133), channel_id=1, source_target_pairs={{0,4},{4,8},{8,12},{12,16},{16,20},{20,24},{24,28},{28,0},{1,5},{5... | collective-permute-start | bytes 786440 | tf_op jit(solution)/shard_map/ppermute | solution.py:866
  446.3 10.4 %collective-permute-start.23 = (bf16[32,8,256]{2,1,0:T(8,128)(2,1)}, bf16[32,8,256]{2,1,0:T(8,128)(2,1)S(1)}, u32[]{:S(2)}, u32[]{:S(2)}) collective-permute-start(bf16[32,8,256]{2,1,0:T(8,128)(2,1)} %get-tuple-element.132), channel_id=1, source_target_pairs={{0,1},{1,2},{2,3},{3,0},{4,5},{5,6},{6,7},{7,4},{8,9},{9,10},{10,1... | collective-permute-start | bytes 393224 | tf_op jit(solution)/shard_map/ppermute | solution.py:865
  447.8 8.9 %collective-permute-start.25 = (bf16[8,8,256]{2,1,0:T(8,128)(2,1)}, bf16[8,8,256]{2,1,0:T(8,128)(2,1)S(1)}, u32[]{:S(2)}, u32[]{:S(2)}) collective-permute-start(bf16[8,8,256]{2,1,0:T(8,128)(2,1)} %get-tuple-element.134), channel_id=1, source_target_pairs={{0,5},{1,6},{2,7},{3,4},{4,9},{5,10},{6,11},{7,8},{8,13},{9,14},{1... | collective-permute-start | bytes 98312 | tf_op jit(solution)/shard_map/ppermute | solution.py:867
  (43 other events, 311.4 us)

commit v4 on v3

--- a/solution.py
+++ b/solution.py
@@ -19,6 +19,7 @@
 STEPS = 2
 SPAN = WIN * WIN
 LANES = 128
+GROUP = 8
 TOK = N // PATCH
 
 SIGMAS = (0.8, 0.5, 0.3)
@@ -174,8 +175,8 @@
 def column_constants(devices, rows):
     s = np.arange(devices)
     small = embed_complex(wheel(devices, s[:, None] * s[None, :]), 1, 2)
-    wide = devices * 2 * PATCH
-    outer = np.einsum("qpsr,xy->qpxsry", small, np.eye(PATCH)).reshape(wide, wide)
+    wide = devices * 2 * GROUP
+    outer = np.einsum("qpsr,xy->qpxsry", small, np.eye(GROUP)).reshape(wide, wide)
     kr = s[:, None] + devices * np.arange(rows)[None, :]
     angle = wheel(N, kr[:, :, None] * np.arange(rows)[None, None, :])
     inner = embed_complex(angle, 1, 2).reshape(devices, 2 * rows, 2 * rows) / N
@@ -326,7 +327,7 @@
         copy.start()
     inner_ref, scale_ref, inner_t_ref, outer_t_ref = targets[:4]
     devices, _, rows, width = mid_ref.shape
-    wide = devices * 2 * PATCH
+    wide = devices * 2 * GROUP
     if halved:
         lane = lane_index((devices, PATCH, width))
         centre = flag_ref[0] == 1
@@ -334,32 +335,34 @@
         hidden = (lane == half) | (centre & (lane == 0))
         real_lane = (lane < half) | (centre & (lane == half))
 
-    def load(group):
-        place = slice(group * PATCH, (group + 1) * PATCH)
+    def load(place):
         if not halved:
-            return x_ref[:, :, place, :].reshape(wide, width)
-        piece = x_ref[:, place, :]
-        other = swap_halves(piece.astype(F32))
-        other = jnp.where(hidden, jnp.zeros_like(other), other).astype(BF16)
-        return jnp.stack([piece, other], axis=1).reshape(wide, width)
-
-    def store(group, value):
-        place = slice(group * PATCH, (group + 1) * PATCH)
-        value = value.reshape(devices, 2, PATCH, width)
+            return x_ref[:, :, place, :].astype(F32)
+        piece = x_ref[:, place, :].astype(F32)
+        other = swap_halves(piece)
+        return jnp.stack([piece, jnp.where(hidden, jnp.zeros_like(other), other)], axis=1)
+
+    def store(place, value):
         if halved:
             value = jnp.where(real_lane, value[:, 0], swap_halves(value[:, 1])).astype(BF16)
             out_ref[:, place, :] = value
         else:
             out_ref[:, :, place, :] = value.astype(BF16)
 
-    for pair in range(0, rows // PATCH, 2):
-        result = mm(outer_ref[...], jnp.concatenate([load(pair), load(pair + 1)], axis=1))
-        result = result.astype(BF16)
-        for n in range(2):
-            place = slice((pair + n) * PATCH, (pair + n + 1) * PATCH)
-            mid_ref[:, :, place, :] = result[:, n * width : (n + 1) * width].reshape(
-                devices, 2, PATCH, width
-            )
+    def outer(matrix_ref, value):
+        groups = [
+            value[:, :, n : n + GROUP, :].reshape(wide, width) for n in range(0, PATCH, GROUP)
+        ]
+        result = mm(matrix_ref[...], jnp.concatenate(groups, axis=1).astype(BF16))
+        parts = [
+            result[:, n : n + width].reshape(devices, 2, GROUP, width)
+            for n in range(0, result.shape[1], width)
+        ]
+        return jnp.concatenate(parts, axis=2)
+
+    for top in range(0, rows, PATCH):
+        place = slice(top, top + PATCH)
+        mid_ref[:, :, place, :] = outer(outer_ref, load(place)).astype(BF16)
 
     for n, copy in enumerate(copies):
         if n != 3:
@@ -386,17 +389,9 @@
     lax.fori_loop(0, devices, step, 0, unroll=8)
     copies[3].wait()
 
-    for pair in range(0, rows // PATCH, 2):
-        both = jnp.concatenate(
-            [
-                mid_ref[:, :, n * PATCH : (n + 1) * PATCH, :].reshape(wide, width)
-                for n in (pair, pair + 1)
-            ],
-            axis=1,
-        )
-        result = mm(outer_t_ref[...], both)
-        store(pair, result[:, :width])
-        store(pair + 1, result[:, width:])
+    for top in range(0, rows, PATCH):
+        place = slice(top, top + PATCH)
+        store(place, outer(outer_t_ref, mid_ref[:, :, place, :].astype(F32)))
 
 
 def turned(value, devices):
@@ -516,6 +511,7 @@
     )
     if halved:
         moved, beside = lax.optimization_barrier((moved, beside))
+        beside = from_neighbours(beside, 1)
     spaces = [pltpu.SMEM, pltpu.VMEM][: len(extra)] + [pltpu.VMEM] * 2 + [pl.ANY] * len(away)
     wave = pl.pallas_call(
         functools.partial(column_kernel, halved),
@@ -526,6 +522,8 @@
         + [pltpu.SemaphoreType.DMA((len(away),))],
         compiler_params=PARAMS,
     )(*extra, moved, outer, *away)
+    if halved:
+        wave, beside = lax.optimization_barrier((wave, beside))
     returned = lax.all_to_all(wave, ("ty", "tx"), split_axis=0, concat_axis=0, tiled=True)
     if not halved:
         returned, beside = lax.optimization_barrier((returned, beside))
@@ -594,7 +592,7 @@
 
 def swin_band(flow, wait, bias_ref, gain_ref, weight_refs, scratch):
     qkv_ref, proj_ref, up_ref, down_ref = weight_refs
-    mixed_ref, score_ref, prob_ref, *active_ref = scratch
+    mixed_ref, score_ref, prob_ref, active_ref = scratch
     count = flow.shape[0] // SPAN
     pairs = HEADS // 2
     depth = D // HEADS
@@ -646,19 +644,10 @@
     flow = flow + mm(mixed_ref[:, :D], proj_ref[...])
     normed = layer_norm(flow, gain_ref[1:2, :])
     chunks = up_ref.shape[1] // D
-    if active_ref:
-        for c in range(chunks):
-            part = slice(c * D, (c + 1) * D)
-            active_ref[0][:, part] = gelu_twice(mm(normed, up_ref[:, part]))
-        return flow + 0.5 * mm(active_ref[0][...], down_ref[...])
-    total = jnp.zeros_like(flow)
-    ahead = mm(normed, up_ref[:, :D])
     for c in range(chunks):
-        value = ahead
-        if c + 1 < chunks:
-            ahead = mm(normed, up_ref[:, (c + 1) * D : (c + 2) * D])
-        total = total + mm(gelu_twice(value), down_ref[c * D : (c + 1) * D, :])
-    return flow + 0.5 * total
+        part = slice(c * D, (c + 1) * D)
+        active_ref[:, part] = gelu_twice(mm(normed, up_ref[:, part]))
+    return flow + 0.5 * mm(active_ref[...], down_ref[...])
 
 
 def rolled_band(sign, shift_ref, refs, rows, count=WIN):
@@ -698,17 +687,22 @@
     wait = load_weights(0, sources, targets, sems)
     state = state_ref[...]
     if before is not None:
-        state = state - before * rolled_band(-1, shift_ref, back_refs, rows)
-    turn = pl.program_id(0) ^ shift_ref[2]
-    grad = 0.0
+        state = state - before * rolled_band(-1, shift_ref, back_refs, rows, state.shape[0])
+    height = state.shape[0]
     if parts == 1:
         grad = grad_refs[0][...].astype(F32)
-        count = 0
-    for n in range(0, count * parts, parts):
-        piece = grad_refs[n][...]
-        for m in range(1, parts):
-            piece = jnp.where(turn == m, grad_refs[n + m][...], piece)
-        grad = grad + piece.astype(F32)
+    else:
+        bands = []
+        for k in range(height // WIN):
+            turn = (pl.program_id(0) * (height // WIN) + k) ^ shift_ref[2]
+            band = 0.0
+            for n in range(0, count * parts, parts):
+                piece = grad_refs[n][...]
+                for m in range(1, parts):
+                    piece = jnp.where(turn == m, grad_refs[n + m][...], piece)
+                band = band + piece.astype(F32)
+            bands.append(band)
+        grad = jnp.concatenate(bands, axis=0)
     step = zeta * grad
     half = state - step
     tokens = mm(to_windows(half).astype(BF16), embed_ref[...]).astype(BF16).astype(F32)
@@ -727,8 +721,8 @@
 
     @pl.when(pl.program_id(0) == 0)
     def _():
-        edge_ref[...] = out_ref[...]
-        corner_ref[...] = side_ref[...]
+        edge_ref[...] = out_ref[:WIN]
+        corner_ref[...] = side_ref[:WIN]
 
 
 def write_pieces(turn, refs, value):
@@ -810,20 +804,23 @@
     pieces = [piece for grad in grads for piece in grad]
     fields = [] if sigma is None else [noise]
     feats = D if sigma is None else D + PIXELS
-    specs, shapes = strip_outs(rows, cols, feats)
+    height = 2 * WIN
+    specs, shapes = strip_outs(rows, cols, feats, height)
+    band = band_spec(cols, PIXELS, height)
     return pl.pallas_call(
         functools.partial(first_kernel, zeta, sigma, len(grads), parts, rows, before),
         grid_spec=pltpu.PrefetchScalarGridSpec(
             num_scalar_prefetch=1,
-            grid=(rows // WIN,),
-            in_specs=[band_spec(cols, PIXELS)]
+            grid=(rows // height,),
+            in_specs=[band]
             + [whole(value) for value in back]
-            + [band_spec(cols, PIXELS) if parts == 1 else whole(value) for value in pieces]
-            + [band_spec(cols, PIXELS)] * len(fields)
-            + [bias_spec(cols), whole(w_embed), member(gains, 0)]
+            + [band if parts == 1 else whole(value) for value in pieces]
+            + [band] * len(fields)
+            + [bias_spec(cols, height), whole(w_embed), member(gains, 0)]
             + [pl.BlockSpec(memory_space=pl.ANY)] * len(weights),
-            out_specs=[band_spec(cols, PIXELS)] + specs,
-            scratch_shapes=band_scratch(cols, weights),
+            out_specs=[band] + specs,
+            scratch_shapes=band_scratch(cols, weights, height)
+            + [pltpu.VMEM((height * cols, weights[2].shape[2]), BF16)],
         ),
         out_shape=[jax.ShapeDtypeStruct((rows, cols, PIXELS), F32)] + shapes,
         compiler_params=PARAMS,
@@ -932,7 +929,7 @@
     if len(out_refs) == 1:
         out_refs[0][...] = result
     else:
-        write_pieces(pl.program_id(0) ^ place_ref[2], out_refs, result)
+        write_pieces(pl.program_id(0) ^ place_ref[0], out_refs, result)
 
 
 def to_tile_kernel(sigma, scale, rows, *refs):
@@ -1009,17 +1006,15 @@
     devices = lax.axis_size("ty") * lax.axis_size("tx")
     lanes = lax.axis_size("tx")
     fast = N // devices == TOK // 2 and rows == lanes * WIN and lanes & (lanes - 1) == 0
-    places = [
-        jnp.concatenate([offsets[step], lax.axis_index("tx")[None]]).astype(jnp.int32)
-        for step in range(STEPS)
-    ]
+    column = lax.axis_index("tx").astype(jnp.int32)[None]
+    places = [jnp.concatenate([offsets[step], column]) for step in range(STEPS)]
     row_index = lax.axis_index("ty") * rows + counting(rows)
     col_index = lax.axis_index("tx") * cols + counting(cols)
     weights = (w_qkv, w_proj, w_up, w_down, norm_gains)
     w_embed = w_embed.reshape(PATCH, PATCH, D).transpose(1, 0, 2).reshape(PIXELS, D)
     w_unembed = w_unembed.reshape(D, PATCH, PATCH).transpose(0, 2, 1).reshape(D, PIXELS)
-    state = patches_of(image[None], 0, places[0])[0]
-    extras = [patches_of(noise, step, places[0])[0] for step in range(STEPS - 1)] + [None]
+    state = patches_of(image[None], 0, column)[0]
+    extras = [patches_of(noise, step, column)[0] for step in range(STEPS - 1)] + [None]
     first_bias = bias_of(None, key_mask)
     biases = []
     for step in range(STEPS):
@@ -1036,7 +1031,7 @@
         half = weight.shape[0] // 2
         lines = (weight[half:], weight[:1])
         grad, (beside, lines) = patch_gradient(
-            patches_of(image[None], 0, places[0], BF16, lanes), scale, data, None, None,
+            patches_of(image[None], 0, column, BF16, lanes), scale, data, None, None,
             (beside, lines),
         )
         grad, lines = lax.optimization_barrier((grad, lines))
@@ -1047,7 +1042,7 @@
         if not fast:
             tile = image if step == 0 else tile_of(state, before, shift, back, 0.0, noise, 0)
             grad = plain_gradient(tile, gains, observed, vis_weight)
-            grad = patches_of(grad.astype(F32)[None], 0, places[0], BF16)[0]
+            grad = patches_of(grad.astype(F32)[None], 0, column, BF16)[0]
             grads = [[grad]]
         elif step > 0:
             grad, back = patch_gradient(moving, scale, None, shift, mirror, back)
@@ -1065,8 +1060,9 @@
             before, shift, from_neighbours(first, -1), biases[step], w_unembed, weights,
             lanes if fast and not last else 0,
         )
-        rolled, moving = rolled[:4], rolled[4:]
-        back = from_neighbours(rolled, 1)
+        back, moving = rolled[:4], rolled[4:]
+        if last or not fast:
+            back = from_neighbours(back, 1)
     return tile_of(state, before, shift, back, SIGMAS[STEPS], noise, STEPS - 1)
 
 

time: 475 us -> 474 us (level)
  waiting for transfers between devices: 137 us -> 149 us
  Pallas kernels: 200 us -> 191 us
    all_to_all x2, waiting for transfers between devices: 18.7 us -> 41.3 us  [patch_gradient(): lax.all_to_all(sent.reshape(part), ('ty', 'tx'), split_axis=0, concat_axi...]
    ppermute x4, waiting for transfers between devices: 33.1 us -> 21.6 us  [from_neighbours(): lax.ppermute(corner, ('ty', 'tx'), across)]
    unnamed x96 -> x98, local copies, waits for them, and re-layouts: 25 us -> 22.8 us
  transfers between devices with their start and end apart: 30 -> 30, of which waited for: 18 -> 17; matrix products, arithmetic and copies ran while one was open for 12% -> 12% of each run, Pallas kernels for 10% -> 12%
where the time goes in v4:
time: 474 us; the launch traced here: 466 us
  Pallas kernels  191 us (40%)
  waiting for transfers between devices  149 us (31%)
  starting transfers between devices  53.7 us (11%)
  local copies, waits for them, and re-layouts  47.1 us (10%)
  other arithmetic  18.7 us (4%)
  between operations  5.8 us (1%)
    pallas_call x2, Pallas kernels, second_block(): pl.pallas_call(functools.partial(second_kernel, sigma, rows, parts), grid...  55.3 us
    pallas_call x2, Pallas kernels, first_block(): pl.pallas_call(functools.partial(first_kernel, zeta, sigma, len(grads), p...  54.4 us
    all_to_all x2, waiting for transfers between devices, patch_gradient(): lax.all_to_all(wave, ('ty', 'tx'), split_axis=0, concat_axis=0, tiled=True)  45.2 us
    all_to_all x2, waiting for transfers between devices, patch_gradient(): lax.all_to_all(sent.reshape(part), ('ty', 'tx'), split_axis=0, concat_axi...  41.3 us
    ppermute x12, waiting for transfers between devices, swap_pieces(): lax.ppermute(pieces[m], 'tx', [(k, k ^ m) for k in range(lanes)])  40.2 us
    pallas_call x2, Pallas kernels, patch_gradient(): pl.pallas_call(functools.partial(column_kernel, halved), in_specs=[pl.Blo...  23.4 us
    unnamed x98, local copies, waits for them, and re-layouts  22.8 us
    ppermute x4, waiting for transfers between devices, from_neighbours(): lax.ppermute(corner, ('ty', 'tx'), across)  21.6 us
  transfers between devices with their start and end apart: 30, of which 17 were waited for; matrix products, arithmetic and copies ran while one was open for 12% of the time, Pallas kernels for 12%

profile of v4, /device:TPU:0, one launch (start us, length us, event | category | flops | bytes accessed | tf_op | source)
XLA Modules:
  0.0 466.0 jit_solution(12810423955999788622)
XLA Ops:
  0.0 5.7 %shard_map.298 = (bf16[8,64,256]{2,1,0:T(8,128)(2,1)}, bf16[8,64,256]{2,1,0:T(8,128)(2,1)}, bf16[8,64,256]{2,1,0:T(8,128)(2,1)}, bf16[8,64,256]{2,1,0:T(8,128)(2,1)}) custom-call(s32[1]{0:T(128)} %bitcast.1.place_ref, f32[1,512,1024]{2,1,0:T(8,128)} %bitcast.67, bf16[1024,1024]{1,0:T(8,128)(2,1)} %constant.98.clone.order_ref), custom_call_target="tpu_custom_call" | custom-call | tf_op jit(solution)/shard_map/pallas_call | solution.py:963
  16.0 6.3 %collective-permute-done.1.refs_2_ = bf16[8,64,256]{2,1,0:T(8,128)(2,1)S(1)} collective-permute-done((bf16[8,64,256]{2,1,0:T(8,128)(2,1)}, bf16[8,64,256]{2,1,0:T(8,128)(2,1)S(1)}, u32[]{:S(2)}, u32[]{:S(2)}) %collective-permute-start.1) | collective-permute-done | bytes 262176 | tf_op jit(solution)/shard_map/ppermute | solution.py:466
  23.0 5.8 %shard_map.299 = bf16[16,2,2,128,128]{4,3,2,1,0:T(8,128)(2,1)} custom-call(bf16[8,64,256]{2,1,0:T(8,128)(2,1)} %get-tuple-element.75.refs_0_, bf16[8,64,256]{2,1,0:T(8,128)(2,1)} %copy-done.12, bf16[8,64,256]{2,1,0:T(8,128)(2,1)} %copy-done.13, bf16[8,64,256]{2,1,0:T(8,128)(2,1)} %copy-done.14, bf16[256,512]{1,0:T(8,128)(2,1)} %pad_maximum_fusion.5.refs_4_.first_ref, ...), custom_call_target="tpu_custom_call" | custom-call | tf_op jit(solution)/shard_map/pallas_call | solution.py:502
  28.8 5.0 %all-to-all-start = ((bf16[32,2,128,128]{3,2,1,0:T(8,128)(2,1)}), bf16[32,2,128,128]{3,2,1,0:T(8,128)(2,1)}, u32[]{:S(2)}, u32[]{:S(2)}) async-start(bf16[32,2,128,128]{3,2,1,0:T(8,128)(2,1)} %bitcast.70), calls=%async_computation | async-start | bytes 4194304 | tf_op jit(solution)/shard_map/all_to_all | solution.py:509
  35.8 4.7 %fusion.18 = (f32[1,128,4096]{2,1,0:T(8,128)}, f32[1,128,4096]{2,1,0:T(8,128)}) fusion(f32[2,128,4096]{2,1,0:T(8,128)} %param.36), kind=kLoop, calls=%fused_computation.77 | loop fusion | bytes 8388608 | tf_op jit(solution)/shard_map/slice | solution.py:403
  65.1 17.4 %all-to-all-done.refs_0_ = bf16[32,2,128,128]{3,2,1,0:T(8,128)(2,1)} async-done(((bf16[32,2,128,128]{3,2,1,0:T(8,128)(2,1)}), bf16[32,2,128,128]{3,2,1,0:T(8,128)(2,1)}, u32[]{:S(2)}, u32[]{:S(2)}) %all-to-all-start) | async-done | bytes 2097184 | tf_op jit(solution)/shard_map/all_to_all | solution.py:509
  82.5 12.3 %shard_map.300 = bf16[32,2,128,128]{3,2,1,0:T(8,128)(2,1)} custom-call(bf16[32,2,128,128]{3,2,1,0:T(8,128)(2,1)} %all-to-all-done.refs_0_, bf16[512,512]{1,0:T(8,128)(2,1)} %constant.99.clone.refs_1_.refs_3_, bf16[32,256,256]{2,1,0:T(8,128)(2,1)} %constant.101.clone.refs_2_.refs_4_, bf16[32,128,128]{2,1,0:T(8,128)(2,1)} %bitcast.65, ...), custom_call_target="tpu_custom_call" | custom-call | tf_op jit(solution)/shard_map/pallas_call | solution.py:516
  99.5 6.5 %shard_map.301.refs_1_ = f32[32,64,256]{2,1,0:T(8,128)} custom-call(s32[1]{0:T(128)} %bitcast.1.place_ref, f32[1,512,1024]{2,1,0:T(8,128)} %bitcast.68, bf16[1024,1024]{1,0:T(8,128)(2,1)} %constant.98.clone.order_ref), custom_call_target="tpu_custom_call" | custom-call | tf_op jit(solution)/shard_map/pallas_call | solution.py:963
  107.4 6.6 %shard_map.302.refs_6_ = f32[32,64,256]{2,1,0:T(8,128)} custom-call(s32[1]{0:T(128)} %bitcast.1.place_ref, f32[2,512,1024]{2,1,0:T(8,128)} %refs_6_.4, bf16[1024,1024]{1,0:T(8,128)(2,1)} %constant.98.clone.order_ref), custom_call_target="tpu_custom_call" | custom-call | tf_op jit(solution)/shard_map/pallas_call | solution.py:963
  128.7 19.5 %all-to-all-done.1 = bf16[32,2,128,128]{3,2,1,0:T(8,128)(2,1)S(1)} async-done(((bf16[32,2,128,128]{3,2,1,0:T(8,128)(2,1)}), bf16[32,2,128,128]{3,2,1,0:T(8,128)(2,1)S(1)}, u32[]{:S(2)}, u32[]{:S(2)}) %all-to-all-start.1) | async-done | bytes 2097184 | tf_op jit(solution)/shard_map/all_to_all | solution.py:527
  149.6 7.4 %shard_map.303 = (bf16[8,64,256]{2,1,0:T(8,128)(2,1)}, bf16[8,64,256]{2,1,0:T(8,128)(2,1)}, bf16[8,64,256]{2,1,0:T(8,128)(2,1)}, bf16[8,64,256]{2,1,0:T(8,128)(2,1)}) custom-call(bf16[16,2,2,128,128]{4,3,2,1,0:T(8,128)(2,1)} %bitcast.69, bf16[256,512]{1,0:T(8,128)(2,1)} %pad_maximum_fusion.5.refs_4_.first_ref, ...), custom_call_target="tpu_custom_call" | custom-call | tf_op jit(solution)/shard_map/pallas_call | solution.py:530
  160.4 5.9 %collective-permute-done.3.refs_3_.refs_7_ = bf16[8,64,256]{2,1,0:T(8,128)(2,1)S(1)} collective-permute-done((bf16[8,64,256]{2,1,0:T(8,128)(2,1)}, bf16[8,64,256]{2,1,0:T(8,128)(2,1)S(1)}, u32[]{:S(2)}, u32[]{:S(2)}) %collective-permute-start.3) | collective-permute-done | bytes 262176 | tf_op jit(solution)/shard_map/ppermute | solution.py:466
  166.4 5.5 %collective-permute-done.4.refs_4_.refs_8_ = bf16[8,64,256]{2,1,0:T(8,128)(2,1)S(1)} collective-permute-done((bf16[8,64,256]{2,1,0:T(8,128)(2,1)}, bf16[8,64,256]{2,1,0:T(8,128)(2,1)S(1)}, u32[]{:S(2)}, u32[]{:S(2)}) %collective-permute-start.4) | collective-permute-done | bytes 262176 | tf_op jit(solution)/shard_map/ppermute | solution.py:466
  176.0 27.5 %shard_map.304 = (f32[32,64,256]{2,1,0:T(8,128)}, bf16[32,64,768]{2,1,0:T(8,128)(2,1)}, bf16[32,8,768]{2,1,0:T(8,128)(2,1)}, bf16[8,64,768]{2,1,0:T(8,128)(2,1)}, bf16[8,8,768]{2,1,0:T(8,128)(2,1)}) custom-call(s32[3]{0:T(128)} %pad_add_fusion.1.refs_0_, f32[32,64,256]{2,1,0:T(8,128)} %shard_map.301.refs_1_, ...), custom_call_target="tpu_custom_call" | custom-call | tf_op jit(solution)/shard_map/pallas_call | solution.py:810
  203.5 5.2 %collective-permute-start.9 = (bf16[8,64,768]{2,1,0:T(8,128)(2,1)}, bf16[8,64,768]{2,1,0:T(8,128)(2,1)S(1)}, u32[]{:S(2)}, u32[]{:S(2)}) collective-permute-start(bf16[8,64,768]{2,1,0:T(8,128)(2,1)} %get-tuple-element.103), channel_id=1, source_target_pairs={{0,28},{4,0},{8,4},{12,8},{16,12},{20,16},{24,20},{28,24},{1,29},{... | collective-permute-start | bytes 2359304 | tf_op jit(solution)/shard_map/ppermute | solution.py:863
  212.1 7.5 %collective-permute-done.10.refs_4_ = bf16[8,8,768]{2,1,0:T(8,128)(2,1)S(1)} collective-permute-done((bf16[8,8,768]{2,1,0:T(8,128)(2,1)}, bf16[8,8,768]{2,1,0:T(8,128)(2,1)S(1)}, u32[]{:S(2)}, u32[]{:S(2)}) %collective-permute-start.10) | collective-permute-done | bytes 98336 | tf_op jit(solution)/shard_map/ppermute | solution.py:864
  222.2 28.4 %shard_map.305 = (bf16[32,64,256]{2,1,0:T(8,128)(2,1)}, bf16[32,8,256]{2,1,0:T(8,128)(2,1)}, bf16[8,64,256]{2,1,0:T(8,128)(2,1)}, bf16[8,8,256]{2,1,0:T(8,128)(2...) custom-call(s32[3]{0:T(128)} %pad_add_fusion.1.refs_0_, ...), custom_call_target="tpu_custom_call" | custom-call | tf_op jit(solution)/shard_map/pallas_call | solution.py:837
  255.4 5.2 %collective-permute-done.11.refs_1_ = bf16[8,64,256]{2,1,0:T(8,128)(2,1)S(1)} collective-permute-done((bf16[8,64,256]{2,1,0:T(8,128)(2,1)}, bf16[8,64,256]{2,1,0:T(8,128)(2,1)S(1)}, u32[]{:S(2)}, u32[]{:S(2)}) %collective-permute-start.11) | collective-permute-done | bytes 262176 | tf_op jit(solution)/shard_map/ppermute | solution.py:466
  266.0 6.1 %shard_map.306 = bf16[16,2,128,128]{3,2,1,0:T(8,128)(2,1)} custom-call(bf16[8,64,256]{2,1,0:T(8,128)(2,1)} %get-tuple-element.107.refs_0_, bf16[8,64,256]{2,1,0:T(8,128)(2,1)} %copy-done.25, bf16[8,64,256]{2,1,0:T(8,128)(2,1)} %copy-done.26, bf16[8,64,256]{2,1,0:T(8,128)(2,1)} %copy-done.27, bf16[256,512]{1,0:T(8,128)(2,1)} %pad_maximum_fusion.6.refs_4_, ...), custom_call_target="tpu_custom_call" | custom-call | tf_op jit(solution)/shard_map/pallas_call | solution.py:502
  272.1 5.4 %all-to-all-start.2 = ((bf16[32,128,128]{2,1,0:T(8,128)(2,1)}), bf16[32,128,128]{2,1,0:T(8,128)(2,1)S(1)}, u32[]{:S(2)}, u32[]{:S(2)}) async-start(bf16[32,128,128]{2,1,0:T(8,128)(2,1)} %bitcast.73), calls=%async_computation.2 | async-start | bytes 2097152 | tf_op jit(solution)/shard_map/all_to_all | solution.py:509
  280.1 23.9 %all-to-all-done.2.refs_2_ = bf16[32,128,128]{2,1,0:T(8,128)(2,1)S(1)} async-done(((bf16[32,128,128]{2,1,0:T(8,128)(2,1)}), bf16[32,128,128]{2,1,0:T(8,128)(2,1)S(1)}, u32[]{:S(2)}, u32[]{:S(2)}) %all-to-all-start.2) | async-done | bytes 1048608 | tf_op jit(solution)/shard_map/all_to_all | solution.py:509
  308.5 5.4 %shard_map.307.refs_5_ = bf16[32,128,128]{2,1,0:T(8,128)(2,1)} custom-call(bf16[32,128,128]{2,1,0:T(8,128)(2,1)} %bitcast.66, bf16[32,128,128]{2,1,0:T(8,128)(2,1)} %bitcast.72, bf16[2,128,128]{2,1,0:T(8,128)(2,1)} %add_convert_fusion.pick_ref, bf16[2,128,128]{2,1,0:T(8,128)(2,1)} %constant.113.clone.flip_ref), custom_call_target="tpu_custom_call" | custom-call | tf_op jit(solution)/shard_map/pallas_call | solution.py:447
  314.7 11.1 %shard_map.308 = bf16[32,128,128]{2,1,0:T(8,128)(2,1)} custom-call(s32[1]{0:T(128)} %bitcast.28.refs_0_, f32[32,2,8,128]{3,2,1,0:T(8,128)} %broadcast_in_dim.79.refs_1_, bf16[32,128,128]{2,1,0:T(8,128)(2,1)} %copy-done.1, bf16[512,512]{1,0:T(8,128)(2,1)} %constant.99.clone.refs_1_.refs_3_, bf16[32,256,256]{2,1,0:T(8,128)(2,1)} %constant.101.clone.refs_2_.refs_4_, ...), custom_call_target="tpu_custom_call" | custom-call | tf_op jit(solution)/shard_map/pallas_call | solution.py:516
  326.0 5.2 %all-to-all-start.3 = ((bf16[32,128,128]{2,1,0:T(8,128)(2,1)}), bf16[32,128,128]{2,1,0:T(8,128)(2,1)S(1)}, u32[]{:S(2)}, u32[]{:S(2)}) async-start(bf16[32,128,128]{2,1,0:T(8,128)(2,1)} %shard_map.308), calls=%async_computation.3 | async-start | bytes 2097152 | tf_op jit(solution)/shard_map/all_to_all | solution.py:527
  331.9 25.7 %all-to-all-done.3 = bf16[32,128,128]{2,1,0:T(8,128)(2,1)S(1)} async-done(((bf16[32,128,128]{2,1,0:T(8,128)(2,1)}), bf16[32,128,128]{2,1,0:T(8,128)(2,1)S(1)}, u32[]{:S(2)}, u32[]{:S(2)}) %all-to-all-start.3) | async-done | bytes 1048608 | tf_op jit(solution)/shard_map/all_to_all | solution.py:527
  358.6 6.4 %shard_map.309 = (bf16[8,64,256]{2,1,0:T(8,128)(2,1)}, bf16[8,64,256]{2,1,0:T(8,128)(2,1)}, bf16[8,64,256]{2,1,0:T(8,128)(2,1)}, bf16[8,64,256]{2,1,0:T(8,128)(2,1)}) custom-call(bf16[16,2,128,128]{3,2,1,0:T(8,128)(2,1)} %bitcast.74, bf16[256,512]{1,0:T(8,128)(2,1)} %pad_maximum_fusion.7.first_ref, f32[2,256,256]{2,1,0:T(8,128)} %constant.107.clone.refs_5_.twist_ref, ...), custom_call_target="tpu_custom_call" | custom-call | tf_op jit(solution)/shard_map/pallas_call | solution.py:530
  368.6 5.9 %collective-permute-done.17.refs_11_ = bf16[8,64,256]{2,1,0:T(8,128)(2,1)S(1)} collective-permute-done((bf16[8,64,256]{2,1,0:T(8,128)(2,1)}, bf16[8,64,256]{2,1,0:T(8,128)(2,1)S(1)}, u32[]{:S(2)}, u32[]{:S(2)}) %collective-permute-start.17) | collective-permute-done | bytes 262176 | tf_op jit(solution)/shard_map/ppermute | solution.py:466
  381.0 26.9 %shard_map.310 = (f32[32,64,256]{2,1,0:T(8,128)}, bf16[32,64,512]{2,1,0:T(8,128)(2,1)}, bf16[32,8,512]{2,1,0:T(8,128)(2,1)}, bf16[8,64,512]{2,1,0:T(8,128)(2,1)}, bf16[8,8,512]{2,1,0:T(8,128)(2,1)}) custom-call(s32[3]{0:T(128)} %pad_add_fusion.1.refs_0_, f32[32,64,256]{2,1,0:T(8,128)} %get-tuple-element.94.refs_1_, ...), custom_call_target="tpu_custom_call" | custom-call | tf_op jit(solution)/shard_map/pallas_call | solution.py:810
  412.3 6.0 %collective-permute-done.22.refs_4_ = bf16[8,8,512]{2,1,0:T(8,128)(2,1)S(1)} collective-permute-done((bf16[8,8,512]{2,1,0:T(8,128)(2,1)}, bf16[8,8,512]{2,1,0:T(8,128)(2,1)S(1)}, u32[]{:S(2)}, u32[]{:S(2)}) %collective-permute-start.22) | collective-permute-done | bytes 65568 | tf_op jit(solution)/shard_map/ppermute | solution.py:864
  419.2 26.9 %shard_map.311 = (bf16[32,64,256]{2,1,0:T(8,128)(2,1)}, bf16[32,8,256]{2,1,0:T(8,128)(2,1)}, bf16[8,64,256]{2,1,0:T(8,128)(2,1)}, bf16[8,8,256]{2,1,0:T(8,128)(2,1)}) custom-call(s32[3]{0:T(128)} %pad_add_fusion.refs_0_, bf16[32,64,512]{2,1,0:T(8,128)(2,1)} %get-tuple-element.136.refs_1_, bf16[32,8,512]{2,1,0:T(8,128)(2,1)} %copy-done.11, ...), custom_call_target="tpu_custom_call" | custom-call | tf_op jit(solution)/shard_map/pallas_call | solution.py:837
  448.4 8.1 %collective-permute-done.25.refs_5_ = bf16[8,8,256]{2,1,0:T(8,128)(2,1)S(1)} collective-permute-done((bf16[8,8,256]{2,1,0:T(8,128)(2,1)}, bf16[8,8,256]{2,1,0:T(8,128)(2,1)S(1)}, u32[]{:S(2)}, u32[]{:S(2)}) %collective-permute-start.25) | collective-permute-done | bytes 32800 | tf_op jit(solution)/shard_map/ppermute | solution.py:864
  457.3 8.5 %shard_map.312 = f32[512,1024]{1,0:T(8,128)} custom-call(s32[3]{0:T(128)} %pad_add_fusion.refs_0_, f32[32,64,256]{2,1,0:T(8,128)} %get-tuple-element.135.refs_1_, bf16[32,64,256]{2,1,0:T(8,128)(2,1)} %get-tuple-element.141.refs_2_, bf16[32,8,256]{2,1,0:T(8,128)(2,1)} %copy-done.35, bf16[8,64,256]{2,1,0:T(8,128)(2,1)} %copy-done.15, ...), custom_call_target="tpu_custom_call" | custom-call | tf_op jit(solution)/shard_map/pallas_call | solution.py:982
  (193 shorter events, 106.3 us)
Async XLA Ops:
  5.7 10.3 %collective-permute-start = (bf16[8,64,256]{2,1,0:T(8,128)(2,1)}, bf16[8,64,256]{2,1,0:T(8,128)(2,1)S(1)}, u32[]{:S(2)}, u32[]{:S(2)}) collective-permute-start(bf16[8,64,256]{2,1,0:T(8,128)(2,1)} %get-tuple-element.76), channel_id=1, source_target_pairs={{0,1},{1,0},{2,3},{3,2},{4,5},{5,4},{6,7},{7,6},{8,9},{9,8},{10,11... | collective-permute-start | bytes 786440 | tf_op jit(solution)/shard_map/ppermute | solution.py:466
  8.6 13.6 %collective-permute-start.1 = (bf16[8,64,256]{2,1,0:T(8,128)(2,1)}, bf16[8,64,256]{2,1,0:T(8,128)(2,1)S(1)}, u32[]{:S(2)}, u32[]{:S(2)}) collective-permute-start(bf16[8,64,256]{2,1,0:T(8,128)(2,1)} %get-tuple-element.77), channel_id=1, source_target_pairs={{0,2},{1,3},{2,0},{3,1},{4,6},{5,7},{6,4},{7,5},{8,10},{9,11},{10,... | collective-permute-start | bytes 786440 | tf_op jit(solution)/shard_map/ppermute | solution.py:466
  10.1 12.1 %collective-permute-start.2 = (bf16[8,64,256]{2,1,0:T(8,128)(2,1)}, bf16[8,64,256]{2,1,0:T(8,128)(2,1)S(1)}, u32[]{:S(2)}, u32[]{:S(2)}) collective-permute-start(bf16[8,64,256]{2,1,0:T(8,128)(2,1)} %get-tuple-element.78), channel_id=1, source_target_pairs={{0,3},{1,2},{2,1},{3,0},{4,7},{5,6},{6,5},{7,4},{8,11},{9,10},{10,... | collective-permute-start | bytes 786440 | tf_op jit(solution)/shard_map/ppermute | solution.py:466
  28.8 53.7 %all-to-all-start = ((bf16[32,2,128,128]{3,2,1,0:T(8,128)(2,1)}), bf16[32,2,128,128]{3,2,1,0:T(8,128)(2,1)}, u32[]{:S(2)}, u32[]{:S(2)}) async-start(bf16[32,2,128,128]{3,2,1,0:T(8,128)(2,1)} %bitcast.70), calls=%async_computation | async-start | bytes 4194304 | tf_op jit(solution)/shard_map/all_to_all | solution.py:509
  94.9 53.4 %all-to-all-start.1 = ((bf16[32,2,128,128]{3,2,1,0:T(8,128)(2,1)}), bf16[32,2,128,128]{3,2,1,0:T(8,128)(2,1)S(1)}, u32[]{:S(2)}, u32[]{:S(2)}) async-start(bf16[32,2,128,128]{3,2,1,0:T(8,128)(2,1)} %shard_map.300), calls=%async_computation.1 | async-start | bytes 4194304 | tf_op jit(solution)/shard_map/all_to_all | solution.py:527
  156.9 9.4 %collective-permute-start.3 = (bf16[8,64,256]{2,1,0:T(8,128)(2,1)}, bf16[8,64,256]{2,1,0:T(8,128)(2,1)S(1)}, u32[]{:S(2)}, u32[]{:S(2)}) collective-permute-start(bf16[8,64,256]{2,1,0:T(8,128)(2,1)} %get-tuple-element.82), channel_id=1, source_target_pairs={{0,1},{1,0},{2,3},{3,2},{4,5},{5,4},{6,7},{7,6},{8,9},{9,8},{10,11... | collective-permute-start | bytes 786440 | tf_op jit(solution)/shard_map/ppermute | solution.py:466
  158.4 13.4 %collective-permute-start.4 = (bf16[8,64,256]{2,1,0:T(8,128)(2,1)}, bf16[8,64,256]{2,1,0:T(8,128)(2,1)S(1)}, u32[]{:S(2)}, u32[]{:S(2)}) collective-permute-start(bf16[8,64,256]{2,1,0:T(8,128)(2,1)} %get-tuple-element.83), channel_id=1, source_target_pairs={{0,2},{1,3},{2,0},{3,1},{4,6},{5,7},{6,4},{7,5},{8,10},{9,11},{10,... | collective-permute-start | bytes 786440 | tf_op jit(solution)/shard_map/ppermute | solution.py:466
  159.9 11.9 %collective-permute-start.5 = (bf16[8,64,256]{2,1,0:T(8,128)(2,1)}, bf16[8,64,256]{2,1,0:T(8,128)(2,1)S(1)}, u32[]{:S(2)}, u32[]{:S(2)}) collective-permute-start(bf16[8,64,256]{2,1,0:T(8,128)(2,1)} %get-tuple-element.84), channel_id=1, source_target_pairs={{0,3},{1,2},{2,1},{3,0},{4,7},{5,6},{6,5},{7,4},{8,11},{9,10},{10,... | collective-permute-start | bytes 786440 | tf_op jit(solution)/shard_map/ppermute | solution.py:466
  173.6 29.9 %collective-permute-start.6 = (bf16[64,4096]{1,0:T(8,128)(2,1)S(1)}, bf16[64,4096]{1,0:T(8,128)(2,1)S(1)}, u32[]{:S(2)}, u32[]{:S(2)}) collective-permute-start(bf16[64,4096]{1,0:T(8,128)(2,1)S(1)} %copy.84), channel_id=1, source_target_pairs={{0,31},{1,30},{2,29},{3,28},{4,27},{5,26},{6,25},{7,24},{8,23},{9,... | collective-permute-start | bytes 1572872 | tf_op jit(solution)/shard_map/ppermute | solution.py:427
  175.3 28.2 %collective-permute-start.7 = (bf16[1,4096]{1,0:T(2,128)(2,1)S(1)}, bf16[1,4096]{1,0:T(2,128)(2,1)S(1)}, u32[]{:S(2)}, u32[]{:S(2)}) collective-permute-start(bf16[1,4096]{1,0:T(2,128)(2,1)S(1)} %copy.85), channel_id=1, source_target_pairs={{1,31},{2,30},{3,29},{4,28},{5,27},{6,26},{7,25},{8,24},{9,23},{10... | collective-permute-start | bytes 24584 | tf_op jit(solution)/shard_map/ppermute | solution.py:428
  203.5 17.1 %collective-permute-start.9 = (bf16[8,64,768]{2,1,0:T(8,128)(2,1)}, bf16[8,64,768]{2,1,0:T(8,128)(2,1)S(1)}, u32[]{:S(2)}, u32[]{:S(2)}) collective-permute-start(bf16[8,64,768]{2,1,0:T(8,128)(2,1)} %get-tuple-element.103), channel_id=1, source_target_pairs={{0,28},{4,0},{8,4},{12,8},{16,12},{20,16},{24,20},{28,24},{1,29},{... | collective-permute-start | bytes 2359304 | tf_op jit(solution)/shard_map/ppermute | solution.py:863
  208.7 11.9 %collective-permute-start.8 = (bf16[32,8,768]{2,1,0:T(8,128)(2,1)}, bf16[32,8,768]{2,1,0:T(8,128)(2,1)S(1)}, u32[]{:S(2)}, u32[]{:S(2)}) collective-permute-start(bf16[32,8,768]{2,1,0:T(8,128)(2,1)} %get-tuple-element.102), channel_id=1, source_target_pairs={{0,3},{1,0},{2,1},{3,2},{4,7},{5,4},{6,5},{7,6},{8,11},{9,8},{10,9... | collective-permute-start | bytes 1179656 | tf_op jit(solution)/shard_map/ppermute | solution.py:862
  210.2 9.4 %collective-permute-start.10 = (bf16[8,8,768]{2,1,0:T(8,128)(2,1)}, bf16[8,8,768]{2,1,0:T(8,128)(2,1)S(1)}, u32[]{:S(2)}, u32[]{:S(2)}) collective-permute-start(bf16[8,8,768]{2,1,0:T(8,128)(2,1)} %get-tuple-element.104), channel_id=1, source_target_pairs={{0,31},{1,28},{2,29},{3,30},{4,3},{5,0},{6,1},{7,2},{8,7},{9,4},{1... | collective-permute-start | bytes 294920 | tf_op jit(solution)/shard_map/ppermute | solution.py:864
  212.1 42.5 %copy-start.23 = (bf16[64,512]{1,0:T(8,128)(2,1)S(1)}, bf16[64,512]{1,0:T(8,128)(2,1)}, u32[]{:S(2)}) copy-start(bf16[64,512]{1,0:T(8,128)(2,1)} %get-tuple-element.156) | copy-start | bytes 196612
  212.1 42.5 %copy-start.24 = (bf16[64,512]{1,0:T(8,128)(2,1)S(1)}, bf16[64,512]{1,0:T(8,128)(2,1)}, u32[]{:S(2)}) copy-start(bf16[64,512]{1,0:T(8,128)(2,1)} %get-tuple-element.157) | copy-start | bytes 196612
  250.6 9.9 %collective-permute-start.11 = (bf16[8,64,256]{2,1,0:T(8,128)(2,1)}, bf16[8,64,256]{2,1,0:T(8,128)(2,1)S(1)}, u32[]{:S(2)}, u32[]{:S(2)}) collective-permute-start(bf16[8,64,256]{2,1,0:T(8,128)(2,1)} %get-tuple-element.108), channel_id=1, source_target_pairs={{0,1},{1,0},{2,3},{3,2},{4,5},{5,4},{6,7},{7,6},{8,9},{9,8},{10,11... | collective-permute-start | bytes 786440 | tf_op jit(solution)/shard_map/ppermute | solution.py:466
  253.1 12.1 %collective-permute-start.12 = (bf16[8,64,256]{2,1,0:T(8,128)(2,1)}, bf16[8,64,256]{2,1,0:T(8,128)(2,1)S(1)}, u32[]{:S(2)}, u32[]{:S(2)}) collective-permute-start(bf16[8,64,256]{2,1,0:T(8,128)(2,1)} %get-tuple-element.109), channel_id=1, source_target_pairs={{0,2},{1,3},{2,0},{3,1},{4,6},{5,7},{6,4},{7,5},{8,10},{9,11},{10,... | collective-permute-start | bytes 786440 | tf_op jit(solution)/shard_map/ppermute | solution.py:466
  254.5 10.6 %collective-permute-start.13 = (bf16[8,64,256]{2,1,0:T(8,128)(2,1)}, bf16[8,64,256]{2,1,0:T(8,128)(2,1)S(1)}, u32[]{:S(2)}, u32[]{:S(2)}) collective-permute-start(bf16[8,64,256]{2,1,0:T(8,128)(2,1)} %get-tuple-element.110), channel_id=1, source_target_pairs={{0,3},{1,2},{2,1},{3,0},{4,7},{5,6},{6,5},{7,4},{8,11},{9,10},{10,... | collective-permute-start | bytes 786440 | tf_op jit(solution)/shard_map/ppermute | solution.py:466
  272.1 31.9 %all-to-all-start.2 = ((bf16[32,128,128]{2,1,0:T(8,128)(2,1)}), bf16[32,128,128]{2,1,0:T(8,128)(2,1)S(1)}, u32[]{:S(2)}, u32[]{:S(2)}) async-start(bf16[32,128,128]{2,1,0:T(8,128)(2,1)} %bitcast.73), calls=%async_computation.2 | async-start | bytes 2097152 | tf_op jit(solution)/shard_map/all_to_all | solution.py:509
  303.9 22.0 %collective-permute-start.14 = (bf16[32,8,256]{2,1,0:T(8,128)(2,1)}, bf16[32,8,256]{2,1,0:T(8,128)(2,1)S(1)}, u32[]{:S(2)}, u32[]{:S(2)}) collective-permute-start(bf16[32,8,256]{2,1,0:T(8,128)(2,1)} %get-tuple-element.123), channel_id=1, source_target_pairs={{0,1},{1,2},{2,3},{3,0},{4,5},{5,6},{6,7},{7,4},{8,9},{9,10},{10,1... | collective-permute-start | bytes 393224 | tf_op jit(solution)/shard_map/ppermute | solution.py:862
  305.3 20.7 %collective-permute-start.15 = (bf16[8,64,256]{2,1,0:T(8,128)(2,1)S(1)}, bf16[8,64,256]{2,1,0:T(8,128)(2,1)S(1)}, u32[]{:S(2)}, u32[]{:S(2)}) collective-permute-start(bf16[8,64,256]{2,1,0:T(8,128)(2,1)S(1)} %copy-done.44), channel_id=1, source_target_pairs={{0,4},{4,8},{8,12},{12,16},{16,20},{20,24},{24,28},{28,0},{1,5},{5... | collective-permute-start | bytes 786440 | tf_op jit(solution)/shard_map/ppermute | solution.py:863
  305.4 20.5 %collective-permute-start.16 = (bf16[8,8,256]{2,1,0:T(8,128)(2,1)S(1)}, bf16[8,8,256]{2,1,0:T(8,128)(2,1)S(1)}, u32[]{:S(2)}, u32[]{:S(2)}) collective-permute-start(bf16[8,8,256]{2,1,0:T(8,128)(2,1)S(1)} %copy-done.45), channel_id=1, source_target_pairs={{0,5},{1,6},{2,7},{3,4},{4,9},{5,10},{6,11},{7,8},{8,13},{9,14},{1... | collective-permute-start | bytes 98312 | tf_op jit(solution)/shard_map/ppermute | solution.py:864
  326.0 31.6 %all-to-all-start.3 = ((bf16[32,128,128]{2,1,0:T(8,128)(2,1)}), bf16[32,128,128]{2,1,0:T(8,128)(2,1)S(1)}, u32[]{:S(2)}, u32[]{:S(2)}) async-start(bf16[32,128,128]{2,1,0:T(8,128)(2,1)} %shard_map.308), calls=%async_computation.3 | async-start | bytes 2097152 | tf_op jit(solution)/shard_map/all_to_all | solution.py:527
  365.0 9.5 %collective-permute-start.17 = (bf16[8,64,256]{2,1,0:T(8,128)(2,1)}, bf16[8,64,256]{2,1,0:T(8,128)(2,1)S(1)}, u32[]{:S(2)}, u32[]{:S(2)}) collective-permute-start(bf16[8,64,256]{2,1,0:T(8,128)(2,1)} %get-tuple-element.132), channel_id=1, source_target_pairs={{0,1},{1,0},{2,3},{3,2},{4,5},{5,4},{6,7},{7,6},{8,9},{9,8},{10,11... | collective-permute-start | bytes 786440 | tf_op jit(solution)/shard_map/ppermute | solution.py:466
  366.4 12.3 %collective-permute-start.18 = (bf16[8,64,256]{2,1,0:T(8,128)(2,1)}, bf16[8,64,256]{2,1,0:T(8,128)(2,1)S(1)}, u32[]{:S(2)}, u32[]{:S(2)}) collective-permute-start(bf16[8,64,256]{2,1,0:T(8,128)(2,1)} %get-tuple-element.133), channel_id=1, source_target_pairs={{0,2},{1,3},{2,0},{3,1},{4,6},{5,7},{6,4},{7,5},{8,10},{9,11},{10,... | collective-permute-start | bytes 786440 | tf_op jit(solution)/shard_map/ppermute | solution.py:466
  367.8 12.4 %collective-permute-start.19 = (bf16[8,64,256]{2,1,0:T(8,128)(2,1)}, bf16[8,64,256]{2,1,0:T(8,128)(2,1)S(1)}, u32[]{:S(2)}, u32[]{:S(2)}) collective-permute-start(bf16[8,64,256]{2,1,0:T(8,128)(2,1)} %get-tuple-element.134), channel_id=1, source_target_pairs={{0,3},{1,2},{2,1},{3,0},{4,7},{5,6},{6,5},{7,4},{8,11},{9,10},{10,... | collective-permute-start | bytes 786440 | tf_op jit(solution)/shard_map/ppermute | solution.py:466
  407.9 10.4 %collective-permute-start.21 = (bf16[8,64,512]{2,1,0:T(8,128)(2,1)}, bf16[8,64,512]{2,1,0:T(8,128)(2,1)S(1)}, u32[]{:S(2)}, u32[]{:S(2)}) collective-permute-start(bf16[8,64,512]{2,1,0:T(8,128)(2,1)} %get-tuple-element.138), channel_id=1, source_target_pairs={{0,28},{4,0},{8,4},{12,8},{16,12},{20,16},{24,20},{28,24},{1,29},{... | collective-permute-start | bytes 1572872 | tf_op jit(solution)/shard_map/ppermute | solution.py:863
  407.9 10.3 %collective-permute-start.20 = (bf16[32,8,512]{2,1,0:T(8,128)(2,1)}, bf16[32,8,512]{2,1,0:T(8,128)(2,1)S(1)}, u32[]{:S(2)}, u32[]{:S(2)}) collective-permute-start(bf16[32,8,512]{2,1,0:T(8,128)(2,1)} %get-tuple-element.137), channel_id=1, source_target_pairs={{0,3},{1,0},{2,1},{3,2},{4,7},{5,4},{6,5},{7,6},{8,11},{9,8},{10,9... | collective-permute-start | bytes 786440 | tf_op jit(solution)/shard_map/ppermute | solution.py:862
  409.9 8.4 %collective-permute-start.22 = (bf16[8,8,512]{2,1,0:T(8,128)(2,1)}, bf16[8,8,512]{2,1,0:T(8,128)(2,1)S(1)}, u32[]{:S(2)}, u32[]{:S(2)}) collective-permute-start(bf16[8,8,512]{2,1,0:T(8,128)(2,1)} %get-tuple-element.139), channel_id=1, source_target_pairs={{0,31},{1,28},{2,29},{3,30},{4,3},{5,0},{6,1},{7,2},{8,7},{9,4},{1... | collective-permute-start | bytes 196616 | tf_op jit(solution)/shard_map/ppermute | solution.py:864
  446.1 10.4 %collective-permute-start.24 = (bf16[8,64,256]{2,1,0:T(8,128)(2,1)}, bf16[8,64,256]{2,1,0:T(8,128)(2,1)S(1)}, u32[]{:S(2)}, u32[]{:S(2)}) collective-permute-start(bf16[8,64,256]{2,1,0:T(8,128)(2,1)} %get-tuple-element.143), channel_id=1, source_target_pairs={{0,4},{4,8},{8,12},{12,16},{16,20},{20,24},{24,28},{28,0},{1,5},{5... | collective-permute-start | bytes 786440 | tf_op jit(solution)/shard_map/ppermute | solution.py:863
  446.2 10.3 %collective-permute-start.23 = (bf16[32,8,256]{2,1,0:T(8,128)(2,1)}, bf16[32,8,256]{2,1,0:T(8,128)(2,1)S(1)}, u32[]{:S(2)}, u32[]{:S(2)}) collective-permute-start(bf16[32,8,256]{2,1,0:T(8,128)(2,1)} %get-tuple-element.142), channel_id=1, source_target_pairs={{0,1},{1,2},{2,3},{3,0},{4,5},{5,6},{6,7},{7,4},{8,9},{9,10},{10,1... | collective-permute-start | bytes 393224 | tf_op jit(solution)/shard_map/ppermute | solution.py:862
  447.7 8.9 %collective-permute-start.25 = (bf16[8,8,256]{2,1,0:T(8,128)(2,1)}, bf16[8,8,256]{2,1,0:T(8,128)(2,1)S(1)}, u32[]{:S(2)}, u32[]{:S(2)}) collective-permute-start(bf16[8,8,256]{2,1,0:T(8,128)(2,1)} %get-tuple-element.144), channel_id=1, source_target_pairs={{0,5},{1,6},{2,7},{3,4},{4,9},{5,10},{6,11},{7,8},{8,13},{9,14},{1... | collective-permute-start | bytes 98312 | tf_op jit(solution)/shard_map/ppermute | solution.py:864
  (44 other events, 480.4 us)

commit v5 on v4

--- a/solution.py
+++ b/solution.py
@@ -20,6 +20,7 @@
 SPAN = WIN * WIN
 LANES = 128
 GROUP = 8
+HEIGHT = 2 * WIN
 TOK = N // PATCH
 
 SIGMAS = (0.8, 0.5, 0.3)
@@ -505,13 +506,14 @@
     if halved:
         sent, mirror, shift = lax.optimization_barrier((sent, mirror, shift))
         extra = (middle.astype(jnp.int32).reshape(1), phase_table(shift[0], devices, slab))
-        away = (inner, mirrored_weight(scale, *mirror), inner_t, outer_t)
+        table = mirrored_weight(scale, *mirror)
     moved = lax.all_to_all(
         sent.reshape(part), ("ty", "tx"), split_axis=0, concat_axis=0, tiled=True
     )
     if halved:
-        moved, beside = lax.optimization_barrier((moved, beside))
+        moved, table, beside = lax.optimization_barrier((moved, table, beside))
         beside = from_neighbours(beside, 1)
+        away = (inner, table, inner_t, outer_t)
     spaces = [pltpu.SMEM, pltpu.VMEM][: len(extra)] + [pltpu.VMEM] * 2 + [pl.ANY] * len(away)
     wave = pl.pallas_call(
         functools.partial(column_kernel, halved),
@@ -650,10 +652,20 @@
     return flow + 0.5 * mm(active_ref[...], down_ref[...])
 
 
-def rolled_band(sign, shift_ref, refs, rows, count=WIN):
-    main_ref, side_ref, edge_ref, corner_ref = refs
-    cols = main_ref.shape[1]
-    top = pl.program_id(0) * count + sign * shift_ref[0]
+def row_of(refs, row):
+    size = refs[0].shape[0]
+    value = refs[-1][jnp.clip(row - size * (len(refs) - 1), 0, size - 1)]
+    for n in range(len(refs) - 2, -1, -1):
+        here = refs[n][jnp.clip(row - size * n, 0, size - 1)]
+        value = jnp.where(row < size * (n + 1), here, value)
+    return value
+
+
+def rolled_band(sign, top, shift_ref, refs, rows, count):
+    *refs, edge_ref, corner_ref = refs
+    main_refs, side_refs = refs[: len(refs) // 2], refs[len(refs) // 2 :]
+    cols = main_refs[0].shape[1]
+    top = top + sign * shift_ref[0]
     behind = -rows if sign > 0 else WIN
     beside = -cols if sign > 0 else WIN
 
@@ -667,34 +679,37 @@
     for j in range(count):
         row = top + j
         inside = (row >= 0) & (row < rows)
-        here, there = jnp.clip(row, 0, rows - 1), jnp.clip(row + behind, 0, WIN - 1)
-        main = jnp.where(inside, main_ref[here], edge_ref[there])
-        side = jnp.where(inside, side_ref[here], corner_ref[there])
+        there = jnp.clip(row + behind, 0, WIN - 1)
+        main = jnp.where(inside, row_of(main_refs, row), edge_ref[there])
+        side = jnp.where(inside, row_of(side_refs, row), corner_ref[there])
         band.append(mm(pick_main, main) + mm(pick_side, side))
     return jnp.stack(band)
 
 
-def first_kernel(zeta, sigma, count, parts, rows, before, *refs):
+def first_kernel(begin, zeta, sigma, count, parts, rows, before, backs, *refs):
     shift_ref, state_ref, *refs = refs
     if before is not None:
-        back_refs, refs = refs[:4], refs[4:]
+        back_refs, refs = refs[:backs], refs[backs:]
     grad_refs, refs = refs[: count * parts], refs[count * parts :]
     if sigma is not None:
         noise_ref, *refs = refs
     bias_ref, embed_ref, gain_ref, *sources = refs[:7]
-    base_ref, out_ref, side_ref, edge_ref, corner_ref, *scratch = refs[7:]
+    base_ref, out_ref, side_ref, *scratch = refs[7:]
+    if begin == 0:
+        edge_ref, corner_ref, *scratch = scratch
     targets, sems, scratch = scratch[:4], scratch[4], scratch[5:]
     wait = load_weights(0, sources, targets, sems)
     state = state_ref[...]
     if before is not None:
-        state = state - before * rolled_band(-1, shift_ref, back_refs, rows, state.shape[0])
+        top = begin * state.shape[0]
+        state = state - before * rolled_band(-1, top, shift_ref, back_refs, rows, state.shape[0])
     height = state.shape[0]
     if parts == 1:
         grad = grad_refs[0][...].astype(F32)
     else:
         bands = []
         for k in range(height // WIN):
-            turn = (pl.program_id(0) * (height // WIN) + k) ^ shift_ref[2]
+            turn = (begin * (height // WIN) + k) ^ shift_ref[2]
             band = 0.0
             for n in range(0, count * parts, parts):
                 piece = grad_refs[n][...]
@@ -719,8 +734,7 @@
         out_ref[:, :, D:] = change
         side_ref[:, :, D:] = change[:, :WIN]
 
-    @pl.when(pl.program_id(0) == 0)
-    def _():
+    if begin == 0:
         edge_ref[...] = out_ref[:WIN]
         corner_ref[...] = side_ref[:WIN]
 
@@ -734,28 +748,32 @@
         pl.when(turn == m)(write)
 
 
-def second_kernel(sigma, rows, parts, *refs):
+def second_kernel(begin, edged, sigma, rows, tiles, parts, *refs):
     shift_ref, *refs = refs
-    tile_refs, refs = refs[:4], refs[4:]
+    tile_refs, refs = refs[:tiles], refs[tiles:]
     bias_ref, unembed_ref, gain_ref, *sources = refs[:7]
-    out_ref, side_ref, edge_ref, corner_ref, *scratch = refs[7:]
+    out_ref, side_ref, *scratch = refs[7:]
+    if edged:
+        edge_ref, corner_ref, *scratch = scratch
     state_refs, scratch = scratch[:parts], scratch[parts:]
     targets, sems, scratch = scratch[:4], scratch[4], scratch[5:]
     wait = load_weights(1, sources, targets, sems)
     height, cols, _ = out_ref.shape
-    band = rolled_band(1, shift_ref, tile_refs, rows, height)
+    here = pl.program_id(0) + begin
+    band = rolled_band(1, here * height, shift_ref, tile_refs, rows, height)
     tokens = to_windows(band[:, :, :D])
     flow = swin_band(tokens, wait, bias_ref, gain_ref, targets, scratch)
     estimate = from_windows(mm(flow.astype(BF16), unembed_ref[...]), cols)
     narrow = estimate.astype(BF16)
     out_ref[...] = narrow
     side_ref[...] = narrow[:, cols - WIN :]
-    edge_ref[...] = narrow[height - WIN :]
-    corner_ref[...] = narrow[height - WIN :, cols - WIN :]
+    if edged:
+        edge_ref[...] = narrow[height - WIN :]
+        corner_ref[...] = narrow[height - WIN :, cols - WIN :]
     if parts > 0:
         change = (band[:, :, D:] - sigma * estimate).astype(BF16)
         for n in range(height // WIN):
-            turn = (pl.program_id(0) * (height // WIN) + n) ^ shift_ref[2]
+            turn = (here * (height // WIN) + n) ^ shift_ref[2]
             write_pieces(turn, state_refs, change[n * WIN : (n + 1) * WIN])
 
 
@@ -769,82 +787,93 @@
     return pl.BlockSpec((None,) + array.shape[1:], lambda *_: place)
 
 
-def band_spec(cols, feats, height=WIN):
-    return pl.BlockSpec((height, cols, feats), lambda n, *_: (n, 0, 0))
-
-
-def bias_spec(cols, height=WIN):
+def band_spec(cols, feats, height=WIN, begin=0):
+    return pl.BlockSpec((height, cols, feats), lambda n, *_: (n + begin, 0, 0))
+
+
+def bias_spec(cols, height, begin):
     count = height * cols // SPAN
-    return pl.BlockSpec((count, SPAN, 2 * SPAN), lambda n, *_: (n, 0, 0))
-
-
-def band_scratch(cols, weights, height=WIN):
+    return pl.BlockSpec((count, SPAN, 2 * SPAN), lambda n, *_: (n + begin, 0, 0))
+
+
+def band_scratch(cols, weights, height):
     count = height * cols // SPAN
     return [pltpu.VMEM(value.shape[1:], BF16) for value in weights] + [
         pltpu.SemaphoreType.DMA((len(weights),)),
         pltpu.VMEM((height * cols, 3 * D), BF16),
         pltpu.VMEM((count, SPAN, HEADS * SPAN), F32),
         pltpu.VMEM((count, SPAN, HEADS * SPAN), BF16),
+        pltpu.VMEM((height * cols, weights[2].shape[2]), BF16),
     ]
 
 
-def strip_outs(rows, cols, feats, height=WIN):
+def strip_outs(rows, cols, feats, height, edged):
     specs = [band_spec(cols, feats, height), band_spec(WIN, feats, height)]
-    specs += [
-        pl.BlockSpec((WIN, width, feats), lambda *_: (0, 0, 0)) for width in (cols, WIN)
-    ]
-    shapes = [(rows, cols), (rows, WIN), (WIN, cols), (WIN, WIN)]
+    shapes = [(rows, cols), (rows, WIN)]
+    if edged:
+        specs += [
+            pl.BlockSpec((WIN, width, feats), lambda *_: (0, 0, 0)) for width in (cols, WIN)
+        ]
+        shapes += [(WIN, cols), (WIN, WIN)]
     return specs, [jax.ShapeDtypeStruct(shape + (feats,), BF16) for shape in shapes]
 
 
-def first_block(zeta, sigma, state, before, shift, back, grads, noise, bias, w_embed, weights):
+def flat(tile):
+    return [*tile[0], *tile[1], *tile[2:]]
+
+
+def first_block(
+    begin, rows, zeta, sigma, state, before, shift, back, grads, noise, bias, w_embed, weights
+):
     *weights, gains = weights
-    rows, cols, _ = state.shape
+    height, cols = HEIGHT, state.shape[1]
     parts = len(grads[0])
     pieces = [piece for grad in grads for piece in grad]
     fields = [] if sigma is None else [noise]
     feats = D if sigma is None else D + PIXELS
-    height = 2 * WIN
-    specs, shapes = strip_outs(rows, cols, feats, height)
-    band = band_spec(cols, PIXELS, height)
+    specs, shapes = strip_outs(height, cols, feats, height, begin == 0)
+    back = flat(back) if back else []
+    band = band_spec(cols, PIXELS, height, begin)
+    alone = band_spec(cols, PIXELS, height)
     return pl.pallas_call(
-        functools.partial(first_kernel, zeta, sigma, len(grads), parts, rows, before),
+        functools.partial(
+            first_kernel, begin, zeta, sigma, len(grads), parts, rows, before, len(back)
+        ),
         grid_spec=pltpu.PrefetchScalarGridSpec(
             num_scalar_prefetch=1,
-            grid=(rows // height,),
-            in_specs=[band]
+            grid=(1,),
+            in_specs=[alone if state.shape[0] == height else band]
             + [whole(value) for value in back]
             + [band if parts == 1 else whole(value) for value in pieces]
             + [band] * len(fields)
-            + [bias_spec(cols, height), whole(w_embed), member(gains, 0)]
+            + [bias_spec(cols, height, begin), whole(w_embed), member(gains, 0)]
             + [pl.BlockSpec(memory_space=pl.ANY)] * len(weights),
-            out_specs=[band] + specs,
-            scratch_shapes=band_scratch(cols, weights, height)
-            + [pltpu.VMEM((height * cols, weights[2].shape[2]), BF16)],
+            out_specs=[alone] + specs,
+            scratch_shapes=band_scratch(cols, weights, height),
         ),
-        out_shape=[jax.ShapeDtypeStruct((rows, cols, PIXELS), F32)] + shapes,
+        out_shape=[jax.ShapeDtypeStruct((height, cols, PIXELS), F32)] + shapes,
         compiler_params=PARAMS,
     )(shift, state, *back, *pieces, *fields, bias, w_embed, gains, *weights)
 
 
-def second_block(sigma, shift, tile, bias, w_unembed, weights, parts):
+def second_block(begin, steps, rows, sigma, shift, tile, bias, w_unembed, weights, parts):
     *weights, gains = weights
-    rows, cols, _ = tile[0].shape
-    height = 2 * WIN
-    specs, shapes = strip_outs(rows, cols, PIXELS, height)
+    height, cols = HEIGHT, tile[0][0].shape[1]
+    tile = flat(tile)
+    edged = (begin + steps) * height == rows
+    specs, shapes = strip_outs(steps * height, cols, PIXELS, height, edged)
     specs += [pl.BlockSpec((WIN, cols, PIXELS), lambda *_: (0, 0, 0))] * parts
     shapes += [jax.ShapeDtypeStruct((WIN, cols, PIXELS), BF16)] * parts
     return pl.pallas_call(
-        functools.partial(second_kernel, sigma, rows, parts),
+        functools.partial(second_kernel, begin, edged, sigma, rows, len(tile), parts),
         grid_spec=pltpu.PrefetchScalarGridSpec(
             num_scalar_prefetch=1,
-            grid=(rows // height,),
+            grid=(steps,),
             in_specs=[whole(value) for value in tile]
-            + [bias_spec(cols, height), whole(w_unembed), member(gains, 1)]
+            + [bias_spec(cols, height, begin), whole(w_unembed), member(gains, 1)]
             + [pl.BlockSpec(memory_space=pl.ANY)] * len(weights),
             out_specs=specs,
-            scratch_shapes=band_scratch(cols, weights, height)
-            + [pltpu.VMEM((height * cols, weights[2].shape[2]), BF16)],
+            scratch_shapes=band_scratch(cols, weights, height),
         ),
         out_shape=shapes,
         compiler_params=PARAMS,
@@ -852,15 +881,15 @@
 
 
 def from_neighbours(tile, by):
-    main, side, edge, corner = tile
+    mains, sides, edge, corner = tile
     ty, tx = lax.axis_size("ty"), lax.axis_size("tx")
-    across = [
-        (i * tx + k, (i + by) % ty * tx + (k + by) % tx) for i in range(ty) for k in range(tx)
-    ]
+    down = [(i, (i + by) % ty) for i in range(ty)]
+    along = [(k, (k + by) % tx) for k in range(tx)]
+    across = [(i * tx + k, i_to * tx + k_to) for i, i_to in down for k, k_to in along]
     return (
-        main,
-        lax.ppermute(side, "tx", [(k, (k + by) % tx) for k in range(tx)]),
-        lax.ppermute(edge, "ty", [(i, (i + by) % ty) for i in range(ty)]),
+        mains,
+        [lax.ppermute(side, "tx", along) for side in sides],
+        lax.ppermute(edge, "ty", down),
         lax.ppermute(corner, ("ty", "tx"), across),
     )
 
@@ -932,14 +961,19 @@
         write_pieces(pl.program_id(0) ^ place_ref[0], out_refs, result)
 
 
-def to_tile_kernel(sigma, scale, rows, *refs):
-    shift_ref, base_ref, *refs = refs
-    noise_ref, order_ref, out_ref = refs[4:]
-    count, cols, _ = base_ref.shape
+def to_tile_kernel(sigma, scale, rows, bases, *refs):
+    shift_ref, *refs = refs
+    base_refs, refs = refs[:bases], refs[bases:]
+    *back_refs, noise_ref, order_ref, out_ref = refs
+    count, cols, _ = base_refs[0].shape
+    here = pl.program_id(0)
+    base = base_refs[0][...]
+    for n in range(1, bases):
+        base = jnp.where(here * count < n * (rows // bases), base, base_refs[n][...])
     parts = LANES // cols
     groups = PATCH // parts
     width = groups * PATCH
-    state = base_ref[...] - sigma * rolled_band(-1, shift_ref, refs[:4], rows)
+    state = base - sigma * rolled_band(-1, here * count, shift_ref, back_refs, rows, count)
     bands = []
     for i in range(count):
         stacked = jnp.concatenate(
@@ -976,15 +1010,23 @@
     )(place, tiles, order)
 
 
-def tile_of(base, sigma, shift, back, scale, noise, j):
-    rows, cols, _ = base.shape
+def tile_of(bases, sigma, shift, back, scale, noise, j):
+    size, cols, _ = bases[0].shape
+    rows, steps = size * len(bases), size // WIN
     order = jnp.asarray(lane_order(cols)[1])
+    back = flat(back)
+
+    def part(m):
+        return pl.BlockSpec(
+            (WIN, cols, PIXELS), lambda n, *_: (jnp.clip(n - m * steps, 0, steps - 1), 0, 0)
+        )
+
     return pl.pallas_call(
-        functools.partial(to_tile_kernel, sigma, scale, rows),
+        functools.partial(to_tile_kernel, sigma, scale, rows, len(bases)),
         grid_spec=pltpu.PrefetchScalarGridSpec(
             num_scalar_prefetch=1,
             grid=(rows // WIN,),
-            in_specs=[band_spec(cols, PIXELS)]
+            in_specs=[part(m) for m in range(len(bases))]
             + [whole(value) for value in back]
             + [
                 pl.BlockSpec((None, WIN * PATCH, cols * PATCH), lambda n, *_: (j, n, 0)),
@@ -994,7 +1036,7 @@
         ),
         out_shape=jax.ShapeDtypeStruct((rows * PATCH, cols * PATCH), F32),
         compiler_params=PARAMS,
-    )(shift, base, *back, noise, order)
+    )(shift, *bases, *back, noise, order)
 
 
 def per_device(
@@ -1024,7 +1066,8 @@
         )
         biases.append(bias_of(labels, None))
     beside = (state, extras, first_bias, biases, w_embed, w_unembed)
-    shift, before, back, moving, mirror = places[0], None, (), None, None
+    shift, before, back, moving, mirror = places[0], None, None, None, None
+    halves = rows // HEIGHT
     grads = []
     if fast:
         weight, scale, data = spectrum_inputs(gains, observed, vis_weight, devices)
@@ -1038,6 +1081,7 @@
         mirror = mirrored_exchange(*lines, devices)
         grads = [grad]
         state, extras, first_bias, biases, w_embed, w_unembed = beside
+    state = [state] * halves
     for step in range(STEPS):
         if not fast:
             tile = image if step == 0 else tile_of(state, before, shift, back, 0.0, noise, 0)
@@ -1049,18 +1093,28 @@
             grads = grads + [grad]
         last = step + 1 == STEPS
         sigma = None if last else SIGMAS[step + 1]
-        state, *first = first_block(
-            STEP_SIZES[step], sigma, state, before, shift, back, grads, extras[step], first_bias,
-            w_embed, weights,
-        )
+        blocks = [
+            first_block(
+                m, rows, STEP_SIZES[step], sigma, state[m], before, shift, back, grads,
+                extras[step], first_bias, w_embed, weights,
+            )
+            for m in range(halves)
+        ]
+        state, mains, sides = zip(*(block[:3] for block in blocks))
         shift, before = places[step], SIGMAS[step]
         if fast and step == 0:
-            first, mirror = lax.optimization_barrier((first, mirror))
-        rolled = second_block(
-            before, shift, from_neighbours(first, -1), biases[step], w_unembed, weights,
-            lanes if fast and not last else 0,
-        )
-        back, moving = rolled[:4], rolled[4:]
+            sides, mirror = lax.optimization_barrier((sides, mirror))
+        first = from_neighbours((mains, sides, *blocks[0][3:]), -1)
+        spans = [(m, 1) for m in range(halves)] if last else [(0, halves)]
+        rolled = [
+            second_block(
+                m, steps, rows, before, shift, first, biases[step], w_unembed, weights,
+                lanes if fast and not last else 0,
+            )
+            for m, steps in spans
+        ]
+        back = ([part[0] for part in rolled], [part[1] for part in rolled], *rolled[-1][2:4])
+        moving = rolled[-1][4:]
         if last or not fast:
             back = from_neighbours(back, 1)
     return tile_of(state, before, shift, back, SIGMAS[STEPS], noise, STEPS - 1)

time: 474 us -> 490 us (1.034)
  Pallas kernels: 191 us -> 204 us
    pallas_call x5 -> x8, Pallas kernels: 118 us -> 131 us  [the longest x4 62.2 us: first_block(): pl.pallas_call(functools.partial(first_kernel, begin, zeta, sigma, len(gr...]
    ppermute x1, waiting for transfers between devices: 0.01 us -> 12.6 us  [mirrored_exchange(): line = lax.ppermute(line, ('ty', 'tx'), partner)]
    ppermute x4, waiting for transfers between devices: 21.6 us -> 14.9 us  [from_neighbours(): lax.ppermute(corner, ('ty', 'tx'), across)]
    all_to_all x2, waiting for transfers between devices: 41.3 us -> 34.8 us  [patch_gradient(): lax.all_to_all(sent.reshape(part), ('ty', 'tx'), split_axis=0, concat_axi...]
    all_to_all x2, starting transfers between devices: 10.5 us -> 16 us  [patch_gradient(): lax.all_to_all(sent.reshape(part), ('ty', 'tx'), split_axis=0, concat_axi...]
    ppermute x8 -> x11, starting transfers between devices: 11.5 us -> 8.81 us  [the longest x7 6.96 us: from_neighbours(): lax.ppermute(side, 'tx', along)]
    unnamed x98 -> x116, local copies, waits for them, and re-layouts: 22.8 us -> 22.5 us
  transfers between devices with their start and end apart: 30 -> 33, of which waited for: 17 -> 19; matrix products, arithmetic and copies ran while one was open for 12% -> 12% of each run, Pallas kernels for 12% -> 16%
where the time goes in v5:
time: 490 us; the launch traced here: 482 us
  Pallas kernels  204 us (42%)
  waiting for transfers between devices  148 us (30%)
  starting transfers between devices  56.2 us (11%)
  local copies, waits for them, and re-layouts  51 us (10%)
  other arithmetic  16.8 us (3%)
  between operations  5.73 us (1%)
    pallas_call x4, Pallas kernels, first_block(): pl.pallas_call(functools.partial(first_kernel, begin, zeta, sigma, len(gr...  62.2 us
    pallas_call x3, Pallas kernels, second_block(): pl.pallas_call(functools.partial(second_kernel, begin, edged, sigma, rows...  59.9 us
    all_to_all x2, waiting for transfers between devices, patch_gradient(): lax.all_to_all(wave, ('ty', 'tx'), split_axis=0, concat_axis=0, tiled=True)  42.9 us
    ppermute x12, waiting for transfers between devices, swap_pieces(): lax.ppermute(pieces[m], 'tx', [(k, k ^ m) for k in range(lanes)])  38.3 us
    all_to_all x2, waiting for transfers between devices, patch_gradient(): lax.all_to_all(sent.reshape(part), ('ty', 'tx'), split_axis=0, concat_axi...  34.8 us
    pallas_call x2, Pallas kernels, patch_gradient(): pl.pallas_call(functools.partial(column_kernel, halved), in_specs=[pl.Blo...  23.4 us
    unnamed x116, local copies, waits for them, and re-layouts  22.5 us
    pallas_call x3, Pallas kernels, patches_of(): pl.pallas_call(functools.partial(to_patches_kernel, kind == BF16), grid_s...  18.7 us
  transfers between devices with their start and end apart: 33, of which 19 were waited for; matrix products, arithmetic and copies ran while one was open for 12% of the time, Pallas kernels for 16%

profile of v5, /device:TPU:0, one launch (start us, length us, event | category | flops | bytes accessed | tf_op | source)
XLA Modules:
  0.0 481.7 jit_solution(12921889166582684480)
XLA Ops:
  0.0 5.7 %shard_map.298 = (bf16[8,64,256]{2,1,0:T(8,128)(2,1)}, bf16[8,64,256]{2,1,0:T(8,128)(2,1)}, bf16[8,64,256]{2,1,0:T(8,128)(2,1)}, bf16[8,64,256]{2,1,0:T(8,128)(2,1)}) custom-call(s32[1]{0:T(128)} %bitcast.1.place_ref, f32[1,512,1024]{2,1,0:T(8,128)} %bitcast.67, bf16[1024,1024]{1,0:T(8,128)(2,1)} %constant.98.clone.order_ref), custom_call_target="tpu_custom_call" | custom-call | tf_op jit(solution)/shard_map/pallas_call | solution.py:997
  16.0 6.3 %collective-permute-done.1.refs_2_ = bf16[8,64,256]{2,1,0:T(8,128)(2,1)S(1)} collective-permute-done((bf16[8,64,256]{2,1,0:T(8,128)(2,1)}, bf16[8,64,256]{2,1,0:T(8,128)(2,1)S(1)}, u32[]{:S(2)}, u32[]{:S(2)}) %collective-permute-start.1) | collective-permute-done | bytes 262176 | tf_op jit(solution)/shard_map/ppermute | solution.py:467
  23.1 5.8 %shard_map.299 = bf16[16,2,2,128,128]{4,3,2,1,0:T(8,128)(2,1)} custom-call(bf16[8,64,256]{2,1,0:T(8,128)(2,1)} %get-tuple-element.82.refs_0_, bf16[8,64,256]{2,1,0:T(8,128)(2,1)} %copy-done.18, bf16[8,64,256]{2,1,0:T(8,128)(2,1)} %copy-done.19, bf16[8,64,256]{2,1,0:T(8,128)(2,1)} %copy-done.20, bf16[256,512]{1,0:T(8,128)(2,1)} %pad_maximum_fusion.5.refs_4_.first_ref, ...), custom_call_target="tpu_custom_call" | custom-call | tf_op jit(solution)/shard_map/pallas_call | solution.py:503
  28.8 5.1 %all-to-all-start = ((bf16[32,2,128,128]{3,2,1,0:T(8,128)(2,1)}), bf16[32,2,128,128]{3,2,1,0:T(8,128)(2,1)}, u32[]{:S(2)}, u32[]{:S(2)}) async-start(bf16[32,2,128,128]{3,2,1,0:T(8,128)(2,1)} %bitcast.70), calls=%async_computation | async-start | bytes 4194304 | tf_op jit(solution)/shard_map/all_to_all | solution.py:510
  64.9 17.7 %all-to-all-done.refs_0_ = bf16[32,2,128,128]{3,2,1,0:T(8,128)(2,1)} async-done(((bf16[32,2,128,128]{3,2,1,0:T(8,128)(2,1)}), bf16[32,2,128,128]{3,2,1,0:T(8,128)(2,1)}, u32[]{:S(2)}, u32[]{:S(2)}) %all-to-all-start) | async-done | bytes 2097184 | tf_op jit(solution)/shard_map/all_to_all | solution.py:510
  82.6 12.4 %shard_map.300 = bf16[32,2,128,128]{3,2,1,0:T(8,128)(2,1)} custom-call(bf16[32,2,128,128]{3,2,1,0:T(8,128)(2,1)} %all-to-all-done.refs_0_, bf16[512,512]{1,0:T(8,128)(2,1)} %constant.99.clone.refs_1_.refs_3_, bf16[32,256,256]{2,1,0:T(8,128)(2,1)} %constant.101.clone.refs_2_.refs_4_, bf16[32,128,128]{2,1,0:T(8,128)(2,1)} %bitcast.65, ...), custom_call_target="tpu_custom_call" | custom-call | tf_op jit(solution)/shard_map/pallas_call | solution.py:518
  99.6 6.5 %shard_map.301.refs_1_ = f32[32,64,256]{2,1,0:T(8,128)} custom-call(s32[1]{0:T(128)} %bitcast.1.place_ref, f32[1,512,1024]{2,1,0:T(8,128)} %bitcast.68, bf16[1024,1024]{1,0:T(8,128)(2,1)} %constant.98.clone.order_ref), custom_call_target="tpu_custom_call" | custom-call | tf_op jit(solution)/shard_map/pallas_call | solution.py:997
  110.8 6.5 %shard_map.302.refs_6_ = f32[32,64,256]{2,1,0:T(8,128)} custom-call(s32[1]{0:T(128)} %bitcast.1.place_ref, f32[2,512,1024]{2,1,0:T(8,128)} %refs_9_.11, bf16[1024,1024]{1,0:T(8,128)(2,1)} %constant.98.clone.order_ref), custom_call_target="tpu_custom_call" | custom-call | tf_op jit(solution)/shard_map/pallas_call | solution.py:997
  131.1 17.2 %all-to-all-done.1 = bf16[32,2,128,128]{3,2,1,0:T(8,128)(2,1)S(1)} async-done(((bf16[32,2,128,128]{3,2,1,0:T(8,128)(2,1)}), bf16[32,2,128,128]{3,2,1,0:T(8,128)(2,1)S(1)}, u32[]{:S(2)}, u32[]{:S(2)}) %all-to-all-start.1) | async-done | bytes 2097184 | tf_op jit(solution)/shard_map/all_to_all | solution.py:529
  149.6 7.4 %shard_map.303 = (bf16[8,64,256]{2,1,0:T(8,128)(2,1)}, bf16[8,64,256]{2,1,0:T(8,128)(2,1)}, bf16[8,64,256]{2,1,0:T(8,128)(2,1)}, bf16[8,64,256]{2,1,0:T(8,128)(2,1)}) custom-call(bf16[16,2,2,128,128]{4,3,2,1,0:T(8,128)(2,1)} %bitcast.69, bf16[256,512]{1,0:T(8,128)(2,1)} %pad_maximum_fusion.5.refs_4_.first_ref, ...), custom_call_target="tpu_custom_call" | custom-call | tf_op jit(solution)/shard_map/pallas_call | solution.py:532
  166.4 5.5 %collective-permute-done.4.refs_4_.refs_8_ = bf16[8,64,256]{2,1,0:T(8,128)(2,1)S(1)} collective-permute-done((bf16[8,64,256]{2,1,0:T(8,128)(2,1)}, bf16[8,64,256]{2,1,0:T(8,128)(2,1)S(1)}, u32[]{:S(2)}, u32[]{:S(2)}) %collective-permute-start.4) | collective-permute-done | bytes 262176 | tf_op jit(solution)/shard_map/ppermute | solution.py:467
  172.7 15.8 %shard_map.304 = (f32[16,64,256]{2,1,0:T(8,128)}, bf16[16,64,768]{2,1,0:T(8,128)(2,1)}, bf16[16,8,768]{2,1,0:T(8,128)(2,1)}, bf16[8,64,768]{2,1,0:T(8,128)(2,1)}, bf16[8,8,768]{2,1,0:T(8,128)(2,1)}) custom-call(s32[3]{0:T(128)} %pad_add_fusion.1.refs_0_, f32[32,64,256]{2,1,0:T(8,128)} %shard_map.301.refs_1_, ...), custom_call_target="tpu_custom_call" | custom-call | tf_op jit(solution)/shard_map/pallas_call | solution.py:838
  193.9 15.6 %shard_map.305 = (f32[16,64,256]{2,1,0:T(8,128)}, bf16[16,64,768]{2,1,0:T(8,128)(2,1)}, bf16[16,8,768]{2,1,0:T(8,128)(2,1)}) custom-call(s32[3]{0:T(128)} %pad_add_fusion.1.refs_0_, f32[32,64,256]{2,1,0:T(8,128)} %shard_map.301.refs_1_, bf16[8,64,256]{2,1,0:T(8,128)(2,1)} %get-tuple-element.94.refs_2_.refs_6_, bf16[8,64,256]{2,1,0:T(8,128)(2,1)} %copy-done.1, ...), custom_call_target="tpu_custom_call" | custom-call | tf_op jit(solution)/shard_map/pallas_call | solution.py:838
  209.5 12.6 %collective-permute-done.7 = bf16[1,4096]{1,0:T(2,128)(2,1)S(1)} collective-permute-done((bf16[1,4096]{1,0:T(2,128)(2,1)S(1)}, bf16[1,4096]{1,0:T(2,128)(2,1)S(1)}, u32[]{:S(2)}, u32[]{:S(2)}) %collective-permute-start.7) | collective-permute-done | bytes 8224 | tf_op jit(solution)/shard_map/ppermute | solution.py:429
  232.7 28.5 %shard_map.306 = (bf16[32,64,256]{2,1,0:T(8,128)(2,1)}, bf16[32,8,256]{2,1,0:T(8,128)(2,1)}, bf16[8,64,256]{2,1,0:T(8,128)(2,1)}, bf16[8,8,256]{2,1,0:T(8,128)(2...) custom-call(s32[3]{0:T(128)} %pad_add_fusion.1.refs_0_, ...), custom_call_target="tpu_custom_call" | custom-call | tf_op jit(solution)/shard_map/pallas_call | solution.py:867
  265.4 5.2 %collective-permute-done.12.refs_1_ = bf16[8,64,256]{2,1,0:T(8,128)(2,1)S(1)} collective-permute-done((bf16[8,64,256]{2,1,0:T(8,128)(2,1)}, bf16[8,64,256]{2,1,0:T(8,128)(2,1)S(1)}, u32[]{:S(2)}, u32[]{:S(2)}) %collective-permute-start.12) | collective-permute-done | bytes 262176 | tf_op jit(solution)/shard_map/ppermute | solution.py:467
  274.9 6.2 %shard_map.307 = bf16[16,2,128,128]{3,2,1,0:T(8,128)(2,1)} custom-call(bf16[8,64,256]{2,1,0:T(8,128)(2,1)} %get-tuple-element.114.refs_0_, bf16[8,64,256]{2,1,0:T(8,128)(2,1)} %copy-done.29, bf16[8,64,256]{2,1,0:T(8,128)(2,1)} %copy-done.30, bf16[8,64,256]{2,1,0:T(8,128)(2,1)} %copy-done.31, bf16[256,512]{1,0:T(8,128)(2,1)} %pad_maximum_fusion.6.refs_4_, ...), custom_call_target="tpu_custom_call" | custom-call | tf_op jit(solution)/shard_map/pallas_call | solution.py:503
  281.1 11.0 %all-to-all-start.2 = ((bf16[32,128,128]{2,1,0:T(8,128)(2,1)}), bf16[32,128,128]{2,1,0:T(8,128)(2,1)S(1)}, u32[]{:S(2)}, u32[]{:S(2)}) async-start(bf16[32,128,128]{2,1,0:T(8,128)(2,1)} %bitcast.77), calls=%async_computation.2 | async-start | bytes 2097152 | tf_op jit(solution)/shard_map/all_to_all | solution.py:510
  296.0 5.4 %shard_map.308.refs_5_ = bf16[32,128,128]{2,1,0:T(8,128)(2,1)} custom-call(bf16[32,128,128]{2,1,0:T(8,128)(2,1)} %bitcast.66, bf16[32,128,128]{2,1,0:T(8,128)(2,1)} %bitcast.75, bf16[2,128,128]{2,1,0:T(8,128)(2,1)} %add_convert_fusion.pick_ref, bf16[2,128,128]{2,1,0:T(8,128)(2,1)} %constant.113.clone.flip_ref), custom_call_target="tpu_custom_call" | custom-call | tf_op jit(solution)/shard_map/pallas_call | solution.py:448
  301.4 17.1 %all-to-all-done.2.refs_2_ = bf16[32,128,128]{2,1,0:T(8,128)(2,1)S(1)} async-done(((bf16[32,128,128]{2,1,0:T(8,128)(2,1)}), bf16[32,128,128]{2,1,0:T(8,128)(2,1)S(1)}, u32[]{:S(2)}, u32[]{:S(2)}) %all-to-all-start.2) | async-done | bytes 1048608 | tf_op jit(solution)/shard_map/all_to_all | solution.py:510
  322.2 11.0 %shard_map.309 = bf16[32,128,128]{2,1,0:T(8,128)(2,1)} custom-call(s32[1]{0:T(128)} %bitcast.28.refs_0_, f32[32,2,8,128]{3,2,1,0:T(8,128)} %broadcast_in_dim.79.refs_1_, bf16[32,128,128]{2,1,0:T(8,128)(2,1)} %copy-done.4, bf16[512,512]{1,0:T(8,128)(2,1)} %constant.99.clone.refs_1_.refs_3_, bf16[32,256,256]{2,1,0:T(8,128)(2,1)} %constant.101.clone.refs_2_.refs_4_, ...), custom_call_target="tpu_custom_call" | custom-call | tf_op jit(solution)/shard_map/pallas_call | solution.py:518
  333.3 5.2 %all-to-all-start.3 = ((bf16[32,128,128]{2,1,0:T(8,128)(2,1)}), bf16[32,128,128]{2,1,0:T(8,128)(2,1)S(1)}, u32[]{:S(2)}, u32[]{:S(2)}) async-start(bf16[32,128,128]{2,1,0:T(8,128)(2,1)} %shard_map.309), calls=%async_computation.3 | async-start | bytes 2097152 | tf_op jit(solution)/shard_map/all_to_all | solution.py:529
  339.3 25.7 %all-to-all-done.3 = bf16[32,128,128]{2,1,0:T(8,128)(2,1)S(1)} async-done(((bf16[32,128,128]{2,1,0:T(8,128)(2,1)}), bf16[32,128,128]{2,1,0:T(8,128)(2,1)S(1)}, u32[]{:S(2)}, u32[]{:S(2)}) %all-to-all-start.3) | async-done | bytes 1048608 | tf_op jit(solution)/shard_map/all_to_all | solution.py:529
  365.9 6.4 %shard_map.310 = (bf16[8,64,256]{2,1,0:T(8,128)(2,1)}, bf16[8,64,256]{2,1,0:T(8,128)(2,1)}, bf16[8,64,256]{2,1,0:T(8,128)(2,1)}, bf16[8,64,256]{2,1,0:T(8,128)(2,1)}) custom-call(bf16[16,2,128,128]{3,2,1,0:T(8,128)(2,1)} %bitcast.78, bf16[256,512]{1,0:T(8,128)(2,1)} %pad_maximum_fusion.7.first_ref, f32[2,256,256]{2,1,0:T(8,128)} %constant.107.clone.refs_5_.twist_ref, ...), custom_call_target="tpu_custom_call" | custom-call | tf_op jit(solution)/shard_map/pallas_call | solution.py:532
  375.9 5.9 %collective-permute-done.18.refs_11_ = bf16[8,64,256]{2,1,0:T(8,128)(2,1)S(1)} collective-permute-done((bf16[8,64,256]{2,1,0:T(8,128)(2,1)}, bf16[8,64,256]{2,1,0:T(8,128)(2,1)S(1)}, u32[]{:S(2)}, u32[]{:S(2)}) %collective-permute-start.18) | collective-permute-done | bytes 262176 | tf_op jit(solution)/shard_map/ppermute | solution.py:467
  388.3 15.4 %shard_map.311 = (f32[16,64,256]{2,1,0:T(8,128)}, bf16[16,64,512]{2,1,0:T(8,128)(2,1)}, bf16[16,8,512]{2,1,0:T(8,128)(2,1)}, bf16[8,64,512]{2,1,0:T(8,128)(2,1)}, bf16[8,8,512]{2,1,0:T(8,128)(2,1)}) custom-call(s32[3]{0:T(128)} %pad_add_fusion.1.refs_0_, f32[16,64,256]{2,1,0:T(8,128)} %get-tuple-element.101.refs_1_, ...), custom_call_target="tpu_custom_call" | custom-call | tf_op jit(solution)/shard_map/pallas_call | solution.py:838
  403.9 15.4 %shard_map.312 = (f32[16,64,256]{2,1,0:T(8,128)}, bf16[16,64,512]{2,1,0:T(8,128)(2,1)}, bf16[16,8,512]{2,1,0:T(8,128)(2,1)}) custom-call(s32[3]{0:T(128)} %pad_add_fusion.1.refs_0_, f32[16,64,256]{2,1,0:T(8,128)} %get-tuple-element.144.refs_1_, bf16[32,64,256]{2,1,0:T(8,128)(2,1)} %get-tuple-element.134.refs_2_, bf16[32,8,256]{2,1,0:T(8,128)(2,1)} %copy-done.14, ...), custom_call_target="tpu_custom_call" | custom-call | tf_op jit(solution)/shard_map/pallas_call | solution.py:838
  424.7 5.1 %collective-permute-done.24.refs_6_ = bf16[8,8,512]{2,1,0:T(8,128)(2,1)S(1)} collective-permute-done((bf16[8,8,512]{2,1,0:T(8,128)(2,1)S(1)}, bf16[8,8,512]{2,1,0:T(8,128)(2,1)S(1)}, u32[]{:S(2)}, u32[]{:S(2)}) %collective-permute-start.24) | collective-permute-done | bytes 65568 | tf_op jit(solution)/shard_map/ppermute | solution.py:893
  430.6 15.8 %shard_map.314 = (bf16[16,64,256]{2,1,0:T(8,128)(2,1)}, bf16[16,8,256]{2,1,0:T(8,128)(2,1)}, bf16[8,64,256]{2,1,0:T(8,128)(2,1)}, bf16[8,8,256]{2,1,0:T(8,128)(2,1)}) custom-call(s32[3]{0:T(128)} %pad_add_fusion.refs_0_, bf16[16,64,512]{2,1,0:T(8,128)(2,1)} %get-tuple-element.146.refs_1_, bf16[16,64,512]{2,1,0:T(8,128)(2,1)} %get-tuple-element.147.refs_2_, ...), custom_call_target="tpu_custom_call" | custom-call | tf_op jit(solution)/shard_map/pallas_call | solution.py:867
  448.2 15.7 %shard_map.313 = (bf16[16,64,256]{2,1,0:T(8,128)(2,1)}, bf16[16,8,256]{2,1,0:T(8,128)(2,1)}) custom-call(s32[3]{0:T(128)} %pad_add_fusion.refs_0_, bf16[16,64,512]{2,1,0:T(8,128)(2,1)} %get-tuple-element.146.refs_1_, bf16[16,64,512]{2,1,0:T(8,128)(2,1)} %get-tuple-element.147.refs_2_, bf16[16,8,512]{2,1,0:T(8,128)(2,1)} %copy-done.16, ...), custom_call_target="tpu_custom_call" | custom-call | tf_op jit(solution)/shard_map/pallas_call | solution.py:867
  465.8 5.9 %collective-permute-done.28.refs_8_ = bf16[8,8,256]{2,1,0:T(8,128)(2,1)S(1)} collective-permute-done((bf16[8,8,256]{2,1,0:T(8,128)(2,1)S(1)}, bf16[8,8,256]{2,1,0:T(8,128)(2,1)S(1)}, u32[]{:S(2)}, u32[]{:S(2)}) %collective-permute-start.28) | collective-permute-done | bytes 32800 | tf_op jit(solution)/shard_map/ppermute | solution.py:893
  472.5 8.7 %shard_map.315 = f32[512,1024]{1,0:T(8,128)} custom-call(s32[3]{0:T(128)} %pad_add_fusion.refs_0_, f32[16,64,256]{2,1,0:T(8,128)} %get-tuple-element.143.refs_1_, f32[16,64,256]{2,1,0:T(8,128)} %get-tuple-element.145.refs_2_, bf16[16,64,256]{2,1,0:T(8,128)(2,1)} %get-tuple-element.153.refs_3_, bf16[16,64,256]{2,1,0:T(8,128)(2,1)} %get-tuple-element.154.refs_4_, ...), custom_call_target="tpu_custom_call" | custom-call | tf_op jit(solution)/shard_map/pallas_call | solution.py:1024
  (220 shorter events, 126.6 us)
Async XLA Ops:
  5.7 10.3 %collective-permute-start = (bf16[8,64,256]{2,1,0:T(8,128)(2,1)}, bf16[8,64,256]{2,1,0:T(8,128)(2,1)S(1)}, u32[]{:S(2)}, u32[]{:S(2)}) collective-permute-start(bf16[8,64,256]{2,1,0:T(8,128)(2,1)} %get-tuple-element.83), channel_id=1, source_target_pairs={{0,1},{1,0},{2,3},{3,2},{4,5},{5,4},{6,7},{7,6},{8,9},{9,8},{10,11... | collective-permute-start | bytes 786440 | tf_op jit(solution)/shard_map/ppermute | solution.py:467
  8.7 13.6 %collective-permute-start.1 = (bf16[8,64,256]{2,1,0:T(8,128)(2,1)}, bf16[8,64,256]{2,1,0:T(8,128)(2,1)S(1)}, u32[]{:S(2)}, u32[]{:S(2)}) collective-permute-start(bf16[8,64,256]{2,1,0:T(8,128)(2,1)} %get-tuple-element.84), channel_id=1, source_target_pairs={{0,2},{1,3},{2,0},{3,1},{4,6},{5,7},{6,4},{7,5},{8,10},{9,11},{10,... | collective-permute-start | bytes 786440 | tf_op jit(solution)/shard_map/ppermute | solution.py:467
  10.2 12.1 %collective-permute-start.2 = (bf16[8,64,256]{2,1,0:T(8,128)(2,1)}, bf16[8,64,256]{2,1,0:T(8,128)(2,1)S(1)}, u32[]{:S(2)}, u32[]{:S(2)}) collective-permute-start(bf16[8,64,256]{2,1,0:T(8,128)(2,1)} %get-tuple-element.85), channel_id=1, source_target_pairs={{0,3},{1,2},{2,1},{3,0},{4,7},{5,6},{6,5},{7,4},{8,11},{9,10},{10,... | collective-permute-start | bytes 786440 | tf_op jit(solution)/shard_map/ppermute | solution.py:467
  28.8 53.7 %all-to-all-start = ((bf16[32,2,128,128]{3,2,1,0:T(8,128)(2,1)}), bf16[32,2,128,128]{3,2,1,0:T(8,128)(2,1)}, u32[]{:S(2)}, u32[]{:S(2)}) async-start(bf16[32,2,128,128]{3,2,1,0:T(8,128)(2,1)} %bitcast.70), calls=%async_computation | async-start | bytes 4194304 | tf_op jit(solution)/shard_map/all_to_all | solution.py:510
  95.0 53.3 %all-to-all-start.1 = ((bf16[32,2,128,128]{3,2,1,0:T(8,128)(2,1)}), bf16[32,2,128,128]{3,2,1,0:T(8,128)(2,1)S(1)}, u32[]{:S(2)}, u32[]{:S(2)}) async-start(bf16[32,2,128,128]{3,2,1,0:T(8,128)(2,1)} %shard_map.300), calls=%async_computation.1 | async-start | bytes 4194304 | tf_op jit(solution)/shard_map/all_to_all | solution.py:529
  157.0 9.4 %collective-permute-start.3 = (bf16[8,64,256]{2,1,0:T(8,128)(2,1)}, bf16[8,64,256]{2,1,0:T(8,128)(2,1)S(1)}, u32[]{:S(2)}, u32[]{:S(2)}) collective-permute-start(bf16[8,64,256]{2,1,0:T(8,128)(2,1)} %get-tuple-element.89), channel_id=1, source_target_pairs={{0,1},{1,0},{2,3},{3,2},{4,5},{5,4},{6,7},{7,6},{8,9},{9,8},{10,11... | collective-permute-start | bytes 786440 | tf_op jit(solution)/shard_map/ppermute | solution.py:467
  158.5 13.4 %collective-permute-start.4 = (bf16[8,64,256]{2,1,0:T(8,128)(2,1)}, bf16[8,64,256]{2,1,0:T(8,128)(2,1)S(1)}, u32[]{:S(2)}, u32[]{:S(2)}) collective-permute-start(bf16[8,64,256]{2,1,0:T(8,128)(2,1)} %get-tuple-element.90), channel_id=1, source_target_pairs={{0,2},{1,3},{2,0},{3,1},{4,6},{5,7},{6,4},{7,5},{8,10},{9,11},{10,... | collective-permute-start | bytes 786440 | tf_op jit(solution)/shard_map/ppermute | solution.py:467
  160.0 11.9 %collective-permute-start.5 = (bf16[8,64,256]{2,1,0:T(8,128)(2,1)}, bf16[8,64,256]{2,1,0:T(8,128)(2,1)S(1)}, u32[]{:S(2)}, u32[]{:S(2)}) collective-permute-start(bf16[8,64,256]{2,1,0:T(8,128)(2,1)} %get-tuple-element.91), channel_id=1, source_target_pairs={{0,3},{1,2},{2,1},{3,0},{4,7},{5,6},{6,5},{7,4},{8,11},{9,10},{10,... | collective-permute-start | bytes 786440 | tf_op jit(solution)/shard_map/ppermute | solution.py:467
  188.6 43.1 %collective-permute-start.10 = (bf16[8,64,768]{2,1,0:T(8,128)(2,1)}, bf16[8,64,768]{2,1,0:T(8,128)(2,1)S(1)}, u32[]{:S(2)}, u32[]{:S(2)}) collective-permute-start(bf16[8,64,768]{2,1,0:T(8,128)(2,1)} %get-tuple-element.110), channel_id=1, source_target_pairs={{0,28},{4,0},{8,4},{12,8},{16,12},{20,16},{24,20},{28,24},{1,29},{... | collective-permute-start | bytes 2359304 | tf_op jit(solution)/shard_map/ppermute | solution.py:892
  191.3 30.8 %collective-permute-start.6 = (bf16[64,4096]{1,0:T(8,128)(2,1)}, bf16[64,4096]{1,0:T(8,128)(2,1)S(1)}, u32[]{:S(2)}, u32[]{:S(2)}) collective-permute-start(bf16[64,4096]{1,0:T(8,128)(2,1)} %copy.86), channel_id=1, source_target_pairs={{0,31},{1,30},{2,29},{3,28},{4,27},{5,26},{6,25},{7,24},{8,23},{9,... | collective-permute-start | bytes 1572872 | tf_op jit(solution)/shard_map/ppermute | solution.py:428
  193.9 28.2 %collective-permute-start.7 = (bf16[1,4096]{1,0:T(2,128)(2,1)S(1)}, bf16[1,4096]{1,0:T(2,128)(2,1)S(1)}, u32[]{:S(2)}, u32[]{:S(2)}) collective-permute-start(bf16[1,4096]{1,0:T(2,128)(2,1)S(1)} %copy.87), channel_id=1, source_target_pairs={{1,31},{2,30},{3,29},{4,28},{5,27},{6,26},{7,25},{8,24},{9,23},{10... | collective-permute-start | bytes 24584 | tf_op jit(solution)/shard_map/ppermute | solution.py:429
  222.1 6.5 %collective-permute-start.8 = (bf16[16,8,768]{2,1,0:T(8,128)(2,1)S(1)}, bf16[16,8,768]{2,1,0:T(8,128)(2,1)S(1)}, u32[]{:S(2)}, u32[]{:S(2)}) collective-permute-start(bf16[16,8,768]{2,1,0:T(8,128)(2,1)S(1)} %copy-done.48), channel_id=1, source_target_pairs={{0,3},{1,0},{2,1},{3,2},{4,7},{5,4},{6,5},{7,6},{8,11},{9,8},{10,9... | collective-permute-start | bytes 589832 | tf_op jit(solution)/shard_map/ppermute | solution.py:891
  222.1 9.6 %collective-permute-start.9 = (bf16[16,8,768]{2,1,0:T(8,128)(2,1)}, bf16[16,8,768]{2,1,0:T(8,128)(2,1)S(1)}, u32[]{:S(2)}, u32[]{:S(2)}) collective-permute-start(bf16[16,8,768]{2,1,0:T(8,128)(2,1)} %get-tuple-element.109), channel_id=1, source_target_pairs={{0,3},{1,0},{2,1},{3,2},{4,7},{5,4},{6,5},{7,6},{8,11},{9,8},{10,9... | collective-permute-start | bytes 589832 | tf_op jit(solution)/shard_map/ppermute | solution.py:891
  261.1 9.5 %collective-permute-start.12 = (bf16[8,64,256]{2,1,0:T(8,128)(2,1)}, bf16[8,64,256]{2,1,0:T(8,128)(2,1)S(1)}, u32[]{:S(2)}, u32[]{:S(2)}) collective-permute-start(bf16[8,64,256]{2,1,0:T(8,128)(2,1)} %get-tuple-element.115), channel_id=1, source_target_pairs={{0,1},{1,0},{2,3},{3,2},{4,5},{5,4},{6,7},{7,6},{8,9},{9,8},{10,11... | collective-permute-start | bytes 786440 | tf_op jit(solution)/shard_map/ppermute | solution.py:467
  261.9 12.2 %collective-permute-start.13 = (bf16[8,64,256]{2,1,0:T(8,128)(2,1)}, bf16[8,64,256]{2,1,0:T(8,128)(2,1)S(1)}, u32[]{:S(2)}, u32[]{:S(2)}) collective-permute-start(bf16[8,64,256]{2,1,0:T(8,128)(2,1)} %get-tuple-element.116), channel_id=1, source_target_pairs={{0,2},{1,3},{2,0},{3,1},{4,6},{5,7},{6,4},{7,5},{8,10},{9,11},{10,... | collective-permute-start | bytes 786440 | tf_op jit(solution)/shard_map/ppermute | solution.py:467
  261.9 12.2 %collective-permute-start.14 = (bf16[8,64,256]{2,1,0:T(8,128)(2,1)}, bf16[8,64,256]{2,1,0:T(8,128)(2,1)S(1)}, u32[]{:S(2)}, u32[]{:S(2)}) collective-permute-start(bf16[8,64,256]{2,1,0:T(8,128)(2,1)} %get-tuple-element.117), channel_id=1, source_target_pairs={{0,3},{1,2},{2,1},{3,0},{4,7},{5,6},{6,5},{7,4},{8,11},{9,10},{10,... | collective-permute-start | bytes 786440 | tf_op jit(solution)/shard_map/ppermute | solution.py:467
  281.1 37.4 %all-to-all-start.2 = ((bf16[32,128,128]{2,1,0:T(8,128)(2,1)}), bf16[32,128,128]{2,1,0:T(8,128)(2,1)S(1)}, u32[]{:S(2)}, u32[]{:S(2)}) async-start(bf16[32,128,128]{2,1,0:T(8,128)(2,1)} %bitcast.77), calls=%async_computation.2 | async-start | bytes 2097152 | tf_op jit(solution)/shard_map/all_to_all | solution.py:510
  318.5 14.8 %collective-permute-start.16 = (bf16[8,64,256]{2,1,0:T(8,128)(2,1)S(1)}, bf16[8,64,256]{2,1,0:T(8,128)(2,1)S(1)}, u32[]{:S(2)}, u32[]{:S(2)}) collective-permute-start(bf16[8,64,256]{2,1,0:T(8,128)(2,1)S(1)} %copy-done.47), channel_id=1, source_target_pairs={{0,4},{4,8},{8,12},{12,16},{16,20},{20,24},{24,28},{28,0},{1,5},{5... | collective-permute-start | bytes 786440 | tf_op jit(solution)/shard_map/ppermute | solution.py:892
  318.5 14.8 %collective-permute-start.15 = (bf16[32,8,256]{2,1,0:T(8,128)(2,1)S(1)}, bf16[32,8,256]{2,1,0:T(8,128)(2,1)S(1)}, u32[]{:S(2)}, u32[]{:S(2)}) collective-permute-start(bf16[32,8,256]{2,1,0:T(8,128)(2,1)S(1)} %copy-done.49), channel_id=1, source_target_pairs={{0,1},{1,2},{2,3},{3,0},{4,5},{5,6},{6,7},{7,4},{8,9},{9,10},{10,1... | collective-permute-start | bytes 393224 | tf_op jit(solution)/shard_map/ppermute | solution.py:891
  320.0 13.2 %collective-permute-start.17 = (bf16[8,8,256]{2,1,0:T(8,128)(2,1)S(1)}, bf16[8,8,256]{2,1,0:T(8,128)(2,1)S(1)}, u32[]{:S(2)}, u32[]{:S(2)}) collective-permute-start(bf16[8,8,256]{2,1,0:T(8,128)(2,1)S(1)} %copy-done.53), channel_id=1, source_target_pairs={{0,5},{1,6},{2,7},{3,4},{4,9},{5,10},{6,11},{7,8},{8,13},{9,14},{1... | collective-permute-start | bytes 98312 | tf_op jit(solution)/shard_map/ppermute | solution.py:893
  333.3 31.6 %all-to-all-start.3 = ((bf16[32,128,128]{2,1,0:T(8,128)(2,1)}), bf16[32,128,128]{2,1,0:T(8,128)(2,1)S(1)}, u32[]{:S(2)}, u32[]{:S(2)}) async-start(bf16[32,128,128]{2,1,0:T(8,128)(2,1)} %shard_map.309), calls=%async_computation.3 | async-start | bytes 2097152 | tf_op jit(solution)/shard_map/all_to_all | solution.py:529
  372.3 9.5 %collective-permute-start.18 = (bf16[8,64,256]{2,1,0:T(8,128)(2,1)}, bf16[8,64,256]{2,1,0:T(8,128)(2,1)S(1)}, u32[]{:S(2)}, u32[]{:S(2)}) collective-permute-start(bf16[8,64,256]{2,1,0:T(8,128)(2,1)} %get-tuple-element.140), channel_id=1, source_target_pairs={{0,1},{1,0},{2,3},{3,2},{4,5},{5,4},{6,7},{7,6},{8,9},{9,8},{10,11... | collective-permute-start | bytes 786440 | tf_op jit(solution)/shard_map/ppermute | solution.py:467
  373.7 12.3 %collective-permute-start.19 = (bf16[8,64,256]{2,1,0:T(8,128)(2,1)}, bf16[8,64,256]{2,1,0:T(8,128)(2,1)S(1)}, u32[]{:S(2)}, u32[]{:S(2)}) collective-permute-start(bf16[8,64,256]{2,1,0:T(8,128)(2,1)} %get-tuple-element.141), channel_id=1, source_target_pairs={{0,2},{1,3},{2,0},{3,1},{4,6},{5,7},{6,4},{7,5},{8,10},{9,11},{10,... | collective-permute-start | bytes 786440 | tf_op jit(solution)/shard_map/ppermute | solution.py:467
  375.1 12.4 %collective-permute-start.20 = (bf16[8,64,256]{2,1,0:T(8,128)(2,1)}, bf16[8,64,256]{2,1,0:T(8,128)(2,1)S(1)}, u32[]{:S(2)}, u32[]{:S(2)}) collective-permute-start(bf16[8,64,256]{2,1,0:T(8,128)(2,1)} %get-tuple-element.142), channel_id=1, source_target_pairs={{0,3},{1,2},{2,1},{3,0},{4,7},{5,6},{6,5},{7,4},{8,11},{9,10},{10,... | collective-permute-start | bytes 786440 | tf_op jit(solution)/shard_map/ppermute | solution.py:467
  403.6 26.1 %collective-permute-start.23 = (bf16[8,64,512]{2,1,0:T(8,128)(2,1)}, bf16[8,64,512]{2,1,0:T(8,128)(2,1)S(1)}, u32[]{:S(2)}, u32[]{:S(2)}) collective-permute-start(bf16[8,64,512]{2,1,0:T(8,128)(2,1)} %get-tuple-element.150), channel_id=1, source_target_pairs={{0,28},{4,0},{8,4},{12,8},{16,12},{20,16},{24,20},{28,24},{1,29},{... | collective-permute-start | bytes 1572872 | tf_op jit(solution)/shard_map/ppermute | solution.py:892
  419.4 10.4 %collective-permute-start.22 = (bf16[16,8,512]{2,1,0:T(8,128)(2,1)}, bf16[16,8,512]{2,1,0:T(8,128)(2,1)S(1)}, u32[]{:S(2)}, u32[]{:S(2)}) collective-permute-start(bf16[16,8,512]{2,1,0:T(8,128)(2,1)} %get-tuple-element.149), channel_id=1, source_target_pairs={{0,3},{1,0},{2,1},{3,2},{4,7},{5,4},{6,5},{7,6},{8,11},{9,8},{10,9... | collective-permute-start | bytes 393224 | tf_op jit(solution)/shard_map/ppermute | solution.py:891
  421.3 8.5 %collective-permute-start.21 = (bf16[16,8,512]{2,1,0:T(8,128)(2,1)S(1)}, bf16[16,8,512]{2,1,0:T(8,128)(2,1)S(1)}, u32[]{:S(2)}, u32[]{:S(2)}) collective-permute-start(bf16[16,8,512]{2,1,0:T(8,128)(2,1)S(1)} %copy-done.50), channel_id=1, source_target_pairs={{0,3},{1,0},{2,1},{3,2},{4,7},{5,4},{6,5},{7,6},{8,11},{9,8},{10,9... | collective-permute-start | bytes 393224 | tf_op jit(solution)/shard_map/ppermute | solution.py:891
  422.3 7.4 %collective-permute-start.24 = (bf16[8,8,512]{2,1,0:T(8,128)(2,1)S(1)}, bf16[8,8,512]{2,1,0:T(8,128)(2,1)S(1)}, u32[]{:S(2)}, u32[]{:S(2)}) collective-permute-start(bf16[8,8,512]{2,1,0:T(8,128)(2,1)S(1)} %copy-done.52), channel_id=1, source_target_pairs={{0,31},{1,28},{2,29},{3,30},{4,3},{5,0},{6,1},{7,2},{8,7},{9,4},{1... | collective-permute-start | bytes 196616 | tf_op jit(solution)/shard_map/ppermute | solution.py:893
  446.4 25.3 %collective-permute-start.27 = (bf16[8,64,256]{2,1,0:T(8,128)(2,1)}, bf16[8,64,256]{2,1,0:T(8,128)(2,1)S(1)}, u32[]{:S(2)}, u32[]{:S(2)}) collective-permute-start(bf16[8,64,256]{2,1,0:T(8,128)(2,1)} %get-tuple-element.157), channel_id=1, source_target_pairs={{0,4},{4,8},{8,12},{12,16},{16,20},{20,24},{24,28},{28,0},{1,5},{5... | collective-permute-start | bytes 786440 | tf_op jit(solution)/shard_map/ppermute | solution.py:892
  446.5 25.2 %collective-permute-start.26 = (bf16[16,8,256]{2,1,0:T(8,128)(2,1)}, bf16[16,8,256]{2,1,0:T(8,128)(2,1)S(1)}, u32[]{:S(2)}, u32[]{:S(2)}) collective-permute-start(bf16[16,8,256]{2,1,0:T(8,128)(2,1)} %get-tuple-element.156), channel_id=1, source_target_pairs={{0,1},{1,2},{2,3},{3,0},{4,5},{5,6},{6,7},{7,4},{8,9},{9,10},{10,1... | collective-permute-start | bytes 196616 | tf_op jit(solution)/shard_map/ppermute | solution.py:891
  463.9 7.9 %collective-permute-start.25 = (bf16[16,8,256]{2,1,0:T(8,128)(2,1)}, bf16[16,8,256]{2,1,0:T(8,128)(2,1)S(1)}, u32[]{:S(2)}, u32[]{:S(2)}) collective-permute-start(bf16[16,8,256]{2,1,0:T(8,128)(2,1)} %get-tuple-element.155), channel_id=1, source_target_pairs={{0,1},{1,2},{2,3},{3,0},{4,5},{5,6},{6,7},{7,4},{8,9},{9,10},{10,1... | collective-permute-start | bytes 196616 | tf_op jit(solution)/shard_map/ppermute | solution.py:891
  464.8 6.9 %collective-permute-start.28 = (bf16[8,8,256]{2,1,0:T(8,128)(2,1)S(1)}, bf16[8,8,256]{2,1,0:T(8,128)(2,1)S(1)}, u32[]{:S(2)}, u32[]{:S(2)}) collective-permute-start(bf16[8,8,256]{2,1,0:T(8,128)(2,1)S(1)} %copy-done.54), channel_id=1, source_target_pairs={{0,5},{1,6},{2,7},{3,4},{4,9},{5,10},{6,11},{7,8},{8,13},{9,14},{1... | collective-permute-start | bytes 98312 | tf_op jit(solution)/shard_map/ppermute | solution.py:893
  (56 other events, 640.8 us)

commit v6 on v4

--- a/solution.py
+++ b/solution.py
@@ -205,7 +205,7 @@
         out_ref[:, 1, :, rows, :] = result[..., half:]
         return carry
 
-    lax.fori_loop(0, count, step, 0, unroll=4)
+    lax.fori_loop(0, count, step, 0, unroll=8)
 
 
 def row_inverse(v_ref, first_ref, twist_ref, second_ref, *out_refs):
@@ -231,7 +231,7 @@
             out_ref[i] = result[m * cols : (m + 1) * cols]
         return carry
 
-    lax.fori_loop(0, count, step, 0, unroll=4)
+    lax.fori_loop(0, count, step, 0, unroll=8)
 
 
 def lane_index(shape):
@@ -272,7 +272,7 @@
         packed(upper[:, 0], imag, rows, slice(PATCH // 2, PATCH))
         return carry
 
-    lax.fori_loop(0, count, step, 0, unroll=4)
+    lax.fori_loop(0, count, step, 0, unroll=8)
 
 
 def row_inverse_half(v_ref, first_ref, twist_ref, lower_ref, upper_ref, *out_refs):
@@ -309,7 +309,7 @@
             out_ref[i] = result[m * cols : (m + 1) * cols]
         return carry
 
-    lax.fori_loop(0, count, step, 0, unroll=4)
+    lax.fori_loop(0, count, step, 0, unroll=8)
 
 
 def column_kernel(halved, *refs):
@@ -505,13 +505,14 @@
     if halved:
         sent, mirror, shift = lax.optimization_barrier((sent, mirror, shift))
         extra = (middle.astype(jnp.int32).reshape(1), phase_table(shift[0], devices, slab))
-        away = (inner, mirrored_weight(scale, *mirror), inner_t, outer_t)
+        table = mirrored_weight(scale, *mirror)
     moved = lax.all_to_all(
         sent.reshape(part), ("ty", "tx"), split_axis=0, concat_axis=0, tiled=True
     )
     if halved:
-        moved, beside = lax.optimization_barrier((moved, beside))
+        moved, table, beside = lax.optimization_barrier((moved, table, beside))
         beside = from_neighbours(beside, 1)
+        away = (inner, table, inner_t, outer_t)
     spaces = [pltpu.SMEM, pltpu.VMEM][: len(extra)] + [pltpu.VMEM] * 2 + [pl.ANY] * len(away)
     wave = pl.pallas_call(
         functools.partial(column_kernel, halved),
@@ -590,7 +591,7 @@
     return wait
 
 
-def swin_band(flow, wait, bias_ref, gain_ref, weight_refs, scratch):
+def swin_band(flow, wait, bias_ref, gain_ref, weight_refs, scratch, staggered):
     qkv_ref, proj_ref, up_ref, down_ref = weight_refs
     mixed_ref, score_ref, prob_ref, active_ref = scratch
     count = flow.shape[0] // SPAN
@@ -633,13 +634,16 @@
             mixture = mm(prob_ref[w, :, lanes], value, TN)
             mixed_ref[rows, lanes] = jnp.where(lower, mixture[:SPAN], mixture[SPAN:]).astype(BF16)
 
-    for turn in range(count + 2):
-        if turn < count:
-            scores_of(turn)
-        if 0 <= turn - 1 < count:
-            probs_of(turn - 1)
-        if 0 <= turn - 2:
-            mixture_of(turn - 2)
+    passes = (scores_of, probs_of, mixture_of)
+    if staggered:
+        for turn in range(count + 2):
+            for n, run in enumerate(passes):
+                if 0 <= turn - n < count:
+                    run(turn - n)
+    else:
+        for run in passes:
+            for w in range(count):
+                run(w)
     wait((1, 2, 3))
     flow = flow + mm(mixed_ref[:, :D], proj_ref[...])
     normed = layer_norm(flow, gain_ref[1:2, :])
@@ -657,12 +661,11 @@
     behind = -rows if sign > 0 else WIN
     beside = -cols if sign > 0 else WIN
 
-    def pick(width, offset):
-        source = lax.broadcasted_iota(jnp.int32, (cols, width), 1)
-        wanted = lax.broadcasted_iota(jnp.int32, (cols, width), 0) + sign * shift_ref[1] + offset
-        return jnp.where(source == wanted, 1.0, 0.0).astype(BF16)
-
-    pick_main, pick_side = pick(cols, 0), pick(WIN, beside)
+    source = lax.broadcasted_iota(jnp.int32, (cols, cols + WIN), 1)
+    wanted = lax.broadcasted_iota(jnp.int32, (cols, cols + WIN), 0) + sign * shift_ref[1]
+    found = (source < cols) & (source == wanted)
+    found = found | (source >= cols) & (source - cols == wanted + beside)
+    pick = jnp.where(found, 1.0, 0.0).astype(BF16)
     band = []
     for j in range(count):
         row = top + j
@@ -670,7 +673,7 @@
         here, there = jnp.clip(row, 0, rows - 1), jnp.clip(row + behind, 0, WIN - 1)
         main = jnp.where(inside, main_ref[here], edge_ref[there])
         side = jnp.where(inside, side_ref[here], corner_ref[there])
-        band.append(mm(pick_main, main) + mm(pick_side, side))
+        band.append(mm(pick, jnp.concatenate([main, side], axis=0)))
     return jnp.stack(band)
 
 
@@ -706,7 +709,7 @@
     step = zeta * grad
     half = state - step
     tokens = mm(to_windows(half).astype(BF16), embed_ref[...]).astype(BF16).astype(F32)
-    flow = swin_band(tokens, wait, bias_ref, gain_ref, targets, scratch)
+    flow = swin_band(tokens, wait, bias_ref, gain_ref, targets, scratch, True)
     result = from_windows(flow, half.shape[1]).astype(BF16)
     out_ref[:, :, :D] = result
     side_ref[:, :, :D] = result[:, :WIN]
@@ -745,7 +748,7 @@
     height, cols, _ = out_ref.shape
     band = rolled_band(1, shift_ref, tile_refs, rows, height)
     tokens = to_windows(band[:, :, :D])
-    flow = swin_band(tokens, wait, bias_ref, gain_ref, targets, scratch)
+    flow = swin_band(tokens, wait, bias_ref, gain_ref, targets, scratch, False)
     estimate = from_windows(mm(flow.astype(BF16), unembed_ref[...]), cols)
     narrow = estimate.astype(BF16)
     out_ref[...] = narrow

time: 474 us -> 465 us (0.981)
  waiting for transfers between devices: 149 us -> 142 us
    all_to_all x2, waiting for transfers between devices: 41.3 us -> 34.5 us  [patch_gradient(): lax.all_to_all(sent.reshape(part), ('ty', 'tx'), split_axis=0, concat_axi...]
    unnamed x98 -> x102, local copies, waits for them, and re-layouts: 22.8 us -> 23.4 us
where the time goes in v6:
time: 465 us; the launch traced here: 457 us
  Pallas kernels  189 us (41%)
  waiting for transfers between devices  142 us (31%)
  starting transfers between devices  53.2 us (11%)
  local copies, waits for them, and re-layouts  47.7 us (10%)
  other arithmetic  18.7 us (4%)
  between operations  6 us (1%)
    pallas_call x2, Pallas kernels, second_block(): pl.pallas_call(functools.partial(second_kernel, sigma, rows, parts), grid...  54.4 us
    pallas_call x2, Pallas kernels, first_block(): pl.pallas_call(functools.partial(first_kernel, zeta, sigma, len(grads), p...  54 us
    all_to_all x2, waiting for transfers between devices, patch_gradient(): lax.all_to_all(wave, ('ty', 'tx'), split_axis=0, concat_axis=0, tiled=True)  44.4 us
    ppermute x12, waiting for transfers between devices, swap_pieces(): lax.ppermute(pieces[m], 'tx', [(k, k ^ m) for k in range(lanes)])  40.1 us
    all_to_all x2, waiting for transfers between devices, patch_gradient(): lax.all_to_all(sent.reshape(part), ('ty', 'tx'), split_axis=0, concat_axi...  34.5 us
    pallas_call x2, Pallas kernels, patch_gradient(): pl.pallas_call(functools.partial(column_kernel, halved), in_specs=[pl.Blo...  23.4 us
    unnamed x102, local copies, waits for them, and re-layouts  23.4 us
    ppermute x4, waiting for transfers between devices, from_neighbours(): lax.ppermute(corner, ('ty', 'tx'), across)  21.8 us
  transfers between devices with their start and end apart: 30, of which 17 were waited for; matrix products, arithmetic and copies ran while one was open for 12% of the time, Pallas kernels for 12%

profile of v6, /device:TPU:0, one launch (start us, length us, event | category | flops | bytes accessed | tf_op | source)
XLA Modules:
  0.0 456.5 jit_solution(15496873028607282083)
XLA Ops:
  0.0 5.7 %shard_map.298 = (bf16[8,64,256]{2,1,0:T(8,128)(2,1)}, bf16[8,64,256]{2,1,0:T(8,128)(2,1)}, bf16[8,64,256]{2,1,0:T(8,128)(2,1)}, bf16[8,64,256]{2,1,0:T(8,128)(2,1)}) custom-call(s32[1]{0:T(128)} %bitcast.1.place_ref, f32[1,512,1024]{2,1,0:T(8,128)} %bitcast.67, bf16[1024,1024]{1,0:T(8,128)(2,1)} %constant.98.clone.order_ref), custom_call_target="tpu_custom_call" | custom-call | tf_op jit(solution)/shard_map/pallas_call | solution.py:966
  16.0 6.3 %collective-permute-done.1.refs_2_ = bf16[8,64,256]{2,1,0:T(8,128)(2,1)S(1)} collective-permute-done((bf16[8,64,256]{2,1,0:T(8,128)(2,1)}, bf16[8,64,256]{2,1,0:T(8,128)(2,1)S(1)}, u32[]{:S(2)}, u32[]{:S(2)}) %collective-permute-start.1) | collective-permute-done | bytes 262176 | tf_op jit(solution)/shard_map/ppermute | solution.py:466
  23.0 5.5 %shard_map.299 = bf16[16,2,2,128,128]{4,3,2,1,0:T(8,128)(2,1)} custom-call(bf16[8,64,256]{2,1,0:T(8,128)(2,1)} %get-tuple-element.76.refs_0_, bf16[8,64,256]{2,1,0:T(8,128)(2,1)} %copy-done.13, bf16[8,64,256]{2,1,0:T(8,128)(2,1)} %copy-done.14, bf16[8,64,256]{2,1,0:T(8,128)(2,1)} %copy-done.15, bf16[256,512]{1,0:T(8,128)(2,1)} %pad_maximum_fusion.5.refs_4_.first_ref, ...), custom_call_target="tpu_custom_call" | custom-call | tf_op jit(solution)/shard_map/pallas_call | solution.py:502
  28.5 5.0 %all-to-all-start = ((bf16[32,2,128,128]{3,2,1,0:T(8,128)(2,1)}), bf16[32,2,128,128]{3,2,1,0:T(8,128)(2,1)}, u32[]{:S(2)}, u32[]{:S(2)}) async-start(bf16[32,2,128,128]{3,2,1,0:T(8,128)(2,1)} %bitcast.70), calls=%async_computation | async-start | bytes 4194304 | tf_op jit(solution)/shard_map/all_to_all | solution.py:509
  43.1 4.7 %fusion.17 = (f32[1,128,4096]{2,1,0:T(8,128)}, f32[1,128,4096]{2,1,0:T(8,128)}) fusion(f32[2,128,4096]{2,1,0:T(8,128)} %param.37), kind=kLoop, calls=%fused_computation.76 | loop fusion | bytes 8388608 | tf_op jit(solution)/shard_map/slice | solution.py:407
  64.8 17.5 %all-to-all-done.refs_0_ = bf16[32,2,128,128]{3,2,1,0:T(8,128)(2,1)} async-done(((bf16[32,2,128,128]{3,2,1,0:T(8,128)(2,1)}), bf16[32,2,128,128]{3,2,1,0:T(8,128)(2,1)}, u32[]{:S(2)}, u32[]{:S(2)}) %all-to-all-start) | async-done | bytes 2097184 | tf_op jit(solution)/shard_map/all_to_all | solution.py:509
  82.2 12.4 %shard_map.300 = bf16[32,2,128,128]{3,2,1,0:T(8,128)(2,1)} custom-call(bf16[32,2,128,128]{3,2,1,0:T(8,128)(2,1)} %all-to-all-done.refs_0_, bf16[512,512]{1,0:T(8,128)(2,1)} %constant.99.clone.refs_1_.refs_3_, bf16[32,256,256]{2,1,0:T(8,128)(2,1)} %constant.101.clone.refs_2_.refs_4_, bf16[32,128,128]{2,1,0:T(8,128)(2,1)} %bitcast.65, ...), custom_call_target="tpu_custom_call" | custom-call | tf_op jit(solution)/shard_map/pallas_call | solution.py:517
  99.2 6.5 %shard_map.301.refs_1_ = f32[32,64,256]{2,1,0:T(8,128)} custom-call(s32[1]{0:T(128)} %bitcast.1.place_ref, f32[1,512,1024]{2,1,0:T(8,128)} %bitcast.68, bf16[1024,1024]{1,0:T(8,128)(2,1)} %constant.98.clone.order_ref), custom_call_target="tpu_custom_call" | custom-call | tf_op jit(solution)/shard_map/pallas_call | solution.py:966
  107.0 6.6 %shard_map.302.refs_6_ = f32[32,64,256]{2,1,0:T(8,128)} custom-call(s32[1]{0:T(128)} %bitcast.1.place_ref, f32[2,512,1024]{2,1,0:T(8,128)} %refs_6_.4, bf16[1024,1024]{1,0:T(8,128)(2,1)} %constant.98.clone.order_ref), custom_call_target="tpu_custom_call" | custom-call | tf_op jit(solution)/shard_map/pallas_call | solution.py:966
  129.2 18.7 %all-to-all-done.1 = bf16[32,2,128,128]{3,2,1,0:T(8,128)(2,1)S(1)} async-done(((bf16[32,2,128,128]{3,2,1,0:T(8,128)(2,1)}), bf16[32,2,128,128]{3,2,1,0:T(8,128)(2,1)S(1)}, u32[]{:S(2)}, u32[]{:S(2)}) %all-to-all-start.1) | async-done | bytes 2097184 | tf_op jit(solution)/shard_map/all_to_all | solution.py:528
  149.3 7.2 %shard_map.303 = (bf16[8,64,256]{2,1,0:T(8,128)(2,1)}, bf16[8,64,256]{2,1,0:T(8,128)(2,1)}, bf16[8,64,256]{2,1,0:T(8,128)(2,1)}, bf16[8,64,256]{2,1,0:T(8,128)(2,1)}) custom-call(bf16[16,2,2,128,128]{4,3,2,1,0:T(8,128)(2,1)} %bitcast.69, bf16[256,512]{1,0:T(8,128)(2,1)} %pad_maximum_fusion.5.refs_4_.first_ref, ...), custom_call_target="tpu_custom_call" | custom-call | tf_op jit(solution)/shard_map/pallas_call | solution.py:531
  160.0 5.9 %collective-permute-done.3.refs_3_.refs_7_ = bf16[8,64,256]{2,1,0:T(8,128)(2,1)S(1)} collective-permute-done((bf16[8,64,256]{2,1,0:T(8,128)(2,1)}, bf16[8,64,256]{2,1,0:T(8,128)(2,1)S(1)}, u32[]{:S(2)}, u32[]{:S(2)}) %collective-permute-start.3) | collective-permute-done | bytes 262176 | tf_op jit(solution)/shard_map/ppermute | solution.py:466
  165.9 5.5 %collective-permute-done.4.refs_4_.refs_8_ = bf16[8,64,256]{2,1,0:T(8,128)(2,1)S(1)} collective-permute-done((bf16[8,64,256]{2,1,0:T(8,128)(2,1)}, bf16[8,64,256]{2,1,0:T(8,128)(2,1)S(1)}, u32[]{:S(2)}, u32[]{:S(2)}) %collective-permute-start.4) | collective-permute-done | bytes 262176 | tf_op jit(solution)/shard_map/ppermute | solution.py:466
  175.6 27.2 %shard_map.304 = (f32[32,64,256]{2,1,0:T(8,128)}, bf16[32,64,768]{2,1,0:T(8,128)(2,1)}, bf16[32,8,768]{2,1,0:T(8,128)(2,1)}, bf16[8,64,768]{2,1,0:T(8,128)(2,1)}, bf16[8,8,768]{2,1,0:T(8,128)(2,1)}) custom-call(s32[3]{0:T(128)} %pad_add_fusion.1.refs_0_, f32[32,64,256]{2,1,0:T(8,128)} %shard_map.301.refs_1_, ...), custom_call_target="tpu_custom_call" | custom-call | tf_op jit(solution)/shard_map/pallas_call | solution.py:813
  202.8 5.2 %collective-permute-start.9 = (bf16[8,64,768]{2,1,0:T(8,128)(2,1)}, bf16[8,64,768]{2,1,0:T(8,128)(2,1)S(1)}, u32[]{:S(2)}, u32[]{:S(2)}) collective-permute-start(bf16[8,64,768]{2,1,0:T(8,128)(2,1)} %get-tuple-element.104), channel_id=1, source_target_pairs={{0,28},{4,0},{8,4},{12,8},{16,12},{20,16},{24,20},{28,24},{1,29},{... | collective-permute-start | bytes 2359304 | tf_op jit(solution)/shard_map/ppermute | solution.py:866
  211.3 7.6 %collective-permute-done.10.refs_4_ = bf16[8,8,768]{2,1,0:T(8,128)(2,1)S(1)} collective-permute-done((bf16[8,8,768]{2,1,0:T(8,128)(2,1)}, bf16[8,8,768]{2,1,0:T(8,128)(2,1)S(1)}, u32[]{:S(2)}, u32[]{:S(2)}) %collective-permute-start.10) | collective-permute-done | bytes 98336 | tf_op jit(solution)/shard_map/ppermute | solution.py:867
  221.5 28.2 %shard_map.305 = (bf16[32,64,256]{2,1,0:T(8,128)(2,1)}, bf16[32,8,256]{2,1,0:T(8,128)(2,1)}, bf16[8,64,256]{2,1,0:T(8,128)(2,1)}, bf16[8,8,256]{2,1,0:T(8,128)(2...) custom-call(s32[3]{0:T(128)} %pad_add_fusion.1.refs_0_, ...), custom_call_target="tpu_custom_call" | custom-call | tf_op jit(solution)/shard_map/pallas_call | solution.py:840
  254.4 5.2 %collective-permute-done.11.refs_1_ = bf16[8,64,256]{2,1,0:T(8,128)(2,1)S(1)} collective-permute-done((bf16[8,64,256]{2,1,0:T(8,128)(2,1)}, bf16[8,64,256]{2,1,0:T(8,128)(2,1)S(1)}, u32[]{:S(2)}, u32[]{:S(2)}) %collective-permute-start.11) | collective-permute-done | bytes 262176 | tf_op jit(solution)/shard_map/ppermute | solution.py:466
  265.0 5.8 %shard_map.306 = bf16[16,2,128,128]{3,2,1,0:T(8,128)(2,1)} custom-call(bf16[8,64,256]{2,1,0:T(8,128)(2,1)} %get-tuple-element.108.refs_0_, bf16[8,64,256]{2,1,0:T(8,128)(2,1)} %copy-done.26, bf16[8,64,256]{2,1,0:T(8,128)(2,1)} %copy-done.27, bf16[8,64,256]{2,1,0:T(8,128)(2,1)} %copy-done.28, bf16[256,512]{1,0:T(8,128)(2,1)} %pad_maximum_fusion.6.refs_4_, ...), custom_call_target="tpu_custom_call" | custom-call | tf_op jit(solution)/shard_map/pallas_call | solution.py:502
  270.8 5.2 %all-to-all-start.2 = ((bf16[32,128,128]{2,1,0:T(8,128)(2,1)}), bf16[32,128,128]{2,1,0:T(8,128)(2,1)S(1)}, u32[]{:S(2)}, u32[]{:S(2)}) async-start(bf16[32,128,128]{2,1,0:T(8,128)(2,1)} %bitcast.73), calls=%async_computation.2 | async-start | bytes 2097152 | tf_op jit(solution)/shard_map/all_to_all | solution.py:509
  280.0 5.4 %shard_map.307.refs_5_ = bf16[32,128,128]{2,1,0:T(8,128)(2,1)} custom-call(bf16[32,128,128]{2,1,0:T(8,128)(2,1)} %bitcast.66, bf16[32,128,128]{2,1,0:T(8,128)(2,1)} %bitcast.71, bf16[2,128,128]{2,1,0:T(8,128)(2,1)} %add_convert_fusion.pick_ref, bf16[2,128,128]{2,1,0:T(8,128)(2,1)} %constant.113.clone.flip_ref), custom_call_target="tpu_custom_call" | custom-call | tf_op jit(solution)/shard_map/pallas_call | solution.py:447
  285.4 17.0 %all-to-all-done.2.refs_2_ = bf16[32,128,128]{2,1,0:T(8,128)(2,1)S(1)} async-done(((bf16[32,128,128]{2,1,0:T(8,128)(2,1)}), bf16[32,128,128]{2,1,0:T(8,128)(2,1)S(1)}, u32[]{:S(2)}, u32[]{:S(2)}) %all-to-all-start.2) | async-done | bytes 1048608 | tf_op jit(solution)/shard_map/all_to_all | solution.py:509
  306.4 11.0 %shard_map.308 = bf16[32,128,128]{2,1,0:T(8,128)(2,1)} custom-call(s32[1]{0:T(128)} %bitcast.28.refs_0_, f32[32,2,8,128]{3,2,1,0:T(8,128)} %broadcast_in_dim.79.refs_1_, bf16[32,128,128]{2,1,0:T(8,128)(2,1)} %copy-done.1, bf16[512,512]{1,0:T(8,128)(2,1)} %constant.99.clone.refs_1_.refs_3_, bf16[32,256,256]{2,1,0:T(8,128)(2,1)} %constant.101.clone.refs_2_.refs_4_, ...), custom_call_target="tpu_custom_call" | custom-call | tf_op jit(solution)/shard_map/pallas_call | solution.py:517
  317.5 5.0 %all-to-all-start.3 = ((bf16[32,128,128]{2,1,0:T(8,128)(2,1)}), bf16[32,128,128]{2,1,0:T(8,128)(2,1)S(1)}, u32[]{:S(2)}, u32[]{:S(2)}) async-start(bf16[32,128,128]{2,1,0:T(8,128)(2,1)} %shard_map.308), calls=%async_computation.3 | async-start | bytes 2097152 | tf_op jit(solution)/shard_map/all_to_all | solution.py:528
  323.4 25.7 %all-to-all-done.3 = bf16[32,128,128]{2,1,0:T(8,128)(2,1)S(1)} async-done(((bf16[32,128,128]{2,1,0:T(8,128)(2,1)}), bf16[32,128,128]{2,1,0:T(8,128)(2,1)S(1)}, u32[]{:S(2)}, u32[]{:S(2)}) %all-to-all-start.3) | async-done | bytes 1048608 | tf_op jit(solution)/shard_map/all_to_all | solution.py:528
  350.0 6.0 %shard_map.309 = (bf16[8,64,256]{2,1,0:T(8,128)(2,1)}, bf16[8,64,256]{2,1,0:T(8,128)(2,1)}, bf16[8,64,256]{2,1,0:T(8,128)(2,1)}, bf16[8,64,256]{2,1,0:T(8,128)(2,1)}) custom-call(bf16[16,2,128,128]{3,2,1,0:T(8,128)(2,1)} %bitcast.74, bf16[256,512]{1,0:T(8,128)(2,1)} %pad_maximum_fusion.7.first_ref, f32[2,256,256]{2,1,0:T(8,128)} %constant.107.clone.refs_5_.twist_ref, ...), custom_call_target="tpu_custom_call" | custom-call | tf_op jit(solution)/shard_map/pallas_call | solution.py:531
  359.6 5.9 %collective-permute-done.17.refs_11_ = bf16[8,64,256]{2,1,0:T(8,128)(2,1)S(1)} collective-permute-done((bf16[8,64,256]{2,1,0:T(8,128)(2,1)}, bf16[8,64,256]{2,1,0:T(8,128)(2,1)S(1)}, u32[]{:S(2)}, u32[]{:S(2)}) %collective-permute-start.17) | collective-permute-done | bytes 262176 | tf_op jit(solution)/shard_map/ppermute | solution.py:466
  372.0 26.9 %shard_map.310 = (f32[32,64,256]{2,1,0:T(8,128)}, bf16[32,64,512]{2,1,0:T(8,128)(2,1)}, bf16[32,8,512]{2,1,0:T(8,128)(2,1)}, bf16[8,64,512]{2,1,0:T(8,128)(2,1)}, bf16[8,8,512]{2,1,0:T(8,128)(2,1)}) custom-call(s32[3]{0:T(128)} %pad_add_fusion.1.refs_0_, f32[32,64,256]{2,1,0:T(8,128)} %get-tuple-element.95.refs_1_, ...), custom_call_target="tpu_custom_call" | custom-call | tf_op jit(solution)/shard_map/pallas_call | solution.py:813
  403.2 6.1 %collective-permute-done.22.refs_4_ = bf16[8,8,512]{2,1,0:T(8,128)(2,1)S(1)} collective-permute-done((bf16[8,8,512]{2,1,0:T(8,128)(2,1)}, bf16[8,8,512]{2,1,0:T(8,128)(2,1)S(1)}, u32[]{:S(2)}, u32[]{:S(2)}) %collective-permute-start.22) | collective-permute-done | bytes 65568 | tf_op jit(solution)/shard_map/ppermute | solution.py:867
  410.2 26.2 %shard_map.311 = (bf16[32,64,256]{2,1,0:T(8,128)(2,1)}, bf16[32,8,256]{2,1,0:T(8,128)(2,1)}, bf16[8,64,256]{2,1,0:T(8,128)(2,1)}, bf16[8,8,256]{2,1,0:T(8,128)(2,1)}) custom-call(s32[3]{0:T(128)} %pad_add_fusion.refs_0_, bf16[32,64,512]{2,1,0:T(8,128)(2,1)} %get-tuple-element.138.refs_1_, bf16[32,8,512]{2,1,0:T(8,128)(2,1)} %copy-done.12, ...), custom_call_target="tpu_custom_call" | custom-call | tf_op jit(solution)/shard_map/pallas_call | solution.py:840
  438.6 8.2 %collective-permute-done.25.refs_5_ = bf16[8,8,256]{2,1,0:T(8,128)(2,1)S(1)} collective-permute-done((bf16[8,8,256]{2,1,0:T(8,128)(2,1)}, bf16[8,8,256]{2,1,0:T(8,128)(2,1)S(1)}, u32[]{:S(2)}, u32[]{:S(2)}) %collective-permute-start.25) | collective-permute-done | bytes 32800 | tf_op jit(solution)/shard_map/ppermute | solution.py:867
  447.6 8.5 %shard_map.312 = f32[512,1024]{1,0:T(8,128)} custom-call(s32[3]{0:T(128)} %pad_add_fusion.refs_0_, f32[32,64,256]{2,1,0:T(8,128)} %get-tuple-element.137.refs_1_, bf16[32,64,256]{2,1,0:T(8,128)(2,1)} %get-tuple-element.143.refs_2_, bf16[32,8,256]{2,1,0:T(8,128)(2,1)} %copy-done.36, bf16[8,64,256]{2,1,0:T(8,128)(2,1)} %copy-done.16, ...), custom_call_target="tpu_custom_call" | custom-call | tf_op jit(solution)/shard_map/pallas_call | solution.py:985
  (197 shorter events, 106.9 us)
Async XLA Ops:
  5.7 10.3 %collective-permute-start = (bf16[8,64,256]{2,1,0:T(8,128)(2,1)}, bf16[8,64,256]{2,1,0:T(8,128)(2,1)S(1)}, u32[]{:S(2)}, u32[]{:S(2)}) collective-permute-start(bf16[8,64,256]{2,1,0:T(8,128)(2,1)} %get-tuple-element.77), channel_id=1, source_target_pairs={{0,1},{1,0},{2,3},{3,2},{4,5},{5,4},{6,7},{7,6},{8,9},{9,8},{10,11... | collective-permute-start | bytes 786440 | tf_op jit(solution)/shard_map/ppermute | solution.py:466
  8.6 13.6 %collective-permute-start.1 = (bf16[8,64,256]{2,1,0:T(8,128)(2,1)}, bf16[8,64,256]{2,1,0:T(8,128)(2,1)S(1)}, u32[]{:S(2)}, u32[]{:S(2)}) collective-permute-start(bf16[8,64,256]{2,1,0:T(8,128)(2,1)} %get-tuple-element.78), channel_id=1, source_target_pairs={{0,2},{1,3},{2,0},{3,1},{4,6},{5,7},{6,4},{7,5},{8,10},{9,11},{10,... | collective-permute-start | bytes 786440 | tf_op jit(solution)/shard_map/ppermute | solution.py:466
  10.1 12.1 %collective-permute-start.2 = (bf16[8,64,256]{2,1,0:T(8,128)(2,1)}, bf16[8,64,256]{2,1,0:T(8,128)(2,1)S(1)}, u32[]{:S(2)}, u32[]{:S(2)}) collective-permute-start(bf16[8,64,256]{2,1,0:T(8,128)(2,1)} %get-tuple-element.79), channel_id=1, source_target_pairs={{0,3},{1,2},{2,1},{3,0},{4,7},{5,6},{6,5},{7,4},{8,11},{9,10},{10,... | collective-permute-start | bytes 786440 | tf_op jit(solution)/shard_map/ppermute | solution.py:466
  28.5 53.7 %all-to-all-start = ((bf16[32,2,128,128]{3,2,1,0:T(8,128)(2,1)}), bf16[32,2,128,128]{3,2,1,0:T(8,128)(2,1)}, u32[]{:S(2)}, u32[]{:S(2)}) async-start(bf16[32,2,128,128]{3,2,1,0:T(8,128)(2,1)} %bitcast.70), calls=%async_computation | async-start | bytes 4194304 | tf_op jit(solution)/shard_map/all_to_all | solution.py:509
  94.6 53.3 %all-to-all-start.1 = ((bf16[32,2,128,128]{3,2,1,0:T(8,128)(2,1)}), bf16[32,2,128,128]{3,2,1,0:T(8,128)(2,1)S(1)}, u32[]{:S(2)}, u32[]{:S(2)}) async-start(bf16[32,2,128,128]{3,2,1,0:T(8,128)(2,1)} %shard_map.300), calls=%async_computation.1 | async-start | bytes 4194304 | tf_op jit(solution)/shard_map/all_to_all | solution.py:528
  156.5 9.4 %collective-permute-start.3 = (bf16[8,64,256]{2,1,0:T(8,128)(2,1)}, bf16[8,64,256]{2,1,0:T(8,128)(2,1)S(1)}, u32[]{:S(2)}, u32[]{:S(2)}) collective-permute-start(bf16[8,64,256]{2,1,0:T(8,128)(2,1)} %get-tuple-element.83), channel_id=1, source_target_pairs={{0,1},{1,0},{2,3},{3,2},{4,5},{5,4},{6,7},{7,6},{8,9},{9,8},{10,11... | collective-permute-start | bytes 786440 | tf_op jit(solution)/shard_map/ppermute | solution.py:466
  158.0 13.4 %collective-permute-start.4 = (bf16[8,64,256]{2,1,0:T(8,128)(2,1)}, bf16[8,64,256]{2,1,0:T(8,128)(2,1)S(1)}, u32[]{:S(2)}, u32[]{:S(2)}) collective-permute-start(bf16[8,64,256]{2,1,0:T(8,128)(2,1)} %get-tuple-element.84), channel_id=1, source_target_pairs={{0,2},{1,3},{2,0},{3,1},{4,6},{5,7},{6,4},{7,5},{8,10},{9,11},{10,... | collective-permute-start | bytes 786440 | tf_op jit(solution)/shard_map/ppermute | solution.py:466
  159.5 11.9 %collective-permute-start.5 = (bf16[8,64,256]{2,1,0:T(8,128)(2,1)}, bf16[8,64,256]{2,1,0:T(8,128)(2,1)S(1)}, u32[]{:S(2)}, u32[]{:S(2)}) collective-permute-start(bf16[8,64,256]{2,1,0:T(8,128)(2,1)} %get-tuple-element.85), channel_id=1, source_target_pairs={{0,3},{1,2},{2,1},{3,0},{4,7},{5,6},{6,5},{7,4},{8,11},{9,10},{10,... | collective-permute-start | bytes 786440 | tf_op jit(solution)/shard_map/ppermute | solution.py:466
  173.2 29.6 %collective-permute-start.6 = (bf16[64,4096]{1,0:T(8,128)(2,1)S(1)}, bf16[64,4096]{1,0:T(8,128)(2,1)S(1)}, u32[]{:S(2)}, u32[]{:S(2)}) collective-permute-start(bf16[64,4096]{1,0:T(8,128)(2,1)S(1)} %copy.84), channel_id=1, source_target_pairs={{0,31},{1,30},{2,29},{3,28},{4,27},{5,26},{6,25},{7,24},{8,23},{9,... | collective-permute-start | bytes 1572872 | tf_op jit(solution)/shard_map/ppermute | solution.py:427
  174.8 27.9 %collective-permute-start.7 = (bf16[1,4096]{1,0:T(2,128)(2,1)S(1)}, bf16[1,4096]{1,0:T(2,128)(2,1)S(1)}, u32[]{:S(2)}, u32[]{:S(2)}) collective-permute-start(bf16[1,4096]{1,0:T(2,128)(2,1)S(1)} %copy.85), channel_id=1, source_target_pairs={{1,31},{2,30},{3,29},{4,28},{5,27},{6,26},{7,25},{8,24},{9,23},{10... | collective-permute-start | bytes 24584 | tf_op jit(solution)/shard_map/ppermute | solution.py:428
  202.7 46.9 %copy-start.8 = (bf16[64,4096]{1,0:T(8,128)(2,1)}, bf16[64,4096]{1,0:T(8,128)(2,1)S(1)}, u32[]{:S(2)}) copy-start(bf16[64,4096]{1,0:T(8,128)(2,1)S(1)} %collective-permute-done.6) | copy-start | bytes 1572868
  202.8 17.1 %collective-permute-start.9 = (bf16[8,64,768]{2,1,0:T(8,128)(2,1)}, bf16[8,64,768]{2,1,0:T(8,128)(2,1)S(1)}, u32[]{:S(2)}, u32[]{:S(2)}) collective-permute-start(bf16[8,64,768]{2,1,0:T(8,128)(2,1)} %get-tuple-element.104), channel_id=1, source_target_pairs={{0,28},{4,0},{8,4},{12,8},{16,12},{20,16},{24,20},{28,24},{1,29},{... | collective-permute-start | bytes 2359304 | tf_op jit(solution)/shard_map/ppermute | solution.py:866
  208.0 11.9 %collective-permute-start.8 = (bf16[32,8,768]{2,1,0:T(8,128)(2,1)}, bf16[32,8,768]{2,1,0:T(8,128)(2,1)S(1)}, u32[]{:S(2)}, u32[]{:S(2)}) collective-permute-start(bf16[32,8,768]{2,1,0:T(8,128)(2,1)} %get-tuple-element.103), channel_id=1, source_target_pairs={{0,3},{1,0},{2,1},{3,2},{4,7},{5,4},{6,5},{7,6},{8,11},{9,8},{10,9... | collective-permute-start | bytes 1179656 | tf_op jit(solution)/shard_map/ppermute | solution.py:865
  209.4 9.4 %collective-permute-start.10 = (bf16[8,8,768]{2,1,0:T(8,128)(2,1)}, bf16[8,8,768]{2,1,0:T(8,128)(2,1)S(1)}, u32[]{:S(2)}, u32[]{:S(2)}) collective-permute-start(bf16[8,8,768]{2,1,0:T(8,128)(2,1)} %get-tuple-element.105), channel_id=1, source_target_pairs={{0,31},{1,28},{2,29},{3,30},{4,3},{5,0},{6,1},{7,2},{8,7},{9,4},{1... | collective-permute-start | bytes 294920 | tf_op jit(solution)/shard_map/ppermute | solution.py:867
  211.3 42.4 %copy-start.25 = (bf16[64,512]{1,0:T(8,128)(2,1)S(1)}, bf16[64,512]{1,0:T(8,128)(2,1)}, u32[]{:S(2)}) copy-start(bf16[64,512]{1,0:T(8,128)(2,1)} %get-tuple-element.159) | copy-start | bytes 196612
  249.7 9.9 %collective-permute-start.11 = (bf16[8,64,256]{2,1,0:T(8,128)(2,1)}, bf16[8,64,256]{2,1,0:T(8,128)(2,1)S(1)}, u32[]{:S(2)}, u32[]{:S(2)}) collective-permute-start(bf16[8,64,256]{2,1,0:T(8,128)(2,1)} %get-tuple-element.109), channel_id=1, source_target_pairs={{0,1},{1,0},{2,3},{3,2},{4,5},{5,4},{6,7},{7,6},{8,9},{9,8},{10,11... | collective-permute-start | bytes 786440 | tf_op jit(solution)/shard_map/ppermute | solution.py:466
  252.2 12.0 %collective-permute-start.12 = (bf16[8,64,256]{2,1,0:T(8,128)(2,1)}, bf16[8,64,256]{2,1,0:T(8,128)(2,1)S(1)}, u32[]{:S(2)}, u32[]{:S(2)}) collective-permute-start(bf16[8,64,256]{2,1,0:T(8,128)(2,1)} %get-tuple-element.110), channel_id=1, source_target_pairs={{0,2},{1,3},{2,0},{3,1},{4,6},{5,7},{6,4},{7,5},{8,10},{9,11},{10,... | collective-permute-start | bytes 786440 | tf_op jit(solution)/shard_map/ppermute | solution.py:466
  253.6 10.6 %collective-permute-start.13 = (bf16[8,64,256]{2,1,0:T(8,128)(2,1)}, bf16[8,64,256]{2,1,0:T(8,128)(2,1)S(1)}, u32[]{:S(2)}, u32[]{:S(2)}) collective-permute-start(bf16[8,64,256]{2,1,0:T(8,128)(2,1)} %get-tuple-element.111), channel_id=1, source_target_pairs={{0,3},{1,2},{2,1},{3,0},{4,7},{5,6},{6,5},{7,4},{8,11},{9,10},{10,... | collective-permute-start | bytes 786440 | tf_op jit(solution)/shard_map/ppermute | solution.py:466
  270.8 31.6 %all-to-all-start.2 = ((bf16[32,128,128]{2,1,0:T(8,128)(2,1)}), bf16[32,128,128]{2,1,0:T(8,128)(2,1)S(1)}, u32[]{:S(2)}, u32[]{:S(2)}) async-start(bf16[32,128,128]{2,1,0:T(8,128)(2,1)} %bitcast.73), calls=%async_computation.2 | async-start | bytes 2097152 | tf_op jit(solution)/shard_map/all_to_all | solution.py:509
  302.4 15.1 %collective-permute-start.14 = (bf16[32,8,256]{2,1,0:T(8,128)(2,1)S(1)}, bf16[32,8,256]{2,1,0:T(8,128)(2,1)S(1)}, u32[]{:S(2)}, u32[]{:S(2)}) collective-permute-start(bf16[32,8,256]{2,1,0:T(8,128)(2,1)S(1)} %copy-done.46), channel_id=1, source_target_pairs={{0,1},{1,2},{2,3},{3,0},{4,5},{5,6},{6,7},{7,4},{8,9},{9,10},{10,1... | collective-permute-start | bytes 393224 | tf_op jit(solution)/shard_map/ppermute | solution.py:865
  303.8 13.8 %collective-permute-start.15 = (bf16[8,64,256]{2,1,0:T(8,128)(2,1)S(1)}, bf16[8,64,256]{2,1,0:T(8,128)(2,1)S(1)}, u32[]{:S(2)}, u32[]{:S(2)}) collective-permute-start(bf16[8,64,256]{2,1,0:T(8,128)(2,1)S(1)} %copy-done.45), channel_id=1, source_target_pairs={{0,4},{4,8},{8,12},{12,16},{16,20},{20,24},{24,28},{28,0},{1,5},{5... | collective-permute-start | bytes 786440 | tf_op jit(solution)/shard_map/ppermute | solution.py:866
  303.9 13.6 %collective-permute-start.16 = (bf16[8,8,256]{2,1,0:T(8,128)(2,1)S(1)}, bf16[8,8,256]{2,1,0:T(8,128)(2,1)S(1)}, u32[]{:S(2)}, u32[]{:S(2)}) collective-permute-start(bf16[8,8,256]{2,1,0:T(8,128)(2,1)S(1)} %copy-done.47), channel_id=1, source_target_pairs={{0,5},{1,6},{2,7},{3,4},{4,9},{5,10},{6,11},{7,8},{8,13},{9,14},{1... | collective-permute-start | bytes 98312 | tf_op jit(solution)/shard_map/ppermute | solution.py:867
  317.5 31.5 %all-to-all-start.3 = ((bf16[32,128,128]{2,1,0:T(8,128)(2,1)}), bf16[32,128,128]{2,1,0:T(8,128)(2,1)S(1)}, u32[]{:S(2)}, u32[]{:S(2)}) async-start(bf16[32,128,128]{2,1,0:T(8,128)(2,1)} %shard_map.308), calls=%async_computation.3 | async-start | bytes 2097152 | tf_op jit(solution)/shard_map/all_to_all | solution.py:528
  356.0 9.5 %collective-permute-start.17 = (bf16[8,64,256]{2,1,0:T(8,128)(2,1)}, bf16[8,64,256]{2,1,0:T(8,128)(2,1)S(1)}, u32[]{:S(2)}, u32[]{:S(2)}) collective-permute-start(bf16[8,64,256]{2,1,0:T(8,128)(2,1)} %get-tuple-element.134), channel_id=1, source_target_pairs={{0,1},{1,0},{2,3},{3,2},{4,5},{5,4},{6,7},{7,6},{8,9},{9,8},{10,11... | collective-permute-start | bytes 786440 | tf_op jit(solution)/shard_map/ppermute | solution.py:466
  357.4 12.3 %collective-permute-start.18 = (bf16[8,64,256]{2,1,0:T(8,128)(2,1)}, bf16[8,64,256]{2,1,0:T(8,128)(2,1)S(1)}, u32[]{:S(2)}, u32[]{:S(2)}) collective-permute-start(bf16[8,64,256]{2,1,0:T(8,128)(2,1)} %get-tuple-element.135), channel_id=1, source_target_pairs={{0,2},{1,3},{2,0},{3,1},{4,6},{5,7},{6,4},{7,5},{8,10},{9,11},{10,... | collective-permute-start | bytes 786440 | tf_op jit(solution)/shard_map/ppermute | solution.py:466
  358.8 12.4 %collective-permute-start.19 = (bf16[8,64,256]{2,1,0:T(8,128)(2,1)}, bf16[8,64,256]{2,1,0:T(8,128)(2,1)S(1)}, u32[]{:S(2)}, u32[]{:S(2)}) collective-permute-start(bf16[8,64,256]{2,1,0:T(8,128)(2,1)} %get-tuple-element.136), channel_id=1, source_target_pairs={{0,3},{1,2},{2,1},{3,0},{4,7},{5,6},{6,5},{7,4},{8,11},{9,10},{10,... | collective-permute-start | bytes 786440 | tf_op jit(solution)/shard_map/ppermute | solution.py:466
  398.8 10.4 %collective-permute-start.21 = (bf16[8,64,512]{2,1,0:T(8,128)(2,1)}, bf16[8,64,512]{2,1,0:T(8,128)(2,1)S(1)}, u32[]{:S(2)}, u32[]{:S(2)}) collective-permute-start(bf16[8,64,512]{2,1,0:T(8,128)(2,1)} %get-tuple-element.140), channel_id=1, source_target_pairs={{0,28},{4,0},{8,4},{12,8},{16,12},{20,16},{24,20},{28,24},{1,29},{... | collective-permute-start | bytes 1572872 | tf_op jit(solution)/shard_map/ppermute | solution.py:866
  398.9 10.3 %collective-permute-start.20 = (bf16[32,8,512]{2,1,0:T(8,128)(2,1)}, bf16[32,8,512]{2,1,0:T(8,128)(2,1)S(1)}, u32[]{:S(2)}, u32[]{:S(2)}) collective-permute-start(bf16[32,8,512]{2,1,0:T(8,128)(2,1)} %get-tuple-element.139), channel_id=1, source_target_pairs={{0,3},{1,0},{2,1},{3,2},{4,7},{5,4},{6,5},{7,6},{8,11},{9,8},{10,9... | collective-permute-start | bytes 786440 | tf_op jit(solution)/shard_map/ppermute | solution.py:865
  400.8 8.4 %collective-permute-start.22 = (bf16[8,8,512]{2,1,0:T(8,128)(2,1)}, bf16[8,8,512]{2,1,0:T(8,128)(2,1)S(1)}, u32[]{:S(2)}, u32[]{:S(2)}) collective-permute-start(bf16[8,8,512]{2,1,0:T(8,128)(2,1)} %get-tuple-element.141), channel_id=1, source_target_pairs={{0,31},{1,28},{2,29},{3,30},{4,3},{5,0},{6,1},{7,2},{8,7},{9,4},{1... | collective-permute-start | bytes 196616 | tf_op jit(solution)/shard_map/ppermute | solution.py:867
  436.4 10.4 %collective-permute-start.24 = (bf16[8,64,256]{2,1,0:T(8,128)(2,1)}, bf16[8,64,256]{2,1,0:T(8,128)(2,1)S(1)}, u32[]{:S(2)}, u32[]{:S(2)}) collective-permute-start(bf16[8,64,256]{2,1,0:T(8,128)(2,1)} %get-tuple-element.145), channel_id=1, source_target_pairs={{0,4},{4,8},{8,12},{12,16},{16,20},{20,24},{24,28},{28,0},{1,5},{5... | collective-permute-start | bytes 786440 | tf_op jit(solution)/shard_map/ppermute | solution.py:866
  436.4 10.4 %collective-permute-start.23 = (bf16[32,8,256]{2,1,0:T(8,128)(2,1)}, bf16[32,8,256]{2,1,0:T(8,128)(2,1)S(1)}, u32[]{:S(2)}, u32[]{:S(2)}) collective-permute-start(bf16[32,8,256]{2,1,0:T(8,128)(2,1)} %get-tuple-element.144), channel_id=1, source_target_pairs={{0,1},{1,2},{2,3},{3,0},{4,5},{5,6},{6,7},{7,4},{8,9},{9,10},{10,1... | collective-permute-start | bytes 393224 | tf_op jit(solution)/shard_map/ppermute | solution.py:865
  437.9 8.9 %collective-permute-start.25 = (bf16[8,8,256]{2,1,0:T(8,128)(2,1)}, bf16[8,8,256]{2,1,0:T(8,128)(2,1)S(1)}, u32[]{:S(2)}, u32[]{:S(2)}) collective-permute-start(bf16[8,8,256]{2,1,0:T(8,128)(2,1)} %get-tuple-element.146), channel_id=1, source_target_pairs={{0,5},{1,6},{2,7},{3,4},{4,9},{5,10},{6,11},{7,8},{8,13},{9,14},{1... | collective-permute-start | bytes 98312 | tf_op jit(solution)/shard_map/ppermute | solution.py:867
  (46 other events, 505.1 us)

commit v7 on v6

--- a/solution.py
+++ b/solution.py
@@ -386,7 +386,7 @@
         mid_ref[q] = mm(inner_t_ref[q], back).astype(BF16).reshape(2, rows, width)
         return carry
 
-    lax.fori_loop(0, devices, step, 0, unroll=8)
+    lax.fori_loop(0, devices, step, 0, unroll=16)
     copies[3].wait()
 
     for top in range(0, rows, PATCH):
@@ -591,7 +591,7 @@
     return wait
 
 
-def swin_band(flow, wait, bias_ref, gain_ref, weight_refs, scratch, staggered):
+def swin_band(flow, wait, bias_ref, gain_ref, weight_refs, scratch):
     qkv_ref, proj_ref, up_ref, down_ref = weight_refs
     mixed_ref, score_ref, prob_ref, active_ref = scratch
     count = flow.shape[0] // SPAN
@@ -634,16 +634,9 @@
             mixture = mm(prob_ref[w, :, lanes], value, TN)
             mixed_ref[rows, lanes] = jnp.where(lower, mixture[:SPAN], mixture[SPAN:]).astype(BF16)
 
-    passes = (scores_of, probs_of, mixture_of)
-    if staggered:
-        for turn in range(count + 2):
-            for n, run in enumerate(passes):
-                if 0 <= turn - n < count:
-                    run(turn - n)
-    else:
-        for run in passes:
-            for w in range(count):
-                run(w)
+    for run in (scores_of, probs_of, mixture_of):
+        for w in range(count):
+            run(w)
     wait((1, 2, 3))
     flow = flow + mm(mixed_ref[:, :D], proj_ref[...])
     normed = layer_norm(flow, gain_ref[1:2, :])
@@ -709,7 +702,7 @@
     step = zeta * grad
     half = state - step
     tokens = mm(to_windows(half).astype(BF16), embed_ref[...]).astype(BF16).astype(F32)
-    flow = swin_band(tokens, wait, bias_ref, gain_ref, targets, scratch, True)
+    flow = swin_band(tokens, wait, bias_ref, gain_ref, targets, scratch)
     result = from_windows(flow, half.shape[1]).astype(BF16)
     out_ref[:, :, :D] = result
     side_ref[:, :, :D] = result[:, :WIN]
@@ -748,7 +741,7 @@
     height, cols, _ = out_ref.shape
     band = rolled_band(1, shift_ref, tile_refs, rows, height)
     tokens = to_windows(band[:, :, :D])
-    flow = swin_band(tokens, wait, bias_ref, gain_ref, targets, scratch, False)
+    flow = swin_band(tokens, wait, bias_ref, gain_ref, targets, scratch)
     estimate = from_windows(mm(flow.astype(BF16), unembed_ref[...]), cols)
     narrow = estimate.astype(BF16)
     out_ref[...] = narrow
@@ -935,25 +928,33 @@
         write_pieces(pl.program_id(0) ^ place_ref[0], out_refs, result)
 
 
-def to_tile_kernel(sigma, scale, rows, *refs):
-    shift_ref, base_ref, *refs = refs
-    noise_ref, order_ref, out_ref = refs[4:]
-    count, cols, _ = base_ref.shape
+def lanes_of(patches):
+    count, cols, _ = patches.shape
     parts = LANES // cols
     groups = PATCH // parts
     width = groups * PATCH
-    state = base_ref[...] - sigma * rolled_band(-1, shift_ref, refs[:4], rows)
     bands = []
     for i in range(count):
         stacked = jnp.concatenate(
-            [state[i, :, h * width : (h + 1) * width] for h in range(parts)], axis=0
+            [patches[i, :, h * width : (h + 1) * width] for h in range(parts)], axis=0
         )
         turned = stacked.T
         bands.append(
             jnp.concatenate([turned[g * PATCH : (g + 1) * PATCH] for g in range(groups)], axis=1)
         )
-    moved = move_lanes(jnp.concatenate(bands, axis=0), order_ref[...])
+    return jnp.concatenate(bands, axis=0)
+
+
+def base_tile_kernel(scale, base_ref, noise_ref, order_ref, out_ref):
+    moved = move_lanes(lanes_of(base_ref[...]), order_ref[...])
     out_ref[...] = moved + scale * noise_ref[...]
+
+
+def last_tile_kernel(sigma, rows, shift_ref, tile_ref, *refs):
+    *back_refs, order_ref, out_ref = refs
+    estimate = rolled_band(-1, shift_ref, back_refs, rows)
+    moved = mm(lanes_of(estimate).astype(BF16), order_ref[...])
+    out_ref[...] = tile_ref[...] - sigma * moved
 
 
 def patches_of(tiles, j, place, kind=F32, parts=1):
@@ -982,22 +983,31 @@
 def tile_of(base, sigma, shift, back, scale, noise, j):
     rows, cols, _ = base.shape
     order = jnp.asarray(lane_order(cols)[1])
+    tile_spec = pl.BlockSpec((WIN * PATCH, cols * PATCH), lambda n, *_: (n, 0))
+    shape = jax.ShapeDtypeStruct((rows * PATCH, cols * PATCH), F32)
+    tile = pl.pallas_call(
+        functools.partial(base_tile_kernel, scale),
+        grid=(rows // WIN,),
+        in_specs=[
+            band_spec(cols, PIXELS),
+            pl.BlockSpec((None, WIN * PATCH, cols * PATCH), lambda n, *_: (j, n, 0)),
+            whole(order),
+        ],
+        out_specs=tile_spec,
+        out_shape=shape,
+        compiler_params=PARAMS,
+    )(base, noise, order)
     return pl.pallas_call(
-        functools.partial(to_tile_kernel, sigma, scale, rows),
+        functools.partial(last_tile_kernel, sigma, rows),
         grid_spec=pltpu.PrefetchScalarGridSpec(
             num_scalar_prefetch=1,
             grid=(rows // WIN,),
-            in_specs=[band_spec(cols, PIXELS)]
-            + [whole(value) for value in back]
-            + [
-                pl.BlockSpec((None, WIN * PATCH, cols * PATCH), lambda n, *_: (j, n, 0)),
-                whole(order),
-            ],
-            out_specs=pl.BlockSpec((WIN * PATCH, cols * PATCH), lambda n, *_: (n, 0)),
+            in_specs=[tile_spec] + [whole(value) for value in back] + [whole(order)],
+            out_specs=tile_spec,
         ),
-        out_shape=jax.ShapeDtypeStruct((rows * PATCH, cols * PATCH), F32),
+        out_shape=shape,
         compiler_params=PARAMS,
-    )(shift, base, *back, noise, order)
+    )(shift, tile, *back, order)
 
 
 def per_device(
@@ -1037,8 +1047,6 @@
             patches_of(image[None], 0, column, BF16, lanes), scale, data, None, None,
             (beside, lines),
         )
-        grad, lines = lax.optimization_barrier((grad, lines))
-        mirror = mirrored_exchange(*lines, devices)
         grads = [grad]
         state, extras, first_bias, biases, w_embed, w_unembed = beside
     for step in range(STEPS):
@@ -1057,13 +1065,17 @@
             w_embed, weights,
         )
         shift, before = places[step], SIGMAS[step]
+        first = from_neighbours(first, -1)
         if fast and step == 0:
-            first, mirror = lax.optimization_barrier((first, mirror))
+            first, lines = lax.optimization_barrier((first, lines))
+            mirror = mirrored_exchange(*lines, devices)
         rolled = second_block(
-            before, shift, from_neighbours(first, -1), biases[step], w_unembed, weights,
+            before, shift, first, biases[step], w_unembed, weights,
             lanes if fast and not last else 0,
         )
         back, moving = rolled[:4], rolled[4:]
+        if fast and step == 0:
+            moving, mirror = lax.optimization_barrier((moving, mirror))
         if last or not fast:
             back = from_neighbours(back, 1)
     return tile_of(state, before, shift, back, SIGMAS[STEPS], noise, STEPS - 1)

time: 465 us -> 463 us (level)
  waiting for transfers between devices: 142 us -> 135 us
    ppermute x4, waiting for transfers between devices: 21.8 us -> 15.9 us  [from_neighbours(): lax.ppermute(corner, ('ty', 'tx'), across)]
    pallas_call x1 -> x2, Pallas kernels: 8.52 us -> 14 us  [the longest x1 7.12 us: tile_of(): pl.pallas_call(functools.partial(last_tile_kernel, sigma, rows), grid_spe...]
  transfers between devices with their start and end apart: 30 -> 30, of which waited for: 17 -> 17; matrix products, arithmetic and copies ran while one was open for 12% -> 13% of each run, Pallas kernels for 12% -> 14%
where the time goes in v7:
time: 463 us; the launch traced here: 454 us
  Pallas kernels  193 us (42%)
  waiting for transfers between devices  135 us (29%)
  starting transfers between devices  51.9 us (11%)
  local copies, waits for them, and re-layouts  49 us (11%)
  other arithmetic  18.8 us (4%)
  between operations  6.21 us (1%)
    pallas_call x2, Pallas kernels, second_block(): pl.pallas_call(functools.partial(second_kernel, sigma, rows, parts), grid...  54.6 us
    pallas_call x2, Pallas kernels, first_block(): pl.pallas_call(functools.partial(first_kernel, zeta, sigma, len(grads), p...  53.6 us
    all_to_all x2, waiting for transfers between devices, patch_gradient(): lax.all_to_all(wave, ('ty', 'tx'), split_axis=0, concat_axis=0, tiled=True)  44 us
    ppermute x12, waiting for transfers between devices, swap_pieces(): lax.ppermute(pieces[m], 'tx', [(k, k ^ m) for k in range(lanes)])  40.8 us
    all_to_all x2, waiting for transfers between devices, patch_gradient(): lax.all_to_all(sent.reshape(part), ('ty', 'tx'), split_axis=0, concat_axi...  33.4 us
    unnamed x102, local copies, waits for them, and re-layouts  24 us
    pallas_call x2, Pallas kernels, patch_gradient(): pl.pallas_call(functools.partial(column_kernel, halved), in_specs=[pl.Blo...  22.2 us
    pallas_call x3, Pallas kernels, patches_of(): pl.pallas_call(functools.partial(to_patches_kernel, kind == BF16), grid_s...  18.8 us
  transfers between devices with their start and end apart: 30, of which 17 were waited for; matrix products, arithmetic and copies ran while one was open for 13% of the time, Pallas kernels for 14%

profile of v7, /device:TPU:0, one launch (start us, length us, event | category | flops | bytes accessed | tf_op | source)
XLA Modules:
  0.0 453.6 jit_solution(13536886374421452495)
XLA Ops:
  0.0 5.7 %shard_map.298 = (bf16[8,64,256]{2,1,0:T(8,128)(2,1)}, bf16[8,64,256]{2,1,0:T(8,128)(2,1)}, bf16[8,64,256]{2,1,0:T(8,128)(2,1)}, bf16[8,64,256]{2,1,0:T(8,128)(2,1)}) custom-call(s32[1]{0:T(128)} %bitcast.1.place_ref, f32[1,512,1024]{2,1,0:T(8,128)} %bitcast.67, bf16[1024,1024]{1,0:T(8,128)(2,1)} %constant.98.clone.order_ref), custom_call_target="tpu_custom_call" | custom-call | tf_op jit(solution)/shard_map/pallas_call | solution.py:967
  16.0 6.3 %collective-permute-done.1.refs_2_ = bf16[8,64,256]{2,1,0:T(8,128)(2,1)S(1)} collective-permute-done((bf16[8,64,256]{2,1,0:T(8,128)(2,1)}, bf16[8,64,256]{2,1,0:T(8,128)(2,1)S(1)}, u32[]{:S(2)}, u32[]{:S(2)}) %collective-permute-start.1) | collective-permute-done | bytes 262176 | tf_op jit(solution)/shard_map/ppermute | solution.py:466
  23.0 5.5 %shard_map.299 = bf16[16,2,2,128,128]{4,3,2,1,0:T(8,128)(2,1)} custom-call(bf16[8,64,256]{2,1,0:T(8,128)(2,1)} %get-tuple-element.76.refs_0_, bf16[8,64,256]{2,1,0:T(8,128)(2,1)} %copy-done.13, bf16[8,64,256]{2,1,0:T(8,128)(2,1)} %copy-done.14, bf16[8,64,256]{2,1,0:T(8,128)(2,1)} %copy-done.15, bf16[256,512]{1,0:T(8,128)(2,1)} %pad_maximum_fusion.5.refs_4_.first_ref, ...), custom_call_target="tpu_custom_call" | custom-call | tf_op jit(solution)/shard_map/pallas_call | solution.py:502
  28.5 5.0 %all-to-all-start = ((bf16[32,2,128,128]{3,2,1,0:T(8,128)(2,1)}), bf16[32,2,128,128]{3,2,1,0:T(8,128)(2,1)}, u32[]{:S(2)}, u32[]{:S(2)}) async-start(bf16[32,2,128,128]{3,2,1,0:T(8,128)(2,1)} %bitcast.70), calls=%async_computation | async-start | bytes 4194304 | tf_op jit(solution)/shard_map/all_to_all | solution.py:509
  35.5 4.7 %fusion.18 = (f32[1,128,4096]{2,1,0:T(8,128)}, f32[1,128,4096]{2,1,0:T(8,128)}) fusion(f32[2,128,4096]{2,1,0:T(8,128)} %param.36), kind=kLoop, calls=%fused_computation.77 | loop fusion | bytes 8388608 | tf_op jit(solution)/shard_map/slice | solution.py:403
  43.1 4.7 %fusion.17 = (f32[1,128,4096]{2,1,0:T(8,128)}, f32[1,128,4096]{2,1,0:T(8,128)}) fusion(f32[2,128,4096]{2,1,0:T(8,128)} %param.37), kind=kLoop, calls=%fused_computation.76 | loop fusion | bytes 8388608 | tf_op jit(solution)/shard_map/slice | solution.py:407
  64.8 17.5 %all-to-all-done.refs_0_ = bf16[32,2,128,128]{3,2,1,0:T(8,128)(2,1)} async-done(((bf16[32,2,128,128]{3,2,1,0:T(8,128)(2,1)}), bf16[32,2,128,128]{3,2,1,0:T(8,128)(2,1)}, u32[]{:S(2)}, u32[]{:S(2)}) %all-to-all-start) | async-done | bytes 2097184 | tf_op jit(solution)/shard_map/all_to_all | solution.py:509
  82.2 11.7 %shard_map.300 = bf16[32,2,128,128]{3,2,1,0:T(8,128)(2,1)} custom-call(bf16[32,2,128,128]{3,2,1,0:T(8,128)(2,1)} %all-to-all-done.refs_0_, bf16[512,512]{1,0:T(8,128)(2,1)} %constant.99.clone.refs_1_.refs_3_, bf16[32,256,256]{2,1,0:T(8,128)(2,1)} %constant.101.clone.refs_2_.refs_4_, bf16[32,128,128]{2,1,0:T(8,128)(2,1)} %bitcast.65, ...), custom_call_target="tpu_custom_call" | custom-call | tf_op jit(solution)/shard_map/pallas_call | solution.py:517
  93.9 4.5 %all-to-all-start.1 = ((bf16[32,2,128,128]{3,2,1,0:T(8,128)(2,1)}), bf16[32,2,128,128]{3,2,1,0:T(8,128)(2,1)S(1)}, u32[]{:S(2)}, u32[]{:S(2)}) async-start(bf16[32,2,128,128]{3,2,1,0:T(8,128)(2,1)} %shard_map.300), calls=%async_computation.1 | async-start | bytes 4194304 | tf_op jit(solution)/shard_map/all_to_all | solution.py:528
  98.5 6.5 %shard_map.301.refs_1_ = f32[32,64,256]{2,1,0:T(8,128)} custom-call(s32[1]{0:T(128)} %bitcast.1.place_ref, f32[1,512,1024]{2,1,0:T(8,128)} %bitcast.68, bf16[1024,1024]{1,0:T(8,128)(2,1)} %constant.98.clone.order_ref), custom_call_target="tpu_custom_call" | custom-call | tf_op jit(solution)/shard_map/pallas_call | solution.py:967
  106.4 6.6 %shard_map.302.refs_6_ = f32[32,64,256]{2,1,0:T(8,128)} custom-call(s32[1]{0:T(128)} %bitcast.1.place_ref, f32[2,512,1024]{2,1,0:T(8,128)} %noise_ref.1, bf16[1024,1024]{1,0:T(8,128)(2,1)} %constant.98.clone.order_ref), custom_call_target="tpu_custom_call" | custom-call | tf_op jit(solution)/shard_map/pallas_call | solution.py:967
  128.8 18.4 %all-to-all-done.1 = bf16[32,2,128,128]{3,2,1,0:T(8,128)(2,1)S(1)} async-done(((bf16[32,2,128,128]{3,2,1,0:T(8,128)(2,1)}), bf16[32,2,128,128]{3,2,1,0:T(8,128)(2,1)S(1)}, u32[]{:S(2)}, u32[]{:S(2)}) %all-to-all-start.1) | async-done | bytes 2097184 | tf_op jit(solution)/shard_map/all_to_all | solution.py:528
  148.5 7.2 %shard_map.303 = (bf16[8,64,256]{2,1,0:T(8,128)(2,1)}, bf16[8,64,256]{2,1,0:T(8,128)(2,1)}, bf16[8,64,256]{2,1,0:T(8,128)(2,1)}, bf16[8,64,256]{2,1,0:T(8,128)(2,1)}) custom-call(bf16[16,2,2,128,128]{4,3,2,1,0:T(8,128)(2,1)} %bitcast.69, bf16[256,512]{1,0:T(8,128)(2,1)} %pad_maximum_fusion.5.refs_4_.first_ref, ...), custom_call_target="tpu_custom_call" | custom-call | tf_op jit(solution)/shard_map/pallas_call | solution.py:531
  159.9 5.3 %collective-permute-done.3.refs_3_.refs_7_ = bf16[8,64,256]{2,1,0:T(8,128)(2,1)S(1)} collective-permute-done((bf16[8,64,256]{2,1,0:T(8,128)(2,1)}, bf16[8,64,256]{2,1,0:T(8,128)(2,1)S(1)}, u32[]{:S(2)}, u32[]{:S(2)}) %collective-permute-start.3) | collective-permute-done | bytes 262176 | tf_op jit(solution)/shard_map/ppermute | solution.py:466
  165.1 5.5 %collective-permute-done.4.refs_4_.refs_8_ = bf16[8,64,256]{2,1,0:T(8,128)(2,1)S(1)} collective-permute-done((bf16[8,64,256]{2,1,0:T(8,128)(2,1)}, bf16[8,64,256]{2,1,0:T(8,128)(2,1)S(1)}, u32[]{:S(2)}, u32[]{:S(2)}) %collective-permute-start.4) | collective-permute-done | bytes 262176 | tf_op jit(solution)/shard_map/ppermute | solution.py:466
  171.5 27.0 %shard_map.304 = (f32[32,64,256]{2,1,0:T(8,128)}, bf16[32,64,768]{2,1,0:T(8,128)(2,1)}, bf16[32,8,768]{2,1,0:T(8,128)(2,1)}, bf16[8,64,768]{2,1,0:T(8,128)(2,1)}, bf16[8,8,768]{2,1,0:T(8,128)(2,1)}) custom-call(s32[3]{0:T(128)} %pad_add_fusion.1.refs_0_, f32[32,64,256]{2,1,0:T(8,128)} %shard_map.301.refs_1_, ...), custom_call_target="tpu_custom_call" | custom-call | tf_op jit(solution)/shard_map/pallas_call | solution.py:806
  203.3 8.6 %collective-permute-done.8.refs_4_ = bf16[8,8,768]{2,1,0:T(8,128)(2,1)S(1)} collective-permute-done((bf16[8,8,768]{2,1,0:T(8,128)(2,1)}, bf16[8,8,768]{2,1,0:T(8,128)(2,1)S(1)}, u32[]{:S(2)}, u32[]{:S(2)}) %collective-permute-start.8) | collective-permute-done | bytes 98336 | tf_op jit(solution)/shard_map/ppermute | solution.py:860
  219.2 28.4 %shard_map.305 = (bf16[32,64,256]{2,1,0:T(8,128)(2,1)}, bf16[32,8,256]{2,1,0:T(8,128)(2,1)}, bf16[8,64,256]{2,1,0:T(8,128)(2,1)}, bf16[8,8,256]{2,1,0:T(8,128)(2...) custom-call(s32[3]{0:T(128)} %pad_add_fusion.1.refs_0_, ...), custom_call_target="tpu_custom_call" | custom-call | tf_op jit(solution)/shard_map/pallas_call | solution.py:833
  257.0 6.9 %collective-permute-done.12.refs_2_ = bf16[8,64,256]{2,1,0:T(8,128)(2,1)S(1)} collective-permute-done((bf16[8,64,256]{2,1,0:T(8,128)(2,1)}, bf16[8,64,256]{2,1,0:T(8,128)(2,1)S(1)}, u32[]{:S(2)}, u32[]{:S(2)}) %collective-permute-start.12) | collective-permute-done | bytes 262176 | tf_op jit(solution)/shard_map/ppermute | solution.py:466
  265.3 5.7 %shard_map.306 = bf16[16,2,128,128]{3,2,1,0:T(8,128)(2,1)} custom-call(bf16[8,64,256]{2,1,0:T(8,128)(2,1)} %get-tuple-element.108.refs_0_, bf16[8,64,256]{2,1,0:T(8,128)(2,1)} %copy-done.26, bf16[8,64,256]{2,1,0:T(8,128)(2,1)} %copy-done.27, bf16[8,64,256]{2,1,0:T(8,128)(2,1)} %copy-done.28, bf16[256,512]{1,0:T(8,128)(2,1)} %pad_maximum_fusion.6.refs_4_, ...), custom_call_target="tpu_custom_call" | custom-call | tf_op jit(solution)/shard_map/pallas_call | solution.py:502
  280.4 5.4 %shard_map.307.refs_5_ = bf16[32,128,128]{2,1,0:T(8,128)(2,1)} custom-call(bf16[32,128,128]{2,1,0:T(8,128)(2,1)} %bitcast.66, bf16[32,128,128]{2,1,0:T(8,128)(2,1)} %bitcast.71, bf16[2,128,128]{2,1,0:T(8,128)(2,1)} %add_convert_fusion.pick_ref, bf16[2,128,128]{2,1,0:T(8,128)(2,1)} %constant.113.clone.flip_ref), custom_call_target="tpu_custom_call" | custom-call | tf_op jit(solution)/shard_map/pallas_call | solution.py:447
  285.8 15.9 %all-to-all-done.2.refs_2_ = bf16[32,128,128]{2,1,0:T(8,128)(2,1)S(1)} async-done(((bf16[32,128,128]{2,1,0:T(8,128)(2,1)}), bf16[32,128,128]{2,1,0:T(8,128)(2,1)S(1)}, u32[]{:S(2)}, u32[]{:S(2)}) %all-to-all-start.2) | async-done | bytes 1048608 | tf_op jit(solution)/shard_map/all_to_all | solution.py:509
  305.7 10.5 %shard_map.308 = bf16[32,128,128]{2,1,0:T(8,128)(2,1)} custom-call(s32[1]{0:T(128)} %bitcast.28.refs_0_, f32[32,2,8,128]{3,2,1,0:T(8,128)} %broadcast_in_dim.79.refs_1_, bf16[32,128,128]{2,1,0:T(8,128)(2,1)} %copy-done.1, bf16[512,512]{1,0:T(8,128)(2,1)} %constant.99.clone.refs_1_.refs_3_, bf16[32,256,256]{2,1,0:T(8,128)(2,1)} %constant.101.clone.refs_2_.refs_4_, ...), custom_call_target="tpu_custom_call" | custom-call | tf_op jit(solution)/shard_map/pallas_call | solution.py:517
  316.3 5.0 %all-to-all-start.3 = ((bf16[32,128,128]{2,1,0:T(8,128)(2,1)}), bf16[32,128,128]{2,1,0:T(8,128)(2,1)S(1)}, u32[]{:S(2)}, u32[]{:S(2)}) async-start(bf16[32,128,128]{2,1,0:T(8,128)(2,1)} %shard_map.308), calls=%async_computation.3 | async-start | bytes 2097152 | tf_op jit(solution)/shard_map/all_to_all | solution.py:528
  322.1 25.7 %all-to-all-done.3 = bf16[32,128,128]{2,1,0:T(8,128)(2,1)S(1)} async-done(((bf16[32,128,128]{2,1,0:T(8,128)(2,1)}), bf16[32,128,128]{2,1,0:T(8,128)(2,1)S(1)}, u32[]{:S(2)}, u32[]{:S(2)}) %all-to-all-start.3) | async-done | bytes 1048608 | tf_op jit(solution)/shard_map/all_to_all | solution.py:528
  348.7 6.1 %shard_map.309 = (bf16[8,64,256]{2,1,0:T(8,128)(2,1)}, bf16[8,64,256]{2,1,0:T(8,128)(2,1)}, bf16[8,64,256]{2,1,0:T(8,128)(2,1)}, bf16[8,64,256]{2,1,0:T(8,128)(2,1)}) custom-call(bf16[16,2,128,128]{3,2,1,0:T(8,128)(2,1)} %bitcast.74, bf16[256,512]{1,0:T(8,128)(2,1)} %pad_maximum_fusion.7.first_ref, f32[2,256,256]{2,1,0:T(8,128)} %constant.107.clone.refs_5_.twist_ref, ...), custom_call_target="tpu_custom_call" | custom-call | tf_op jit(solution)/shard_map/pallas_call | solution.py:531
  358.3 5.9 %collective-permute-done.17.refs_11_ = bf16[8,64,256]{2,1,0:T(8,128)(2,1)S(1)} collective-permute-done((bf16[8,64,256]{2,1,0:T(8,128)(2,1)}, bf16[8,64,256]{2,1,0:T(8,128)(2,1)S(1)}, u32[]{:S(2)}, u32[]{:S(2)}) %collective-permute-start.17) | collective-permute-done | bytes 262176 | tf_op jit(solution)/shard_map/ppermute | solution.py:466
  370.7 26.6 %shard_map.310 = (f32[32,64,256]{2,1,0:T(8,128)}, bf16[32,64,512]{2,1,0:T(8,128)(2,1)}, bf16[32,8,512]{2,1,0:T(8,128)(2,1)}, bf16[8,64,512]{2,1,0:T(8,128)(2,1)}, bf16[8,8,512]{2,1,0:T(8,128)(2,1)}) custom-call(s32[3]{0:T(128)} %pad_add_fusion.1.refs_0_, f32[32,64,256]{2,1,0:T(8,128)} %get-tuple-element.89.refs_1_, ...), custom_call_target="tpu_custom_call" | custom-call | tf_op jit(solution)/shard_map/pallas_call | solution.py:806
  401.7 6.0 %collective-permute-done.22.refs_4_ = bf16[8,8,512]{2,1,0:T(8,128)(2,1)S(1)} collective-permute-done((bf16[8,8,512]{2,1,0:T(8,128)(2,1)}, bf16[8,8,512]{2,1,0:T(8,128)(2,1)S(1)}, u32[]{:S(2)}, u32[]{:S(2)}) %collective-permute-start.22) | collective-permute-done | bytes 65568 | tf_op jit(solution)/shard_map/ppermute | solution.py:860
  408.7 26.2 %shard_map.312 = (bf16[32,64,256]{2,1,0:T(8,128)(2,1)}, bf16[32,8,256]{2,1,0:T(8,128)(2,1)}, bf16[8,64,256]{2,1,0:T(8,128)(2,1)}, bf16[8,8,256]{2,1,0:T(8,128)(2,1)}) custom-call(s32[3]{0:T(128)} %pad_add_fusion.refs_0_.shift_ref, bf16[32,64,512]{2,1,0:T(8,128)(2,1)} %get-tuple-element.138.refs_1_, bf16[32,8,512]{2,1,0:T(8,128)(2,1)} %copy-done.12, ...), custom_call_target="tpu_custom_call" | custom-call | tf_op jit(solution)/shard_map/pallas_call | solution.py:833
  437.1 6.9 %shard_map.311.tile_ref = f32[512,1024]{1,0:T(8,128)} custom-call(f32[32,64,256]{2,1,0:T(8,128)} %get-tuple-element.137.base_ref, f32[2,512,1024]{2,1,0:T(8,128)} %noise_ref.1, bf16[1024,1024]{1,0:T(8,128)(2,1)} %constant.114.clone.order_ref.refs_4_), custom_call_target="tpu_custom_call" | custom-call | tf_op jit(solution)/shard_map/pallas_call | solution.py:988
  446.1 7.1 %shard_map.313 = f32[512,1024]{1,0:T(8,128)} custom-call(s32[3]{0:T(128)} %pad_add_fusion.refs_0_.shift_ref, f32[512,1024]{1,0:T(8,128)} %shard_map.311.tile_ref, bf16[32,64,256]{2,1,0:T(8,128)(2,1)} %get-tuple-element.143.refs_0_, bf16[32,8,256]{2,1,0:T(8,128)(2,1)} %copy-done.36, bf16[8,64,256]{2,1,0:T(8,128)(2,1)} %copy-done.16, ...), custom_call_target="tpu_custom_call" | custom-call | tf_op jit(solution)/shard_map/pallas_call | solution.py:1000
  (198 shorter events, 108.6 us)
Async XLA Ops:
  5.7 10.3 %collective-permute-start = (bf16[8,64,256]{2,1,0:T(8,128)(2,1)}, bf16[8,64,256]{2,1,0:T(8,128)(2,1)S(1)}, u32[]{:S(2)}, u32[]{:S(2)}) collective-permute-start(bf16[8,64,256]{2,1,0:T(8,128)(2,1)} %get-tuple-element.77), channel_id=1, source_target_pairs={{0,1},{1,0},{2,3},{3,2},{4,5},{5,4},{6,7},{7,6},{8,9},{9,8},{10,11... | collective-permute-start | bytes 786440 | tf_op jit(solution)/shard_map/ppermute | solution.py:466
  8.6 13.6 %collective-permute-start.1 = (bf16[8,64,256]{2,1,0:T(8,128)(2,1)}, bf16[8,64,256]{2,1,0:T(8,128)(2,1)S(1)}, u32[]{:S(2)}, u32[]{:S(2)}) collective-permute-start(bf16[8,64,256]{2,1,0:T(8,128)(2,1)} %get-tuple-element.78), channel_id=1, source_target_pairs={{0,2},{1,3},{2,0},{3,1},{4,6},{5,7},{6,4},{7,5},{8,10},{9,11},{10,... | collective-permute-start | bytes 786440 | tf_op jit(solution)/shard_map/ppermute | solution.py:466
  10.1 12.1 %collective-permute-start.2 = (bf16[8,64,256]{2,1,0:T(8,128)(2,1)}, bf16[8,64,256]{2,1,0:T(8,128)(2,1)S(1)}, u32[]{:S(2)}, u32[]{:S(2)}) collective-permute-start(bf16[8,64,256]{2,1,0:T(8,128)(2,1)} %get-tuple-element.79), channel_id=1, source_target_pairs={{0,3},{1,2},{2,1},{3,0},{4,7},{5,6},{6,5},{7,4},{8,11},{9,10},{10,... | collective-permute-start | bytes 786440 | tf_op jit(solution)/shard_map/ppermute | solution.py:466
  28.5 53.7 %all-to-all-start = ((bf16[32,2,128,128]{3,2,1,0:T(8,128)(2,1)}), bf16[32,2,128,128]{3,2,1,0:T(8,128)(2,1)}, u32[]{:S(2)}, u32[]{:S(2)}) async-start(bf16[32,2,128,128]{3,2,1,0:T(8,128)(2,1)} %bitcast.70), calls=%async_computation | async-start | bytes 4194304 | tf_op jit(solution)/shard_map/all_to_all | solution.py:509
  93.9 53.3 %all-to-all-start.1 = ((bf16[32,2,128,128]{3,2,1,0:T(8,128)(2,1)}), bf16[32,2,128,128]{3,2,1,0:T(8,128)(2,1)S(1)}, u32[]{:S(2)}, u32[]{:S(2)}) async-start(bf16[32,2,128,128]{3,2,1,0:T(8,128)(2,1)} %shard_map.300), calls=%async_computation.1 | async-start | bytes 4194304 | tf_op jit(solution)/shard_map/all_to_all | solution.py:528
  155.7 9.4 %collective-permute-start.3 = (bf16[8,64,256]{2,1,0:T(8,128)(2,1)}, bf16[8,64,256]{2,1,0:T(8,128)(2,1)S(1)}, u32[]{:S(2)}, u32[]{:S(2)}) collective-permute-start(bf16[8,64,256]{2,1,0:T(8,128)(2,1)} %get-tuple-element.83), channel_id=1, source_target_pairs={{0,1},{1,0},{2,3},{3,2},{4,5},{5,4},{6,7},{7,6},{8,9},{9,8},{10,11... | collective-permute-start | bytes 786440 | tf_op jit(solution)/shard_map/ppermute | solution.py:466
  157.2 13.4 %collective-permute-start.4 = (bf16[8,64,256]{2,1,0:T(8,128)(2,1)}, bf16[8,64,256]{2,1,0:T(8,128)(2,1)S(1)}, u32[]{:S(2)}, u32[]{:S(2)}) collective-permute-start(bf16[8,64,256]{2,1,0:T(8,128)(2,1)} %get-tuple-element.84), channel_id=1, source_target_pairs={{0,2},{1,3},{2,0},{3,1},{4,6},{5,7},{6,4},{7,5},{8,10},{9,11},{10,... | collective-permute-start | bytes 786440 | tf_op jit(solution)/shard_map/ppermute | solution.py:466
  158.7 11.9 %collective-permute-start.5 = (bf16[8,64,256]{2,1,0:T(8,128)(2,1)}, bf16[8,64,256]{2,1,0:T(8,128)(2,1)S(1)}, u32[]{:S(2)}, u32[]{:S(2)}) collective-permute-start(bf16[8,64,256]{2,1,0:T(8,128)(2,1)} %get-tuple-element.85), channel_id=1, source_target_pairs={{0,3},{1,2},{2,1},{3,0},{4,7},{5,6},{6,5},{7,4},{8,11},{9,10},{10,... | collective-permute-start | bytes 786440 | tf_op jit(solution)/shard_map/ppermute | solution.py:466
  171.5 41.7 %copy-start.2 = (bf16[64,4096]{0,1:T(8,128)(2,1)S(1)}, bf16[64,4096]{0,1:T(8,128)(2,1)}, u32[]{:S(2)}) copy-start(bf16[64,4096]{0,1:T(8,128)(2,1)} %slice.57) | copy-start | bytes 1572868
  198.5 13.9 %collective-permute-start.7 = (bf16[8,64,768]{2,1,0:T(8,128)(2,1)}, bf16[8,64,768]{2,1,0:T(8,128)(2,1)S(1)}, u32[]{:S(2)}, u32[]{:S(2)}) collective-permute-start(bf16[8,64,768]{2,1,0:T(8,128)(2,1)} %get-tuple-element.92), channel_id=1, source_target_pairs={{0,28},{4,0},{8,4},{12,8},{16,12},{20,16},{24,20},{28,24},{1,29},{... | collective-permute-start | bytes 2359304 | tf_op jit(solution)/shard_map/ppermute | solution.py:859
  199.6 12.8 %collective-permute-start.6 = (bf16[32,8,768]{2,1,0:T(8,128)(2,1)}, bf16[32,8,768]{2,1,0:T(8,128)(2,1)S(1)}, u32[]{:S(2)}, u32[]{:S(2)}) collective-permute-start(bf16[32,8,768]{2,1,0:T(8,128)(2,1)} %get-tuple-element.91), channel_id=1, source_target_pairs={{0,3},{1,0},{2,1},{3,2},{4,7},{5,4},{6,5},{7,6},{8,11},{9,8},{10,9... | collective-permute-start | bytes 1179656 | tf_op jit(solution)/shard_map/ppermute | solution.py:858
  200.3 11.6 %collective-permute-start.8 = (bf16[8,8,768]{2,1,0:T(8,128)(2,1)}, bf16[8,8,768]{2,1,0:T(8,128)(2,1)S(1)}, u32[]{:S(2)}, u32[]{:S(2)}) collective-permute-start(bf16[8,8,768]{2,1,0:T(8,128)(2,1)} %get-tuple-element.93), channel_id=1, source_target_pairs={{0,31},{1,28},{2,29},{3,30},{4,3},{5,0},{6,1},{7,2},{8,7},{9,4},{1... | collective-permute-start | bytes 294920 | tf_op jit(solution)/shard_map/ppermute | solution.py:860
  214.4 33.2 %collective-permute-start.9 = (bf16[64,4096]{1,0:T(8,128)(2,1)}, bf16[64,4096]{1,0:T(8,128)(2,1)S(1)}, u32[]{:S(2)}, u32[]{:S(2)}) collective-permute-start(bf16[64,4096]{1,0:T(8,128)(2,1)} %copy.85), channel_id=1, source_target_pairs={{0,31},{1,30},{2,29},{3,28},{4,27},{5,26},{6,25},{7,24},{8,23},{9,... | collective-permute-start | bytes 1572872 | tf_op jit(solution)/shard_map/ppermute | solution.py:427
  218.3 29.3 %collective-permute-start.10 = (bf16[1,4096]{1,0:T(2,128)(2,1)S(1)}, bf16[1,4096]{1,0:T(2,128)(2,1)S(1)}, u32[]{:S(2)}, u32[]{:S(2)}) collective-permute-start(bf16[1,4096]{1,0:T(2,128)(2,1)S(1)} %copy.86), channel_id=1, source_target_pairs={{1,31},{2,30},{3,29},{4,28},{5,27},{6,26},{7,25},{8,24},{9,23},{10... | collective-permute-start | bytes 24584 | tf_op jit(solution)/shard_map/ppermute | solution.py:428
  247.6 9.4 %collective-permute-start.11 = (bf16[8,64,256]{2,1,0:T(8,128)(2,1)}, bf16[8,64,256]{2,1,0:T(8,128)(2,1)S(1)}, u32[]{:S(2)}, u32[]{:S(2)}) collective-permute-start(bf16[8,64,256]{2,1,0:T(8,128)(2,1)} %get-tuple-element.109), channel_id=1, source_target_pairs={{0,1},{1,0},{2,3},{3,2},{4,5},{5,4},{6,7},{7,6},{8,9},{9,8},{10,11... | collective-permute-start | bytes 786440 | tf_op jit(solution)/shard_map/ppermute | solution.py:466
  250.0 13.9 %collective-permute-start.12 = (bf16[8,64,256]{2,1,0:T(8,128)(2,1)}, bf16[8,64,256]{2,1,0:T(8,128)(2,1)S(1)}, u32[]{:S(2)}, u32[]{:S(2)}) collective-permute-start(bf16[8,64,256]{2,1,0:T(8,128)(2,1)} %get-tuple-element.110), channel_id=1, source_target_pairs={{0,2},{1,3},{2,0},{3,1},{4,6},{5,7},{6,4},{7,5},{8,10},{9,11},{10,... | collective-permute-start | bytes 786440 | tf_op jit(solution)/shard_map/ppermute | solution.py:466
  251.5 12.4 %collective-permute-start.13 = (bf16[8,64,256]{2,1,0:T(8,128)(2,1)}, bf16[8,64,256]{2,1,0:T(8,128)(2,1)S(1)}, u32[]{:S(2)}, u32[]{:S(2)}) collective-permute-start(bf16[8,64,256]{2,1,0:T(8,128)(2,1)} %get-tuple-element.111), channel_id=1, source_target_pairs={{0,3},{1,2},{2,1},{3,0},{4,7},{5,6},{6,5},{7,4},{8,11},{9,10},{10,... | collective-permute-start | bytes 786440 | tf_op jit(solution)/shard_map/ppermute | solution.py:466
  271.1 30.6 %all-to-all-start.2 = ((bf16[32,128,128]{2,1,0:T(8,128)(2,1)}), bf16[32,128,128]{2,1,0:T(8,128)(2,1)S(1)}, u32[]{:S(2)}, u32[]{:S(2)}) async-start(bf16[32,128,128]{2,1,0:T(8,128)(2,1)} %bitcast.73), calls=%async_computation.2 | async-start | bytes 2097152 | tf_op jit(solution)/shard_map/all_to_all | solution.py:509
  301.7 14.5 %collective-permute-start.14 = (bf16[32,8,256]{2,1,0:T(8,128)(2,1)S(1)}, bf16[32,8,256]{2,1,0:T(8,128)(2,1)S(1)}, u32[]{:S(2)}, u32[]{:S(2)}) collective-permute-start(bf16[32,8,256]{2,1,0:T(8,128)(2,1)S(1)} %copy-done.46), channel_id=1, source_target_pairs={{0,1},{1,2},{2,3},{3,0},{4,5},{5,6},{6,7},{7,4},{8,9},{9,10},{10,1... | collective-permute-start | bytes 393224 | tf_op jit(solution)/shard_map/ppermute | solution.py:858
  303.0 13.2 %collective-permute-start.15 = (bf16[8,64,256]{2,1,0:T(8,128)(2,1)S(1)}, bf16[8,64,256]{2,1,0:T(8,128)(2,1)S(1)}, u32[]{:S(2)}, u32[]{:S(2)}) collective-permute-start(bf16[8,64,256]{2,1,0:T(8,128)(2,1)S(1)} %copy-done.45), channel_id=1, source_target_pairs={{0,4},{4,8},{8,12},{12,16},{16,20},{20,24},{24,28},{28,0},{1,5},{5... | collective-permute-start | bytes 786440 | tf_op jit(solution)/shard_map/ppermute | solution.py:859
  303.2 13.0 %collective-permute-start.16 = (bf16[8,8,256]{2,1,0:T(8,128)(2,1)S(1)}, bf16[8,8,256]{2,1,0:T(8,128)(2,1)S(1)}, u32[]{:S(2)}, u32[]{:S(2)}) collective-permute-start(bf16[8,8,256]{2,1,0:T(8,128)(2,1)S(1)} %copy-done.47), channel_id=1, source_target_pairs={{0,5},{1,6},{2,7},{3,4},{4,9},{5,10},{6,11},{7,8},{8,13},{9,14},{1... | collective-permute-start | bytes 98312 | tf_op jit(solution)/shard_map/ppermute | solution.py:860
  316.2 38.6 %copy-start.39 = (bf16[8,8,256]{2,1,0:T(8,128)(2,1)}, bf16[8,8,256]{2,1,0:T(8,128)(2,1)S(1)}, u32[]{:S(2)}) copy-start(bf16[8,8,256]{2,1,0:T(8,128)(2,1)S(1)} %collective-permute-done.16.refs_5_) | copy-start | bytes 98308
  316.3 31.5 %all-to-all-start.3 = ((bf16[32,128,128]{2,1,0:T(8,128)(2,1)}), bf16[32,128,128]{2,1,0:T(8,128)(2,1)S(1)}, u32[]{:S(2)}, u32[]{:S(2)}) async-start(bf16[32,128,128]{2,1,0:T(8,128)(2,1)} %shard_map.308), calls=%async_computation.3 | async-start | bytes 2097152 | tf_op jit(solution)/shard_map/all_to_all | solution.py:528
  354.8 9.5 %collective-permute-start.17 = (bf16[8,64,256]{2,1,0:T(8,128)(2,1)}, bf16[8,64,256]{2,1,0:T(8,128)(2,1)S(1)}, u32[]{:S(2)}, u32[]{:S(2)}) collective-permute-start(bf16[8,64,256]{2,1,0:T(8,128)(2,1)} %get-tuple-element.134), channel_id=1, source_target_pairs={{0,1},{1,0},{2,3},{3,2},{4,5},{5,4},{6,7},{7,6},{8,9},{9,8},{10,11... | collective-permute-start | bytes 786440 | tf_op jit(solution)/shard_map/ppermute | solution.py:466
  356.2 12.3 %collective-permute-start.18 = (bf16[8,64,256]{2,1,0:T(8,128)(2,1)}, bf16[8,64,256]{2,1,0:T(8,128)(2,1)S(1)}, u32[]{:S(2)}, u32[]{:S(2)}) collective-permute-start(bf16[8,64,256]{2,1,0:T(8,128)(2,1)} %get-tuple-element.135), channel_id=1, source_target_pairs={{0,2},{1,3},{2,0},{3,1},{4,6},{5,7},{6,4},{7,5},{8,10},{9,11},{10,... | collective-permute-start | bytes 786440 | tf_op jit(solution)/shard_map/ppermute | solution.py:466
  357.6 12.4 %collective-permute-start.19 = (bf16[8,64,256]{2,1,0:T(8,128)(2,1)}, bf16[8,64,256]{2,1,0:T(8,128)(2,1)S(1)}, u32[]{:S(2)}, u32[]{:S(2)}) collective-permute-start(bf16[8,64,256]{2,1,0:T(8,128)(2,1)} %get-tuple-element.136), channel_id=1, source_target_pairs={{0,3},{1,2},{2,1},{3,0},{4,7},{5,6},{6,5},{7,4},{8,11},{9,10},{10,... | collective-permute-start | bytes 786440 | tf_op jit(solution)/shard_map/ppermute | solution.py:466
  397.4 10.4 %collective-permute-start.21 = (bf16[8,64,512]{2,1,0:T(8,128)(2,1)}, bf16[8,64,512]{2,1,0:T(8,128)(2,1)S(1)}, u32[]{:S(2)}, u32[]{:S(2)}) collective-permute-start(bf16[8,64,512]{2,1,0:T(8,128)(2,1)} %get-tuple-element.140), channel_id=1, source_target_pairs={{0,28},{4,0},{8,4},{12,8},{16,12},{20,16},{24,20},{28,24},{1,29},{... | collective-permute-start | bytes 1572872 | tf_op jit(solution)/shard_map/ppermute | solution.py:859
  397.4 10.3 %collective-permute-start.20 = (bf16[32,8,512]{2,1,0:T(8,128)(2,1)}, bf16[32,8,512]{2,1,0:T(8,128)(2,1)S(1)}, u32[]{:S(2)}, u32[]{:S(2)}) collective-permute-start(bf16[32,8,512]{2,1,0:T(8,128)(2,1)} %get-tuple-element.139), channel_id=1, source_target_pairs={{0,3},{1,0},{2,1},{3,2},{4,7},{5,4},{6,5},{7,6},{8,11},{9,8},{10,9... | collective-permute-start | bytes 786440 | tf_op jit(solution)/shard_map/ppermute | solution.py:858
  399.4 8.4 %collective-permute-start.22 = (bf16[8,8,512]{2,1,0:T(8,128)(2,1)}, bf16[8,8,512]{2,1,0:T(8,128)(2,1)S(1)}, u32[]{:S(2)}, u32[]{:S(2)}) collective-permute-start(bf16[8,8,512]{2,1,0:T(8,128)(2,1)} %get-tuple-element.141), channel_id=1, source_target_pairs={{0,31},{1,28},{2,29},{3,30},{4,3},{5,0},{6,1},{7,2},{8,7},{9,4},{1... | collective-permute-start | bytes 196616 | tf_op jit(solution)/shard_map/ppermute | solution.py:860
  434.9 10.4 %collective-permute-start.24 = (bf16[8,64,256]{2,1,0:T(8,128)(2,1)}, bf16[8,64,256]{2,1,0:T(8,128)(2,1)S(1)}, u32[]{:S(2)}, u32[]{:S(2)}) collective-permute-start(bf16[8,64,256]{2,1,0:T(8,128)(2,1)} %get-tuple-element.145), channel_id=1, source_target_pairs={{0,4},{4,8},{8,12},{12,16},{16,20},{20,24},{24,28},{28,0},{1,5},{5... | collective-permute-start | bytes 786440 | tf_op jit(solution)/shard_map/ppermute | solution.py:859
  434.9 10.4 %collective-permute-start.23 = (bf16[32,8,256]{2,1,0:T(8,128)(2,1)}, bf16[32,8,256]{2,1,0:T(8,128)(2,1)S(1)}, u32[]{:S(2)}, u32[]{:S(2)}) collective-permute-start(bf16[32,8,256]{2,1,0:T(8,128)(2,1)} %get-tuple-element.144), channel_id=1, source_target_pairs={{0,1},{1,2},{2,3},{3,0},{4,5},{5,6},{6,7},{7,4},{8,9},{9,10},{10,1... | collective-permute-start | bytes 393224 | tf_op jit(solution)/shard_map/ppermute | solution.py:858
  436.4 8.9 %collective-permute-start.25 = (bf16[8,8,256]{2,1,0:T(8,128)(2,1)}, bf16[8,8,256]{2,1,0:T(8,128)(2,1)S(1)}, u32[]{:S(2)}, u32[]{:S(2)}) collective-permute-start(bf16[8,8,256]{2,1,0:T(8,128)(2,1)} %get-tuple-element.146), channel_id=1, source_target_pairs={{0,5},{1,6},{2,7},{3,4},{4,9},{5,10},{6,11},{7,8},{8,13},{9,14},{1... | collective-permute-start | bytes 98312 | tf_op jit(solution)/shard_map/ppermute | solution.py:860
  (46 other events, 486.3 us)

commit v8 on v7

--- a/solution.py
+++ b/solution.py
@@ -208,10 +208,25 @@
     lax.fori_loop(0, count, step, 0, unroll=8)
 
 
-def row_inverse(v_ref, first_ref, twist_ref, second_ref, *out_refs):
+def load_bands(source, target, sems, count):
+    def copy(i):
+        rows = pl.ds(pl.multiple_of(i * PATCH, PATCH), PATCH)
+        return pltpu.make_async_copy(
+            source.at[..., rows, :], target.at[..., rows, :], sems.at[i]
+        )
+
+    for i in range(count):
+        copy(i).start()
+    return lambda i: copy(i).wait()
+
+
+def row_inverse(v_hbm, first_ref, twist_ref, second_ref, *refs):
+    *out_refs, v_ref, sems = refs
     count, cols, _ = out_refs[0].shape
+    wait = load_bands(v_hbm, v_ref, sems, count)
 
     def step(i, carry):
+        wait(i)
         rows = pl.ds(pl.multiple_of(i * PATCH, PATCH), PATCH)
         wide = jnp.concatenate(
             [
@@ -275,8 +290,10 @@
     lax.fori_loop(0, count, step, 0, unroll=8)
 
 
-def row_inverse_half(v_ref, first_ref, twist_ref, lower_ref, upper_ref, *out_refs):
+def row_inverse_half(v_hbm, first_ref, twist_ref, lower_ref, upper_ref, *refs):
+    *out_refs, v_ref, sems = refs
     count, cols, _ = out_refs[0].shape
+    wait = load_bands(v_hbm, v_ref, sems, count)
     half = TOK // 2
 
     def unpacked(rows, high):
@@ -286,6 +303,7 @@
         return jnp.where(left, even, swap_halves(odd)), jnp.where(left, swap_halves(even), odd)
 
     def step(i, carry):
+        wait(i)
         rows = pl.ds(pl.multiple_of(i * PATCH, PATCH), PATCH)
         real, imag = unpacked(rows, slice(0, PATCH // 2))
         lower = jnp.stack([real, imag], axis=1).reshape(PIXELS, half)
@@ -386,7 +404,7 @@
         mid_ref[q] = mm(inner_t_ref[q], back).astype(BF16).reshape(2, rows, width)
         return carry
 
-    lax.fori_loop(0, devices, step, 0, unroll=16)
+    lax.fori_loop(0, devices, step, 0, unroll=32)
     copies[3].wait()
 
     for top in range(0, rows, PATCH):
@@ -530,7 +548,10 @@
         returned, beside = lax.optimization_barrier((returned, beside))
     slabs = pl.pallas_call(
         backward[0],
+        in_specs=[pl.BlockSpec(memory_space=pltpu.HBM)]
+        + [pl.BlockSpec(memory_space=pltpu.VMEM)] * len(backward[1]),
         out_shape=[jax.ShapeDtypeStruct((own, cols, PIXELS), BF16)] * lanes,
+        scratch_shapes=[pltpu.VMEM(split, BF16), pltpu.SemaphoreType.DMA((own,))],
         compiler_params=PARAMS,
     )(returned.reshape(split), *backward[1])
     return swap_pieces(slabs), beside

time: 463 us -> 462 us (level); the launches traced: 454 us -> 458 us
  no operation moved by 1% of the time
where the time goes in v8:
time: 462 us; the launch traced here: 458 us
  Pallas kernels  197 us (43%)
  waiting for transfers between devices  135 us (29%)
  starting transfers between devices  52.1 us (11%)
  local copies, waits for them, and re-layouts  49 us (11%)
  other arithmetic  18.8 us (4%)
  between operations  6.24 us (1%)
    pallas_call x2, Pallas kernels, second_block(): pl.pallas_call(functools.partial(second_kernel, sigma, rows, parts), grid...  54.6 us
    pallas_call x2, Pallas kernels, first_block(): pl.pallas_call(functools.partial(first_kernel, zeta, sigma, len(grads), p...  53.7 us
    all_to_all x2, waiting for transfers between devices, patch_gradient(): lax.all_to_all(wave, ('ty', 'tx'), split_axis=0, concat_axis=0, tiled=True)  44 us
    ppermute x12, waiting for transfers between devices, swap_pieces(): lax.ppermute(pieces[m], 'tx', [(k, k ^ m) for k in range(lanes)])  40.8 us
    all_to_all x2, waiting for transfers between devices, patch_gradient(): lax.all_to_all(sent.reshape(part), ('ty', 'tx'), split_axis=0, concat_axi...  33.4 us
    unnamed x102, local copies, waits for them, and re-layouts  24 us
    pallas_call x2, Pallas kernels, patch_gradient(): pl.pallas_call(functools.partial(column_kernel, halved), in_specs=[pl.Blo...  21.5 us
    pallas_call x3, Pallas kernels, patches_of(): pl.pallas_call(functools.partial(to_patches_kernel, kind == BF16), grid_s...  18.8 us
  transfers between devices with their start and end apart: 30, of which 17 were waited for; matrix products, arithmetic and copies ran while one was open for 13% of the time, Pallas kernels for 14%

profile of v8, /device:TPU:0, one launch (start us, length us, event | category | flops | bytes accessed | tf_op | source)
XLA Modules:
  0.0 457.7 jit_solution(16117804972705884163)
XLA Ops:
  0.0 5.7 %shard_map.298 = (bf16[8,64,256]{2,1,0:T(8,128)(2,1)}, bf16[8,64,256]{2,1,0:T(8,128)(2,1)}, bf16[8,64,256]{2,1,0:T(8,128)(2,1)}, bf16[8,64,256]{2,1,0:T(8,128)(2,1)}) custom-call(s32[1]{0:T(128)} %bitcast.1.place_ref, f32[1,512,1024]{2,1,0:T(8,128)} %bitcast.67, bf16[1024,1024]{1,0:T(8,128)(2,1)} %constant.98.clone.order_ref), custom_call_target="tpu_custom_call" | custom-call | tf_op jit(solution)/shard_map/pallas_call | solution.py:988
  16.0 6.3 %collective-permute-done.1.refs_2_ = bf16[8,64,256]{2,1,0:T(8,128)(2,1)S(1)} collective-permute-done((bf16[8,64,256]{2,1,0:T(8,128)(2,1)}, bf16[8,64,256]{2,1,0:T(8,128)(2,1)S(1)}, u32[]{:S(2)}, u32[]{:S(2)}) %collective-permute-start.1) | collective-permute-done | bytes 262176 | tf_op jit(solution)/shard_map/ppermute | solution.py:484
  23.0 5.5 %shard_map.299 = bf16[16,2,2,128,128]{4,3,2,1,0:T(8,128)(2,1)} custom-call(bf16[8,64,256]{2,1,0:T(8,128)(2,1)} %get-tuple-element.76.refs_0_, bf16[8,64,256]{2,1,0:T(8,128)(2,1)} %copy-done.13, bf16[8,64,256]{2,1,0:T(8,128)(2,1)} %copy-done.14, bf16[8,64,256]{2,1,0:T(8,128)(2,1)} %copy-done.15, bf16[256,512]{1,0:T(8,128)(2,1)} %pad_maximum_fusion.5.refs_4_.first_ref, ...), custom_call_target="tpu_custom_call" | custom-call | tf_op jit(solution)/shard_map/pallas_call | solution.py:520
  28.5 5.2 %all-to-all-start = ((bf16[32,2,128,128]{3,2,1,0:T(8,128)(2,1)}), bf16[32,2,128,128]{3,2,1,0:T(8,128)(2,1)}, u32[]{:S(2)}, u32[]{:S(2)}) async-start(bf16[32,2,128,128]{3,2,1,0:T(8,128)(2,1)} %bitcast.70), calls=%async_computation | async-start | bytes 4194304 | tf_op jit(solution)/shard_map/all_to_all | solution.py:527
  35.6 4.7 %fusion.18 = (f32[1,128,4096]{2,1,0:T(8,128)}, f32[1,128,4096]{2,1,0:T(8,128)}) fusion(f32[2,128,4096]{2,1,0:T(8,128)} %param.36), kind=kLoop, calls=%fused_computation.77 | loop fusion | bytes 8388608 | tf_op jit(solution)/shard_map/slice | solution.py:421
  43.2 4.7 %fusion.17 = (f32[1,128,4096]{2,1,0:T(8,128)}, f32[1,128,4096]{2,1,0:T(8,128)}) fusion(f32[2,128,4096]{2,1,0:T(8,128)} %param.37), kind=kLoop, calls=%fused_computation.76 | loop fusion | bytes 8388608 | tf_op jit(solution)/shard_map/slice | solution.py:425
  64.9 17.5 %all-to-all-done.refs_0_ = bf16[32,2,128,128]{3,2,1,0:T(8,128)(2,1)} async-done(((bf16[32,2,128,128]{3,2,1,0:T(8,128)(2,1)}), bf16[32,2,128,128]{3,2,1,0:T(8,128)(2,1)}, u32[]{:S(2)}, u32[]{:S(2)}) %all-to-all-start) | async-done | bytes 2097184 | tf_op jit(solution)/shard_map/all_to_all | solution.py:527
  82.4 11.3 %shard_map.300 = bf16[32,2,128,128]{3,2,1,0:T(8,128)(2,1)} custom-call(bf16[32,2,128,128]{3,2,1,0:T(8,128)(2,1)} %all-to-all-done.refs_0_, bf16[512,512]{1,0:T(8,128)(2,1)} %constant.99.clone.refs_1_.refs_3_, bf16[32,256,256]{2,1,0:T(8,128)(2,1)} %constant.101.clone.refs_2_.refs_4_, bf16[32,128,128]{2,1,0:T(8,128)(2,1)} %bitcast.65, ...), custom_call_target="tpu_custom_call" | custom-call | tf_op jit(solution)/shard_map/pallas_call | solution.py:535
  93.8 4.5 all-to-all-start.1
  98.3 6.5 %shard_map.301.refs_1_ = f32[32,64,256]{2,1,0:T(8,128)} custom-call(s32[1]{0:T(128)} %bitcast.1.place_ref, f32[1,512,1024]{2,1,0:T(8,128)} %bitcast.68, bf16[1024,1024]{1,0:T(8,128)(2,1)} %constant.98.clone.order_ref), custom_call_target="tpu_custom_call" | custom-call | tf_op jit(solution)/shard_map/pallas_call | solution.py:988
  106.2 6.6 %shard_map.302.refs_6_ = f32[32,64,256]{2,1,0:T(8,128)} custom-call(s32[1]{0:T(128)} %bitcast.1.place_ref, f32[2,512,1024]{2,1,0:T(8,128)} %noise_ref.1, bf16[1024,1024]{1,0:T(8,128)(2,1)} %constant.98.clone.order_ref), custom_call_target="tpu_custom_call" | custom-call | tf_op jit(solution)/shard_map/pallas_call | solution.py:988
  128.7 18.4 %all-to-all-done.1 = bf16[32,2,128,128]{3,2,1,0:T(8,128)(2,1)S(1)} async-done(((bf16[32,2,128,128]{3,2,1,0:T(8,128)(2,1)}), bf16[32,2,128,128]{3,2,1,0:T(8,128)(2,1)S(1)}, u32[]{:S(2)}, u32[]{:S(2)}) %all-to-all-start.1) | async-done | bytes 2097184 | tf_op jit(solution)/shard_map/all_to_all | solution.py:546
  148.3 8.7 %shard_map.303 = (bf16[8,64,256]{2,1,0:T(8,128)(2,1)}, bf16[8,64,256]{2,1,0:T(8,128)(2,1)}, bf16[8,64,256]{2,1,0:T(8,128)(2,1)}, bf16[8,64,256]{2,1,0:T(8,128)(2,1)}) custom-call(bf16[16,2,2,128,128]{4,3,2,1,0:T(8,128)(2,1)} %bitcast.69, bf16[256,512]{1,0:T(8,128)(2,1)} %pad_maximum_fusion.5.refs_4_.first_ref, ...), custom_call_target="tpu_custom_call" | custom-call | tf_op jit(solution)/shard_map/pallas_call | solution.py:549
  161.2 5.3 %collective-permute-done.3.refs_3_.refs_7_ = bf16[8,64,256]{2,1,0:T(8,128)(2,1)S(1)} collective-permute-done((bf16[8,64,256]{2,1,0:T(8,128)(2,1)}, bf16[8,64,256]{2,1,0:T(8,128)(2,1)S(1)}, u32[]{:S(2)}, u32[]{:S(2)}) %collective-permute-start.3) | collective-permute-done | bytes 262176 | tf_op jit(solution)/shard_map/ppermute | solution.py:484
  166.5 5.5 %collective-permute-done.4.refs_4_.refs_8_ = bf16[8,64,256]{2,1,0:T(8,128)(2,1)S(1)} collective-permute-done((bf16[8,64,256]{2,1,0:T(8,128)(2,1)}, bf16[8,64,256]{2,1,0:T(8,128)(2,1)S(1)}, u32[]{:S(2)}, u32[]{:S(2)}) %collective-permute-start.4) | collective-permute-done | bytes 262176 | tf_op jit(solution)/shard_map/ppermute | solution.py:484
  172.8 27.1 %shard_map.304 = (f32[32,64,256]{2,1,0:T(8,128)}, bf16[32,64,768]{2,1,0:T(8,128)(2,1)}, bf16[32,8,768]{2,1,0:T(8,128)(2,1)}, bf16[8,64,768]{2,1,0:T(8,128)(2,1)}, bf16[8,8,768]{2,1,0:T(8,128)(2,1)}) custom-call(s32[3]{0:T(128)} %pad_add_fusion.1.refs_0_, f32[32,64,256]{2,1,0:T(8,128)} %shard_map.301.refs_1_, ...), custom_call_target="tpu_custom_call" | custom-call | tf_op jit(solution)/shard_map/pallas_call | solution.py:827
  204.6 8.6 %collective-permute-done.8.refs_4_ = bf16[8,8,768]{2,1,0:T(8,128)(2,1)S(1)} collective-permute-done((bf16[8,8,768]{2,1,0:T(8,128)(2,1)}, bf16[8,8,768]{2,1,0:T(8,128)(2,1)S(1)}, u32[]{:S(2)}, u32[]{:S(2)}) %collective-permute-start.8) | collective-permute-done | bytes 98336 | tf_op jit(solution)/shard_map/ppermute | solution.py:881
  220.6 28.4 %shard_map.305 = (bf16[32,64,256]{2,1,0:T(8,128)(2,1)}, bf16[32,8,256]{2,1,0:T(8,128)(2,1)}, bf16[8,64,256]{2,1,0:T(8,128)(2,1)}, bf16[8,8,256]{2,1,0:T(8,128)(2...) custom-call(s32[3]{0:T(128)} %pad_add_fusion.1.refs_0_, ...), custom_call_target="tpu_custom_call" | custom-call | tf_op jit(solution)/shard_map/pallas_call | solution.py:854
  258.4 6.9 %collective-permute-done.12.refs_2_ = bf16[8,64,256]{2,1,0:T(8,128)(2,1)S(1)} collective-permute-done((bf16[8,64,256]{2,1,0:T(8,128)(2,1)}, bf16[8,64,256]{2,1,0:T(8,128)(2,1)S(1)}, u32[]{:S(2)}, u32[]{:S(2)}) %collective-permute-start.12) | collective-permute-done | bytes 262176 | tf_op jit(solution)/shard_map/ppermute | solution.py:484
  266.7 5.7 %shard_map.306 = bf16[16,2,128,128]{3,2,1,0:T(8,128)(2,1)} custom-call(bf16[8,64,256]{2,1,0:T(8,128)(2,1)} %get-tuple-element.108.refs_0_, bf16[8,64,256]{2,1,0:T(8,128)(2,1)} %copy-done.26, bf16[8,64,256]{2,1,0:T(8,128)(2,1)} %copy-done.27, bf16[8,64,256]{2,1,0:T(8,128)(2,1)} %copy-done.28, bf16[256,512]{1,0:T(8,128)(2,1)} %pad_maximum_fusion.6.refs_4_, ...), custom_call_target="tpu_custom_call" | custom-call | tf_op jit(solution)/shard_map/pallas_call | solution.py:520
  281.8 5.4 %shard_map.307.refs_5_ = bf16[32,128,128]{2,1,0:T(8,128)(2,1)} custom-call(bf16[32,128,128]{2,1,0:T(8,128)(2,1)} %bitcast.66, bf16[32,128,128]{2,1,0:T(8,128)(2,1)} %bitcast.71, bf16[2,128,128]{2,1,0:T(8,128)(2,1)} %add_convert_fusion.pick_ref, bf16[2,128,128]{2,1,0:T(8,128)(2,1)} %constant.113.clone.flip_ref), custom_call_target="tpu_custom_call" | custom-call | tf_op jit(solution)/shard_map/pallas_call | solution.py:465
  287.2 15.9 %all-to-all-done.2.refs_2_ = bf16[32,128,128]{2,1,0:T(8,128)(2,1)S(1)} async-done(((bf16[32,128,128]{2,1,0:T(8,128)(2,1)}), bf16[32,128,128]{2,1,0:T(8,128)(2,1)S(1)}, u32[]{:S(2)}, u32[]{:S(2)}) %all-to-all-start.2) | async-done | bytes 1048608 | tf_op jit(solution)/shard_map/all_to_all | solution.py:527
  307.1 10.2 %shard_map.308 = bf16[32,128,128]{2,1,0:T(8,128)(2,1)} custom-call(s32[1]{0:T(128)} %bitcast.28.refs_0_, f32[32,2,8,128]{3,2,1,0:T(8,128)} %broadcast_in_dim.79.refs_1_, bf16[32,128,128]{2,1,0:T(8,128)(2,1)} %copy-done.1, bf16[512,512]{1,0:T(8,128)(2,1)} %constant.99.clone.refs_1_.refs_3_, bf16[32,256,256]{2,1,0:T(8,128)(2,1)} %constant.101.clone.refs_2_.refs_4_, ...), custom_call_target="tpu_custom_call" | custom-call | tf_op jit(solution)/shard_map/pallas_call | solution.py:535
  317.3 5.0 %all-to-all-start.3 = ((bf16[32,128,128]{2,1,0:T(8,128)(2,1)}), bf16[32,128,128]{2,1,0:T(8,128)(2,1)S(1)}, u32[]{:S(2)}, u32[]{:S(2)}) async-start(bf16[32,128,128]{2,1,0:T(8,128)(2,1)} %shard_map.308), calls=%async_computation.3 | async-start | bytes 2097152 | tf_op jit(solution)/shard_map/all_to_all | solution.py:546
  323.2 25.7 %all-to-all-done.3 = bf16[32,128,128]{2,1,0:T(8,128)(2,1)S(1)} async-done(((bf16[32,128,128]{2,1,0:T(8,128)(2,1)}), bf16[32,128,128]{2,1,0:T(8,128)(2,1)S(1)}, u32[]{:S(2)}, u32[]{:S(2)}) %all-to-all-start.3) | async-done | bytes 1048608 | tf_op jit(solution)/shard_map/all_to_all | solution.py:546
  349.8 9.0 %shard_map.309 = (bf16[8,64,256]{2,1,0:T(8,128)(2,1)}, bf16[8,64,256]{2,1,0:T(8,128)(2,1)}, bf16[8,64,256]{2,1,0:T(8,128)(2,1)}, bf16[8,64,256]{2,1,0:T(8,128)(2,1)}) custom-call(bf16[16,2,128,128]{3,2,1,0:T(8,128)(2,1)} %bitcast.74, bf16[256,512]{1,0:T(8,128)(2,1)} %pad_maximum_fusion.7.first_ref, f32[2,256,256]{2,1,0:T(8,128)} %constant.107.clone.refs_5_.twist_ref, ...), custom_call_target="tpu_custom_call" | custom-call | tf_op jit(solution)/shard_map/pallas_call | solution.py:549
  362.4 5.9 %collective-permute-done.17.refs_11_ = bf16[8,64,256]{2,1,0:T(8,128)(2,1)S(1)} collective-permute-done((bf16[8,64,256]{2,1,0:T(8,128)(2,1)}, bf16[8,64,256]{2,1,0:T(8,128)(2,1)S(1)}, u32[]{:S(2)}, u32[]{:S(2)}) %collective-permute-start.17) | collective-permute-done | bytes 262176 | tf_op jit(solution)/shard_map/ppermute | solution.py:484
  374.8 26.6 %shard_map.310 = (f32[32,64,256]{2,1,0:T(8,128)}, bf16[32,64,512]{2,1,0:T(8,128)(2,1)}, bf16[32,8,512]{2,1,0:T(8,128)(2,1)}, bf16[8,64,512]{2,1,0:T(8,128)(2,1)}, bf16[8,8,512]{2,1,0:T(8,128)(2,1)}) custom-call(s32[3]{0:T(128)} %pad_add_fusion.1.refs_0_, f32[32,64,256]{2,1,0:T(8,128)} %get-tuple-element.89.refs_1_, ...), custom_call_target="tpu_custom_call" | custom-call | tf_op jit(solution)/shard_map/pallas_call | solution.py:827
  405.8 6.0 %collective-permute-done.22.refs_4_ = bf16[8,8,512]{2,1,0:T(8,128)(2,1)S(1)} collective-permute-done((bf16[8,8,512]{2,1,0:T(8,128)(2,1)}, bf16[8,8,512]{2,1,0:T(8,128)(2,1)S(1)}, u32[]{:S(2)}, u32[]{:S(2)}) %collective-permute-start.22) | collective-permute-done | bytes 65568 | tf_op jit(solution)/shard_map/ppermute | solution.py:881
  412.7 26.2 %shard_map.312 = (bf16[32,64,256]{2,1,0:T(8,128)(2,1)}, bf16[32,8,256]{2,1,0:T(8,128)(2,1)}, bf16[8,64,256]{2,1,0:T(8,128)(2,1)}, bf16[8,8,256]{2,1,0:T(8,128)(2,1)}) custom-call(s32[3]{0:T(128)} %pad_add_fusion.refs_0_.shift_ref, bf16[32,64,512]{2,1,0:T(8,128)(2,1)} %get-tuple-element.138.refs_1_, bf16[32,8,512]{2,1,0:T(8,128)(2,1)} %copy-done.12, ...), custom_call_target="tpu_custom_call" | custom-call | tf_op jit(solution)/shard_map/pallas_call | solution.py:854
  441.2 6.9 %shard_map.311.tile_ref = f32[512,1024]{1,0:T(8,128)} custom-call(f32[32,64,256]{2,1,0:T(8,128)} %get-tuple-element.137.base_ref, f32[2,512,1024]{2,1,0:T(8,128)} %noise_ref.1, bf16[1024,1024]{1,0:T(8,128)(2,1)} %constant.114.clone.order_ref.refs_4_), custom_call_target="tpu_custom_call" | custom-call | tf_op jit(solution)/shard_map/pallas_call | solution.py:1009
  450.1 7.1 %shard_map.313 = f32[512,1024]{1,0:T(8,128)} custom-call(s32[3]{0:T(128)} %pad_add_fusion.refs_0_.shift_ref, f32[512,1024]{1,0:T(8,128)} %shard_map.311.tile_ref, bf16[32,64,256]{2,1,0:T(8,128)(2,1)} %get-tuple-element.143.refs_0_, bf16[32,8,256]{2,1,0:T(8,128)(2,1)} %copy-done.36, bf16[8,64,256]{2,1,0:T(8,128)(2,1)} %copy-done.16, ...), custom_call_target="tpu_custom_call" | custom-call | tf_op jit(solution)/shard_map/pallas_call | solution.py:1021
  (198 shorter events, 108.6 us)
Async XLA Ops:
  5.7 10.3 %collective-permute-start = (bf16[8,64,256]{2,1,0:T(8,128)(2,1)}, bf16[8,64,256]{2,1,0:T(8,128)(2,1)S(1)}, u32[]{:S(2)}, u32[]{:S(2)}) collective-permute-start(bf16[8,64,256]{2,1,0:T(8,128)(2,1)} %get-tuple-element.77), channel_id=1, source_target_pairs={{0,1},{1,0},{2,3},{3,2},{4,5},{5,4},{6,7},{7,6},{8,9},{9,8},{10,11... | collective-permute-start | bytes 786440 | tf_op jit(solution)/shard_map/ppermute | solution.py:484
  8.6 13.6 %collective-permute-start.1 = (bf16[8,64,256]{2,1,0:T(8,128)(2,1)}, bf16[8,64,256]{2,1,0:T(8,128)(2,1)S(1)}, u32[]{:S(2)}, u32[]{:S(2)}) collective-permute-start(bf16[8,64,256]{2,1,0:T(8,128)(2,1)} %get-tuple-element.78), channel_id=1, source_target_pairs={{0,2},{1,3},{2,0},{3,1},{4,6},{5,7},{6,4},{7,5},{8,10},{9,11},{10,... | collective-permute-start | bytes 786440 | tf_op jit(solution)/shard_map/ppermute | solution.py:484
  10.1 12.1 %collective-permute-start.2 = (bf16[8,64,256]{2,1,0:T(8,128)(2,1)}, bf16[8,64,256]{2,1,0:T(8,128)(2,1)S(1)}, u32[]{:S(2)}, u32[]{:S(2)}) collective-permute-start(bf16[8,64,256]{2,1,0:T(8,128)(2,1)} %get-tuple-element.79), channel_id=1, source_target_pairs={{0,3},{1,2},{2,1},{3,0},{4,7},{5,6},{6,5},{7,4},{8,11},{9,10},{10,... | collective-permute-start | bytes 786440 | tf_op jit(solution)/shard_map/ppermute | solution.py:484
  28.5 53.9 %all-to-all-start = ((bf16[32,2,128,128]{3,2,1,0:T(8,128)(2,1)}), bf16[32,2,128,128]{3,2,1,0:T(8,128)(2,1)}, u32[]{:S(2)}, u32[]{:S(2)}) async-start(bf16[32,2,128,128]{3,2,1,0:T(8,128)(2,1)} %bitcast.70), calls=%async_computation | async-start | bytes 4194304 | tf_op jit(solution)/shard_map/all_to_all | solution.py:527
  93.8 53.2 %all-to-all-start.1 = ((bf16[32,2,128,128]{3,2,1,0:T(8,128)(2,1)}), bf16[32,2,128,128]{3,2,1,0:T(8,128)(2,1)S(1)}, u32[]{:S(2)}, u32[]{:S(2)}) async-start(bf16[32,2,128,128]{3,2,1,0:T(8,128)(2,1)} %shard_map.300), calls=%async_computation.1 | async-start | bytes 4194304 | tf_op jit(solution)/shard_map/all_to_all | solution.py:546
  157.0 9.5 %collective-permute-start.3 = (bf16[8,64,256]{2,1,0:T(8,128)(2,1)}, bf16[8,64,256]{2,1,0:T(8,128)(2,1)S(1)}, u32[]{:S(2)}, u32[]{:S(2)}) collective-permute-start(bf16[8,64,256]{2,1,0:T(8,128)(2,1)} %get-tuple-element.83), channel_id=1, source_target_pairs={{0,1},{1,0},{2,3},{3,2},{4,5},{5,4},{6,7},{7,6},{8,9},{9,8},{10,11... | collective-permute-start | bytes 786440 | tf_op jit(solution)/shard_map/ppermute | solution.py:484
  158.6 13.4 %collective-permute-start.4 = (bf16[8,64,256]{2,1,0:T(8,128)(2,1)}, bf16[8,64,256]{2,1,0:T(8,128)(2,1)S(1)}, u32[]{:S(2)}, u32[]{:S(2)}) collective-permute-start(bf16[8,64,256]{2,1,0:T(8,128)(2,1)} %get-tuple-element.84), channel_id=1, source_target_pairs={{0,2},{1,3},{2,0},{3,1},{4,6},{5,7},{6,4},{7,5},{8,10},{9,11},{10,... | collective-permute-start | bytes 786440 | tf_op jit(solution)/shard_map/ppermute | solution.py:484
  160.0 11.9 %collective-permute-start.5 = (bf16[8,64,256]{2,1,0:T(8,128)(2,1)}, bf16[8,64,256]{2,1,0:T(8,128)(2,1)S(1)}, u32[]{:S(2)}, u32[]{:S(2)}) collective-permute-start(bf16[8,64,256]{2,1,0:T(8,128)(2,1)} %get-tuple-element.85), channel_id=1, source_target_pairs={{0,3},{1,2},{2,1},{3,0},{4,7},{5,6},{6,5},{7,4},{8,11},{9,10},{10,... | collective-permute-start | bytes 786440 | tf_op jit(solution)/shard_map/ppermute | solution.py:484
  172.8 41.8 %copy-start.2 = (bf16[64,4096]{0,1:T(8,128)(2,1)S(1)}, bf16[64,4096]{0,1:T(8,128)(2,1)}, u32[]{:S(2)}) copy-start(bf16[64,4096]{0,1:T(8,128)(2,1)} %slice.57) | copy-start | bytes 1572868
  199.9 13.9 %collective-permute-start.7 = (bf16[8,64,768]{2,1,0:T(8,128)(2,1)}, bf16[8,64,768]{2,1,0:T(8,128)(2,1)S(1)}, u32[]{:S(2)}, u32[]{:S(2)}) collective-permute-start(bf16[8,64,768]{2,1,0:T(8,128)(2,1)} %get-tuple-element.92), channel_id=1, source_target_pairs={{0,28},{4,0},{8,4},{12,8},{16,12},{20,16},{24,20},{28,24},{1,29},{... | collective-permute-start | bytes 2359304 | tf_op jit(solution)/shard_map/ppermute | solution.py:880
  200.9 12.8 %collective-permute-start.6 = (bf16[32,8,768]{2,1,0:T(8,128)(2,1)}, bf16[32,8,768]{2,1,0:T(8,128)(2,1)S(1)}, u32[]{:S(2)}, u32[]{:S(2)}) collective-permute-start(bf16[32,8,768]{2,1,0:T(8,128)(2,1)} %get-tuple-element.91), channel_id=1, source_target_pairs={{0,3},{1,0},{2,1},{3,2},{4,7},{5,4},{6,5},{7,6},{8,11},{9,8},{10,9... | collective-permute-start | bytes 1179656 | tf_op jit(solution)/shard_map/ppermute | solution.py:879
  201.7 11.6 %collective-permute-start.8 = (bf16[8,8,768]{2,1,0:T(8,128)(2,1)}, bf16[8,8,768]{2,1,0:T(8,128)(2,1)S(1)}, u32[]{:S(2)}, u32[]{:S(2)}) collective-permute-start(bf16[8,8,768]{2,1,0:T(8,128)(2,1)} %get-tuple-element.93), channel_id=1, source_target_pairs={{0,31},{1,28},{2,29},{3,30},{4,3},{5,0},{6,1},{7,2},{8,7},{9,4},{1... | collective-permute-start | bytes 294920 | tf_op jit(solution)/shard_map/ppermute | solution.py:881
  215.7 33.3 %collective-permute-start.9 = (bf16[64,4096]{1,0:T(8,128)(2,1)}, bf16[64,4096]{1,0:T(8,128)(2,1)S(1)}, u32[]{:S(2)}, u32[]{:S(2)}) collective-permute-start(bf16[64,4096]{1,0:T(8,128)(2,1)} %copy.85), channel_id=1, source_target_pairs={{0,31},{1,30},{2,29},{3,28},{4,27},{5,26},{6,25},{7,24},{8,23},{9,... | collective-permute-start | bytes 1572872 | tf_op jit(solution)/shard_map/ppermute | solution.py:445
  219.7 29.3 %collective-permute-start.10 = (bf16[1,4096]{1,0:T(2,128)(2,1)S(1)}, bf16[1,4096]{1,0:T(2,128)(2,1)S(1)}, u32[]{:S(2)}, u32[]{:S(2)}) collective-permute-start(bf16[1,4096]{1,0:T(2,128)(2,1)S(1)} %copy.86), channel_id=1, source_target_pairs={{1,31},{2,30},{3,29},{4,28},{5,27},{6,26},{7,25},{8,24},{9,23},{10... | collective-permute-start | bytes 24584 | tf_op jit(solution)/shard_map/ppermute | solution.py:446
  249.1 9.3 %collective-permute-start.11 = (bf16[8,64,256]{2,1,0:T(8,128)(2,1)}, bf16[8,64,256]{2,1,0:T(8,128)(2,1)S(1)}, u32[]{:S(2)}, u32[]{:S(2)}) collective-permute-start(bf16[8,64,256]{2,1,0:T(8,128)(2,1)} %get-tuple-element.109), channel_id=1, source_target_pairs={{0,1},{1,0},{2,3},{3,2},{4,5},{5,4},{6,7},{7,6},{8,9},{9,8},{10,11... | collective-permute-start | bytes 786440 | tf_op jit(solution)/shard_map/ppermute | solution.py:484
  251.4 13.9 %collective-permute-start.12 = (bf16[8,64,256]{2,1,0:T(8,128)(2,1)}, bf16[8,64,256]{2,1,0:T(8,128)(2,1)S(1)}, u32[]{:S(2)}, u32[]{:S(2)}) collective-permute-start(bf16[8,64,256]{2,1,0:T(8,128)(2,1)} %get-tuple-element.110), channel_id=1, source_target_pairs={{0,2},{1,3},{2,0},{3,1},{4,6},{5,7},{6,4},{7,5},{8,10},{9,11},{10,... | collective-permute-start | bytes 786440 | tf_op jit(solution)/shard_map/ppermute | solution.py:484
  252.9 12.4 %collective-permute-start.13 = (bf16[8,64,256]{2,1,0:T(8,128)(2,1)}, bf16[8,64,256]{2,1,0:T(8,128)(2,1)S(1)}, u32[]{:S(2)}, u32[]{:S(2)}) collective-permute-start(bf16[8,64,256]{2,1,0:T(8,128)(2,1)} %get-tuple-element.111), channel_id=1, source_target_pairs={{0,3},{1,2},{2,1},{3,0},{4,7},{5,6},{6,5},{7,4},{8,11},{9,10},{10,... | collective-permute-start | bytes 786440 | tf_op jit(solution)/shard_map/ppermute | solution.py:484
  272.5 30.6 %all-to-all-start.2 = ((bf16[32,128,128]{2,1,0:T(8,128)(2,1)}), bf16[32,128,128]{2,1,0:T(8,128)(2,1)S(1)}, u32[]{:S(2)}, u32[]{:S(2)}) async-start(bf16[32,128,128]{2,1,0:T(8,128)(2,1)} %bitcast.73), calls=%async_computation.2 | async-start | bytes 2097152 | tf_op jit(solution)/shard_map/all_to_all | solution.py:527
  303.1 14.2 %collective-permute-start.14 = (bf16[32,8,256]{2,1,0:T(8,128)(2,1)S(1)}, bf16[32,8,256]{2,1,0:T(8,128)(2,1)S(1)}, u32[]{:S(2)}, u32[]{:S(2)}) collective-permute-start(bf16[32,8,256]{2,1,0:T(8,128)(2,1)S(1)} %copy-done.46), channel_id=1, source_target_pairs={{0,1},{1,2},{2,3},{3,0},{4,5},{5,6},{6,7},{7,4},{8,9},{9,10},{10,1... | collective-permute-start | bytes 393224 | tf_op jit(solution)/shard_map/ppermute | solution.py:879
  304.4 12.9 %collective-permute-start.15 = (bf16[8,64,256]{2,1,0:T(8,128)(2,1)S(1)}, bf16[8,64,256]{2,1,0:T(8,128)(2,1)S(1)}, u32[]{:S(2)}, u32[]{:S(2)}) collective-permute-start(bf16[8,64,256]{2,1,0:T(8,128)(2,1)S(1)} %copy-done.45), channel_id=1, source_target_pairs={{0,4},{4,8},{8,12},{12,16},{16,20},{20,24},{24,28},{28,0},{1,5},{5... | collective-permute-start | bytes 786440 | tf_op jit(solution)/shard_map/ppermute | solution.py:880
  304.6 12.7 %collective-permute-start.16 = (bf16[8,8,256]{2,1,0:T(8,128)(2,1)S(1)}, bf16[8,8,256]{2,1,0:T(8,128)(2,1)S(1)}, u32[]{:S(2)}, u32[]{:S(2)}) collective-permute-start(bf16[8,8,256]{2,1,0:T(8,128)(2,1)S(1)} %copy-done.47), channel_id=1, source_target_pairs={{0,5},{1,6},{2,7},{3,4},{4,9},{5,10},{6,11},{7,8},{8,13},{9,14},{1... | collective-permute-start | bytes 98312 | tf_op jit(solution)/shard_map/ppermute | solution.py:881
  317.3 41.5 %copy-start.39 = (bf16[8,8,256]{2,1,0:T(8,128)(2,1)}, bf16[8,8,256]{2,1,0:T(8,128)(2,1)S(1)}, u32[]{:S(2)}) copy-start(bf16[8,8,256]{2,1,0:T(8,128)(2,1)S(1)} %collective-permute-done.16.refs_5_) | copy-start | bytes 98308
  317.3 31.5 %all-to-all-start.3 = ((bf16[32,128,128]{2,1,0:T(8,128)(2,1)}), bf16[32,128,128]{2,1,0:T(8,128)(2,1)S(1)}, u32[]{:S(2)}, u32[]{:S(2)}) async-start(bf16[32,128,128]{2,1,0:T(8,128)(2,1)} %shard_map.308), calls=%async_computation.3 | async-start | bytes 2097152 | tf_op jit(solution)/shard_map/all_to_all | solution.py:546
  358.8 9.5 %collective-permute-start.17 = (bf16[8,64,256]{2,1,0:T(8,128)(2,1)}, bf16[8,64,256]{2,1,0:T(8,128)(2,1)S(1)}, u32[]{:S(2)}, u32[]{:S(2)}) collective-permute-start(bf16[8,64,256]{2,1,0:T(8,128)(2,1)} %get-tuple-element.134), channel_id=1, source_target_pairs={{0,1},{1,0},{2,3},{3,2},{4,5},{5,4},{6,7},{7,6},{8,9},{9,8},{10,11... | collective-permute-start | bytes 786440 | tf_op jit(solution)/shard_map/ppermute | solution.py:484
  360.2 12.3 %collective-permute-start.18 = (bf16[8,64,256]{2,1,0:T(8,128)(2,1)}, bf16[8,64,256]{2,1,0:T(8,128)(2,1)S(1)}, u32[]{:S(2)}, u32[]{:S(2)}) collective-permute-start(bf16[8,64,256]{2,1,0:T(8,128)(2,1)} %get-tuple-element.135), channel_id=1, source_target_pairs={{0,2},{1,3},{2,0},{3,1},{4,6},{5,7},{6,4},{7,5},{8,10},{9,11},{10,... | collective-permute-start | bytes 786440 | tf_op jit(solution)/shard_map/ppermute | solution.py:484
  361.6 12.4 %collective-permute-start.19 = (bf16[8,64,256]{2,1,0:T(8,128)(2,1)}, bf16[8,64,256]{2,1,0:T(8,128)(2,1)S(1)}, u32[]{:S(2)}, u32[]{:S(2)}) collective-permute-start(bf16[8,64,256]{2,1,0:T(8,128)(2,1)} %get-tuple-element.136), channel_id=1, source_target_pairs={{0,3},{1,2},{2,1},{3,0},{4,7},{5,6},{6,5},{7,4},{8,11},{9,10},{10,... | collective-permute-start | bytes 786440 | tf_op jit(solution)/shard_map/ppermute | solution.py:484
  401.4 10.4 %collective-permute-start.21 = (bf16[8,64,512]{2,1,0:T(8,128)(2,1)}, bf16[8,64,512]{2,1,0:T(8,128)(2,1)S(1)}, u32[]{:S(2)}, u32[]{:S(2)}) collective-permute-start(bf16[8,64,512]{2,1,0:T(8,128)(2,1)} %get-tuple-element.140), channel_id=1, source_target_pairs={{0,28},{4,0},{8,4},{12,8},{16,12},{20,16},{24,20},{28,24},{1,29},{... | collective-permute-start | bytes 1572872 | tf_op jit(solution)/shard_map/ppermute | solution.py:880
  401.5 10.3 %collective-permute-start.20 = (bf16[32,8,512]{2,1,0:T(8,128)(2,1)}, bf16[32,8,512]{2,1,0:T(8,128)(2,1)S(1)}, u32[]{:S(2)}, u32[]{:S(2)}) collective-permute-start(bf16[32,8,512]{2,1,0:T(8,128)(2,1)} %get-tuple-element.139), channel_id=1, source_target_pairs={{0,3},{1,0},{2,1},{3,2},{4,7},{5,4},{6,5},{7,6},{8,11},{9,8},{10,9... | collective-permute-start | bytes 786440 | tf_op jit(solution)/shard_map/ppermute | solution.py:879
  403.4 8.4 %collective-permute-start.22 = (bf16[8,8,512]{2,1,0:T(8,128)(2,1)}, bf16[8,8,512]{2,1,0:T(8,128)(2,1)S(1)}, u32[]{:S(2)}, u32[]{:S(2)}) collective-permute-start(bf16[8,8,512]{2,1,0:T(8,128)(2,1)} %get-tuple-element.141), channel_id=1, source_target_pairs={{0,31},{1,28},{2,29},{3,30},{4,3},{5,0},{6,1},{7,2},{8,7},{9,4},{1... | collective-permute-start | bytes 196616 | tf_op jit(solution)/shard_map/ppermute | solution.py:881
  438.9 10.4 %collective-permute-start.24 = (bf16[8,64,256]{2,1,0:T(8,128)(2,1)}, bf16[8,64,256]{2,1,0:T(8,128)(2,1)S(1)}, u32[]{:S(2)}, u32[]{:S(2)}) collective-permute-start(bf16[8,64,256]{2,1,0:T(8,128)(2,1)} %get-tuple-element.145), channel_id=1, source_target_pairs={{0,4},{4,8},{8,12},{12,16},{16,20},{20,24},{24,28},{28,0},{1,5},{5... | collective-permute-start | bytes 786440 | tf_op jit(solution)/shard_map/ppermute | solution.py:880
  439.0 10.4 %collective-permute-start.23 = (bf16[32,8,256]{2,1,0:T(8,128)(2,1)}, bf16[32,8,256]{2,1,0:T(8,128)(2,1)S(1)}, u32[]{:S(2)}, u32[]{:S(2)}) collective-permute-start(bf16[32,8,256]{2,1,0:T(8,128)(2,1)} %get-tuple-element.144), channel_id=1, source_target_pairs={{0,1},{1,2},{2,3},{3,0},{4,5},{5,6},{6,7},{7,4},{8,9},{9,10},{10,1... | collective-permute-start | bytes 393224 | tf_op jit(solution)/shard_map/ppermute | solution.py:879
  440.4 8.9 %collective-permute-start.25 = (bf16[8,8,256]{2,1,0:T(8,128)(2,1)}, bf16[8,8,256]{2,1,0:T(8,128)(2,1)S(1)}, u32[]{:S(2)}, u32[]{:S(2)}) collective-permute-start(bf16[8,8,256]{2,1,0:T(8,128)(2,1)} %get-tuple-element.146), channel_id=1, source_target_pairs={{0,5},{1,6},{2,7},{3,4},{4,9},{5,10},{6,11},{7,8},{8,13},{9,14},{1... | collective-permute-start | bytes 98312 | tf_op jit(solution)/shard_map/ppermute | solution.py:881
  (46 other events, 493.6 us)

commit v9 on v7

--- a/solution.py
+++ b/solution.py
@@ -386,7 +386,7 @@
         mid_ref[q] = mm(inner_t_ref[q], back).astype(BF16).reshape(2, rows, width)
         return carry
 
-    lax.fori_loop(0, devices, step, 0, unroll=16)
+    lax.fori_loop(0, devices, step, 0, unroll=32)
     copies[3].wait()
 
     for top in range(0, rows, PATCH):

time: 463 us -> 458 us (0.989); the launches traced: 454 us -> 453 us
  no operation moved by 1% of the time
where the time goes in v9:
time: 458 us; the launch traced here: 453 us
  Pallas kernels  192 us (42%)
  waiting for transfers between devices  135 us (29%)
  starting transfers between devices  52.4 us (11%)
  local copies, waits for them, and re-layouts  49 us (11%)
  other arithmetic  18.8 us (4%)
  between operations  6.21 us (1%)
    pallas_call x2, Pallas kernels, second_block(): pl.pallas_call(functools.partial(second_kernel, sigma, rows, parts), grid...  54.5 us
    pallas_call x2, Pallas kernels, first_block(): pl.pallas_call(functools.partial(first_kernel, zeta, sigma, len(grads), p...  53.6 us
    all_to_all x2, waiting for transfers between devices, patch_gradient(): lax.all_to_all(wave, ('ty', 'tx'), split_axis=0, concat_axis=0, tiled=True)  44 us
    ppermute x12, waiting for transfers between devices, swap_pieces(): lax.ppermute(pieces[m], 'tx', [(k, k ^ m) for k in range(lanes)])  40.8 us
    all_to_all x2, waiting for transfers between devices, patch_gradient(): lax.all_to_all(sent.reshape(part), ('ty', 'tx'), split_axis=0, concat_axi...  33.4 us
    unnamed x102, local copies, waits for them, and re-layouts  24 us
    pallas_call x2, Pallas kernels, patch_gradient(): pl.pallas_call(functools.partial(column_kernel, halved), in_specs=[pl.Blo...  21.5 us
    pallas_call x3, Pallas kernels, patches_of(): pl.pallas_call(functools.partial(to_patches_kernel, kind == BF16), grid_s...  18.8 us
  transfers between devices with their start and end apart: 30, of which 17 were waited for; matrix products, arithmetic and copies ran while one was open for 13% of the time, Pallas kernels for 14%

profile of v9, /device:TPU:0, one launch (start us, length us, event | category | flops | bytes accessed | tf_op | source)
XLA Modules:
  0.0 453.4 jit_solution(2628124058164341385)
XLA Ops:
  0.0 5.7 %shard_map.298 = (bf16[8,64,256]{2,1,0:T(8,128)(2,1)}, bf16[8,64,256]{2,1,0:T(8,128)(2,1)}, bf16[8,64,256]{2,1,0:T(8,128)(2,1)}, bf16[8,64,256]{2,1,0:T(8,128)(2,1)}) custom-call(s32[1]{0:T(128)} %bitcast.1.place_ref, f32[1,512,1024]{2,1,0:T(8,128)} %bitcast.67, bf16[1024,1024]{1,0:T(8,128)(2,1)} %constant.98.clone.order_ref), custom_call_target="tpu_custom_call" | custom-call | tf_op jit(solution)/shard_map/pallas_call | solution.py:967
  16.0 6.2 %collective-permute-done.1.refs_2_ = bf16[8,64,256]{2,1,0:T(8,128)(2,1)S(1)} collective-permute-done((bf16[8,64,256]{2,1,0:T(8,128)(2,1)}, bf16[8,64,256]{2,1,0:T(8,128)(2,1)S(1)}, u32[]{:S(2)}, u32[]{:S(2)}) %collective-permute-start.1) | collective-permute-done | bytes 262176 | tf_op jit(solution)/shard_map/ppermute | solution.py:466
  23.0 5.5 %shard_map.299 = bf16[16,2,2,128,128]{4,3,2,1,0:T(8,128)(2,1)} custom-call(bf16[8,64,256]{2,1,0:T(8,128)(2,1)} %get-tuple-element.76.refs_0_, bf16[8,64,256]{2,1,0:T(8,128)(2,1)} %copy-done.13, bf16[8,64,256]{2,1,0:T(8,128)(2,1)} %copy-done.14, bf16[8,64,256]{2,1,0:T(8,128)(2,1)} %copy-done.15, bf16[256,512]{1,0:T(8,128)(2,1)} %pad_maximum_fusion.5.refs_4_.first_ref, ...), custom_call_target="tpu_custom_call" | custom-call | tf_op jit(solution)/shard_map/pallas_call | solution.py:502
  28.5 5.6 %all-to-all-start = ((bf16[32,2,128,128]{3,2,1,0:T(8,128)(2,1)}), bf16[32,2,128,128]{3,2,1,0:T(8,128)(2,1)}, u32[]{:S(2)}, u32[]{:S(2)}) async-start(bf16[32,2,128,128]{3,2,1,0:T(8,128)(2,1)} %bitcast.70), calls=%async_computation | async-start | bytes 4194304 | tf_op jit(solution)/shard_map/all_to_all | solution.py:509
  36.0 4.7 %fusion.18 = (f32[1,128,4096]{2,1,0:T(8,128)}, f32[1,128,4096]{2,1,0:T(8,128)}) fusion(f32[2,128,4096]{2,1,0:T(8,128)} %param.36), kind=kLoop, calls=%fused_computation.77 | loop fusion | bytes 8388608 | tf_op jit(solution)/shard_map/slice | solution.py:403
  43.6 4.7 %fusion.17 = (f32[1,128,4096]{2,1,0:T(8,128)}, f32[1,128,4096]{2,1,0:T(8,128)}) fusion(f32[2,128,4096]{2,1,0:T(8,128)} %param.37), kind=kLoop, calls=%fused_computation.76 | loop fusion | bytes 8388608 | tf_op jit(solution)/shard_map/slice | solution.py:407
  65.3 17.5 %all-to-all-done.refs_0_ = bf16[32,2,128,128]{3,2,1,0:T(8,128)(2,1)} async-done(((bf16[32,2,128,128]{3,2,1,0:T(8,128)(2,1)}), bf16[32,2,128,128]{3,2,1,0:T(8,128)(2,1)}, u32[]{:S(2)}, u32[]{:S(2)}) %all-to-all-start) | async-done | bytes 2097184 | tf_op jit(solution)/shard_map/all_to_all | solution.py:509
  82.8 11.3 %shard_map.300 = bf16[32,2,128,128]{3,2,1,0:T(8,128)(2,1)} custom-call(bf16[32,2,128,128]{3,2,1,0:T(8,128)(2,1)} %all-to-all-done.refs_0_, bf16[512,512]{1,0:T(8,128)(2,1)} %constant.99.clone.refs_1_.refs_3_, bf16[32,256,256]{2,1,0:T(8,128)(2,1)} %constant.101.clone.refs_2_.refs_4_, bf16[32,128,128]{2,1,0:T(8,128)(2,1)} %bitcast.65, ...), custom_call_target="tpu_custom_call" | custom-call | tf_op jit(solution)/shard_map/pallas_call | solution.py:517
  94.1 4.5 all-to-all-start.1
  98.6 6.5 %shard_map.301.refs_1_ = f32[32,64,256]{2,1,0:T(8,128)} custom-call(s32[1]{0:T(128)} %bitcast.1.place_ref, f32[1,512,1024]{2,1,0:T(8,128)} %bitcast.68, bf16[1024,1024]{1,0:T(8,128)(2,1)} %constant.98.clone.order_ref), custom_call_target="tpu_custom_call" | custom-call | tf_op jit(solution)/shard_map/pallas_call | solution.py:967
  106.5 6.6 %shard_map.302.refs_6_ = f32[32,64,256]{2,1,0:T(8,128)} custom-call(s32[1]{0:T(128)} %bitcast.1.place_ref, f32[2,512,1024]{2,1,0:T(8,128)} %noise_ref.1, bf16[1024,1024]{1,0:T(8,128)(2,1)} %constant.98.clone.order_ref), custom_call_target="tpu_custom_call" | custom-call | tf_op jit(solution)/shard_map/pallas_call | solution.py:967
  129.0 18.4 %all-to-all-done.1 = bf16[32,2,128,128]{3,2,1,0:T(8,128)(2,1)S(1)} async-done(((bf16[32,2,128,128]{3,2,1,0:T(8,128)(2,1)}), bf16[32,2,128,128]{3,2,1,0:T(8,128)(2,1)S(1)}, u32[]{:S(2)}, u32[]{:S(2)}) %all-to-all-start.1) | async-done | bytes 2097184 | tf_op jit(solution)/shard_map/all_to_all | solution.py:528
  148.6 7.2 %shard_map.303 = (bf16[8,64,256]{2,1,0:T(8,128)(2,1)}, bf16[8,64,256]{2,1,0:T(8,128)(2,1)}, bf16[8,64,256]{2,1,0:T(8,128)(2,1)}, bf16[8,64,256]{2,1,0:T(8,128)(2,1)}) custom-call(bf16[16,2,2,128,128]{4,3,2,1,0:T(8,128)(2,1)} %bitcast.69, bf16[256,512]{1,0:T(8,128)(2,1)} %pad_maximum_fusion.5.refs_4_.first_ref, ...), custom_call_target="tpu_custom_call" | custom-call | tf_op jit(solution)/shard_map/pallas_call | solution.py:531
  160.0 5.3 %collective-permute-done.3.refs_3_.refs_7_ = bf16[8,64,256]{2,1,0:T(8,128)(2,1)S(1)} collective-permute-done((bf16[8,64,256]{2,1,0:T(8,128)(2,1)}, bf16[8,64,256]{2,1,0:T(8,128)(2,1)S(1)}, u32[]{:S(2)}, u32[]{:S(2)}) %collective-permute-start.3) | collective-permute-done | bytes 262176 | tf_op jit(solution)/shard_map/ppermute | solution.py:466
  165.3 5.5 %collective-permute-done.4.refs_4_.refs_8_ = bf16[8,64,256]{2,1,0:T(8,128)(2,1)S(1)} collective-permute-done((bf16[8,64,256]{2,1,0:T(8,128)(2,1)}, bf16[8,64,256]{2,1,0:T(8,128)(2,1)S(1)}, u32[]{:S(2)}, u32[]{:S(2)}) %collective-permute-start.4) | collective-permute-done | bytes 262176 | tf_op jit(solution)/shard_map/ppermute | solution.py:466
  171.6 27.0 %shard_map.304 = (f32[32,64,256]{2,1,0:T(8,128)}, bf16[32,64,768]{2,1,0:T(8,128)(2,1)}, bf16[32,8,768]{2,1,0:T(8,128)(2,1)}, bf16[8,64,768]{2,1,0:T(8,128)(2,1)}, bf16[8,8,768]{2,1,0:T(8,128)(2,1)}) custom-call(s32[3]{0:T(128)} %pad_add_fusion.1.refs_0_, f32[32,64,256]{2,1,0:T(8,128)} %shard_map.301.refs_1_, ...), custom_call_target="tpu_custom_call" | custom-call | tf_op jit(solution)/shard_map/pallas_call | solution.py:806
  203.4 8.6 %collective-permute-done.8.refs_4_ = bf16[8,8,768]{2,1,0:T(8,128)(2,1)S(1)} collective-permute-done((bf16[8,8,768]{2,1,0:T(8,128)(2,1)}, bf16[8,8,768]{2,1,0:T(8,128)(2,1)S(1)}, u32[]{:S(2)}, u32[]{:S(2)}) %collective-permute-start.8) | collective-permute-done | bytes 98336 | tf_op jit(solution)/shard_map/ppermute | solution.py:860
  219.3 28.3 %shard_map.305 = (bf16[32,64,256]{2,1,0:T(8,128)(2,1)}, bf16[32,8,256]{2,1,0:T(8,128)(2,1)}, bf16[8,64,256]{2,1,0:T(8,128)(2,1)}, bf16[8,8,256]{2,1,0:T(8,128)(2...) custom-call(s32[3]{0:T(128)} %pad_add_fusion.1.refs_0_, ...), custom_call_target="tpu_custom_call" | custom-call | tf_op jit(solution)/shard_map/pallas_call | solution.py:833
  257.1 6.8 %collective-permute-done.12.refs_2_ = bf16[8,64,256]{2,1,0:T(8,128)(2,1)S(1)} collective-permute-done((bf16[8,64,256]{2,1,0:T(8,128)(2,1)}, bf16[8,64,256]{2,1,0:T(8,128)(2,1)S(1)}, u32[]{:S(2)}, u32[]{:S(2)}) %collective-permute-start.12) | collective-permute-done | bytes 262176 | tf_op jit(solution)/shard_map/ppermute | solution.py:466
  265.4 5.7 %shard_map.306 = bf16[16,2,128,128]{3,2,1,0:T(8,128)(2,1)} custom-call(bf16[8,64,256]{2,1,0:T(8,128)(2,1)} %get-tuple-element.108.refs_0_, bf16[8,64,256]{2,1,0:T(8,128)(2,1)} %copy-done.26, bf16[8,64,256]{2,1,0:T(8,128)(2,1)} %copy-done.27, bf16[8,64,256]{2,1,0:T(8,128)(2,1)} %copy-done.28, bf16[256,512]{1,0:T(8,128)(2,1)} %pad_maximum_fusion.6.refs_4_, ...), custom_call_target="tpu_custom_call" | custom-call | tf_op jit(solution)/shard_map/pallas_call | solution.py:502
  280.5 5.4 %shard_map.307.refs_5_ = bf16[32,128,128]{2,1,0:T(8,128)(2,1)} custom-call(bf16[32,128,128]{2,1,0:T(8,128)(2,1)} %bitcast.66, bf16[32,128,128]{2,1,0:T(8,128)(2,1)} %bitcast.71, bf16[2,128,128]{2,1,0:T(8,128)(2,1)} %add_convert_fusion.pick_ref, bf16[2,128,128]{2,1,0:T(8,128)(2,1)} %constant.113.clone.flip_ref), custom_call_target="tpu_custom_call" | custom-call | tf_op jit(solution)/shard_map/pallas_call | solution.py:447
  285.9 15.9 %all-to-all-done.2.refs_2_ = bf16[32,128,128]{2,1,0:T(8,128)(2,1)S(1)} async-done(((bf16[32,128,128]{2,1,0:T(8,128)(2,1)}), bf16[32,128,128]{2,1,0:T(8,128)(2,1)S(1)}, u32[]{:S(2)}, u32[]{:S(2)}) %all-to-all-start.2) | async-done | bytes 1048608 | tf_op jit(solution)/shard_map/all_to_all | solution.py:509
  305.8 10.2 %shard_map.308 = bf16[32,128,128]{2,1,0:T(8,128)(2,1)} custom-call(s32[1]{0:T(128)} %bitcast.28.refs_0_, f32[32,2,8,128]{3,2,1,0:T(8,128)} %broadcast_in_dim.79.refs_1_, bf16[32,128,128]{2,1,0:T(8,128)(2,1)} %copy-done.1, bf16[512,512]{1,0:T(8,128)(2,1)} %constant.99.clone.refs_1_.refs_3_, bf16[32,256,256]{2,1,0:T(8,128)(2,1)} %constant.101.clone.refs_2_.refs_4_, ...), custom_call_target="tpu_custom_call" | custom-call | tf_op jit(solution)/shard_map/pallas_call | solution.py:517
  316.1 5.0 %all-to-all-start.3 = ((bf16[32,128,128]{2,1,0:T(8,128)(2,1)}), bf16[32,128,128]{2,1,0:T(8,128)(2,1)S(1)}, u32[]{:S(2)}, u32[]{:S(2)}) async-start(bf16[32,128,128]{2,1,0:T(8,128)(2,1)} %shard_map.308), calls=%async_computation.3 | async-start | bytes 2097152 | tf_op jit(solution)/shard_map/all_to_all | solution.py:528
  321.9 25.7 %all-to-all-done.3 = bf16[32,128,128]{2,1,0:T(8,128)(2,1)S(1)} async-done(((bf16[32,128,128]{2,1,0:T(8,128)(2,1)}), bf16[32,128,128]{2,1,0:T(8,128)(2,1)S(1)}, u32[]{:S(2)}, u32[]{:S(2)}) %all-to-all-start.3) | async-done | bytes 1048608 | tf_op jit(solution)/shard_map/all_to_all | solution.py:528
  348.5 6.1 %shard_map.309 = (bf16[8,64,256]{2,1,0:T(8,128)(2,1)}, bf16[8,64,256]{2,1,0:T(8,128)(2,1)}, bf16[8,64,256]{2,1,0:T(8,128)(2,1)}, bf16[8,64,256]{2,1,0:T(8,128)(2,1)}) custom-call(bf16[16,2,128,128]{3,2,1,0:T(8,128)(2,1)} %bitcast.74, bf16[256,512]{1,0:T(8,128)(2,1)} %pad_maximum_fusion.7.first_ref, f32[2,256,256]{2,1,0:T(8,128)} %constant.107.clone.refs_5_.twist_ref, ...), custom_call_target="tpu_custom_call" | custom-call | tf_op jit(solution)/shard_map/pallas_call | solution.py:531
  358.1 5.9 %collective-permute-done.17.refs_11_ = bf16[8,64,256]{2,1,0:T(8,128)(2,1)S(1)} collective-permute-done((bf16[8,64,256]{2,1,0:T(8,128)(2,1)}, bf16[8,64,256]{2,1,0:T(8,128)(2,1)S(1)}, u32[]{:S(2)}, u32[]{:S(2)}) %collective-permute-start.17) | collective-permute-done | bytes 262176 | tf_op jit(solution)/shard_map/ppermute | solution.py:466
  370.5 26.6 %shard_map.310 = (f32[32,64,256]{2,1,0:T(8,128)}, bf16[32,64,512]{2,1,0:T(8,128)(2,1)}, bf16[32,8,512]{2,1,0:T(8,128)(2,1)}, bf16[8,64,512]{2,1,0:T(8,128)(2,1)}, bf16[8,8,512]{2,1,0:T(8,128)(2,1)}) custom-call(s32[3]{0:T(128)} %pad_add_fusion.1.refs_0_, f32[32,64,256]{2,1,0:T(8,128)} %get-tuple-element.89.refs_1_, ...), custom_call_target="tpu_custom_call" | custom-call | tf_op jit(solution)/shard_map/pallas_call | solution.py:806
  401.5 6.0 %collective-permute-done.22.refs_4_ = bf16[8,8,512]{2,1,0:T(8,128)(2,1)S(1)} collective-permute-done((bf16[8,8,512]{2,1,0:T(8,128)(2,1)}, bf16[8,8,512]{2,1,0:T(8,128)(2,1)S(1)}, u32[]{:S(2)}, u32[]{:S(2)}) %collective-permute-start.22) | collective-permute-done | bytes 65568 | tf_op jit(solution)/shard_map/ppermute | solution.py:860
  408.5 26.2 %shard_map.312 = (bf16[32,64,256]{2,1,0:T(8,128)(2,1)}, bf16[32,8,256]{2,1,0:T(8,128)(2,1)}, bf16[8,64,256]{2,1,0:T(8,128)(2,1)}, bf16[8,8,256]{2,1,0:T(8,128)(2,1)}) custom-call(s32[3]{0:T(128)} %pad_add_fusion.refs_0_.shift_ref, bf16[32,64,512]{2,1,0:T(8,128)(2,1)} %get-tuple-element.138.refs_1_, bf16[32,8,512]{2,1,0:T(8,128)(2,1)} %copy-done.12, ...), custom_call_target="tpu_custom_call" | custom-call | tf_op jit(solution)/shard_map/pallas_call | solution.py:833
  436.9 6.9 %shard_map.311.tile_ref = f32[512,1024]{1,0:T(8,128)} custom-call(f32[32,64,256]{2,1,0:T(8,128)} %get-tuple-element.137.base_ref, f32[2,512,1024]{2,1,0:T(8,128)} %noise_ref.1, bf16[1024,1024]{1,0:T(8,128)(2,1)} %constant.114.clone.order_ref.refs_4_), custom_call_target="tpu_custom_call" | custom-call | tf_op jit(solution)/shard_map/pallas_call | solution.py:988
  445.9 7.1 %shard_map.313 = f32[512,1024]{1,0:T(8,128)} custom-call(s32[3]{0:T(128)} %pad_add_fusion.refs_0_.shift_ref, f32[512,1024]{1,0:T(8,128)} %shard_map.311.tile_ref, bf16[32,64,256]{2,1,0:T(8,128)(2,1)} %get-tuple-element.143.refs_0_, bf16[32,8,256]{2,1,0:T(8,128)(2,1)} %copy-done.36, bf16[8,64,256]{2,1,0:T(8,128)(2,1)} %copy-done.16, ...), custom_call_target="tpu_custom_call" | custom-call | tf_op jit(solution)/shard_map/pallas_call | solution.py:1000
  (198 shorter events, 108.6 us)
Async XLA Ops:
  5.7 10.3 %collective-permute-start = (bf16[8,64,256]{2,1,0:T(8,128)(2,1)}, bf16[8,64,256]{2,1,0:T(8,128)(2,1)S(1)}, u32[]{:S(2)}, u32[]{:S(2)}) collective-permute-start(bf16[8,64,256]{2,1,0:T(8,128)(2,1)} %get-tuple-element.77), channel_id=1, source_target_pairs={{0,1},{1,0},{2,3},{3,2},{4,5},{5,4},{6,7},{7,6},{8,9},{9,8},{10,11... | collective-permute-start | bytes 786440 | tf_op jit(solution)/shard_map/ppermute | solution.py:466
  8.6 13.6 %collective-permute-start.1 = (bf16[8,64,256]{2,1,0:T(8,128)(2,1)}, bf16[8,64,256]{2,1,0:T(8,128)(2,1)S(1)}, u32[]{:S(2)}, u32[]{:S(2)}) collective-permute-start(bf16[8,64,256]{2,1,0:T(8,128)(2,1)} %get-tuple-element.78), channel_id=1, source_target_pairs={{0,2},{1,3},{2,0},{3,1},{4,6},{5,7},{6,4},{7,5},{8,10},{9,11},{10,... | collective-permute-start | bytes 786440 | tf_op jit(solution)/shard_map/ppermute | solution.py:466
  10.1 12.1 %collective-permute-start.2 = (bf16[8,64,256]{2,1,0:T(8,128)(2,1)}, bf16[8,64,256]{2,1,0:T(8,128)(2,1)S(1)}, u32[]{:S(2)}, u32[]{:S(2)}) collective-permute-start(bf16[8,64,256]{2,1,0:T(8,128)(2,1)} %get-tuple-element.79), channel_id=1, source_target_pairs={{0,3},{1,2},{2,1},{3,0},{4,7},{5,6},{6,5},{7,4},{8,11},{9,10},{10,... | collective-permute-start | bytes 786440 | tf_op jit(solution)/shard_map/ppermute | solution.py:466
  28.5 54.3 %all-to-all-start = ((bf16[32,2,128,128]{3,2,1,0:T(8,128)(2,1)}), bf16[32,2,128,128]{3,2,1,0:T(8,128)(2,1)}, u32[]{:S(2)}, u32[]{:S(2)}) async-start(bf16[32,2,128,128]{3,2,1,0:T(8,128)(2,1)} %bitcast.70), calls=%async_computation | async-start | bytes 4194304 | tf_op jit(solution)/shard_map/all_to_all | solution.py:509
  94.1 53.2 %all-to-all-start.1 = ((bf16[32,2,128,128]{3,2,1,0:T(8,128)(2,1)}), bf16[32,2,128,128]{3,2,1,0:T(8,128)(2,1)S(1)}, u32[]{:S(2)}, u32[]{:S(2)}) async-start(bf16[32,2,128,128]{3,2,1,0:T(8,128)(2,1)} %shard_map.300), calls=%async_computation.1 | async-start | bytes 4194304 | tf_op jit(solution)/shard_map/all_to_all | solution.py:528
  155.9 9.4 %collective-permute-start.3 = (bf16[8,64,256]{2,1,0:T(8,128)(2,1)}, bf16[8,64,256]{2,1,0:T(8,128)(2,1)S(1)}, u32[]{:S(2)}, u32[]{:S(2)}) collective-permute-start(bf16[8,64,256]{2,1,0:T(8,128)(2,1)} %get-tuple-element.83), channel_id=1, source_target_pairs={{0,1},{1,0},{2,3},{3,2},{4,5},{5,4},{6,7},{7,6},{8,9},{9,8},{10,11... | collective-permute-start | bytes 786440 | tf_op jit(solution)/shard_map/ppermute | solution.py:466
  157.4 13.4 %collective-permute-start.4 = (bf16[8,64,256]{2,1,0:T(8,128)(2,1)}, bf16[8,64,256]{2,1,0:T(8,128)(2,1)S(1)}, u32[]{:S(2)}, u32[]{:S(2)}) collective-permute-start(bf16[8,64,256]{2,1,0:T(8,128)(2,1)} %get-tuple-element.84), channel_id=1, source_target_pairs={{0,2},{1,3},{2,0},{3,1},{4,6},{5,7},{6,4},{7,5},{8,10},{9,11},{10,... | collective-permute-start | bytes 786440 | tf_op jit(solution)/shard_map/ppermute | solution.py:466
  158.8 11.9 %collective-permute-start.5 = (bf16[8,64,256]{2,1,0:T(8,128)(2,1)}, bf16[8,64,256]{2,1,0:T(8,128)(2,1)S(1)}, u32[]{:S(2)}, u32[]{:S(2)}) collective-permute-start(bf16[8,64,256]{2,1,0:T(8,128)(2,1)} %get-tuple-element.85), channel_id=1, source_target_pairs={{0,3},{1,2},{2,1},{3,0},{4,7},{5,6},{6,5},{7,4},{8,11},{9,10},{10,... | collective-permute-start | bytes 786440 | tf_op jit(solution)/shard_map/ppermute | solution.py:466
  171.6 41.7 %copy-start.2 = (bf16[64,4096]{0,1:T(8,128)(2,1)S(1)}, bf16[64,4096]{0,1:T(8,128)(2,1)}, u32[]{:S(2)}) copy-start(bf16[64,4096]{0,1:T(8,128)(2,1)} %slice.57) | copy-start | bytes 1572868
  198.6 13.9 %collective-permute-start.7 = (bf16[8,64,768]{2,1,0:T(8,128)(2,1)}, bf16[8,64,768]{2,1,0:T(8,128)(2,1)S(1)}, u32[]{:S(2)}, u32[]{:S(2)}) collective-permute-start(bf16[8,64,768]{2,1,0:T(8,128)(2,1)} %get-tuple-element.92), channel_id=1, source_target_pairs={{0,28},{4,0},{8,4},{12,8},{16,12},{20,16},{24,20},{28,24},{1,29},{... | collective-permute-start | bytes 2359304 | tf_op jit(solution)/shard_map/ppermute | solution.py:859
  199.7 12.8 %collective-permute-start.6 = (bf16[32,8,768]{2,1,0:T(8,128)(2,1)}, bf16[32,8,768]{2,1,0:T(8,128)(2,1)S(1)}, u32[]{:S(2)}, u32[]{:S(2)}) collective-permute-start(bf16[32,8,768]{2,1,0:T(8,128)(2,1)} %get-tuple-element.91), channel_id=1, source_target_pairs={{0,3},{1,0},{2,1},{3,2},{4,7},{5,4},{6,5},{7,6},{8,11},{9,8},{10,9... | collective-permute-start | bytes 1179656 | tf_op jit(solution)/shard_map/ppermute | solution.py:858
  200.4 11.6 %collective-permute-start.8 = (bf16[8,8,768]{2,1,0:T(8,128)(2,1)}, bf16[8,8,768]{2,1,0:T(8,128)(2,1)S(1)}, u32[]{:S(2)}, u32[]{:S(2)}) collective-permute-start(bf16[8,8,768]{2,1,0:T(8,128)(2,1)} %get-tuple-element.93), channel_id=1, source_target_pairs={{0,31},{1,28},{2,29},{3,30},{4,3},{5,0},{6,1},{7,2},{8,7},{9,4},{1... | collective-permute-start | bytes 294920 | tf_op jit(solution)/shard_map/ppermute | solution.py:860
  214.5 33.2 %collective-permute-start.9 = (bf16[64,4096]{1,0:T(8,128)(2,1)}, bf16[64,4096]{1,0:T(8,128)(2,1)S(1)}, u32[]{:S(2)}, u32[]{:S(2)}) collective-permute-start(bf16[64,4096]{1,0:T(8,128)(2,1)} %copy.85), channel_id=1, source_target_pairs={{0,31},{1,30},{2,29},{3,28},{4,27},{5,26},{6,25},{7,24},{8,23},{9,... | collective-permute-start | bytes 1572872 | tf_op jit(solution)/shard_map/ppermute | solution.py:427
  218.4 29.3 %collective-permute-start.10 = (bf16[1,4096]{1,0:T(2,128)(2,1)S(1)}, bf16[1,4096]{1,0:T(2,128)(2,1)S(1)}, u32[]{:S(2)}, u32[]{:S(2)}) collective-permute-start(bf16[1,4096]{1,0:T(2,128)(2,1)S(1)} %copy.86), channel_id=1, source_target_pairs={{1,31},{2,30},{3,29},{4,28},{5,27},{6,26},{7,25},{8,24},{9,23},{10... | collective-permute-start | bytes 24584 | tf_op jit(solution)/shard_map/ppermute | solution.py:428
  247.7 9.4 %collective-permute-start.11 = (bf16[8,64,256]{2,1,0:T(8,128)(2,1)}, bf16[8,64,256]{2,1,0:T(8,128)(2,1)S(1)}, u32[]{:S(2)}, u32[]{:S(2)}) collective-permute-start(bf16[8,64,256]{2,1,0:T(8,128)(2,1)} %get-tuple-element.109), channel_id=1, source_target_pairs={{0,1},{1,0},{2,3},{3,2},{4,5},{5,4},{6,7},{7,6},{8,9},{9,8},{10,11... | collective-permute-start | bytes 786440 | tf_op jit(solution)/shard_map/ppermute | solution.py:466
  250.1 13.9 %collective-permute-start.12 = (bf16[8,64,256]{2,1,0:T(8,128)(2,1)}, bf16[8,64,256]{2,1,0:T(8,128)(2,1)S(1)}, u32[]{:S(2)}, u32[]{:S(2)}) collective-permute-start(bf16[8,64,256]{2,1,0:T(8,128)(2,1)} %get-tuple-element.110), channel_id=1, source_target_pairs={{0,2},{1,3},{2,0},{3,1},{4,6},{5,7},{6,4},{7,5},{8,10},{9,11},{10,... | collective-permute-start | bytes 786440 | tf_op jit(solution)/shard_map/ppermute | solution.py:466
  251.6 12.4 %collective-permute-start.13 = (bf16[8,64,256]{2,1,0:T(8,128)(2,1)}, bf16[8,64,256]{2,1,0:T(8,128)(2,1)S(1)}, u32[]{:S(2)}, u32[]{:S(2)}) collective-permute-start(bf16[8,64,256]{2,1,0:T(8,128)(2,1)} %get-tuple-element.111), channel_id=1, source_target_pairs={{0,3},{1,2},{2,1},{3,0},{4,7},{5,6},{6,5},{7,4},{8,11},{9,10},{10,... | collective-permute-start | bytes 786440 | tf_op jit(solution)/shard_map/ppermute | solution.py:466
  271.2 30.6 %all-to-all-start.2 = ((bf16[32,128,128]{2,1,0:T(8,128)(2,1)}), bf16[32,128,128]{2,1,0:T(8,128)(2,1)S(1)}, u32[]{:S(2)}, u32[]{:S(2)}) async-start(bf16[32,128,128]{2,1,0:T(8,128)(2,1)} %bitcast.73), calls=%async_computation.2 | async-start | bytes 2097152 | tf_op jit(solution)/shard_map/all_to_all | solution.py:509
  301.8 14.2 %collective-permute-start.14 = (bf16[32,8,256]{2,1,0:T(8,128)(2,1)S(1)}, bf16[32,8,256]{2,1,0:T(8,128)(2,1)S(1)}, u32[]{:S(2)}, u32[]{:S(2)}) collective-permute-start(bf16[32,8,256]{2,1,0:T(8,128)(2,1)S(1)} %copy-done.46), channel_id=1, source_target_pairs={{0,1},{1,2},{2,3},{3,0},{4,5},{5,6},{6,7},{7,4},{8,9},{9,10},{10,1... | collective-permute-start | bytes 393224 | tf_op jit(solution)/shard_map/ppermute | solution.py:858
  303.1 12.9 %collective-permute-start.15 = (bf16[8,64,256]{2,1,0:T(8,128)(2,1)S(1)}, bf16[8,64,256]{2,1,0:T(8,128)(2,1)S(1)}, u32[]{:S(2)}, u32[]{:S(2)}) collective-permute-start(bf16[8,64,256]{2,1,0:T(8,128)(2,1)S(1)} %copy-done.45), channel_id=1, source_target_pairs={{0,4},{4,8},{8,12},{12,16},{16,20},{20,24},{24,28},{28,0},{1,5},{5... | collective-permute-start | bytes 786440 | tf_op jit(solution)/shard_map/ppermute | solution.py:859
  303.3 12.7 %collective-permute-start.16 = (bf16[8,8,256]{2,1,0:T(8,128)(2,1)S(1)}, bf16[8,8,256]{2,1,0:T(8,128)(2,1)S(1)}, u32[]{:S(2)}, u32[]{:S(2)}) collective-permute-start(bf16[8,8,256]{2,1,0:T(8,128)(2,1)S(1)} %copy-done.47), channel_id=1, source_target_pairs={{0,5},{1,6},{2,7},{3,4},{4,9},{5,10},{6,11},{7,8},{8,13},{9,14},{1... | collective-permute-start | bytes 98312 | tf_op jit(solution)/shard_map/ppermute | solution.py:860
  316.0 38.6 %copy-start.39 = (bf16[8,8,256]{2,1,0:T(8,128)(2,1)}, bf16[8,8,256]{2,1,0:T(8,128)(2,1)S(1)}, u32[]{:S(2)}) copy-start(bf16[8,8,256]{2,1,0:T(8,128)(2,1)S(1)} %collective-permute-done.16.refs_5_) | copy-start | bytes 98308
  316.1 31.5 %all-to-all-start.3 = ((bf16[32,128,128]{2,1,0:T(8,128)(2,1)}), bf16[32,128,128]{2,1,0:T(8,128)(2,1)S(1)}, u32[]{:S(2)}, u32[]{:S(2)}) async-start(bf16[32,128,128]{2,1,0:T(8,128)(2,1)} %shard_map.308), calls=%async_computation.3 | async-start | bytes 2097152 | tf_op jit(solution)/shard_map/all_to_all | solution.py:528
  354.6 9.5 %collective-permute-start.17 = (bf16[8,64,256]{2,1,0:T(8,128)(2,1)}, bf16[8,64,256]{2,1,0:T(8,128)(2,1)S(1)}, u32[]{:S(2)}, u32[]{:S(2)}) collective-permute-start(bf16[8,64,256]{2,1,0:T(8,128)(2,1)} %get-tuple-element.134), channel_id=1, source_target_pairs={{0,1},{1,0},{2,3},{3,2},{4,5},{5,4},{6,7},{7,6},{8,9},{9,8},{10,11... | collective-permute-start | bytes 786440 | tf_op jit(solution)/shard_map/ppermute | solution.py:466
  356.0 12.3 %collective-permute-start.18 = (bf16[8,64,256]{2,1,0:T(8,128)(2,1)}, bf16[8,64,256]{2,1,0:T(8,128)(2,1)S(1)}, u32[]{:S(2)}, u32[]{:S(2)}) collective-permute-start(bf16[8,64,256]{2,1,0:T(8,128)(2,1)} %get-tuple-element.135), channel_id=1, source_target_pairs={{0,2},{1,3},{2,0},{3,1},{4,6},{5,7},{6,4},{7,5},{8,10},{9,11},{10,... | collective-permute-start | bytes 786440 | tf_op jit(solution)/shard_map/ppermute | solution.py:466
  357.4 12.4 %collective-permute-start.19 = (bf16[8,64,256]{2,1,0:T(8,128)(2,1)}, bf16[8,64,256]{2,1,0:T(8,128)(2,1)S(1)}, u32[]{:S(2)}, u32[]{:S(2)}) collective-permute-start(bf16[8,64,256]{2,1,0:T(8,128)(2,1)} %get-tuple-element.136), channel_id=1, source_target_pairs={{0,3},{1,2},{2,1},{3,0},{4,7},{5,6},{6,5},{7,4},{8,11},{9,10},{10,... | collective-permute-start | bytes 786440 | tf_op jit(solution)/shard_map/ppermute | solution.py:466
  397.2 10.4 %collective-permute-start.21 = (bf16[8,64,512]{2,1,0:T(8,128)(2,1)}, bf16[8,64,512]{2,1,0:T(8,128)(2,1)S(1)}, u32[]{:S(2)}, u32[]{:S(2)}) collective-permute-start(bf16[8,64,512]{2,1,0:T(8,128)(2,1)} %get-tuple-element.140), channel_id=1, source_target_pairs={{0,28},{4,0},{8,4},{12,8},{16,12},{20,16},{24,20},{28,24},{1,29},{... | collective-permute-start | bytes 1572872 | tf_op jit(solution)/shard_map/ppermute | solution.py:859
  397.2 10.3 %collective-permute-start.20 = (bf16[32,8,512]{2,1,0:T(8,128)(2,1)}, bf16[32,8,512]{2,1,0:T(8,128)(2,1)S(1)}, u32[]{:S(2)}, u32[]{:S(2)}) collective-permute-start(bf16[32,8,512]{2,1,0:T(8,128)(2,1)} %get-tuple-element.139), channel_id=1, source_target_pairs={{0,3},{1,0},{2,1},{3,2},{4,7},{5,4},{6,5},{7,6},{8,11},{9,8},{10,9... | collective-permute-start | bytes 786440 | tf_op jit(solution)/shard_map/ppermute | solution.py:858
  399.2 8.4 %collective-permute-start.22 = (bf16[8,8,512]{2,1,0:T(8,128)(2,1)}, bf16[8,8,512]{2,1,0:T(8,128)(2,1)S(1)}, u32[]{:S(2)}, u32[]{:S(2)}) collective-permute-start(bf16[8,8,512]{2,1,0:T(8,128)(2,1)} %get-tuple-element.141), channel_id=1, source_target_pairs={{0,31},{1,28},{2,29},{3,30},{4,3},{5,0},{6,1},{7,2},{8,7},{9,4},{1... | collective-permute-start | bytes 196616 | tf_op jit(solution)/shard_map/ppermute | solution.py:860
  434.7 10.4 %collective-permute-start.24 = (bf16[8,64,256]{2,1,0:T(8,128)(2,1)}, bf16[8,64,256]{2,1,0:T(8,128)(2,1)S(1)}, u32[]{:S(2)}, u32[]{:S(2)}) collective-permute-start(bf16[8,64,256]{2,1,0:T(8,128)(2,1)} %get-tuple-element.145), channel_id=1, source_target_pairs={{0,4},{4,8},{8,12},{12,16},{16,20},{20,24},{24,28},{28,0},{1,5},{5... | collective-permute-start | bytes 786440 | tf_op jit(solution)/shard_map/ppermute | solution.py:859
  434.7 10.4 %collective-permute-start.23 = (bf16[32,8,256]{2,1,0:T(8,128)(2,1)}, bf16[32,8,256]{2,1,0:T(8,128)(2,1)S(1)}, u32[]{:S(2)}, u32[]{:S(2)}) collective-permute-start(bf16[32,8,256]{2,1,0:T(8,128)(2,1)} %get-tuple-element.144), channel_id=1, source_target_pairs={{0,1},{1,2},{2,3},{3,0},{4,5},{5,6},{6,7},{7,4},{8,9},{9,10},{10,1... | collective-permute-start | bytes 393224 | tf_op jit(solution)/shard_map/ppermute | solution.py:858
  436.2 8.9 %collective-permute-start.25 = (bf16[8,8,256]{2,1,0:T(8,128)(2,1)}, bf16[8,8,256]{2,1,0:T(8,128)(2,1)S(1)}, u32[]{:S(2)}, u32[]{:S(2)}) collective-permute-start(bf16[8,8,256]{2,1,0:T(8,128)(2,1)} %get-tuple-element.146), channel_id=1, source_target_pairs={{0,5},{1,6},{2,7},{3,4},{4,9},{5,10},{6,11},{7,8},{8,13},{9,14},{1... | collective-permute-start | bytes 98312 | tf_op jit(solution)/shard_map/ppermute | solution.py:860
  (46 other events, 486.1 us)
